TPU v7x, 32 devices: a whole 2x2x4 slice. The times are simulated.
32 devices in a mesh: ty: 8 (over y, x, core), tx: 4 (over z).
Axes of the slice: x: 2, y: 2, z: 4, core: 2. Of those that a mesh axis runs over, the one named last changes fastest.
Arguments:
- spectrum: float32 [2, 4096, 4096], P(None, 'ty', 'tx'), may hold values from -6 to 6
- pupil: float32 [2, 512, 512], replicated, may hold values from -6 to 6
- amplitudes: float32 [96, 512, 512], P(('ty', 'tx')), may hold values from 0 to 3
- offsets: int32 [96, 2], P(('ty', 'tx')), may hold values from 0 to 3584, as said below
- live: int32 [96], P(('ty', 'tx')), may hold values from 0 to 1, as said below
Outputs:
- spectrum_grad: float32 [2, 4096, 4096], P(None, 'ty', 'tx')
- pupil_grad: float32 [2, 512, 512], replicated
Inputs may be any that keep to these rules, and one draw needn't show every extreme that they name: `offsets`: the slots of the device at ty index i and tx index j are i * 4 * 3 + j * 3 to that plus 3 - 1; each such slot's corner has row in [i * 512, (i + 1) * 512) and column in [j * 1024, (j + 1) * 1024), and its window lies inside the spectrum. Each device's live slots come first among its 3 slots, and every device has at least one. Two devices with the same tx index whose ty indices differ by 4 hold together at most 4 live slots; some such pair holds exactly that many, and some device has all 3 slots live.
All inputs are finite; a program needn't handle non-finite values.
Results may differ from a plain program's by a relative error of at most 0.0001.
Values sent between devices are 32-bit elements; how exact they have to be, the bound alone decides.
No kernel may reach another device: no remote copies, remote signals or barrier semaphores. Data moves between devices by JAX's collectives and lax.ppermute only.
A program may use at most 192 MiB of HBM per device.

v0:
```python
import math

import jax
import jax.numpy as jnp
from jax import lax
from jax.sharding import PartitionSpec as P

exact_mode = lax.Precision.HIGHEST


def from_behind(array, axis, by):
    devices = lax.axis_size(axis)
    pairs = [(i, i + by) for i in range(devices) if 0 <= i + by < devices]
    return lax.ppermute(array, axis, pairs)


def dft_tables(length):
    indices = jnp.arange(length, dtype=jnp.int32)
    phases = indices[:, None] * indices[None, :] % length
    angles = phases.astype(jnp.float32) * (2.0 * math.pi / length)
    factor = 1.0 / math.sqrt(length)
    return (jnp.cos(angles) * factor, -jnp.sin(angles) * factor)


def left_product(mat_re, mat_im, val_re, val_im):
    out_re = jnp.einsum("km,smn->skn", mat_re, val_re, precision=exact_mode) - jnp.einsum(
        "km,smn->skn", mat_im, val_im, precision=exact_mode
    )
    out_im = jnp.einsum("km,smn->skn", mat_re, val_im, precision=exact_mode) + jnp.einsum(
        "km,smn->skn", mat_im, val_re, precision=exact_mode
    )
    return (out_re, out_im)


def right_product(val_re, val_im, mat_re, mat_im):
    out_re = jnp.einsum("smn,nk->smk", val_re, mat_re, precision=exact_mode) - jnp.einsum(
        "smn,nk->smk", val_im, mat_im, precision=exact_mode
    )
    out_im = jnp.einsum("smn,nk->smk", val_re, mat_im, precision=exact_mode) + jnp.einsum(
        "smn,nk->smk", val_im, mat_re, precision=exact_mode
    )
    return (out_re, out_im)


def led_terms(windows, measured, pupil, weights):
    cosine, sine = dft_tables(measured.shape[-1])
    win_re = windows[:, 0]
    win_im = windows[:, 1]
    pup_re = pupil[0]
    pup_im = pupil[1]
    prod_re = win_re * pup_re - win_im * pup_im
    prod_im = win_re * pup_im + win_im * pup_re
    half_re, half_im = left_product(cosine, -sine, prod_re, prod_im)
    field_re, field_im = right_product(half_re, half_im, cosine, -sine)
    modulus = jnp.sqrt(field_re * field_re + field_im * field_im + 1.0)
    factor = 1.0 - measured / modulus
    half_re, half_im = left_product(cosine, sine, factor * field_re, factor * field_im)
    back_re, back_im = right_product(half_re, half_im, cosine, sine)
    masks = weights[:, None, None]
    dwin_re = (pup_re * back_re + pup_im * back_im) * masks
    dwin_im = (pup_re * back_im - pup_im * back_re) * masks
    dpup_re = jnp.sum((win_re * back_re + win_im * back_im) * masks, axis=0)
    dpup_im = jnp.sum((win_re * back_im - win_im * back_re) * masks, axis=0)
    return (jnp.stack([dwin_re, dwin_im], axis=1), jnp.stack([dpup_re, dpup_im], axis=0))


def cut_windows(region, rows_local, cols_local, window):
    zero_idx = jnp.zeros((), jnp.int32)
    pieces = [
        lax.dynamic_slice(
            region, (zero_idx, rows_local[number], cols_local[number]), (2, window, window)
        )
        for number in range(rows_local.shape[0])
    ]
    return jnp.stack(pieces, axis=0)


def place_windows(grads, rows_local, cols_local, shape):
    zero_idx = jnp.zeros((), jnp.int32)
    window = grads.shape[-1]
    region = jnp.zeros(shape, jnp.float32)
    for number in range(grads.shape[0]):
        start = (zero_idx, rows_local[number], cols_local[number])
        current = lax.dynamic_slice(region, start, (2, window, window))
        region = lax.dynamic_update_slice(region, current + grads[number], start)
    return region


def body(spectrum, pupil, amplitudes, offsets, live):
    window = pupil.shape[-1]
    tile_rows = spectrum.shape[1]
    tile_cols = spectrum.shape[2]
    rows_local = offsets[:, 0] - lax.axis_index("ty") * tile_rows
    cols_local = offsets[:, 1] - lax.axis_index("tx") * tile_cols
    right_strip = from_behind(spectrum[:, :, :window], "tx", -1)
    widened = jnp.concatenate([spectrum, right_strip], axis=2)
    lower_strip = from_behind(widened, "ty", -1)
    region = jnp.concatenate([widened, lower_strip], axis=1)
    windows = cut_windows(region, rows_local, cols_local, window)
    weights = live.astype(jnp.float32)
    dwin, dpup = led_terms(windows, amplitudes, pupil, weights)
    grad_region = place_windows(dwin, rows_local, cols_local, region.shape)
    back_lower = from_behind(grad_region[:, tile_rows:, :], "ty", 1)
    wide_grad = grad_region[:, :tile_rows, :].at[:, :window, :].add(back_lower)
    back_right = from_behind(wide_grad[:, :, tile_cols:], "tx", 1)
    spec_grad = wide_grad[:, :, :tile_cols].at[:, :, :window].add(back_right)
    pupil_total = lax.psum(dpup, ("ty", "tx"))
    norm_scale = 1.0 / math.sqrt(lax.axis_size("ty") * lax.axis_size("tx"))
    return (spec_grad, pupil_total * norm_scale)


def solution(mesh):
    return jax.shard_map(
        body,
        mesh=mesh,
        in_specs=(
            P(None, "ty", "tx"),
            P(),
            P(("ty", "tx"), None, None),
            P(("ty", "tx"), None),
            P(("ty", "tx")),
        ),
        out_specs=(P(None, "ty", "tx"), P()),
        check_vma=False,
    )
```

profile of v0, /device:TPU:1, one launch (start us, length us, event | category | flops | bytes accessed | tf_op | source)
XLA Modules:
  0.0 651.0 jit_solution(13505408591087890078)
XLA Ops:
  7.2 0.0 all-reduce.2.cloned.1.call-start
  7.2 0.0 copy-start.6
  7.2 1.9 slice.117
  9.1 1.3 collective-permute-start
  10.4 0.0 copy-done.6
  10.5 2.3 constant_dynamic-update-slice_fusion.1
  12.8 45.7 %collective-permute-done = f32[2,512,512]{2,1,0:T(8,128)S(1)} collective-permute-done((f32[2,512,512]{2,1,0:T(8,128)S(1)}, f32[2,512,512]{2,1,0:T(8,128)S(1)}, u32[]{:S(2)}, u32[]{:S(2)}) %collective-permute-start) | collective-permute-done | bytes 2097184 | tf_op jit(solution)/shard_map/ppermute | solution.py:14
  58.5 1.5 constant_dynamic-update-slice_fusion
  60.1 3.1 collective-permute-start.1
  63.2 0.0 copy-done.10
  63.2 0.7 fusion.158
  71.7 0.0 copy-done.11
  75.5 0.0 copy-done.9
  75.5 0.2 slice_bitcast_fusion.3
  75.7 57.7 %collective-permute-done.1 = f32[2,512,1536]{2,1,0:T(8,128)} collective-permute-done((f32[2,512,1536]{2,1,0:T(8,128)}, f32[2,512,1536]{2,1,0:T(8,128)}, u32[]{:S(2)}, u32[]{:S(2)}) %collective-permute-start.1) | collective-permute-done | bytes 6291488 | tf_op jit(solution)/shard_map/ppermute | solution.py:14
  133.4 7.0 %fusion.26 = (f32[1,2,512,512]{3,2,0,1:T(8,128)S(1)}, f32[1,2,512,512]{3,2,0,1:T(8,128)S(1)}, f32[1,2,512,512]{3,2,0,1:T(8,128)S(1)}) fusion(s32[]{:T(128)S(6)} %select_n.65, s32[]{:T(128)S(6)} %select_n.66, f32[2,512,1536]{2,1,0:T(8,128)} %constant_dynamic-update-slice_fusion, f32[2,512,1536]{2,1,0:T(8,128)} %collective-permute-done.1, s32[]{:T(128)S(6)} %select_n.67, ...), kind=kLoop, calls=%fused_computation.47 | loop fusion | flops 1572864 | bytes 18874392 | tf_op jit(solution)/shard_map/stack | solution.py:75
  140.4 1.4 pad_maximum_fusion
  141.8 14.7 %fusion.53 = f32[3,512,512]{2,1,0:T(8,128)S(1)} fusion(f32[3,2,512,512]{3,2,0,1:T(8,128)S(1)} %pad_maximum_fusion, f32[512,512]{1,0:T(8,128)S(1)} %get-tuple-element.44, f32[512,512]{1,0:T(8,128)S(1)} %get-tuple-element.43), kind=kOutput, calls=%fused_computation.76 | convolution fusion | flops 4838653952 | bytes 11534336 | tf_op jit(solution)/shard_map/km,smn->skn/dot_general | solution.py:29
  156.5 14.4 %convolution_add_fusion.1 = f32[3,512,512]{2,1,0:T(8,128)S(1)} fusion(f32[3,512,512]{2,1,0:T(8,128)S(1)} %fusion.53, f32[3,2,512,512]{3,2,0,1:T(8,128)S(1)} %pad_maximum_fusion, f32[512,512]{1,0:T(8,128)S(1)} %get-tuple-element.44, f32[512,512]{1,0:T(8,128)S(1)} %get-tuple-element.43), kind=kOutput, calls=%fused_computation.62 | convolution fusion | flops 4838916096 | bytes 14680064 | tf_op jit(solution)/shard_map/km,smn->skn/dot_general | solution.py:29
  170.9 9.3 %fusion.8 = f32[3,512,512]{2,1,0:T(8,128)S(1)} fusion(f32[3,512,512]{2,1,0:T(8,128)S(1)} %convolution_add_fusion.1), kind=kOutput, calls=%fused_computation.22 | convolution fusion | flops 4835770368 | bytes 6291456 | tf_op jit(solution)/shard_map/smn,nk->smk/dot_general | solution.py:39
  180.2 9.6 %fusion.10 = f32[3,512,512]{2,1,0:T(8,128)S(1)} fusion(f32[3,512,512]{2,1,0:T(8,128)S(1)} %convolution_add_fusion.1), kind=kOutput, calls=%fused_computation.24 | convolution fusion | flops 4836294656 | bytes 6291456 | tf_op jit(solution)/shard_map/smn,nk->smk/dot_general | solution.py:36
  189.8 14.4 %fusion.55 = f32[3,512,512]{2,1,0:T(8,128)S(1)} fusion(f32[3,2,512,512]{3,2,0,1:T(8,128)S(1)} %pad_maximum_fusion, f32[512,512]{1,0:T(8,128)S(1)} %get-tuple-element.44, f32[512,512]{1,0:T(8,128)S(1)} %get-tuple-element.43), kind=kOutput, calls=%fused_computation.78 | convolution fusion | flops 4838653952 | bytes 11534336 | tf_op jit(solution)/shard_map/km,smn->skn/dot_general | solution.py:26
  204.2 14.4 %convolution_subtract_fusion.1 = f32[3,512,512]{2,1,0:T(8,128)S(1)} fusion(f32[3,512,512]{2,1,0:T(8,128)S(1)} %fusion.55, f32[3,2,512,512]{3,2,0,1:T(8,128)S(1)} %pad_maximum_fusion, f32[512,512]{1,0:T(8,128)S(1)} %get-tuple-element.44, f32[512,512]{1,0:T(8,128)S(1)} %get-tuple-element.43), kind=kOutput, calls=%fused_computation.63 | convolution fusion | flops 4838916096 | bytes 14680064 | tf_op jit(solution)/shard_map/km,smn->skn/dot_general | solution.py:26
  218.6 9.7 %fusion.35 = f32[3,512,512]{2,1,0:T(8,128)S(1)} fusion(f32[3,512,512]{2,1,0:T(8,128)S(1)} %fusion.8, f32[3,512,512]{2,1,0:T(8,128)S(1)} %convolution_subtract_fusion.1), kind=kOutput, calls=%fused_computation.57 | convolution fusion | flops 4837081088 | bytes 9437184 | tf_op jit(solution)/shard_map/smn,nk->smk/dot_general | solution.py:39
  228.3 0.0 copy-start.5
  228.4 9.4 %fusion.32 = f32[3,512,512]{2,1,0:T(8,128)S(1)} fusion(f32[3,512,512]{2,1,0:T(8,128)S(1)} %fusion.10, f32[3,512,512]{2,1,0:T(8,128)S(1)} %convolution_subtract_fusion.1), kind=kOutput, calls=%fused_computation.56 | convolution fusion | flops 4836556800 | bytes 9437184 | tf_op jit(solution)/shard_map/smn,nk->smk/dot_general | solution.py:36
  237.8 0.0 copy-done.5
  237.8 14.7 %fusion.58 = f32[3,512,512]{2,1,0:T(8,128)S(1)} fusion(f32[3,512,512]{2,1,0:T(8,128)S(1)} %fusion.35, f32[3,512,512]{2,1,0:T(8,128)S(1)} %copy-done.5, f32[3,512,512]{2,1,0:T(8,128)S(1)} %fusion.32), kind=kOutput, calls=%fused_computation.81 | convolution fusion | flops 4841275392 | bytes 12582912 | tf_op jit(solution)/shard_map/km,smn->skn/dot_general | solution.py:29
  252.5 15.1 %convolution_add_fusion = f32[3,512,512]{2,1,0:T(8,128)S(1)} fusion(f32[3,512,512]{2,1,0:T(8,128)S(1)} %fusion.58, f32[3,512,512]{2,1,0:T(8,128)S(1)} %fusion.32, f32[3,512,512]{2,1,0:T(8,128)S(1)} %copy-done.5, f32[3,512,512]{2,1,0:T(8,128)S(1)} %fusion.35), kind=kOutput, calls=%fused_computation.60 | convolution fusion | flops 4842323968 | bytes 15728640 | tf_op jit(solution)/shard_map/km,smn->skn/dot_general | solution.py:29
  267.6 9.3 %fusion = f32[3,512,512]{2,1,0:T(8,128)S(1)} fusion(f32[3,512,512]{2,1,0:T(8,128)S(1)} %convolution_add_fusion), kind=kOutput, calls=%fused_computation.14 | convolution fusion | flops 4835770368 | bytes 6291456 | tf_op jit(solution)/shard_map/smn,nk->smk/dot_general | solution.py:39
  276.9 15.9 %fusion.2 = f32[3,512,512]{2,1,0:T(8,128)} fusion(f32[3,512,512]{2,1,0:T(8,128)S(1)} %convolution_add_fusion), kind=kOutput, calls=%fused_computation.16 | convolution fusion | flops 4836032512 | bytes 6291456 | tf_op jit(solution)/shard_map/smn,nk->smk/dot_general | solution.py:36
  292.8 14.7 %fusion.61 = f32[3,512,512]{2,1,0:T(8,128)S(1)} fusion(f32[3,512,512]{2,1,0:T(8,128)S(1)} %fusion.32, f32[3,512,512]{2,1,0:T(8,128)S(1)} %copy-done.5, f32[3,512,512]{2,1,0:T(8,128)S(1)} %fusion.35), kind=kOutput, calls=%fused_computation.84 | convolution fusion | flops 4841275392 | bytes 12582912 | tf_op jit(solution)/shard_map/km,smn->skn/dot_general | solution.py:26
  307.5 14.8 %convolution_subtract_fusion = f32[3,512,512]{2,1,0:T(8,128)S(1)} fusion(f32[3,512,512]{2,1,0:T(8,128)S(1)} %fusion.61, f32[3,512,512]{2,1,0:T(8,128)S(1)} %fusion.35, f32[3,512,512]{2,1,0:T(8,128)S(1)} %copy-done.5, f32[3,512,512]{2,1,0:T(8,128)S(1)} %fusion.32), kind=kOutput, calls=%fused_computation.61 | convolution fusion | flops 4842323968 | bytes 15728640 | tf_op jit(solution)/shard_map/km,smn->skn/dot_general | solution.py:26
  322.4 9.7 %fusion.41 = f32[3,512,512]{2,1,0:T(8,128)S(1)} fusion(f32[3,512,512]{2,1,0:T(8,128)S(1)} %fusion, f32[3,512,512]{2,1,0:T(8,128)S(1)} %convolution_subtract_fusion), kind=kOutput, calls=%fused_computation.59 | convolution fusion | flops 4836818944 | bytes 9437184 | tf_op jit(solution)/shard_map/smn,nk->smk/dot_general | solution.py:39
  332.1 20.4 %multiply_reduce_fusion.1 = (f32[512,512]{1,0:T(8,128)}, f32[512,512]{1,0:T(8,128)}, f32[3,1,512,512]{3,2,0,1:T(8,128)S(1)}, f32[3,1,512,512]{3,2,0,1:T(8,128)S(1)}) fusion(f32[3,512,512]{2,1,0:T(8,128)S(1)} %fusion.41, f32[3,2,512,512]{3,2,0,1:T(8,128)S(1)} %pad_maximum_fusion, f32[3]{0:T(128)S(1)} %convert_element_type.37, ...), kind=kOutput, calls=%fused_computation.31 | convolution fusion | flops 4850188288 | bytes 26214412 | tf_op jit(solution)/shard_map/smn,nk->smk/dot_general | solution.py:36
  352.5 1.7 fusion.22
  354.2 0.7 copy-done.1
  354.8 6.1 broadcast_in_dim.2
  361.0 15.0 %dynamic_update_slice.9 = f32[2,1024,1536]{2,1,0:T(8,128)} dynamic-update-slice(f32[2,1024,1536]{2,1,0:T(8,128)} %broadcast_in_dim.2, f32[2,512,512]{2,1,0:T(8,128)} %fusion.22, s32[]{:T(128)} %constant.90.clone.1, s32[]{:T(128)S(6)} %select_n.65, s32[]{:T(128)S(6)} %select_n.66) | dynamic-update-slice | bytes 4194308 | tf_op jit(solution)/shard_map/dynamic_update_slice | solution.py:85
  375.9 4.1 fusion.20
  380.0 15.1 %dynamic_update_slice.10 = f32[2,1024,1536]{2,1,0:T(8,128)} dynamic-update-slice(f32[2,1024,1536]{2,1,0:T(8,128)} %dynamic_update_slice.9, f32[2,512,512]{2,1,0:T(8,128)} %fusion.20, s32[]{:T(128)} %constant.90.clone.1, s32[]{:T(128)S(6)} %select_n.67, s32[]{:T(128)S(6)} %select_n.68) | dynamic-update-slice | bytes 4194308 | tf_op jit(solution)/shard_map/dynamic_update_slice | solution.py:85
  395.1 4.1 fusion.31
  399.2 15.0 %dynamic_update_slice.11 = f32[2,1024,1536]{2,1,0:T(8,128)} dynamic-update-slice(f32[2,1024,1536]{2,1,0:T(8,128)} %dynamic_update_slice.10, f32[2,512,512]{2,1,0:T(8,128)} %fusion.31, s32[]{:T(128)} %constant.90.clone.1, s32[]{:T(128)S(6)} %select_n.69, s32[]{:T(128)S(6)} %select_n.70) | dynamic-update-slice | bytes 4194308 | tf_op jit(solution)/shard_map/dynamic_update_slice | solution.py:85
  414.2 3.4 slice.144
  417.6 2.3 collective-permute-start.2
  419.9 67.9 %collective-permute-done.2 = f32[2,512,1536]{2,1,0:T(8,128)} collective-permute-done((f32[2,512,1536]{2,1,0:T(8,128)S(1)}, f32[2,512,1536]{2,1,0:T(8,128)}, u32[]{:S(2)}, u32[]{:S(2)}) %collective-permute-start.2) | collective-permute-done | bytes 6291488 | tf_op jit(solution)/shard_map/ppermute | solution.py:14
  487.8 0.0 copy-done
  487.8 4.2 slice_add_fusion
  492.0 0.0 copy-start.2
  492.0 2.7 copy-done.2
  494.7 1.5 slice.147
  496.2 3.2 collective-permute-start.3
  499.4 0.0 copy-done.7
  499.4 0.0 copy-done.8
  499.4 1.5 pad_maximum_fusion.2
  500.9 0.0 all-reduce.2.cloned.1.call-update
  500.9 134.8 %all-reduce.2.cloned.1.call-done = f32[2,512,512]{2,1,0:T(8,128)} async-done(((f32[2,512,512]{2,1,0:T(8,128)}), f32[2,512,512]{2,1,0:T(8,128)}) %all-reduce.2.cloned.1.call-update) | async-done | bytes 2097168 | tf_op jit(solution)/shard_map/psum | solution.py:107
  635.7 3.3 broadcast_multiply_fusion
  639.0 0.0 collective-permute-done.3
  639.0 0.8 copy-done.3
  639.9 1.5 slice-done
  641.4 0.5 fusion.29
  641.9 0.0 copy-start.4
  641.9 2.0 copy-done.4
  (11 shorter events, 0.0 us)
Async XLA Ops:
  7.2 628.6 %all-reduce.2.cloned.1.call-start = ((), (), s32[]{:S(2)}) async-start(), calls=%async_computation | async-start | bytes 4194304 | tf_op jit(solution)/shard_map/psum | solution.py:107
  7.2 3.2 copy-start.6
  9.1 49.4 %collective-permute-start = (f32[2,512,512]{2,1,0:T(8,128)S(1)}, f32[2,512,512]{2,1,0:T(8,128)S(1)}, u32[]{:S(2)}, u32[]{:S(2)}) collective-permute-start(f32[2,512,512]{2,1,0:T(8,128)S(1)} %slice.117), channel_id=1, source_target_pairs={{1,0},{2,1},{3,2},{5,4},{6,5},{7,6},{9,8},{10,9},{11,10},{13,12},{... | collective-permute-start | bytes 6291464 | tf_op jit(solution)/shard_map/ppermute | solution.py:14
  12.8 50.4 %copy-start.10 = (s32[3,2]{0,1:T(2,128)S(1)}, s32[3,2]{0,1:T(2,128)}, u32[]{:S(2)}) copy-start(s32[3,2]{0,1:T(2,128)} %param.14) | copy-start | bytes 76
  12.8 58.9 %copy-start.11 = (s32[3]{0:T(128)S(1)}, s32[3]{0:T(128)}, u32[]{:S(2)}) copy-start(s32[3]{0:T(128)} %param.15) | copy-start | bytes 40
  12.8 62.8 %copy-start.9 = (f32[2,512,512]{2,1,0:T(8,128)S(1)}, f32[2,512,512]{2,1,0:T(8,128)}, u32[]{:S(2)}) copy-start(f32[2,512,512]{2,1,0:T(8,128)} %param.12) | copy-start | bytes 6291460
  60.1 73.3 %collective-permute-start.1 = (f32[2,512,1536]{2,1,0:T(8,128)}, f32[2,512,1536]{2,1,0:T(8,128)}, u32[]{:S(2)}, u32[]{:S(2)}) collective-permute-start(f32[2,512,1536]{2,1,0:T(8,128)} %constant_dynamic-update-slice_fusion), channel_id=1, source_target_pairs={{4,0},{8,4},{12,8},{16,12},{20,16},{24,20},{28,24},{5,1},{9,5},{13... | collective-permute-start | bytes 18874376 | tf_op jit(solution)/shard_map/ppermute | solution.py:14
  228.3 9.4 %copy-start.5 = (f32[3,512,512]{2,1,0:T(8,128)S(1)}, f32[3,512,512]{2,1,0:T(8,128)}, u32[]{:S(2)}) copy-start(f32[3,512,512]{2,1,0:T(8,128)} %param.13) | copy-start | bytes 9437188
  352.5 2.4 copy-start.1
  414.2 73.6 %copy-start = (f32[2,1024,1536]{2,1,0:T(8,128)S(1)}, f32[2,1024,1536]{2,1,0:T(8,128)}, u32[]{:S(2)}) copy-start(f32[2,1024,1536]{2,1,0:T(8,128)} %dynamic_update_slice.11) | copy-start | bytes 37748740
  417.6 70.2 %collective-permute-start.2 = (f32[2,512,1536]{2,1,0:T(8,128)S(1)}, f32[2,512,1536]{2,1,0:T(8,128)}, u32[]{:S(2)}, u32[]{:S(2)}) collective-permute-start(f32[2,512,1536]{2,1,0:T(8,128)S(1)} %slice.144), channel_id=1, source_target_pairs={{0,4},{4,8},{8,12},{12,16},{16,20},{20,24},{24,28},{1,5},{5,9},{9,... | collective-permute-start | bytes 18874376 | tf_op jit(solution)/shard_map/ppermute | solution.py:14
  492.0 2.7 copy-start.2
  494.7 4.7 copy-start.7
  494.7 4.7 copy-start.8
  496.2 142.9 %collective-permute-start.3 = (f32[2,512,512]{2,1,0:T(8,128)}, f32[2,512,512]{2,1,0:T(8,128)S(1)}, u32[]{:S(2)}, u32[]{:S(2)}) collective-permute-start(f32[2,512,512]{2,1,0:T(8,128)} %slice.147), channel_id=1, source_target_pairs={{0,1},{1,2},{2,3},{4,5},{5,6},{6,7},{8,9},{9,10},{10,11},{12,13},{... | collective-permute-start | bytes 6291464 | tf_op jit(solution)/shard_map/ppermute | solution.py:14
  635.7 4.2 copy-start.3
  639.0 2.4 slice-start
  641.9 2.0 copy-start.4
Sparse Core Ops, SparseCore 0:
  501.0 134.6 all-reduce.1
where the time goes:
time: 663 us; the launch traced here: 651 us
  waiting for transfers between devices  306 us (46%)
  matrix products  211 us (32%)
  local copies, waits for them, and re-layouts  70.5 us (11%)
  other arithmetic  27.7 us (4%)
  between operations  26.1 us (4%)
  starting transfers between devices  9.95 us (2%)
    ppermute x4, waiting for transfers between devices, from_behind(): return lax.ppermute(array, axis, pairs)  171 us
    psum x1, waiting for transfers between devices, body(): pupil_total = lax.psum(dpup, ('ty', 'tx'))  135 us
    dynamic_update_slice x3, local copies, waits for them, and re-layouts, place_windows(): region = lax.dynamic_update_slice(region, current + grads[number], start)  45.1 us
    dot_general x2, matrix products, right_product(): jnp.einsum('smn,nk->smk', val_re, mat_re, precision=exact_mode)  29.8 us
    dot_general x2, matrix products, left_product(): jnp.einsum('km,smn->skn', mat_im, val_re, precision=exact_mode)  29.7 us
    dot_general x2, matrix products, left_product(): jnp.einsum('km,smn->skn', mat_im, val_im, precision=exact_mode)  29.2 us
    dot_general x2, matrix products, left_product(): jnp.einsum('km,smn->skn', mat_re, val_re, precision=exact_mode)  29.1 us
    dot_general x2, matrix products, left_product(): jnp.einsum('km,smn->skn', mat_re, val_im, precision=exact_mode)  29.1 us
  transfers between devices with their start and end apart: 5, of which 4 were waited for; matrix products, arithmetic and copies ran while one was open for 1% of the time, Pallas kernels for 0%

commit v1 on v0

v1 whole, which is shorter than its diff:
```python
import math

import jax
import jax.numpy as jnp
import ml_dtypes
import numpy as np
from jax import lax
from jax.experimental import pallas as pl
from jax.experimental.pallas import tpu as pltpu
from jax.sharding import PartitionSpec as P

RADIX = 4


def shifted(array, axis, by):
    devices = lax.axis_size(axis)
    pairs = [(i, i + by) for i in range(devices) if 0 <= i + by < devices]
    return lax.ppermute(array, axis, pairs)


def dft_blocks(length):
    short = length // RADIX
    out_idx = np.arange(short)[:, None]
    in_idx = np.arange(short)[None, :]
    blocks = []
    for p in range(RADIX):
        phase = (p * in_idx + RADIX * out_idx * in_idx) % length
        angle = phase * (2.0 * math.pi / length)
        cos = np.cos(angle) / math.sqrt(length)
        sin = np.sin(angle) / math.sqrt(length)
        blocks.append(np.block([[cos, -sin], [sin, cos]]))
    full = np.stack(blocks).astype(np.float32)
    high = full.astype(ml_dtypes.bfloat16)
    low = (full - high.astype(np.float32)).astype(ml_dtypes.bfloat16)
    return high, low


def split(value):
    high = value.astype(jnp.bfloat16)
    low = (value - high.astype(jnp.float32)).astype(jnp.bfloat16)
    return high, low


def dot(lhs, rhs):
    return jnp.dot(lhs, rhs, preferred_element_type=jnp.float32)


def dot3(lhs_hi, lhs_lo, rhs_hi, rhs_lo):
    return dot(lhs_hi, rhs_hi) + (dot(lhs_hi, rhs_lo) + dot(lhs_lo, rhs_hi))


def butterfly(parts, sign):
    (r0, i0), (r1, i1), (r2, i2), (r3, i3) = parts
    sr, si, dr, di = r0 + r2, i0 + i2, r0 - r2, i0 - i2
    tr, ti, er, ei = r1 + r3, i1 + i3, r1 - r3, i1 - i3
    if sign < 0:
        er, ei = -er, -ei
    return [(sr + tr, si + ti), (dr - ei, di + er), (sr - tr, si - ti), (dr + ei, di - er)]


def row_index():
    return lax.broadcasted_iota(jnp.int32, (8, 128), 0)


def lane_index():
    return lax.broadcasted_iota(jnp.int32, (8, 128), 1)


def lane_tiles(tile):
    return [tile[:, i : i + 128] for i in range(0, tile.shape[1], 128)]


def pull_lanes(tile, shift):
    rolled = [pltpu.roll(part, (128 - shift) % 128, 1) for part in lane_tiles(tile)]
    keep = lane_index() < 128 - shift
    return [jnp.where(keep, a, b) for a, b in zip(rolled, rolled[1:])]


def pull_rows(tiles, shift):
    rolled = [[pltpu.roll(part, (8 - shift) % 8, 0) for part in tile] for tile in tiles]
    keep = row_index() < 8 - shift
    return [
        jnp.concatenate([jnp.where(keep, x, y) for x, y in zip(a, b)], axis=1)
        for a, b in zip(rolled, rolled[1:])
    ]


def push_lanes(tile, shift):
    rolled = [pltpu.roll(part, shift, 1) for part in lane_tiles(tile)]
    zero = jnp.zeros((8, 128), jnp.float32)
    keep = lane_index() >= shift
    return [jnp.where(keep, b, a) for a, b in zip([zero] + rolled, rolled + [zero])]


def push_rows(tiles, shift):
    rolled = [[pltpu.roll(part, shift, 0) for part in tile] for tile in tiles]
    keep = row_index() >= shift
    return [
        jnp.concatenate([jnp.where(keep, y, x) for x, y in zip(a, b)], axis=1)
        for a, b in zip(rolled, rolled[1:])
    ]


def slots_kernel(
    meta,
    tile_hbm,
    right_hbm,
    lower_hbm,
    corner_hbm,
    amps_hbm,
    pupil,
    mat_hi,
    mat_lo,
    mat_t_hi,
    mat_t_lo,
    own_out,
    right_out,
    lower_out,
    corner_out,
    dpup,
    region,
    grads,
    win,
    left_hi,
    left_lo,
    right_hi,
    right_lo,
    cols_f32,
    rows_f32,
    dwin,
    amps,
    sems,
):
    side = pupil.shape[-1]
    short = side // RADIX
    tile_rows, tile_cols = tile_hbm.shape[1:]
    slots = amps_hbm.shape[0]
    lanes = 128
    wide = side + lanes

    def pieces(buffer):
        return (
            buffer.at[:, pl.ds(0, tile_rows), pl.ds(0, tile_cols)],
            buffer.at[:, pl.ds(0, tile_rows), pl.ds(tile_cols, side)],
            buffer.at[:, pl.ds(tile_rows, side), pl.ds(0, tile_cols)],
            buffer.at[:, pl.ds(tile_rows, side), pl.ds(tile_cols, side)],
        )

    sources = (tile_hbm, right_hbm, lower_hbm, corner_hbm)
    loads = [
        pltpu.make_async_copy(src, dst, sems.at[n])
        for n, (src, dst) in enumerate(zip(sources, pieces(region)))
    ]
    loads.append(pltpu.make_async_copy(amps_hbm, amps, sems.at[4]))
    for load in loads:
        load.start()

    zero_rows = 16

    @pl.loop(0, grads.shape[1] // zero_rows)
    def _(step):
        rows = pl.ds(pl.multiple_of(step * zero_rows, zero_rows), zero_rows)
        grads[:, rows, :] = jnp.zeros((2, zero_rows, grads.shape[2]), jnp.float32)

    @pl.loop(0, side // zero_rows)
    def _(step):
        rows = pl.ds(pl.multiple_of(step * zero_rows, zero_rows), zero_rows)
        dpup[:, rows, :] = jnp.zeros((2, zero_rows, side), jnp.float32)

    for start in (0, side + 8):
        dwin[:, pl.ds(start, 8), :] = jnp.zeros((2, 8, side), jnp.float32)

    for load in loads:
        load.wait()

    def one_slot(slot):
        row = meta[slot, 0]
        col = meta[slot, 1]
        col_base = pl.multiple_of((col // lanes) * lanes, lanes)
        col_shift = col - col_base
        row_base = pl.multiple_of((row // 8) * 8, 8)
        row_shift = row - row_base

        @pl.loop(0, side // 32)
        def _(step):
            base = pl.multiple_of(step * 32, 32)
            for plane in range(2):
                tiles = []
                for i in range(5):
                    start = pl.multiple_of(row_base + base + 8 * i, 8)
                    tiles.append(region[plane, pl.ds(start, 8), pl.ds(col_base, wide)])
                tiles = [pull_lanes(tile, col_shift) for tile in tiles]
                for i, tile in enumerate(pull_rows(tiles, row_shift)):
                    win[plane, pl.ds(base + 8 * i, 8), :] = tile

        @pl.loop(0, short // 16)
        def _(step):
            base = pl.multiple_of(step * 16, 16)
            for part in range(RADIX):
                cols = pl.ds(part * short, short)
                values = []
                for q in range(RADIX):
                    rows = pl.ds(base + q * short, 16)
                    wr, wi = win[0, rows, cols], win[1, rows, cols]
                    pr, pi = pupil[0, rows, cols], pupil[1, rows, cols]
                    values.append((wr * pr - wi * pi, wr * pi + wi * pr))
                for p, (re, im) in enumerate(butterfly(values, 1)):
                    for offset, value in ((0, re), (short, im)):
                        hi, lo = split(value)
                        rows = pl.ds(base + offset, 16)
                        left_hi[p, rows, cols] = hi
                        left_lo[p, rows, cols] = lo

        for p in range(RADIX):
            for half in range(2):
                cols = pl.ds(half * (side // 2), side // 2)
                rows_f32[p, :, cols] = dot3(
                    mat_hi[p], mat_lo[p], left_hi[p, :, cols], left_lo[p, :, cols]
                )

        for p in range(RADIX):

            @pl.loop(0, short // 16)
            def _(step):
                base = pl.multiple_of(step * 16, 16)
                values = []
                for q in range(RADIX):
                    cols = pl.ds(q * short, short)
                    values.append(
                        (
                            rows_f32[p, pl.ds(base, 16), cols],
                            rows_f32[p, pl.ds(base + short, 16), cols],
                        )
                    )
                for t, (re, im) in enumerate(butterfly(values, 1)):
                    for offset, value in ((0, re), (short, im)):
                        hi, lo = split(value)
                        rows = pl.ds(base + p * short, 16)
                        right_hi[t, rows, pl.ds(offset, short)] = hi
                        right_lo[t, rows, pl.ds(offset, short)] = lo

        for t in range(RADIX):
            for half in range(2):
                rows = pl.ds(half * (side // 2), side // 2)
                field = dot3(right_hi[t, rows, :], right_lo[t, rows, :], mat_t_hi[t], mat_t_lo[t])
                fre, fim = field[:, :short], field[:, short:]
                measured = amps[slot, rows, pl.ds(t * short, short)]
                factor = 1.0 - measured * lax.rsqrt(fre * fre + fim * fim + 1.0)
                residual = jnp.concatenate([factor * fre, factor * fim], axis=1)
                hi, lo = split(residual)
                cols_f32[t, rows, :] = dot3(hi, lo, mat_hi[t], mat_lo[t])

        for p in range(RADIX):

            @pl.loop(0, short // 16)
            def _(step):
                base = pl.multiple_of(step * 16, 16)
                rows = pl.ds(base + p * short, 16)
                values = [
                    (cols_f32[t, rows, pl.ds(0, short)], cols_f32[t, rows, pl.ds(short, short)])
                    for t in range(RADIX)
                ]
                for q, (re, im) in enumerate(butterfly(values, -1)):
                    cols = pl.ds(q * short, short)
                    for offset, value in ((0, re), (short, im)):
                        hi, lo = split(value)
                        left_hi[p, pl.ds(base + offset, 16), cols] = hi
                        left_lo[p, pl.ds(base + offset, 16), cols] = lo

        for p in range(RADIX):
            for half in range(2):
                cols = pl.ds(half * (side // 2), side // 2)
                rows_f32[p, :, cols] = dot3(
                    mat_t_hi[p], mat_t_lo[p], left_hi[p, :, cols], left_lo[p, :, cols]
                )

        @pl.loop(0, short // 8)
        def _(step):
            base = pl.multiple_of(step * 8, 8)
            for part in range(RADIX):
                cols = pl.ds(part * short, short)
                values = [
                    (rows_f32[p, pl.ds(base, 8), cols], rows_f32[p, pl.ds(base + short, 8), cols])
                    for p in range(RADIX)
                ]
                for q, (re, im) in enumerate(butterfly(values, -1)):
                    rows = pl.ds(base + q * short, 8)
                    pr, pi = pupil[0, rows, cols], pupil[1, rows, cols]
                    padded = pl.ds(base + q * short + 8, 8)
                    dwin[0, padded, cols] = pr * re + pi * im
                    dwin[1, padded, cols] = pr * im - pi * re
                    wr, wi = win[0, rows, cols], win[1, rows, cols]
                    dpup[0, rows, cols] += wr * re + wi * im
                    dpup[1, rows, cols] += wr * im - wi * re

        @pl.loop(0, (side + 8) // 40)
        def _(step):
            base = pl.multiple_of(step * 40, 8)
            for plane in range(2):
                tiles = [dwin[plane, pl.ds(base + 8 * i, 8), :] for i in range(6)]
                tiles = [push_lanes(tile, col_shift) for tile in tiles]
                for i, tile in enumerate(push_rows(tiles, row_shift)):
                    start = pl.multiple_of(row_base + base + 8 * i, 8)
                    target = (plane, pl.ds(start, 8), pl.ds(col_base, wide))
                    grads[target] = grads[target] + tile

    @pl.loop(0, slots)
    def _(slot):
        pl.when(meta[slot, 2] != 0)(lambda: one_slot(slot))

    targets = (own_out, right_out, lower_out, corner_out)
    stores = [
        pltpu.make_async_copy(src, dst, sems.at[n])
        for n, (src, dst) in enumerate(zip(pieces(grads), targets))
    ]
    for store in stores:
        store.start()
    for store in stores:
        store.wait()


def slots_call(meta, tile, right, lower, corner, amps, pupil):
    side = pupil.shape[-1]
    short = side // RADIX
    slots = amps.shape[0]
    tile_rows, tile_cols = tile.shape[1:]
    high, low = dft_blocks(side)
    tables = [jnp.asarray(x) for x in (high, low, high.transpose(0, 2, 1), low.transpose(0, 2, 1))]
    whole = pl.BlockSpec(memory_space=pltpu.VMEM)
    anywhere = pl.BlockSpec(memory_space=pl.ANY)
    f32, bf16 = jnp.float32, jnp.bfloat16
    region = (2, tile_rows + side, tile_cols + side)
    return pl.pallas_call(
        slots_kernel,
        out_shape=[
            jax.ShapeDtypeStruct(x.shape, f32) for x in (tile, right, lower, corner, pupil)
        ],
        in_specs=[pl.BlockSpec(memory_space=pltpu.SMEM)] + [anywhere] * 5 + [whole] * 5,
        out_specs=[anywhere] * 4 + [whole],
        scratch_shapes=[
            pltpu.VMEM(region, f32),
            pltpu.VMEM(region, f32),
            pltpu.VMEM((2, side, side), f32),
            pltpu.VMEM((RADIX, 2 * short, side), bf16),
            pltpu.VMEM((RADIX, 2 * short, side), bf16),
            pltpu.VMEM((RADIX, side, 2 * short), bf16),
            pltpu.VMEM((RADIX, side, 2 * short), bf16),
            pltpu.VMEM((RADIX, side, 2 * short), f32),
            pltpu.VMEM((RADIX, 2 * short, side), f32),
            pltpu.VMEM((2, side + 16, side), f32),
            pltpu.VMEM(amps.shape, f32),
            pltpu.SemaphoreType.DMA((5,)),
        ],
        compiler_params=pltpu.CompilerParams(vmem_limit_bytes=56 * 1024 * 1024),
        cost_estimate=pl.CostEstimate(
            flops=slots * 48 * 2 * 4 * short * short * side,
            bytes_accessed=40 * 1024 * 1024,
            transcendentals=slots * side * side,
        ),
        name="slots",
    )(meta, tile, right, lower, corner, amps, pupil, *tables)


def sum_scatter(value, axis, members, inner):
    rows = value.shape[0] // members
    own = lax.axis_index(axis) // inner % members
    size = lax.axis_size(axis)

    def piece(index):
        return lax.dynamic_slice_in_dim(value, index * rows, rows, 0)

    total = piece(own)
    for step in range(1, members):
        total = total + lax.ppermute(
            piece((own + step) % members), axis, cyclic(size, members, inner, step)
        )
    return total


def cyclic(size, members, inner, step):
    pairs = []
    for i in range(size):
        group = i // inner % members
        pairs.append((i, i + ((group + step) % members - group) * inner))
    return pairs


def gather(value, axis, members, inner):
    rows = value.shape[0]
    own = lax.axis_index(axis) // inner % members
    size = lax.axis_size(axis)
    parts = [value]
    for step in range(1, members):
        parts.append(lax.ppermute(value, axis, cyclic(size, members, inner, step)))
    out = jnp.zeros((members * rows,) + value.shape[1:], value.dtype)
    for step, part in enumerate(parts):
        out = lax.dynamic_update_slice_in_dim(out, part, (own - step) % members * rows, 0)
    return out


def pupil_sum(dpup):
    n_ty, n_tx = lax.axis_size("ty"), lax.axis_size("tx")
    flat = dpup.reshape(-1, dpup.shape[-1])
    part = sum_scatter(flat, "ty", 2, 1)
    part = sum_scatter(part, "ty", n_ty // 2, 2)
    part = sum_scatter(part, "tx", n_tx, 1)
    part = part * (1.0 / math.sqrt(n_ty * n_tx))
    part = gather(part, "tx", n_tx, 1)
    part = gather(part, "ty", n_ty // 2, 2)
    part = gather(part, "ty", 2, 1)
    return part.reshape(dpup.shape)


def body(spectrum, pupil, amplitudes, offsets, live):
    side = pupil.shape[-1]
    short = side // RADIX
    slots = amplitudes.shape[0]
    tile_rows, tile_cols = spectrum.shape[1:]
    rows_local = offsets[:, 0] - lax.axis_index("ty") * tile_rows
    cols_local = offsets[:, 1] - lax.axis_index("tx") * tile_cols
    meta = jnp.stack([rows_local, cols_local, live], axis=1)

    right = shifted(spectrum[:, :, :side], "tx", -1)
    lower = shifted(spectrum[:, :side, :], "ty", -1)
    corner = shifted(right[:, :side, :], "ty", -1)
    amps = amplitudes.reshape(slots, short, RADIX, short, RADIX)
    amps = amps.transpose(0, 2, 1, 4, 3).reshape(slots, side, side)

    own_g, right_g, lower_g, corner_g, dpup = slots_call(
        meta, spectrum, right, lower, corner, amps, pupil
    )

    corner_back = shifted(corner_g, "ty", 1)
    lower_back = shifted(lower_g, "ty", 1)
    right_back = shifted(right_g + corner_back, "tx", 1)
    spec_grad = (own_g + lower_back).at[:, :, :side].add(right_back)
    return spec_grad, pupil_sum(dpup)


def solution(mesh):
    return jax.shard_map(
        body,
        mesh=mesh,
        in_specs=(
            P(None, "ty", "tx"),
            P(),
            P(("ty", "tx"), None, None),
            P(("ty", "tx"), None),
            P(("ty", "tx")),
        ),
        out_specs=(P(None, "ty", "tx"), P()),
        check_vma=False,
    )
```

time: 663 us -> 421 us (0.63); the launches traced: 651 us -> 418 us
  matrix products: 211 us -> 0 us
  waiting for transfers between devices: 306 us -> 154 us
  local copies, waits for them, and re-layouts: 70.5 us -> 173 us
  starting transfers between devices: 9.95 us -> 53 us
  between operations: 26.1 us -> 1.06 us
  Pallas kernels: 0 us -> 24.9 us
  other arithmetic: 27.7 us -> 11.8 us
    dot_general x16 -> x0, matrix products: 211 us -> none  [the longest x2 29.8 us: right_product(): jnp.einsum('smn,nk->smk', val_re, mat_re, precision=exact_mode)]
    psum x1 -> x0, waiting for transfers between devices: 135 us -> none  [body(): pupil_total = lax.psum(dpup, ('ty', 'tx'))]
    reshape x0 -> x2, local copies, waits for them, and re-layouts: none -> 108 us  [the longest x1 105 us: body(): amps = amplitudes.reshape(slots, short, RADIX, short, RADIX)]
    transpose x0 -> x1, local copies, waits for them, and re-layouts: none -> 52.3 us  [body(): amps = amps.transpose(0, 2, 1, 4, 3).reshape(slots, side, side)]
    ppermute x4 -> x20, starting transfers between devices: 9.92 us -> 53 us  [the longest x6 37.7 us: shifted(): return lax.ppermute(array, axis, pairs)]
    dynamic_update_slice x3 -> x9, local copies, waits for them, and re-layouts: 45.1 us -> 5.23 us  [gather(): lax.dynamic_update_slice_in_dim(out, part, (own - step) % members * rows, 0)]
    pallas_call x0 -> x1, Pallas kernels: none -> 24.9 us  [slots_call(): pl.pallas_call(slots_kernel, out_shape=[jax.ShapeDtypeStruct(x.shape, f32...]
    ppermute x4 -> x20, waiting for transfers between devices: 171 us -> 154 us  [the longest x7 77.5 us: sum_scatter(): lax.ppermute(piece((own + step) % members), axis, cyclic(size, members, i...]
  transfers between devices with their start and end apart: 5 -> 20, of which waited for: 4 -> 10; matrix products, arithmetic and copies ran while one was open for 1% -> 43% of each run, Pallas kernels for 0% -> 0%
where the time goes in v1:
time: 421 us; the launch traced here: 418 us
  local copies, waits for them, and re-layouts  173 us (41%)
  waiting for transfers between devices  154 us (37%)
  starting transfers between devices  53 us (13%)
  Pallas kernels  24.9 us (6%)
  other arithmetic  11.8 us (3%)
    reshape x1, local copies, waits for them, and re-layouts, body(): amps = amplitudes.reshape(slots, short, RADIX, short, RADIX)  105 us
    ppermute x7, waiting for transfers between devices, sum_scatter(): lax.ppermute(piece((own + step) % members), axis, cyclic(size, members, i...  77.5 us
    ppermute x6, waiting for transfers between devices, shifted(): return lax.ppermute(array, axis, pairs)  65.8 us
    transpose x1, local copies, waits for them, and re-layouts, body(): amps = amps.transpose(0, 2, 1, 4, 3).reshape(slots, side, side)  52.3 us
    ppermute x6, starting transfers between devices, shifted(): return lax.ppermute(array, axis, pairs)  37.7 us
    pallas_call x1, Pallas kernels, slots_call(): pl.pallas_call(slots_kernel, out_shape=[jax.ShapeDtypeStruct(x.shape, f32...  24.9 us
    ppermute x7, waiting for transfers between devices, gather(): parts.append(lax.ppermute(value, axis, cyclic(size, members, inner, step)))  10.4 us
  transfers between devices with their start and end apart: 20, of which 10 were waited for; matrix products, arithmetic and copies ran while one was open for 43% of the time, Pallas kernels for 0%

profile of v1, /device:TPU:1, one launch (start us, length us, event | category | flops | bytes accessed | tf_op | source)
XLA Modules:
  0.0 417.8 jit_solution(11799053531736164549)
XLA Ops:
  0.7 1.9 slice.35
  2.6 1.3 collective-permute-start
  3.9 2.0 collective-permute-start.1
  5.9 46.2 %collective-permute-done.right_hbm = f32[2,512,512]{2,1,0:T(8,128)} collective-permute-done((f32[2,512,512]{2,1,0:T(8,128)S(1)}, f32[2,512,512]{2,1,0:T(8,128)}, u32[]{:S(2)}, u32[]{:S(2)}) %collective-permute-start) | collective-permute-done | bytes 2097184 | tf_op jit(solution)/shard_map/ppermute | solution.py:18
  52.1 3.1 collective-permute-start.2
  55.3 0.1 copy.19
  55.3 0.1 copy.20
  55.4 0.1 copy.17
  55.5 105.2 %reshape.48 = f32[3,128,4,128,4]{4,3,2,1,0:T(8,128)} reshape(f32[3,512,512]{2,1,0:T(8,128)S(1)} %copy-done.2) | data formatting | bytes 6291456 | tf_op jit(solution)/shard_map/reshape | solution.py:426
  160.8 52.3 %copy.18 = f32[3,4,128,4,128]{4,3,2,1,0:T(4,128)S(1)} copy(f32[3,4,128,4,128]{3,4,1,2,0:T(8,128)} %bitcast.1) | data formatting | bytes 6291456 | tf_op jit(solution)/shard_map/transpose | solution.py:427
  213.1 2.8 reshape.49.amps_hbm
  215.9 0.7 pad_add_fusion.meta
  216.6 24.9 %slots.1 = (f32[2,512,1024]{2,1,0:T(8,128)}, f32[2,512,512]{2,1,0:T(8,128)}, f32[2,512,1024]{2,1,0:T(8,128)}, f32[2,512,512]{2,1,0:T(8,128)}, f32[2,512,512]{2,1,0:T(8,128)}) custom-call(s32[3,3]{1,0:T(4,128)} %pad_add_fusion.meta, f32[2,512,1024]{2,1,0:T(8,128)} %tile_hbm.1, f32[2,512,512]{2,1,0:T(8,128)} %collective-permute-done.right_hbm, ...), custom_call_target="tpu_custom_call" | custom-call | flops 9663676416 | bytes 41943040 | tf_op jit(solution)/shard_map/slots/pallas_call | solution.py:333
  241.5 1.4 constant_dynamic-slice_fusion.6
  243.0 0.1 collective-permute-start.6
  243.0 25.5 %collective-permute-start.4 = (f32[2,512,512]{2,1,0:T(8,128)}, f32[2,512,512]{2,1,0:T(8,128)}, u32[]{:S(2)}, u32[]{:S(2)}) collective-permute-start(f32[2,512,512]{2,1,0:T(8,128)} %get-tuple-element.22), channel_id=1, source_target_pairs={{0,4},{4,8},{8,12},{12,16},{16,20},{20,24},{24,28},{1,5},{5,9},{9,... | collective-permute-start | bytes 6291464 | tf_op jit(solution)/shard_map/ppermute | solution.py:18
  268.5 2.4 collective-permute-start.3
  271.0 0.0 collective-permute-done.6
  271.0 1.4 dynamic-slice_add_fusion
  272.4 0.0 copy-start.3
  272.5 0.9 constant_dynamic-slice_fusion.5
  273.4 1.2 collective-permute-start.7
  274.6 0.0 collective-permute-start.8
  274.6 1.2 collective-permute-start.9
  275.8 69.4 %collective-permute-done.7 = f32[128,512]{1,0:T(8,128)} collective-permute-done((f32[128,512]{1,0:T(8,128)}, f32[128,512]{1,0:T(8,128)}, u32[]{:S(2)}, u32[]{:S(2)}) %collective-permute-start.7) | collective-permute-done | bytes 262176 | tf_op jit(solution)/shard_map/ppermute | solution.py:374
  345.1 4.1 collective-permute-done.8
  349.2 0.9 collective-permute-done.9
  350.1 1.2 add_add_fusion
  351.3 0.1 collective-permute-start.10
  351.4 2.4 collective-permute-start.11
  353.8 2.3 collective-permute-start.12
  356.1 1.2 collective-permute-done.10
  357.2 1.9 collective-permute-done.11
  359.2 0.0 collective-permute-done.12
  359.2 0.7 broadcast_in_dim.11
  359.9 0.6 constant_dynamic-update-slice_fusion.9
  360.6 1.7 collective-permute-start.13
  362.3 2.2 collective-permute-start.14
  364.5 3.4 add.190
  367.9 3.5 collective-permute-start.5
  371.4 0.0 collective-permute-done.13
  371.4 0.6 constant_dynamic-update-slice_fusion.8
  372.1 0.0 collective-permute-done.14
  372.1 0.6 constant_dynamic-update-slice_fusion.7
  372.7 0.6 constant_dynamic-update-slice_fusion.6
  373.3 0.3 collective-permute-start.17
  373.6 2.4 collective-permute-start.18
  376.0 0.1 broadcast_in_dim.10
  376.1 1.0 constant_dynamic-update-slice_fusion.5
  377.1 3.7 collective-permute-done.16
  380.8 1.0 constant_dynamic-update-slice_fusion.4
  381.8 4.6 %collective-permute-done.17 = f32[128,512]{1,0:T(8,128)S(1)} collective-permute-done((f32[128,512]{1,0:T(8,128)}, f32[128,512]{1,0:T(8,128)S(1)}, u32[]{:S(2)}, u32[]{:S(2)}) %collective-permute-start.17) | collective-permute-done | bytes 262176 | tf_op jit(solution)/shard_map/ppermute | solution.py:394
  386.5 1.5 collective-permute-start.19
  388.0 0.2 broadcast_in_dim.9
  388.3 0.0 copy-start.1
  388.3 0.1 constant_dynamic-update-slice_fusion.1
  388.4 2.1 collective-permute-done.19
  390.4 1.3 constant_dynamic-update-slice_fusion
  391.7 0.0 copy-start.5
  391.8 3.9 add.189
  395.6 19.6 %collective-permute-done.5 = f32[2,512,512]{2,1,0:T(8,128)S(1)} collective-permute-done((f32[2,512,512]{2,1,0:T(8,128)}, f32[2,512,512]{2,1,0:T(8,128)S(1)}, u32[]{:S(2)}, u32[]{:S(2)}) %collective-permute-start.5) | collective-permute-done | bytes 2097184 | tf_op jit(solution)/shard_map/ppermute | solution.py:18
  415.2 0.5 fusion
  415.7 0.0 copy-start
  415.7 2.0 copy-done
  (24 shorter events, 0.1 us)
Async XLA Ops:
  0.6 54.6 %copy-start.6 = (s32[3,2]{0,1:T(2,128)S(1)}, s32[3,2]{0,1:T(2,128)}, u32[]{:S(2)}) copy-start(s32[3,2]{0,1:T(2,128)} %param.14) | copy-start | bytes 76
  0.6 54.8 %copy-start.7 = (s32[3]{0:T(128)S(1)}, s32[3]{0:T(128)}, u32[]{:S(2)}) copy-start(s32[3]{0:T(128)} %param.15) | copy-start | bytes 40
  0.7 54.9 %copy-start.2 = (f32[3,512,512]{2,1,0:T(8,128)S(1)}, f32[3,512,512]{2,1,0:T(8,128)}, u32[]{:S(2)}) copy-start(f32[3,512,512]{2,1,0:T(8,128)} %param.13) | copy-start | bytes 9437188
  2.6 49.5 %collective-permute-start = (f32[2,512,512]{2,1,0:T(8,128)S(1)}, f32[2,512,512]{2,1,0:T(8,128)}, u32[]{:S(2)}, u32[]{:S(2)}) collective-permute-start(f32[2,512,512]{2,1,0:T(8,128)S(1)} %slice.35), channel_id=1, source_target_pairs={{1,0},{2,1},{3,2},{5,4},{6,5},{7,6},{9,8},{10,9},{11,10},{13,12},{... | collective-permute-start | bytes 6291464 | tf_op jit(solution)/shard_map/ppermute | solution.py:18
  3.9 212.7 %collective-permute-start.1 = (f32[2,512,1024]{2,1,0:T(8,128)}, f32[2,512,1024]{2,1,0:T(8,128)}, u32[]{:S(2)}, u32[]{:S(2)}) collective-permute-start(f32[2,512,1024]{2,1,0:T(8,128)} %tile_hbm.1), channel_id=1, source_target_pairs={{4,0},{8,4},{12,8},{16,12},{20,16},{24,20},{28,24},{5,1},{9,5},{13... | collective-permute-start | bytes 12582920 | tf_op jit(solution)/shard_map/ppermute | solution.py:18
  52.1 164.5 %collective-permute-start.2 = (f32[2,512,512]{2,1,0:T(8,128)}, f32[2,512,512]{2,1,0:T(8,128)}, u32[]{:S(2)}, u32[]{:S(2)}) collective-permute-start(f32[2,512,512]{2,1,0:T(8,128)} %collective-permute-done.right_hbm), channel_id=1, source_target_pairs={{4,0},{8,4},{12,8},{16,12},{20,16},{24,20},{28,24},{5,1},{9,5},{13... | collective-permute-start | bytes 6291464 | tf_op jit(solution)/shard_map/ppermute | solution.py:18
  241.5 29.5 %copy-start.4 = (f32[2,512,512]{2,1,0:T(8,128)S(1)}, f32[2,512,512]{2,1,0:T(8,128)}, u32[]{:S(2)}) copy-start(f32[2,512,512]{2,1,0:T(8,128)} %get-tuple-element.23) | copy-start | bytes 6291460
  243.0 28.0 %collective-permute-start.6 = (f32[512,512]{1,0:T(8,128)S(1)}, f32[512,512]{1,0:T(8,128)}, u32[]{:S(2)}, u32[]{:S(2)}) collective-permute-start(f32[512,512]{1,0:T(8,128)S(1)} %constant_dynamic-slice_fusion.6), channel_id=1, source_target_pairs={{0,4},{4,0},{8,12},{12,8},{16,20},{20,16},{24,28},{28,24},{1,5},{5... | collective-permute-start | bytes 3145736 | tf_op jit(solution)/shard_map/ppermute | solution.py:374
  243.0 121.5 %collective-permute-start.4 = (f32[2,512,512]{2,1,0:T(8,128)}, f32[2,512,512]{2,1,0:T(8,128)}, u32[]{:S(2)}, u32[]{:S(2)}) collective-permute-start(f32[2,512,512]{2,1,0:T(8,128)} %get-tuple-element.22), channel_id=1, source_target_pairs={{0,4},{4,8},{8,12},{12,16},{16,20},{20,24},{24,28},{1,5},{5,9},{9,... | collective-permute-start | bytes 6291464 | tf_op jit(solution)/shard_map/ppermute | solution.py:18
  268.5 123.2 %collective-permute-start.3 = (f32[2,512,1024]{2,1,0:T(8,128)}, f32[2,512,1024]{2,1,0:T(8,128)}, u32[]{:S(2)}, u32[]{:S(2)}) collective-permute-start(f32[2,512,1024]{2,1,0:T(8,128)} %get-tuple-element.20), channel_id=1, source_target_pairs={{0,4},{4,8},{8,12},{12,16},{16,20},{20,24},{24,28},{1,5},{5,9},{9,... | collective-permute-start | bytes 12582920 | tf_op jit(solution)/shard_map/ppermute | solution.py:18
  272.4 92.1 %copy-start.3 = (f32[2,512,512]{2,1,0:T(8,128)S(1)}, f32[2,512,512]{2,1,0:T(8,128)}, u32[]{:S(2)}) copy-start(f32[2,512,512]{2,1,0:T(8,128)} %get-tuple-element.21) | copy-start | bytes 6291460
  273.4 71.8 %collective-permute-start.7 = (f32[128,512]{1,0:T(8,128)}, f32[128,512]{1,0:T(8,128)}, u32[]{:S(2)}, u32[]{:S(2)}) collective-permute-start(f32[128,512]{1,0:T(8,128)} %get-tuple-element.26), channel_id=1, source_target_pairs={{0,8},{4,12},{8,16},{12,20},{16,24},{20,28},{24,0},{28,4},{1,9},{5... | collective-permute-start | bytes 786440 | tf_op jit(solution)/shard_map/ppermute | solution.py:374
  274.6 74.7 %collective-permute-start.8 = (f32[128,512]{1,0:T(8,128)}, f32[128,512]{1,0:T(8,128)}, u32[]{:S(2)}, u32[]{:S(2)}) collective-permute-start(f32[128,512]{1,0:T(8,128)} %get-tuple-element.28), channel_id=1, source_target_pairs={{0,16},{4,20},{8,24},{12,28},{16,0},{20,4},{24,8},{28,12},{1,17},{... | collective-permute-start | bytes 786440 | tf_op jit(solution)/shard_map/ppermute | solution.py:374
  274.6 75.5 %collective-permute-start.9 = (f32[128,512]{1,0:T(8,128)S(1)}, f32[128,512]{1,0:T(8,128)}, u32[]{:S(2)}, u32[]{:S(2)}) collective-permute-start(f32[128,512]{1,0:T(8,128)S(1)} %get-tuple-element.27), channel_id=1, source_target_pairs={{0,24},{4,28},{8,0},{12,4},{16,8},{20,12},{24,16},{28,20},{1,25},{... | collective-permute-start | bytes 786440 | tf_op jit(solution)/shard_map/ppermute | solution.py:374
  351.3 5.9 %collective-permute-start.10 = (f32[32,512]{1,0:T(8,128)S(1)}, f32[32,512]{1,0:T(8,128)S(1)}, u32[]{:S(2)}, u32[]{:S(2)}) collective-permute-start(f32[32,512]{1,0:T(8,128)S(1)} %get-tuple-element.29), channel_id=1, source_target_pairs={{0,1},{1,2},{2,3},{3,0},{4,5},{5,6},{6,7},{7,4},{8,9},{9,10},{10,1... | collective-permute-start | bytes 196616 | tf_op jit(solution)/shard_map/ppermute | solution.py:374
  351.4 7.8 %collective-permute-start.11 = (f32[32,512]{1,0:T(8,128)S(1)}, f32[32,512]{1,0:T(8,128)S(1)}, u32[]{:S(2)}, u32[]{:S(2)}) collective-permute-start(f32[32,512]{1,0:T(8,128)S(1)} %get-tuple-element.31), channel_id=1, source_target_pairs={{0,2},{1,3},{2,0},{3,1},{4,6},{5,7},{6,4},{7,5},{8,10},{9,11},{10,... | collective-permute-start | bytes 196616 | tf_op jit(solution)/shard_map/ppermute | solution.py:374
  353.8 5.4 %collective-permute-start.12 = (f32[32,512]{1,0:T(8,128)S(1)}, f32[32,512]{1,0:T(8,128)S(1)}, u32[]{:S(2)}, u32[]{:S(2)}) collective-permute-start(f32[32,512]{1,0:T(8,128)S(1)} %get-tuple-element.30), channel_id=1, source_target_pairs={{0,3},{1,0},{2,1},{3,2},{4,7},{5,4},{6,5},{7,6},{8,11},{9,8},{10,9... | collective-permute-start | bytes 196616 | tf_op jit(solution)/shard_map/ppermute | solution.py:374
  360.6 10.8 %collective-permute-start.13 = (f32[32,512]{1,0:T(8,128)S(1)}, f32[32,512]{1,0:T(8,128)S(1)}, u32[]{:S(2)}, u32[]{:S(2)}) collective-permute-start(f32[32,512]{1,0:T(8,128)S(1)} %get-tuple-element.25), channel_id=1, source_target_pairs={{0,1},{1,2},{2,3},{3,0},{4,5},{5,6},{6,7},{7,4},{8,9},{9,10},{10,1... | collective-permute-start | bytes 196616 | tf_op jit(solution)/shard_map/ppermute | solution.py:394
  362.3 9.8 %collective-permute-start.14 = (f32[32,512]{1,0:T(8,128)S(1)}, f32[32,512]{1,0:T(8,128)S(1)}, u32[]{:S(2)}, u32[]{:S(2)}) collective-permute-start(f32[32,512]{1,0:T(8,128)S(1)} %get-tuple-element.25), channel_id=1, source_target_pairs={{0,2},{1,3},{2,0},{3,1},{4,6},{5,7},{6,4},{7,5},{8,10},{9,11},{10,... | collective-permute-start | bytes 196616 | tf_op jit(solution)/shard_map/ppermute | solution.py:394
  364.5 8.2 %collective-permute-start.15 = (f32[32,512]{1,0:T(8,128)S(1)}, f32[32,512]{1,0:T(8,128)S(1)}, u32[]{:S(2)}, u32[]{:S(2)}) collective-permute-start(f32[32,512]{1,0:T(8,128)S(1)} %get-tuple-element.25), channel_id=1, source_target_pairs={{0,3},{1,0},{2,1},{3,2},{4,7},{5,4},{6,5},{7,6},{8,11},{9,8},{10,9... | collective-permute-start | bytes 196616 | tf_op jit(solution)/shard_map/ppermute | solution.py:394
  367.9 47.3 %collective-permute-start.5 = (f32[2,512,512]{2,1,0:T(8,128)}, f32[2,512,512]{2,1,0:T(8,128)S(1)}, u32[]{:S(2)}, u32[]{:S(2)}) collective-permute-start(f32[2,512,512]{2,1,0:T(8,128)} %add.190), channel_id=1, source_target_pairs={{0,1},{1,2},{2,3},{4,5},{5,6},{6,7},{8,9},{9,10},{10,11},{12,13},{... | collective-permute-start | bytes 6291464 | tf_op jit(solution)/shard_map/ppermute | solution.py:18
  373.3 7.5 %collective-permute-start.16 = (f32[128,512]{1,0:T(8,128)}, f32[128,512]{1,0:T(8,128)}, u32[]{:S(2)}, u32[]{:S(2)}) collective-permute-start(f32[128,512]{1,0:T(8,128)} %constant_dynamic-update-slice_fusion.6), channel_id=1, source_target_pairs={{0,8},{4,12},{8,16},{12,20},{16,24},{20,28},{24,0},{28,4},{1,9},{5... | collective-permute-start | bytes 786440 | tf_op jit(solution)/shard_map/ppermute | solution.py:394
  373.3 13.1 %collective-permute-start.17 = (f32[128,512]{1,0:T(8,128)}, f32[128,512]{1,0:T(8,128)S(1)}, u32[]{:S(2)}, u32[]{:S(2)}) collective-permute-start(f32[128,512]{1,0:T(8,128)} %constant_dynamic-update-slice_fusion.6), channel_id=1, source_target_pairs={{0,16},{4,20},{8,24},{12,28},{16,0},{20,4},{24,8},{28,12},{1,17},{... | collective-permute-start | bytes 786440 | tf_op jit(solution)/shard_map/ppermute | solution.py:394
  373.6 12.8 %collective-permute-start.18 = (f32[128,512]{1,0:T(8,128)}, f32[128,512]{1,0:T(8,128)S(1)}, u32[]{:S(2)}, u32[]{:S(2)}) collective-permute-start(f32[128,512]{1,0:T(8,128)} %constant_dynamic-update-slice_fusion.6), channel_id=1, source_target_pairs={{0,24},{4,28},{8,0},{12,4},{16,8},{20,12},{24,16},{28,20},{1,25},{... | collective-permute-start | bytes 786440 | tf_op jit(solution)/shard_map/ppermute | solution.py:394
  386.5 3.9 collective-permute-start.19
  388.3 3.5 copy-start.1
  391.7 3.9 copy-start.5
  415.7 2.0 copy-start

commit v2 on v1

--- a/solution.py
+++ b/solution.py
@@ -10,12 +10,6 @@
 from jax.sharding import PartitionSpec as P
 
 RADIX = 4
-
-
-def shifted(array, axis, by):
-    devices = lax.axis_size(axis)
-    pairs = [(i, i + by) for i in range(devices) if 0 <= i + by < devices]
-    return lax.ppermute(array, axis, pairs)
 
 
 def dft_blocks(length):
@@ -106,7 +100,9 @@
     tile_hbm,
     right_hbm,
     lower_hbm,
-    corner_hbm,
+    corner_a_hbm,
+    corner_up_hbm,
+    corner_side_hbm,
     amps_hbm,
     pupil,
     mat_hi,
@@ -116,7 +112,8 @@
     own_out,
     right_out,
     lower_out,
-    corner_out,
+    corner_a_out,
+    corner_b_out,
     dpup,
     region,
     grads,
@@ -138,22 +135,33 @@
     lanes = 128
     wide = side + lanes
 
+    half = side // 2
+
     def pieces(buffer):
+        top, bottom = pl.ds(0, tile_rows), pl.ds(tile_rows, side)
         return (
-            buffer.at[:, pl.ds(0, tile_rows), pl.ds(0, tile_cols)],
-            buffer.at[:, pl.ds(0, tile_rows), pl.ds(tile_cols, side)],
-            buffer.at[:, pl.ds(tile_rows, side), pl.ds(0, tile_cols)],
-            buffer.at[:, pl.ds(tile_rows, side), pl.ds(tile_cols, side)],
+            buffer.at[:, top, pl.ds(0, tile_cols)],
+            buffer.at[:, top, pl.ds(tile_cols, side)],
+            buffer.at[:, bottom, pl.ds(0, tile_cols)],
+            buffer.at[:, bottom, pl.ds(tile_cols, half)],
+            buffer.at[:, bottom, pl.ds(tile_cols + half, half)],
         )
 
-    sources = (tile_hbm, right_hbm, lower_hbm, corner_hbm)
+    odd = meta[slots, 0]
+    targets = pieces(region)
+    sources = (tile_hbm, right_hbm, lower_hbm, corner_a_hbm)
     loads = [
         pltpu.make_async_copy(src, dst, sems.at[n])
-        for n, (src, dst) in enumerate(zip(sources, pieces(region)))
+        for n, (src, dst) in enumerate(zip(sources, targets))
     ]
-    loads.append(pltpu.make_async_copy(amps_hbm, amps, sems.at[4]))
+    loads.append(pltpu.make_async_copy(amps_hbm, amps, sems.at[5]))
     for load in loads:
         load.start()
+    from_side = pltpu.make_async_copy(corner_side_hbm, targets[4], sems.at[4])
+    from_below = pltpu.make_async_copy(corner_up_hbm, targets[4], sems.at[4])
+    pl.when(odd == 1)(from_side.start)
+    pl.when(odd != 1)(from_below.start)
+    loads.append(from_side)
 
     zero_rows = 16
 
@@ -308,7 +316,7 @@
     def _(slot):
         pl.when(meta[slot, 2] != 0)(lambda: one_slot(slot))
 
-    targets = (own_out, right_out, lower_out, corner_out)
+    targets = (own_out, right_out, lower_out, corner_a_out, corner_b_out)
     stores = [
         pltpu.make_async_copy(src, dst, sems.at[n])
         for n, (src, dst) in enumerate(zip(pieces(grads), targets))
@@ -319,7 +327,7 @@
         store.wait()
 
 
-def slots_call(meta, tile, right, lower, corner, amps, pupil):
+def slots_call(meta, tile, right, lower, corner_a, corner_up, corner_side, amps, pupil):
     side = pupil.shape[-1]
     short = side // RADIX
     slots = amps.shape[0]
@@ -330,13 +338,12 @@
     anywhere = pl.BlockSpec(memory_space=pl.ANY)
     f32, bf16 = jnp.float32, jnp.bfloat16
     region = (2, tile_rows + side, tile_cols + side)
+    outs = (tile, right, lower, corner_a, corner_up, pupil)
     return pl.pallas_call(
         slots_kernel,
-        out_shape=[
-            jax.ShapeDtypeStruct(x.shape, f32) for x in (tile, right, lower, corner, pupil)
-        ],
-        in_specs=[pl.BlockSpec(memory_space=pltpu.SMEM)] + [anywhere] * 5 + [whole] * 5,
-        out_specs=[anywhere] * 4 + [whole],
+        out_shape=[jax.ShapeDtypeStruct(x.shape, f32) for x in outs],
+        in_specs=[pl.BlockSpec(memory_space=pltpu.SMEM)] + [anywhere] * 7 + [whole] * 5,
+        out_specs=[anywhere] * 5 + [whole],
         scratch_shapes=[
             pltpu.VMEM(region, f32),
             pltpu.VMEM(region, f32),
@@ -349,7 +356,7 @@
             pltpu.VMEM((RADIX, 2 * short, side), f32),
             pltpu.VMEM((2, side + 16, side), f32),
             pltpu.VMEM(amps.shape, f32),
-            pltpu.SemaphoreType.DMA((5,)),
+            pltpu.SemaphoreType.DMA((6,)),
         ],
         compiler_params=pltpu.CompilerParams(vmem_limit_bytes=56 * 1024 * 1024),
         cost_estimate=pl.CostEstimate(
@@ -358,81 +365,143 @@
             transcendentals=slots * side * side,
         ),
         name="slots",
-    )(meta, tile, right, lower, corner, amps, pupil, *tables)
-
-
-def sum_scatter(value, axis, members, inner):
-    rows = value.shape[0] // members
-    own = lax.axis_index(axis) // inner % members
-    size = lax.axis_size(axis)
-
-    def piece(index):
-        return lax.dynamic_slice_in_dim(value, index * rows, rows, 0)
-
-    total = piece(own)
-    for step in range(1, members):
-        total = total + lax.ppermute(
-            piece((own + step) % members), axis, cyclic(size, members, inner, step)
-        )
+    )(meta, tile, right, lower, corner_a, corner_up, corner_side, amps, pupil, *tables)
+
+
+def exact_parts(value):
+    hi, rest = split(value)
+    rest = value - hi.astype(jnp.float32)
+    return (hi, *split(rest))
+
+
+def order_kernel(amps, perm_rows, perm_cols, out):
+    value = sum(dot(part, perm_cols[...]) for part in exact_parts(amps[0]))
+    out[0] = sum(dot(perm_rows[...], part) for part in exact_parts(value))
+
+
+def ordered(amps):
+    slots, side, _ = amps.shape
+    index = np.arange(side)
+    perm = np.zeros((side, side), ml_dtypes.bfloat16)
+    perm[index, (index % RADIX) * (side // RADIX) + index // RADIX] = 1
+    block = pl.BlockSpec((1, side, side), lambda s: (s, 0, 0))
+    table = pl.BlockSpec((side, side), lambda s: (0, 0))
+    return pl.pallas_call(
+        order_kernel,
+        grid=(slots,),
+        out_shape=jax.ShapeDtypeStruct(amps.shape, amps.dtype),
+        in_specs=[block, table, table],
+        out_specs=block,
+        cost_estimate=pl.CostEstimate(
+            flops=slots * 12 * side**3, bytes_accessed=8 * slots * side**2, transcendentals=0
+        ),
+        name="ordered",
+    )(amps, jnp.asarray(perm.T), jnp.asarray(perm))
+
+
+def along(axis_pairs, members):
+    n_ty, n_tx = members
+    pairs = []
+    for i in range(n_ty):
+        for j in range(n_tx):
+            target = axis_pairs(i, j)
+            if target is not None and 0 <= target[0] < n_ty and 0 <= target[1] < n_tx:
+                pairs.append((i * n_tx + j, target[0] * n_tx + target[1]))
+    return pairs
+
+
+def send(array, rule):
+    sizes = (lax.axis_size("ty"), lax.axis_size("tx"))
+    return lax.ppermute(array, ("ty", "tx"), along(rule, sizes))
+
+
+def halve(value, bit):
+    rows = value.shape[0] // 2
+    mine = lax.axis_index("ty") // bit % 2
+    kept = lax.dynamic_slice_in_dim(value, mine * rows, rows, 0)
+    sent = lax.dynamic_slice_in_dim(value, (1 - mine) * rows, rows, 0)
+    return kept + lax.ppermute(sent, "ty", [(i, i ^ bit) for i in range(lax.axis_size("ty"))])
+
+
+def double(value, bit):
+    mine = lax.axis_index("ty") // bit % 2
+    other = lax.ppermute(value, "ty", [(i, i ^ bit) for i in range(lax.axis_size("ty"))])
+    first = jnp.where(mine == 0, value, other)
+    second = jnp.where(mine == 0, other, value)
+    return jnp.concatenate([first, second], axis=0)
+
+
+def ring_pairs(size, step):
+    return [(i, (i + step) % size) for i in range(size)]
+
+
+def scatter_tx(value):
+    size, own = lax.axis_size("tx"), lax.axis_index("tx")
+    rows = value.shape[0] // size
+    total = lax.dynamic_slice_in_dim(value, own * rows, rows, 0)
+    for step in range(1, size):
+        piece = lax.dynamic_slice_in_dim(value, (own + step) % size * rows, rows, 0)
+        total = total + lax.ppermute(piece, "tx", ring_pairs(size, step))
     return total
 
 
-def cyclic(size, members, inner, step):
-    pairs = []
-    for i in range(size):
-        group = i // inner % members
-        pairs.append((i, i + ((group + step) % members - group) * inner))
-    return pairs
-
-
-def gather(value, axis, members, inner):
+def gather_tx(value):
+    size, own = lax.axis_size("tx"), lax.axis_index("tx")
     rows = value.shape[0]
-    own = lax.axis_index(axis) // inner % members
-    size = lax.axis_size(axis)
     parts = [value]
-    for step in range(1, members):
-        parts.append(lax.ppermute(value, axis, cyclic(size, members, inner, step)))
-    out = jnp.zeros((members * rows,) + value.shape[1:], value.dtype)
+    for step in range(1, size):
+        parts.append(lax.ppermute(value, "tx", ring_pairs(size, step)))
+    out = jnp.zeros((size * rows,) + value.shape[1:], value.dtype)
     for step, part in enumerate(parts):
-        out = lax.dynamic_update_slice_in_dim(out, part, (own - step) % members * rows, 0)
+        out = lax.dynamic_update_slice_in_dim(out, part, (own - step) % size * rows, 0)
     return out
 
 
 def pupil_sum(dpup):
     n_ty, n_tx = lax.axis_size("ty"), lax.axis_size("tx")
-    flat = dpup.reshape(-1, dpup.shape[-1])
-    part = sum_scatter(flat, "ty", 2, 1)
-    part = sum_scatter(part, "ty", n_ty // 2, 2)
-    part = sum_scatter(part, "tx", n_tx, 1)
-    part = part * (1.0 / math.sqrt(n_ty * n_tx))
-    part = gather(part, "tx", n_tx, 1)
-    part = gather(part, "ty", n_ty // 2, 2)
-    part = gather(part, "ty", 2, 1)
+    bits = [1]
+    bit = n_ty // 2
+    while bit > 1:
+        bits.append(bit)
+        bit //= 2
+    part = dpup.reshape(-1, dpup.shape[-1])
+    for bit in bits:
+        part = halve(part, bit)
+    part = scatter_tx(part) * (1.0 / math.sqrt(n_ty * n_tx))
+    part = gather_tx(part)
+    for bit in reversed(bits):
+        part = double(part, bit)
     return part.reshape(dpup.shape)
 
 
 def body(spectrum, pupil, amplitudes, offsets, live):
     side = pupil.shape[-1]
-    short = side // RADIX
-    slots = amplitudes.shape[0]
+    half = side // 2
     tile_rows, tile_cols = spectrum.shape[1:]
-    rows_local = offsets[:, 0] - lax.axis_index("ty") * tile_rows
-    cols_local = offsets[:, 1] - lax.axis_index("tx") * tile_cols
+    own_ty, own_tx = lax.axis_index("ty"), lax.axis_index("tx")
+    rows_local = offsets[:, 0] - own_ty * tile_rows
+    cols_local = offsets[:, 1] - own_tx * tile_cols
     meta = jnp.stack([rows_local, cols_local, live], axis=1)
-
-    right = shifted(spectrum[:, :, :side], "tx", -1)
-    lower = shifted(spectrum[:, :side, :], "ty", -1)
-    corner = shifted(right[:, :side, :], "ty", -1)
-    amps = amplitudes.reshape(slots, short, RADIX, short, RADIX)
-    amps = amps.transpose(0, 2, 1, 4, 3).reshape(slots, side, side)
-
-    own_g, right_g, lower_g, corner_g, dpup = slots_call(
-        meta, spectrum, right, lower, corner, amps, pupil
+    meta = jnp.concatenate([meta, jnp.full((1, 3), own_ty % 2, jnp.int32)], axis=0)
+
+    right = send(spectrum[:, :, :side], lambda i, j: (i, j - 1))
+    lower = send(spectrum[:, :side, :], lambda i, j: (i - 1, j))
+    corner_a = send(right[:, :, :half], lambda i, j: (i - 1, j))
+    corner_up = send(right[:, :, half:], lambda i, j: (i - 1, j) if i % 2 else None)
+    corner_side = send(lower[:, :, half:side], lambda i, j: (i, j - 1) if i % 2 else None)
+
+    own_g, right_g, lower_g, corner_a_g, corner_b_g, dpup = slots_call(
+        meta, spectrum, right, lower, corner_a, corner_up, corner_side, ordered(amplitudes), pupil
     )
 
-    corner_back = shifted(corner_g, "ty", 1)
-    lower_back = shifted(lower_g, "ty", 1)
-    right_back = shifted(right_g + corner_back, "tx", 1)
+    back_a = send(corner_a_g, lambda i, j: (i + 1, j))
+    back_down = send(corner_b_g, lambda i, j: None if i % 2 else (i + 1, j))
+    back_side = send(corner_b_g, lambda i, j: (i, j + 1) if i % 2 else None)
+    right_total = right_g + jnp.concatenate([back_a, back_down], axis=2)
+    lower_total = lower_g.at[:, :, half:side].add(back_side)
+    right_total, lower_total = lax.optimization_barrier((right_total, lower_total))
+    right_back = send(right_total, lambda i, j: (i, j + 1))
+    lower_back = send(lower_total, lambda i, j: (i + 1, j))
     spec_grad = (own_g + lower_back).at[:, :, :side].add(right_back)
     return spec_grad, pupil_sum(dpup)
 

time: 421 us -> 251 us (0.60)
  local copies, waits for them, and re-layouts: 173 us -> 10.7 us
  waiting for transfers between devices: 154 us -> 116 us
  starting transfers between devices: 53 us -> 72.6 us
  Pallas kernels: 24.9 us -> 32.9 us
  other arithmetic: 11.8 us -> 17.2 us
    reshape x2 -> x0, local copies, waits for them, and re-layouts: 108 us -> none  [the longest x1 105 us: body(): amps = amplitudes.reshape(slots, short, RADIX, short, RADIX)]
    transpose x1 -> x0, local copies, waits for them, and re-layouts: 52.3 us -> none  [body(): amps = amps.transpose(0, 2, 1, 4, 3).reshape(slots, side, side)]
    ppermute x20 -> x22, waiting for transfers between devices: 154 us -> 116 us  [the longest x10 65.5 us: send(): return lax.ppermute(array, ('ty', 'tx'), along(rule, sizes))]
    ppermute x20 -> x22, starting transfers between devices: 53 us -> 72.6 us  [the longest x10 57.8 us: send(): return lax.ppermute(array, ('ty', 'tx'), along(rule, sizes))]
    pallas_call x0 -> x1, Pallas kernels: none -> 8.2 us  [ordered(): pl.pallas_call(order_kernel, grid=(slots,), out_shape=jax.ShapeDtypeStruc...]
    dynamic_update_slice x9 -> x3, local copies, waits for them, and re-layouts: 5.23 us -> 0.03 us  [gather_tx(): lax.dynamic_update_slice_in_dim(out, part, (own - step) % size * rows, 0)]
  transfers between devices with their start and end apart: 20 -> 22, of which waited for: 10 -> 12; matrix products, arithmetic and copies ran while one was open for 43% -> 8% of each run, Pallas kernels for 0% -> 3%
where the time goes in v2:
time: 251 us; the launch traced here: 250 us
  waiting for transfers between devices  116 us (46%)
  starting transfers between devices  72.6 us (29%)
  Pallas kernels  32.9 us (13%)
  other arithmetic  17.2 us (7%)
  local copies, waits for them, and re-layouts  10.7 us (4%)
    ppermute x10, waiting for transfers between devices, send(): return lax.ppermute(array, ('ty', 'tx'), along(rule, sizes))  65.5 us
    ppermute x10, starting transfers between devices, send(): return lax.ppermute(array, ('ty', 'tx'), along(rule, sizes))  57.8 us
    ppermute x3, waiting for transfers between devices, double(): lax.ppermute(value, 'ty', [(i, i ^ bit) for i in range(lax.axis_size('ty'...  33.9 us
    pallas_call x1, Pallas kernels, slots_call(): pl.pallas_call(slots_kernel, out_shape=[jax.ShapeDtypeStruct(x.shape, f32...  24.7 us
    ppermute x3, waiting for transfers between devices, halve(): lax.ppermute(sent, 'ty', [(i, i ^ bit) for i in range(lax.axis_size('ty'))])  9.8 us
    ppermute x3, starting transfers between devices, scatter_tx(): total = total + lax.ppermute(piece, 'tx', ring_pairs(size, step))  9.32 us
    pallas_call x1, Pallas kernels, ordered(): pl.pallas_call(order_kernel, grid=(slots,), out_shape=jax.ShapeDtypeStruc...  8.2 us
  transfers between devices with their start and end apart: 22, of which 12 were waited for; matrix products, arithmetic and copies ran while one was open for 8% of the time, Pallas kernels for 3%

profile of v2, /device:TPU:1, one launch (start us, length us, event | category | flops | bytes accessed | tf_op | source)
XLA Modules:
  0.0 250.3 jit_solution(3222863133881010249)
XLA Ops:
  0.6 2.0 collective-permute-start.1
  2.6 1.8 slice.68
  4.4 1.3 collective-permute-start
  5.7 48.8 %collective-permute-done.right_hbm = f32[2,512,512]{2,1,0:T(8,128)S(1)} collective-permute-done((f32[2,512,512]{2,1,0:T(8,128)S(1)}, f32[2,512,512]{2,1,0:T(8,128)S(1)}, u32[]{:S(2)}, u32[]{:S(2)}) %collective-permute-start) | collective-permute-done | bytes 2097184 | tf_op jit(solution)/shard_map/ppermute | solution.py:415
  54.5 1.4 fusion.1
  55.9 0.3 copy-done.3
  56.1 2.2 collective-permute-start.2
  58.4 2.3 collective-permute-start.3
  60.7 0.0 collective-permute-done.1.lower_hbm
  60.7 0.1 slice.76
  60.8 1.3 collective-permute-start.4
  62.1 0.6 copy-done.4
  62.7 0.1 copy.15
  62.8 0.1 copy.17
  62.9 0.1 copy.16
  63.0 0.1 pad_add_fusion
  63.1 0.6 concatenate.19.meta
  63.7 8.2 %ordered.1.amps_hbm = f32[3,512,512]{2,1,0:T(8,128)} custom-call(f32[3,512,512]{2,1,0:T(8,128)} %amps.1, bf16[512,512]{1,0:T(8,128)(2,1)} %constant.194.clone.perm_rows, bf16[512,512]{1,0:T(8,128)(2,1)} %constant.195.clone.perm_cols), custom_call_target="tpu_custom_call" | custom-call | flops 4831838208 | bytes 6291456 | tf_op jit(solution)/shard_map/ordered/pallas_call | solution.py:389
  71.9 1.3 collective-permute-done.2.corner_a_hbm
  73.2 3.7 %collective-permute-done.4.corner_side_hbm = f32[2,512,256]{2,1,0:T(8,128)} collective-permute-done((f32[2,512,256]{2,1,0:T(8,128)S(1)}, f32[2,512,256]{2,1,0:T(8,128)}, u32[]{:S(2)}, u32[]{:S(2)}) %collective-permute-start.4) | collective-permute-done | bytes 1048608 | tf_op jit(solution)/shard_map/ppermute | solution.py:415
  76.9 24.7 %slots.1 = (f32[2,512,1024]{2,1,0:T(8,128)}, f32[2,512,512]{2,1,0:T(8,128)}, f32[2,512,1024]{2,1,0:T(8,128)}, f32[2,512,256]{2,1,0:T(8,128)}, f32[2,512,256]{2,1,0:T(8,128)}, /*index=5*/f32[2,512,512]{2,1,0:T(8,128)}) custom-call(s32[4,3]{1,0:T(4,128)} %concatenate.19.meta, f32[2,512,1024]{2,1,0:T(8,128)} %tile_hbm.1, f32[2,512,512]{2,1,0:T(8,128)} %copy-done.3, ...), custom_call_target="tpu_custom_call" | custom-call | flops 9663676416 | bytes 41943040 | tf_op jit(solution)/shard_map/slots/pallas_call | solution.py:342
  101.7 1.3 constant_dynamic-slice_fusion.5
  103.0 0.1 collective-permute-start.10
  103.1 1.3 collective-permute-start.6
  104.4 22.6 %collective-permute-start.5 = (f32[2,512,256]{2,1,0:T(8,128)}, f32[2,512,256]{2,1,0:T(8,128)}, u32[]{:S(2)}, u32[]{:S(2)}) collective-permute-start(f32[2,512,256]{2,1,0:T(8,128)} %get-tuple-element.36), channel_id=1, source_target_pairs={{0,4},{1,5},{2,6},{3,7},{4,8},{5,9},{6,10},{7,11},{8,12},{9,13},{1... | collective-permute-start | bytes 3145736 | tf_op jit(solution)/shard_map/ppermute | solution.py:415
  127.0 10.2 %collective-permute-start.7 = (f32[2,512,256]{2,1,0:T(8,128)}, f32[2,512,256]{2,1,0:T(8,128)}, u32[]{:S(2)}, u32[]{:S(2)}) collective-permute-start(f32[2,512,256]{2,1,0:T(8,128)} %get-tuple-element.37), channel_id=1, source_target_pairs={{4,5},{5,6},{6,7},{12,13},{13,14},{14,15},{20,21},{21,22},{22,23},... | collective-permute-start | bytes 3145736 | tf_op jit(solution)/shard_map/ppermute | solution.py:415
  137.3 0.0 collective-permute-done.10
  137.3 1.7 dynamic-slice_add_fusion
  139.0 0.8 constant_dynamic-slice_fusion.4
  139.8 0.0 collective-permute-start.11
  139.8 0.0 collective-permute-done.6
  139.8 0.0 collective-permute-done.5
  139.9 3.3 %maximum_add_fusion = f32[2,512,512]{2,1,0:T(8,128)} fusion(f32[2,512,512]{2,1,0:T(8,128)S(1)} %copy-done.2, f32[2,512,256]{2,1,0:T(8,128)} %collective-permute-done.6, f32[2,512,256]{2,1,0:T(8,128)} %collective-permute-done.5), kind=kLoop, calls=%fused_computation.2 | loop fusion | flops 1048576 | bytes 6291456 | tf_op jit(solution)/shard_map/add | solution.py:500
  143.1 8.8 %collective-permute-done.11 = f32[256,512]{1,0:T(8,128)} collective-permute-done((f32[256,512]{1,0:T(8,128)}, f32[256,512]{1,0:T(8,128)}, u32[]{:S(2)}, u32[]{:S(2)}) %collective-permute-start.11) | collective-permute-done | bytes 524320 | tf_op jit(solution)/shard_map/ppermute | solution.py:423
  151.9 1.1 dynamic-slice_add_fusion.1
  153.1 0.1 collective-permute-start.12
  153.2 2.7 %add_dynamic-update-slice_fusion = f32[2,512,1024]{2,1,0:T(8,128)} fusion(f32[2,512,1024]{2,1,0:T(8,128)} %get-tuple-element.38, f32[2,512,256]{2,1,0:T(8,128)} %collective-permute-done.7), kind=kLoop, calls=%fused_computation.6 | loop fusion | flops 262144 | bytes 3145728 | tf_op jit(solution)/shard_map/scatter-add | solution.py:501
  155.9 3.8 %collective-permute-start.8 = (f32[2,512,1024]{2,1,0:T(8,128)}, f32[2,512,1024]{2,1,0:T(8,128)}, u32[]{:S(2)}, u32[]{:S(2)}) collective-permute-start(f32[2,512,1024]{2,1,0:T(8,128)} %add_dynamic-update-slice_fusion), channel_id=1, source_target_pairs={{0,4},{1,5},{2,6},{3,7},{4,8},{5,9},{6,10},{7,11},{8,12},{9,13},{1... | collective-permute-start | bytes 12582920 | tf_op jit(solution)/shard_map/ppermute | solution.py:415
  159.8 1.0 collective-permute-done.12
  160.9 0.1 collective-permute-start.15
  160.9 8.0 %collective-permute-start.14 = (f32[32,512]{1,0:T(8,128)S(1)}, f32[32,512]{1,0:T(8,128)S(1)}, u32[]{:S(2)}, u32[]{:S(2)}) collective-permute-start(f32[32,512]{1,0:T(8,128)S(1)} %get-tuple-element.54), channel_id=1, source_target_pairs={{0,2},{1,3},{2,0},{3,1},{4,6},{5,7},{6,4},{7,5},{8,10},{9,11},{10,... | collective-permute-start | bytes 196616 | tf_op jit(solution)/shard_map/ppermute | solution.py:444
  168.9 1.3 collective-permute-start.13
  170.2 1.2 collective-permute-done.14
  171.3 3.1 %collective-permute-done.13 = f32[32,512]{1,0:T(8,128)S(1)} collective-permute-done((f32[32,512]{1,0:T(8,128)S(1)}, f32[32,512]{1,0:T(8,128)S(1)}, u32[]{:S(2)}, u32[]{:S(2)}) %collective-permute-start.13) | collective-permute-done | bytes 65568 | tf_op jit(solution)/shard_map/ppermute | solution.py:444
  174.5 0.1 collective-permute-start.16
  174.6 0.3 collective-permute-start.17
  174.9 2.9 %collective-permute-start.18 = (f32[32,512]{1,0:T(8,128)S(1)}, f32[32,512]{1,0:T(8,128)S(1)}, u32[]{:S(2)}, u32[]{:S(2)}) collective-permute-start(f32[32,512]{1,0:T(8,128)S(1)} %get-tuple-element.43), channel_id=1, source_target_pairs={{0,3},{1,0},{2,1},{3,2},{4,7},{5,4},{6,5},{7,6},{8,11},{9,8},{10,9... | collective-permute-start | bytes 196616 | tf_op jit(solution)/shard_map/ppermute | solution.py:453
  177.8 1.7 collective-permute-done.16
  179.5 0.6 collective-permute-done.18
  180.2 1.9 collective-permute-start.19
  182.1 31.0 %collective-permute-done.19 = f32[128,512]{1,0:T(8,128)S(1)} collective-permute-done((f32[128,512]{1,0:T(8,128)S(1)}, f32[128,512]{1,0:T(8,128)S(1)}, u32[]{:S(2)}, u32[]{:S(2)}) %collective-permute-start.19) | collective-permute-done | bytes 262176 | tf_op jit(solution)/shard_map/ppermute | solution.py:428
  213.2 0.1 collective-permute-start.20
  213.3 10.8 %collective-permute-start.9 = (f32[2,512,512]{2,1,0:T(8,128)}, f32[2,512,512]{2,1,0:T(8,128)}, u32[]{:S(2)}, u32[]{:S(2)}) collective-permute-start(f32[2,512,512]{2,1,0:T(8,128)} %maximum_add_fusion), channel_id=1, source_target_pairs={{0,1},{1,2},{2,3},{4,5},{5,6},{6,7},{8,9},{9,10},{10,11},{12,13},{... | collective-permute-start | bytes 6291464 | tf_op jit(solution)/shard_map/ppermute | solution.py:415
  224.2 0.1 broadcast_select_fusion.3
  224.3 1.0 pad_maximum_fusion.1
  225.3 2.9 %collective-permute-done.21 = f32[512,512]{1,0:T(8,128)S(1)} collective-permute-done((f32[512,512]{1,0:T(8,128)}, f32[512,512]{1,0:T(8,128)S(1)}, u32[]{:S(2)}, u32[]{:S(2)}) %collective-permute-start.21) | collective-permute-done | bytes 1048608 | tf_op jit(solution)/shard_map/ppermute | solution.py:428
  228.2 0.2 broadcast_select_fusion.1
  228.5 1.5 pad_maximum_fusion
  229.9 1.4 copy-done.1
  231.4 3.1 %add.135 = f32[2,512,1024]{2,1,0:T(8,128)S(1)} add(f32[2,512,1024]{2,1,0:T(8,128)S(1)} %copy-done.1, f32[2,512,1024]{2,1,0:T(8,128)} %collective-permute-done.8) | non-fusion elementwise | flops 1048576 | bytes 12582912 | tf_op jit(solution)/shard_map/add | solution.py:505
  234.5 11.6 %collective-permute-done.9 = f32[2,512,512]{2,1,0:T(8,128)} collective-permute-done((f32[2,512,512]{2,1,0:T(8,128)}, f32[2,512,512]{2,1,0:T(8,128)}, u32[]{:S(2)}, u32[]{:S(2)}) %collective-permute-start.9) | collective-permute-done | bytes 2097184 | tf_op jit(solution)/shard_map/ppermute | solution.py:415
  246.1 2.1 fusion
  248.3 0.0 copy-start
  248.3 2.0 copy-done
  (28 shorter events, 0.3 us)
Async XLA Ops:
  0.6 60.1 %collective-permute-start.1 = (f32[2,512,1024]{2,1,0:T(8,128)}, f32[2,512,1024]{2,1,0:T(8,128)S(1)}, u32[]{:S(2)}, u32[]{:S(2)}) collective-permute-start(f32[2,512,1024]{2,1,0:T(8,128)} %tile_hbm.1), channel_id=1, source_target_pairs={{4,0},{5,1},{6,2},{7,3},{8,4},{9,5},{10,6},{11,7},{12,8},{13,9},{1... | collective-permute-start | bytes 12582920 | tf_op jit(solution)/shard_map/ppermute | solution.py:415
  4.4 50.1 %collective-permute-start = (f32[2,512,512]{2,1,0:T(8,128)S(1)}, f32[2,512,512]{2,1,0:T(8,128)S(1)}, u32[]{:S(2)}, u32[]{:S(2)}) collective-permute-start(f32[2,512,512]{2,1,0:T(8,128)S(1)} %slice.68), channel_id=1, source_target_pairs={{1,0},{2,1},{3,2},{5,4},{6,5},{7,6},{9,8},{10,9},{11,10},{13,12},{... | collective-permute-start | bytes 6291464 | tf_op jit(solution)/shard_map/ppermute | solution.py:415
  54.5 1.7 copy-start.3
  55.9 6.8 %copy-start.6 = (s32[3]{0:T(128)S(1)}, s32[3]{0:T(128)}, u32[]{:S(2)}) copy-start(s32[3]{0:T(128)} %param.19) | copy-start | bytes 40
  55.9 6.9 %copy-start.5 = (s32[3,2]{0,1:T(2,128)S(1)}, s32[3,2]{0,1:T(2,128)}, u32[]{:S(2)}) copy-start(s32[3,2]{0,1:T(2,128)} %param.18) | copy-start | bytes 76
  56.1 17.1 %collective-permute-start.2 = (f32[2,512,256]{2,1,0:T(8,128)}, f32[2,512,256]{2,1,0:T(8,128)}, u32[]{:S(2)}, u32[]{:S(2)}) collective-permute-start(f32[2,512,256]{2,1,0:T(8,128)} %get-tuple-element.47), channel_id=1, source_target_pairs={{4,0},{5,1},{6,2},{7,3},{8,4},{9,5},{10,6},{11,7},{12,8},{13,9},{1... | collective-permute-start | bytes 3145736 | tf_op jit(solution)/shard_map/ppermute | solution.py:415
  58.4 14.8 %collective-permute-start.3 = (f32[2,512,256]{2,1,0:T(8,128)S(1)}, f32[2,512,256]{2,1,0:T(8,128)}, u32[]{:S(2)}, u32[]{:S(2)}) collective-permute-start(f32[2,512,256]{2,1,0:T(8,128)S(1)} %get-tuple-element.46), channel_id=1, source_target_pairs={{4,0},{5,1},{6,2},{7,3},{12,8},{13,9},{14,10},{15,11},{20,16},{21,... | collective-permute-start | bytes 3145736 | tf_op jit(solution)/shard_map/ppermute | solution.py:415
  60.7 2.0 copy-start.4
  60.8 16.1 %collective-permute-start.4 = (f32[2,512,256]{2,1,0:T(8,128)S(1)}, f32[2,512,256]{2,1,0:T(8,128)}, u32[]{:S(2)}, u32[]{:S(2)}) collective-permute-start(f32[2,512,256]{2,1,0:T(8,128)S(1)} %slice.76), channel_id=1, source_target_pairs={{5,4},{6,5},{7,6},{13,12},{14,13},{15,14},{21,20},{22,21},{23,22},... | collective-permute-start | bytes 3145736 | tf_op jit(solution)/shard_map/ppermute | solution.py:415
  103.0 34.3 %collective-permute-start.10 = (f32[512,512]{1,0:T(8,128)S(1)}, f32[512,512]{1,0:T(8,128)}, u32[]{:S(2)}, u32[]{:S(2)}) collective-permute-start(f32[512,512]{1,0:T(8,128)S(1)} %constant_dynamic-slice_fusion.5), channel_id=1, source_target_pairs={{0,4},{4,0},{8,12},{12,8},{16,20},{20,16},{24,28},{28,24},{1,5},{5... | collective-permute-start | bytes 3145736 | tf_op jit(solution)/shard_map/ppermute | solution.py:423
  103.1 36.8 %collective-permute-start.6 = (f32[2,512,256]{2,1,0:T(8,128)}, f32[2,512,256]{2,1,0:T(8,128)}, u32[]{:S(2)}, u32[]{:S(2)}) collective-permute-start(f32[2,512,256]{2,1,0:T(8,128)} %get-tuple-element.37), channel_id=1, source_target_pairs={{0,4},{1,5},{2,6},{3,7},{8,12},{9,13},{10,14},{11,15},{16,20},{17,... | collective-permute-start | bytes 3145736 | tf_op jit(solution)/shard_map/ppermute | solution.py:415
  104.4 35.5 %collective-permute-start.5 = (f32[2,512,256]{2,1,0:T(8,128)}, f32[2,512,256]{2,1,0:T(8,128)}, u32[]{:S(2)}, u32[]{:S(2)}) collective-permute-start(f32[2,512,256]{2,1,0:T(8,128)} %get-tuple-element.36), channel_id=1, source_target_pairs={{0,4},{1,5},{2,6},{3,7},{4,8},{5,9},{6,10},{7,11},{8,12},{9,13},{1... | collective-permute-start | bytes 3145736 | tf_op jit(solution)/shard_map/ppermute | solution.py:415
  127.0 12.9 %copy-start.2 = (f32[2,512,512]{2,1,0:T(8,128)S(1)}, f32[2,512,512]{2,1,0:T(8,128)}, u32[]{:S(2)}) copy-start(f32[2,512,512]{2,1,0:T(8,128)} %get-tuple-element.35) | copy-start | bytes 6291460
  127.0 26.2 %collective-permute-start.7 = (f32[2,512,256]{2,1,0:T(8,128)}, f32[2,512,256]{2,1,0:T(8,128)}, u32[]{:S(2)}, u32[]{:S(2)}) collective-permute-start(f32[2,512,256]{2,1,0:T(8,128)} %get-tuple-element.37), channel_id=1, source_target_pairs={{4,5},{5,6},{6,7},{12,13},{13,14},{14,15},{20,21},{21,22},{22,23},... | collective-permute-start | bytes 3145736 | tf_op jit(solution)/shard_map/ppermute | solution.py:415
  139.8 12.1 %collective-permute-start.11 = (f32[256,512]{1,0:T(8,128)}, f32[256,512]{1,0:T(8,128)}, u32[]{:S(2)}, u32[]{:S(2)}) collective-permute-start(f32[256,512]{1,0:T(8,128)} %constant_dynamic-slice_fusion.4), channel_id=1, source_target_pairs={{0,16},{4,20},{8,24},{12,28},{16,0},{20,4},{24,8},{28,12},{1,17},{... | collective-permute-start | bytes 1572872 | tf_op jit(solution)/shard_map/ppermute | solution.py:423
  153.1 7.7 %collective-permute-start.12 = (f32[128,512]{1,0:T(8,128)S(1)}, f32[128,512]{1,0:T(8,128)S(1)}, u32[]{:S(2)}, u32[]{:S(2)}) collective-permute-start(f32[128,512]{1,0:T(8,128)S(1)} %constant_dynamic-slice_fusion.3), channel_id=1, source_target_pairs={{0,8},{4,12},{8,0},{12,4},{16,24},{20,28},{24,16},{28,20},{1,9},{5... | collective-permute-start | bytes 786440 | tf_op jit(solution)/shard_map/ppermute | solution.py:423
  155.9 74.0 %collective-permute-start.8 = (f32[2,512,1024]{2,1,0:T(8,128)}, f32[2,512,1024]{2,1,0:T(8,128)}, u32[]{:S(2)}, u32[]{:S(2)}) collective-permute-start(f32[2,512,1024]{2,1,0:T(8,128)} %add_dynamic-update-slice_fusion), channel_id=1, source_target_pairs={{0,4},{1,5},{2,6},{3,7},{4,8},{5,9},{6,10},{7,11},{8,12},{9,13},{1... | collective-permute-start | bytes 12582920 | tf_op jit(solution)/shard_map/ppermute | solution.py:415
  160.9 9.3 %collective-permute-start.15 = (f32[32,512]{1,0:T(8,128)S(1)}, f32[32,512]{1,0:T(8,128)S(1)}, u32[]{:S(2)}, u32[]{:S(2)}) collective-permute-start(f32[32,512]{1,0:T(8,128)S(1)} %get-tuple-element.53), channel_id=1, source_target_pairs={{0,3},{1,0},{2,1},{3,2},{4,7},{5,4},{6,5},{7,6},{8,11},{9,8},{10,9... | collective-permute-start | bytes 196616 | tf_op jit(solution)/shard_map/ppermute | solution.py:444
  160.9 10.4 %collective-permute-start.14 = (f32[32,512]{1,0:T(8,128)S(1)}, f32[32,512]{1,0:T(8,128)S(1)}, u32[]{:S(2)}, u32[]{:S(2)}) collective-permute-start(f32[32,512]{1,0:T(8,128)S(1)} %get-tuple-element.54), channel_id=1, source_target_pairs={{0,2},{1,3},{2,0},{3,1},{4,6},{5,7},{6,4},{7,5},{8,10},{9,11},{10,... | collective-permute-start | bytes 196616 | tf_op jit(solution)/shard_map/ppermute | solution.py:444
  168.9 5.5 %collective-permute-start.13 = (f32[32,512]{1,0:T(8,128)S(1)}, f32[32,512]{1,0:T(8,128)S(1)}, u32[]{:S(2)}, u32[]{:S(2)}) collective-permute-start(f32[32,512]{1,0:T(8,128)S(1)} %get-tuple-element.52), channel_id=1, source_target_pairs={{0,1},{1,2},{2,3},{3,0},{4,5},{5,6},{6,7},{7,4},{8,9},{9,10},{10,1... | collective-permute-start | bytes 196616 | tf_op jit(solution)/shard_map/ppermute | solution.py:444
  174.5 5.0 %collective-permute-start.16 = (f32[32,512]{1,0:T(8,128)S(1)}, f32[32,512]{1,0:T(8,128)S(1)}, u32[]{:S(2)}, u32[]{:S(2)}) collective-permute-start(f32[32,512]{1,0:T(8,128)S(1)} %get-tuple-element.43), channel_id=1, source_target_pairs={{0,1},{1,2},{2,3},{3,0},{4,5},{5,6},{6,7},{7,4},{8,9},{9,10},{10,1... | collective-permute-start | bytes 196616 | tf_op jit(solution)/shard_map/ppermute | solution.py:453
  174.6 4.9 %collective-permute-start.17 = (f32[32,512]{1,0:T(8,128)S(1)}, f32[32,512]{1,0:T(8,128)S(1)}, u32[]{:S(2)}, u32[]{:S(2)}) collective-permute-start(f32[32,512]{1,0:T(8,128)S(1)} %get-tuple-element.43), channel_id=1, source_target_pairs={{0,2},{1,3},{2,0},{3,1},{4,6},{5,7},{6,4},{7,5},{8,10},{9,11},{10,... | collective-permute-start | bytes 196616 | tf_op jit(solution)/shard_map/ppermute | solution.py:453
  174.9 5.2 %collective-permute-start.18 = (f32[32,512]{1,0:T(8,128)S(1)}, f32[32,512]{1,0:T(8,128)S(1)}, u32[]{:S(2)}, u32[]{:S(2)}) collective-permute-start(f32[32,512]{1,0:T(8,128)S(1)} %get-tuple-element.43), channel_id=1, source_target_pairs={{0,3},{1,0},{2,1},{3,2},{4,7},{5,4},{6,5},{7,6},{8,11},{9,8},{10,9... | collective-permute-start | bytes 196616 | tf_op jit(solution)/shard_map/ppermute | solution.py:453
  180.2 32.9 %collective-permute-start.19 = (f32[128,512]{1,0:T(8,128)S(1)}, f32[128,512]{1,0:T(8,128)S(1)}, u32[]{:S(2)}, u32[]{:S(2)}) collective-permute-start(f32[128,512]{1,0:T(8,128)S(1)} %constant_dynamic-update-slice_fusion), channel_id=1, source_target_pairs={{0,8},{4,12},{8,0},{12,4},{16,24},{20,28},{24,16},{28,20},{1,9},{5... | collective-permute-start | bytes 786440 | tf_op jit(solution)/shard_map/ppermute | solution.py:428
  213.2 11.0 %collective-permute-start.20 = (f32[256,512]{1,0:T(8,128)S(1)}, f32[256,512]{1,0:T(8,128)S(1)}, u32[]{:S(2)}, u32[]{:S(2)}) collective-permute-start(f32[256,512]{1,0:T(8,128)S(1)} %pad_maximum_fusion.2), channel_id=1, source_target_pairs={{0,16},{4,20},{8,24},{12,28},{16,0},{20,4},{24,8},{28,12},{1,17},{... | collective-permute-start | bytes 1572872 | tf_op jit(solution)/shard_map/ppermute | solution.py:428
  213.3 32.8 %collective-permute-start.9 = (f32[2,512,512]{2,1,0:T(8,128)}, f32[2,512,512]{2,1,0:T(8,128)}, u32[]{:S(2)}, u32[]{:S(2)}) collective-permute-start(f32[2,512,512]{2,1,0:T(8,128)} %maximum_add_fusion), channel_id=1, source_target_pairs={{0,1},{1,2},{2,3},{4,5},{5,6},{6,7},{8,9},{9,10},{10,11},{12,13},{... | collective-permute-start | bytes 6291464 | tf_op jit(solution)/shard_map/ppermute | solution.py:415
  225.3 2.9 %collective-permute-start.21 = (f32[512,512]{1,0:T(8,128)}, f32[512,512]{1,0:T(8,128)S(1)}, u32[]{:S(2)}, u32[]{:S(2)}) collective-permute-start(f32[512,512]{1,0:T(8,128)} %pad_maximum_fusion.1), channel_id=1, source_target_pairs={{0,4},{4,0},{8,12},{12,8},{16,20},{20,16},{24,28},{28,24},{1,5},{5... | collective-permute-start | bytes 3145736 | tf_op jit(solution)/shard_map/ppermute | solution.py:428
  228.4 2.9 %copy-start.1 = (f32[2,512,1024]{2,1,0:T(8,128)S(1)}, f32[2,512,1024]{2,1,0:T(8,128)}, u32[]{:S(2)}) copy-start(f32[2,512,1024]{2,1,0:T(8,128)} %get-tuple-element.34) | copy-start | bytes 12582916
  248.3 2.0 copy-start

commit v3 on v2

--- a/solution.py
+++ b/solution.py
@@ -39,8 +39,14 @@
     return jnp.dot(lhs, rhs, preferred_element_type=jnp.float32)
 
 
-def dot3(lhs_hi, lhs_lo, rhs_hi, rhs_lo):
-    return dot(lhs_hi, rhs_hi) + (dot(lhs_hi, rhs_lo) + dot(lhs_lo, rhs_hi))
+def left_dot(mat_hi, mat_lo, val_hi, val_lo):
+    lhs = jnp.concatenate([mat_hi, mat_hi, mat_lo], axis=1)
+    return dot(lhs, jnp.concatenate([val_hi, val_lo, val_hi], axis=0))
+
+
+def right_dot(val_hi, val_lo, mat_hi, mat_lo):
+    lhs = jnp.concatenate([val_hi, val_lo, val_hi], axis=1)
+    return dot(lhs, jnp.concatenate([mat_hi, mat_hi, mat_lo], axis=0))
 
 
 def butterfly(parts, sign):
@@ -98,23 +104,29 @@
 def slots_kernel(
     meta,
     tile_hbm,
-    right_hbm,
-    lower_hbm,
+    right_a_hbm,
+    right_b_hbm,
+    lower_a_hbm,
+    lower_b_hbm,
+    lower_c_hbm,
     corner_a_hbm,
     corner_up_hbm,
     corner_side_hbm,
     amps_hbm,
-    pupil,
-    mat_hi,
-    mat_lo,
-    mat_t_hi,
-    mat_t_lo,
+    pupil_hbm,
+    mat_hi_hbm,
+    mat_lo_hbm,
+    mat_t_hi_hbm,
+    mat_t_lo_hbm,
     own_out,
-    right_out,
-    lower_out,
+    right_a_out,
+    right_b_out,
+    lower_a_out,
+    lower_b_out,
+    lower_c_out,
     corner_a_out,
     corner_b_out,
-    dpup,
+    dpup_out,
     region,
     grads,
     win,
@@ -125,8 +137,15 @@
     cols_f32,
     rows_f32,
     dwin,
+    dpup,
     amps,
-    sems,
+    pupil,
+    mat_hi,
+    mat_lo,
+    mat_t_hi,
+    mat_t_lo,
+    in_sems,
+    out_sems,
 ):
     side = pupil.shape[-1]
     short = side // RADIX
@@ -134,34 +153,74 @@
     slots = amps_hbm.shape[0]
     lanes = 128
     wide = side + lanes
-
     half = side // 2
 
     def pieces(buffer):
         top, bottom = pl.ds(0, tile_rows), pl.ds(tile_rows, side)
         return (
             buffer.at[:, top, pl.ds(0, tile_cols)],
-            buffer.at[:, top, pl.ds(tile_cols, side)],
-            buffer.at[:, bottom, pl.ds(0, tile_cols)],
+            buffer.at[:, top, pl.ds(tile_cols, half)],
+            buffer.at[:, top, pl.ds(tile_cols + half, half)],
+            buffer.at[:, bottom, pl.ds(0, half)],
+            buffer.at[:, bottom, pl.ds(half, half)],
+            buffer.at[:, bottom, pl.ds(side, tile_cols - side)],
             buffer.at[:, bottom, pl.ds(tile_cols, half)],
             buffer.at[:, bottom, pl.ds(tile_cols + half, half)],
         )
 
     odd = meta[slots, 0]
     targets = pieces(region)
-    sources = (tile_hbm, right_hbm, lower_hbm, corner_a_hbm)
+    sources = (
+        tile_hbm,
+        right_a_hbm,
+        right_b_hbm,
+        lower_a_hbm,
+        lower_b_hbm,
+        lower_c_hbm,
+        corner_a_hbm,
+    )
     loads = [
-        pltpu.make_async_copy(src, dst, sems.at[n])
+        pltpu.make_async_copy(src, dst, in_sems.at[n])
         for n, (src, dst) in enumerate(zip(sources, targets))
     ]
-    loads.append(pltpu.make_async_copy(amps_hbm, amps, sems.at[5]))
     for load in loads:
         load.start()
-    from_side = pltpu.make_async_copy(corner_side_hbm, targets[4], sems.at[4])
-    from_below = pltpu.make_async_copy(corner_up_hbm, targets[4], sems.at[4])
+    from_side = pltpu.make_async_copy(corner_side_hbm, targets[7], in_sems.at[7])
+    from_below = pltpu.make_async_copy(corner_up_hbm, targets[7], in_sems.at[7])
     pl.when(odd == 1)(from_side.start)
     pl.when(odd != 1)(from_below.start)
     loads.append(from_side)
+    late = (
+        (pupil_hbm, pupil),
+        (mat_hi_hbm, mat_hi),
+        (mat_lo_hbm, mat_lo),
+        (mat_t_hi_hbm, mat_t_hi),
+        (mat_t_lo_hbm, mat_t_lo),
+        (amps_hbm, amps),
+    )
+    late_loads = [
+        pltpu.make_async_copy(src, dst, in_sems.at[8 + n]) for n, (src, dst) in enumerate(late)
+    ]
+    for load in late_loads:
+        load.start()
+
+    outs = (
+        own_out,
+        right_a_out,
+        right_b_out,
+        lower_a_out,
+        lower_b_out,
+        lower_c_out,
+        corner_a_out,
+        corner_b_out,
+    )
+    stores = [
+        pltpu.make_async_copy(src, dst, out_sems.at[n])
+        for n, (src, dst) in enumerate(zip(pieces(grads), outs))
+    ]
+    dpup_store = pltpu.make_async_copy(dpup, dpup_out, out_sems.at[8])
+    lower_stores = stores[3:]
+    upper_stores = stores[:3]
 
     zero_rows = 16
 
@@ -180,6 +239,10 @@
 
     for load in loads:
         load.wait()
+
+    count = meta[0, 2]
+    for slot in range(1, slots):
+        count = count + meta[slot, 2]
 
     def one_slot(slot):
         row = meta[slot, 0]
@@ -200,6 +263,11 @@
                 tiles = [pull_lanes(tile, col_shift) for tile in tiles]
                 for i, tile in enumerate(pull_rows(tiles, row_shift)):
                     win[plane, pl.ds(base + 8 * i, 8), :] = tile
+
+        @pl.when(slot == 0)
+        def _():
+            for load in late_loads:
+                load.wait()
 
         @pl.loop(0, short // 16)
         def _(step):
@@ -222,13 +290,13 @@
         for p in range(RADIX):
             for half in range(2):
                 cols = pl.ds(half * (side // 2), side // 2)
-                rows_f32[p, :, cols] = dot3(
+                rows_f32[p, :, cols] = left_dot(
                     mat_hi[p], mat_lo[p], left_hi[p, :, cols], left_lo[p, :, cols]
                 )
 
         for p in range(RADIX):
 
-            @pl.loop(0, short // 16)
+            @pl.loop(0, short // 16, unroll=2)
             def _(step):
                 base = pl.multiple_of(step * 16, 16)
                 values = []
@@ -250,17 +318,19 @@
         for t in range(RADIX):
             for half in range(2):
                 rows = pl.ds(half * (side // 2), side // 2)
-                field = dot3(right_hi[t, rows, :], right_lo[t, rows, :], mat_t_hi[t], mat_t_lo[t])
+                field = right_dot(
+                    right_hi[t, rows, :], right_lo[t, rows, :], mat_t_hi[t], mat_t_lo[t]
+                )
                 fre, fim = field[:, :short], field[:, short:]
                 measured = amps[slot, rows, pl.ds(t * short, short)]
                 factor = 1.0 - measured * lax.rsqrt(fre * fre + fim * fim + 1.0)
                 residual = jnp.concatenate([factor * fre, factor * fim], axis=1)
                 hi, lo = split(residual)
-                cols_f32[t, rows, :] = dot3(hi, lo, mat_hi[t], mat_lo[t])
+                cols_f32[t, rows, :] = right_dot(hi, lo, mat_hi[t], mat_lo[t])
 
         for p in range(RADIX):
 
-            @pl.loop(0, short // 16)
+            @pl.loop(0, short // 16, unroll=2)
             def _(step):
                 base = pl.multiple_of(step * 16, 16)
                 rows = pl.ds(base + p * short, 16)
@@ -278,7 +348,7 @@
         for p in range(RADIX):
             for half in range(2):
                 cols = pl.ds(half * (side // 2), side // 2)
-                rows_f32[p, :, cols] = dot3(
+                rows_f32[p, :, cols] = left_dot(
                     mat_t_hi[p], mat_t_lo[p], left_hi[p, :, cols], left_lo[p, :, cols]
                 )
 
@@ -301,8 +371,10 @@
                     dpup[0, rows, cols] += wr * re + wi * im
                     dpup[1, rows, cols] += wr * im - wi * re
 
-        @pl.loop(0, (side + 8) // 40)
-        def _(step):
+        last = slot == count - 1
+        pl.when(last)(dpup_store.start)
+
+        def place(step):
             base = pl.multiple_of(step * 40, 8)
             for plane in range(2):
                 tiles = [dwin[plane, pl.ds(base + 8 * i, 8), :] for i in range(6)]
@@ -312,38 +384,49 @@
                     target = (plane, pl.ds(start, 8), pl.ds(col_base, wide))
                     grads[target] = grads[target] + tile
 
-    @pl.loop(0, slots)
-    def _(slot):
-        pl.when(meta[slot, 2] != 0)(lambda: one_slot(slot))
-
-    targets = (own_out, right_out, lower_out, corner_a_out, corner_b_out)
-    stores = [
-        pltpu.make_async_copy(src, dst, sems.at[n])
-        for n, (src, dst) in enumerate(zip(pieces(grads), targets))
-    ]
-    for store in stores:
+        steps = (side + 8) // 40
+        above = (tile_rows - row_base) // 40
+        pl.loop(above, steps)(place)
+
+        @pl.when(last)
+        def _():
+            for store in lower_stores:
+                store.start()
+
+        pl.loop(0, above)(place)
+
+    pl.loop(0, count)(one_slot)
+
+    @pl.when(count == 0)
+    def _():
+        for store in [dpup_store] + lower_stores:
+            store.start()
+        for load in late_loads:
+            load.wait()
+
+    for store in upper_stores:
         store.start()
-    for store in stores:
+    for store in [dpup_store] + stores:
         store.wait()
 
 
-def slots_call(meta, tile, right, lower, corner_a, corner_up, corner_side, amps, pupil):
+def slots_call(meta, tile, parts, amps, pupil):
     side = pupil.shape[-1]
     short = side // RADIX
     slots = amps.shape[0]
     tile_rows, tile_cols = tile.shape[1:]
     high, low = dft_blocks(side)
     tables = [jnp.asarray(x) for x in (high, low, high.transpose(0, 2, 1), low.transpose(0, 2, 1))]
-    whole = pl.BlockSpec(memory_space=pltpu.VMEM)
     anywhere = pl.BlockSpec(memory_space=pl.ANY)
     f32, bf16 = jnp.float32, jnp.bfloat16
     region = (2, tile_rows + side, tile_cols + side)
-    outs = (tile, right, lower, corner_a, corner_up, pupil)
+    outs = (tile, *parts[:-1], pupil)
+    table = pltpu.VMEM(high.shape, bf16)
     return pl.pallas_call(
         slots_kernel,
         out_shape=[jax.ShapeDtypeStruct(x.shape, f32) for x in outs],
-        in_specs=[pl.BlockSpec(memory_space=pltpu.SMEM)] + [anywhere] * 7 + [whole] * 5,
-        out_specs=[anywhere] * 5 + [whole],
+        in_specs=[pl.BlockSpec(memory_space=pltpu.SMEM)] + [anywhere] * (len(parts) + 7),
+        out_specs=[anywhere] * len(outs),
         scratch_shapes=[
             pltpu.VMEM(region, f32),
             pltpu.VMEM(region, f32),
@@ -355,8 +438,15 @@
             pltpu.VMEM((RADIX, side, 2 * short), f32),
             pltpu.VMEM((RADIX, 2 * short, side), f32),
             pltpu.VMEM((2, side + 16, side), f32),
+            pltpu.VMEM((2, side, side), f32),
             pltpu.VMEM(amps.shape, f32),
-            pltpu.SemaphoreType.DMA((6,)),
+            pltpu.VMEM(pupil.shape, f32),
+            table,
+            table,
+            table,
+            table,
+            pltpu.SemaphoreType.DMA((14,)),
+            pltpu.SemaphoreType.DMA((9,)),
         ],
         compiler_params=pltpu.CompilerParams(vmem_limit_bytes=56 * 1024 * 1024),
         cost_estimate=pl.CostEstimate(
@@ -365,7 +455,7 @@
             transcendentals=slots * side * side,
         ),
         name="slots",
-    )(meta, tile, right, lower, corner_a, corner_up, corner_side, amps, pupil, *tables)
+    )(meta, tile, *parts, amps, pupil, *tables)
 
 
 def exact_parts(value):
@@ -415,12 +505,26 @@
     return lax.ppermute(array, ("ty", "tx"), along(rule, sizes))
 
 
-def halve(value, bit):
+def add_kernel(left, right, out):
+    out[...] = left[...] + right[...]
+
+
+def add_beside_transfers(left, right):
+    return pl.pallas_call(
+        add_kernel,
+        out_shape=jax.ShapeDtypeStruct(left.shape, left.dtype),
+        cost_estimate=pl.CostEstimate(flops=60 * 10**9, bytes_accessed=2**27, transcendentals=0),
+        name="add_beside_transfers",
+    )(left, right)
+
+
+def halve(value, bit, beside=False):
     rows = value.shape[0] // 2
     mine = lax.axis_index("ty") // bit % 2
     kept = lax.dynamic_slice_in_dim(value, mine * rows, rows, 0)
     sent = lax.dynamic_slice_in_dim(value, (1 - mine) * rows, rows, 0)
-    return kept + lax.ppermute(sent, "ty", [(i, i ^ bit) for i in range(lax.axis_size("ty"))])
+    received = lax.ppermute(sent, "ty", [(i, i ^ bit) for i in range(lax.axis_size("ty"))])
+    return add_beside_transfers(kept, received) if beside else kept + received
 
 
 def double(value, bit):
@@ -465,8 +569,8 @@
         bits.append(bit)
         bit //= 2
     part = dpup.reshape(-1, dpup.shape[-1])
-    for bit in bits:
-        part = halve(part, bit)
+    for number, bit in enumerate(bits):
+        part = halve(part, bit, number == 1)
     part = scatter_tx(part) * (1.0 / math.sqrt(n_ty * n_tx))
     part = gather_tx(part)
     for bit in reversed(bits):
@@ -484,25 +588,49 @@
     meta = jnp.stack([rows_local, cols_local, live], axis=1)
     meta = jnp.concatenate([meta, jnp.full((1, 3), own_ty % 2, jnp.int32)], axis=0)
 
-    right = send(spectrum[:, :, :side], lambda i, j: (i, j - 1))
-    lower = send(spectrum[:, :side, :], lambda i, j: (i - 1, j))
-    corner_a = send(right[:, :, :half], lambda i, j: (i - 1, j))
-    corner_up = send(right[:, :, half:], lambda i, j: (i - 1, j) if i % 2 else None)
-    corner_side = send(lower[:, :, half:side], lambda i, j: (i, j - 1) if i % 2 else None)
-
-    own_g, right_g, lower_g, corner_a_g, corner_b_g, dpup = slots_call(
-        meta, spectrum, right, lower, corner_a, corner_up, corner_side, ordered(amplitudes), pupil
+    def left(i, j):
+        return (i, j - 1)
+
+    def up(i, j):
+        return (i - 1, j)
+
+    lower_b = send(spectrum[:, :side, half:side], up)
+    right_a = send(spectrum[:, :, :half], left)
+    right_b = send(spectrum[:, :, half:side], left)
+    lower_a = send(spectrum[:, :side, :half], up)
+    lower_c = send(spectrum[:, :side, side:], up)
+    amps = ordered(amplitudes)
+    lower_b, amps = lax.optimization_barrier((lower_b, amps))
+    corner_side = send(lower_b, lambda i, j: (i, j - 1) if i % 2 else None)
+    corner_a = send(right_a[:, :side], up)
+    corner_up = send(right_b[:, :side], lambda i, j: (i - 1, j) if i % 2 else None)
+
+    parts = (right_a, right_b, lower_a, lower_b, lower_c, corner_a, corner_up, corner_side)
+    own_g, *grads, dpup = slots_call(meta, spectrum, parts, amps, pupil)
+    right_a_g, right_b_g, lower_a_g, lower_b_g, lower_c_g, corner_a_g, corner_b_g = grads
+
+    def down(i, j):
+        return (i + 1, j)
+
+    def right(i, j):
+        return (i, j + 1)
+
+    back_side = send(corner_b_g, lambda i, j: (i, j + 1) if i % 2 else None)
+    back_a = send(corner_a_g, down)
+    back_down = send(corner_b_g, lambda i, j: None if i % 2 else (i + 1, j))
+    lower_a = send(lower_a_g, down)
+    lower_c = send(lower_c_g, down)
+    right_b = send(right_b_g + back_down, right)
+    right_a = send(right_a_g + back_a, right)
+    lower_b = send(lower_b_g + back_side, down)
+    spec_grad = jnp.concatenate(
+        [
+            own_g[:, :, :half] + lower_a + right_a,
+            own_g[:, :, half:side] + lower_b + right_b,
+            own_g[:, :, side:] + lower_c,
+        ],
+        axis=2,
     )
-
-    back_a = send(corner_a_g, lambda i, j: (i + 1, j))
-    back_down = send(corner_b_g, lambda i, j: None if i % 2 else (i + 1, j))
-    back_side = send(corner_b_g, lambda i, j: (i, j + 1) if i % 2 else None)
-    right_total = right_g + jnp.concatenate([back_a, back_down], axis=2)
-    lower_total = lower_g.at[:, :, half:side].add(back_side)
-    right_total, lower_total = lax.optimization_barrier((right_total, lower_total))
-    right_back = send(right_total, lambda i, j: (i, j + 1))
-    lower_back = send(lower_total, lambda i, j: (i + 1, j))
-    spec_grad = (own_g + lower_back).at[:, :, :side].add(right_back)
     return spec_grad, pupil_sum(dpup)
 
 

time: 251 us -> 267 us (1.064)
  waiting for transfers between devices: 116 us -> 131 us
  starting transfers between devices: 72.6 us -> 75.5 us
    ppermute x3, starting transfers between devices: 0.15 us -> 23.2 us  [halve(): lax.ppermute(sent, 'ty', [(i, i ^ bit) for i in range(lax.axis_size('ty'))])]
    ppermute x10 -> x16, waiting for transfers between devices: 65.5 us -> 83.7 us  [send(): return lax.ppermute(array, ('ty', 'tx'), along(rule, sizes))]
    ppermute x10 -> x16, starting transfers between devices: 57.8 us -> 41.3 us  [send(): return lax.ppermute(array, ('ty', 'tx'), along(rule, sizes))]
    ppermute x3, waiting for transfers between devices: 33.9 us -> 17.8 us  [double(): lax.ppermute(value, 'ty', [(i, i ^ bit) for i in range(lax.axis_size('ty'...]
    ppermute x3, waiting for transfers between devices: 9.8 us -> 21.9 us  [halve(): lax.ppermute(sent, 'ty', [(i, i ^ bit) for i in range(lax.axis_size('ty'))])]
    scatter-add x2 -> x0, other arithmetic: 4.88 us -> none  [the longest x1 2.75 us: body(): lower_total = lower_g.at[:, :, half:side].add(back_side)]
    ppermute x3, starting transfers between devices: 9.32 us -> 4.63 us  [scatter_tx(): total = total + lax.ppermute(piece, 'tx', ring_pairs(size, step))]
    add x5 -> x7, other arithmetic: 9.3 us -> 13.9 us  [the longest x1 2.87 us: body(): own_g[:, :, side:] + lower_c]
  transfers between devices with their start and end apart: 22 -> 28, of which waited for: 12 -> 17; matrix products, arithmetic and copies ran while one was open for 8% -> 6% of each run, Pallas kernels for 3% -> 3%
where the time goes in v3:
time: 267 us; the launch traced here: 266 us
  waiting for transfers between devices  131 us (49%)
  starting transfers between devices  75.5 us (28%)
  Pallas kernels  31.1 us (12%)
  other arithmetic  19.7 us (7%)
  local copies, waits for them, and re-layouts  8.18 us (3%)
    ppermute x16, waiting for transfers between devices, send(): return lax.ppermute(array, ('ty', 'tx'), along(rule, sizes))  83.7 us
    ppermute x16, starting transfers between devices, send(): return lax.ppermute(array, ('ty', 'tx'), along(rule, sizes))  41.3 us
    ppermute x3, starting transfers between devices, halve(): lax.ppermute(sent, 'ty', [(i, i ^ bit) for i in range(lax.axis_size('ty'))])  23.2 us
    ppermute x3, waiting for transfers between devices, halve(): lax.ppermute(sent, 'ty', [(i, i ^ bit) for i in range(lax.axis_size('ty'))])  21.9 us
    pallas_call x1, Pallas kernels, slots_call(): pl.pallas_call(slots_kernel, out_shape=[jax.ShapeDtypeStruct(x.shape, f32...  20.8 us
    ppermute x3, waiting for transfers between devices, double(): lax.ppermute(value, 'ty', [(i, i ^ bit) for i in range(lax.axis_size('ty'...  17.8 us
    pallas_call x1, Pallas kernels, ordered(): pl.pallas_call(order_kernel, grid=(slots,), out_shape=jax.ShapeDtypeStruc...  8.23 us
  transfers between devices with their start and end apart: 28, of which 17 were waited for; matrix products, arithmetic and copies ran while one was open for 6% of the time, Pallas kernels for 3%

profile of v3, /device:TPU:1, one launch (start us, length us, event | category | flops | bytes accessed | tf_op | source)
XLA Modules:
  0.0 266.4 jit_solution(4283143274937539527)
XLA Ops:
  0.6 2.9 %fusion = (f32[2,512,256]{2,1,0:T(8,128)}, f32[2,512,256]{2,1,0:T(8,128)S(1)}) fusion(f32[2,512,1024]{2,1,0:T(8,128)} %tile_hbm.1), kind=kLoop, calls=%fused_computation.30 | loop fusion | bytes 4194304 | tf_op jit(solution)/shard_map/slice | solution.py:599
  3.5 2.0 collective-permute-start.3
  5.5 1.3 collective-permute-start
  6.8 1.3 collective-permute-start.1
  8.1 0.2 slice.30
  8.3 1.9 collective-permute-start.4
  10.3 1.9 collective-permute-start.2
  12.2 8.2 %ordered.1.amps_hbm = f32[3,512,512]{2,1,0:T(8,128)} custom-call(f32[3,512,512]{2,1,0:T(8,128)} %amps.1, bf16[512,512]{1,0:T(8,128)(2,1)} %constant.141.clone.perm_rows, bf16[512,512]{1,0:T(8,128)(2,1)} %constant.142.clone.perm_cols), custom_call_target="tpu_custom_call" | custom-call | flops 4831838208 | bytes 6291456 | tf_op jit(solution)/shard_map/ordered/pallas_call | solution.py:479
  20.4 0.7 collective-permute-done.3.lower_b_hbm
  21.1 12.8 %collective-permute-done.right_a_hbm = f32[2,512,256]{2,1,0:T(8,128)} collective-permute-done((f32[2,512,256]{2,1,0:T(8,128)S(1)}, f32[2,512,256]{2,1,0:T(8,128)}, u32[]{:S(2)}, u32[]{:S(2)}) %collective-permute-start) | collective-permute-done | bytes 1048608 | tf_op jit(solution)/shard_map/ppermute | solution.py:505
  33.9 1.9 collective-permute-start.5
  35.8 19.9 %collective-permute-done.1.right_b_hbm = f32[2,512,256]{2,1,0:T(8,128)} collective-permute-done((f32[2,512,256]{2,1,0:T(8,128)}, f32[2,512,256]{2,1,0:T(8,128)}, u32[]{:S(2)}, u32[]{:S(2)}) %collective-permute-start.1) | collective-permute-done | bytes 1048608 | tf_op jit(solution)/shard_map/ppermute | solution.py:505
  55.7 3.2 %collective-permute-start.6 = (f32[2,512,256]{2,1,0:T(8,128)}, f32[2,512,256]{2,1,0:T(8,128)}, u32[]{:S(2)}, u32[]{:S(2)}) collective-permute-start(f32[2,512,256]{2,1,0:T(8,128)} %collective-permute-done.1.right_b_hbm), channel_id=1, source_target_pairs={{4,0},{5,1},{6,2},{7,3},{12,8},{13,9},{14,10},{15,11},{20,16},{21,... | collective-permute-start | bytes 3145736 | tf_op jit(solution)/shard_map/ppermute | solution.py:505
  58.9 1.3 collective-permute-start.7
  60.2 0.1 copy.15
  60.3 0.1 copy.17
  60.6 0.6 concatenate.15.meta
  61.2 4.6 %collective-permute-done.5.corner_a_hbm = f32[2,512,256]{2,1,0:T(8,128)} collective-permute-done((f32[2,512,256]{2,1,0:T(8,128)}, f32[2,512,256]{2,1,0:T(8,128)}, u32[]{:S(2)}, u32[]{:S(2)}) %collective-permute-start.5) | collective-permute-done | bytes 1048608 | tf_op jit(solution)/shard_map/ppermute | solution.py:505
  65.7 9.5 %collective-permute-done.7.corner_side_hbm = f32[2,512,256]{2,1,0:T(8,128)} collective-permute-done((f32[2,512,256]{2,1,0:T(8,128)}, f32[2,512,256]{2,1,0:T(8,128)}, u32[]{:S(2)}, u32[]{:S(2)}) %collective-permute-start.7) | collective-permute-done | bytes 1048608 | tf_op jit(solution)/shard_map/ppermute | solution.py:505
  75.2 20.8 %slots.1 = (f32[2,512,1024]{2,1,0:T(8,128)}, f32[2,512,256]{2,1,0:T(8,128)}, f32[2,512,256]{2,1,0:T(8,128)}, f32[2,512,256]{2,1,0:T(8,128)}, f32[2,512,256]{2,1,...) custom-call(s32[4,3]{1,0:T(4,128)} %concatenate.15.meta, ...), custom_call_target="tpu_custom_call" | custom-call | flops 9663676416 | bytes 41943040 | tf_op jit(solution)/shard_map/slots/pallas_call | solution.py:425
  96.0 1.4 constant_dynamic-slice_fusion.6
  97.6 2.7 %collective-permute-done.16 = f32[512,512]{1,0:T(8,128)} collective-permute-done((f32[512,512]{1,0:T(8,128)S(1)}, f32[512,512]{1,0:T(8,128)}, u32[]{:S(2)}, u32[]{:S(2)}) %collective-permute-start.16) | collective-permute-done | bytes 1048608 | tf_op jit(solution)/shard_map/ppermute | solution.py:526
  100.3 1.4 dynamic-slice_add_fusion
  101.8 0.9 constant_dynamic-slice_fusion.4
  102.6 23.1 %collective-permute-start.17 = (f32[256,512]{1,0:T(8,128)S(1)}, f32[256,512]{1,0:T(8,128)S(1)}, u32[]{:S(2)}, u32[]{:S(2)}) collective-permute-start(f32[256,512]{1,0:T(8,128)S(1)} %get-tuple-element.34), channel_id=1, source_target_pairs={{0,16},{4,20},{8,24},{12,28},{16,0},{20,4},{24,8},{28,12},{1,17},{... | collective-permute-start | bytes 1572872 | tf_op jit(solution)/shard_map/ppermute | solution.py:526
  125.7 12.2 %collective-permute-done.17.right = f32[256,512]{1,0:T(8,128)S(1)} collective-permute-done((f32[256,512]{1,0:T(8,128)S(1)}, f32[256,512]{1,0:T(8,128)S(1)}, u32[]{:S(2)}, u32[]{:S(2)}) %collective-permute-start.17) | collective-permute-done | bytes 524320 | tf_op jit(solution)/shard_map/ppermute | solution.py:526
  137.9 0.8 copy-done.9
  138.7 2.1 add_beside_transfers.1
  140.8 1.0 constant_dynamic-slice_fusion.3
  141.9 7.1 %collective-permute-done.18 = f32[128,512]{1,0:T(8,128)S(1)} collective-permute-done((f32[128,512]{1,0:T(8,128)S(1)}, f32[128,512]{1,0:T(8,128)S(1)}, u32[]{:S(2)}, u32[]{:S(2)}) %collective-permute-start.18) | collective-permute-done | bytes 262176 | tf_op jit(solution)/shard_map/ppermute | solution.py:526
  149.0 1.0 dynamic-slice_add_fusion.1
  150.0 2.2 collective-permute-start.21
  152.2 1.0 collective-permute-start.20
  153.2 1.4 collective-permute-start.19
  154.6 2.7 %collective-permute-done.20 = f32[32,512]{1,0:T(8,128)S(1)} collective-permute-done((f32[32,512]{1,0:T(8,128)S(1)}, f32[32,512]{1,0:T(8,128)S(1)}, u32[]{:S(2)}, u32[]{:S(2)}) %collective-permute-start.20) | collective-permute-done | bytes 65568 | tf_op jit(solution)/shard_map/ppermute | solution.py:548
  157.4 1.6 collective-permute-done.19
  159.1 5.3 %collective-permute-start.15 = (f32[2,512,512]{2,1,0:T(8,128)}, f32[2,512,512]{2,1,0:T(8,128)}, u32[]{:S(2)}, u32[]{:S(2)}) collective-permute-start(f32[2,512,512]{2,1,0:T(8,128)} %get-tuple-element.22), channel_id=1, source_target_pairs={{0,4},{1,5},{2,6},{3,7},{4,8},{5,9},{6,10},{7,11},{8,12},{9,13},{1... | collective-permute-start | bytes 6291464 | tf_op jit(solution)/shard_map/ppermute | solution.py:505
  164.4 1.3 collective-permute-start.23
  165.7 2.3 collective-permute-start.24
  168.0 2.8 %collective-permute-done.23 = f32[32,512]{1,0:T(8,128)S(1)} collective-permute-done((f32[32,512]{1,0:T(8,128)S(1)}, f32[32,512]{1,0:T(8,128)S(1)}, u32[]{:S(2)}, u32[]{:S(2)}) %collective-permute-start.23) | collective-permute-done | bytes 65568 | tf_op jit(solution)/shard_map/ppermute | solution.py:557
  170.9 0.2 collective-permute-done.24
  171.0 1.1 collective-permute-start.25
  172.1 2.9 %collective-permute-start.9 = (f32[2,512,256]{2,1,0:T(8,128)}, f32[2,512,256]{2,1,0:T(8,128)S(1)}, u32[]{:S(2)}, u32[]{:S(2)}) collective-permute-start(f32[2,512,256]{2,1,0:T(8,128)} %get-tuple-element.18), channel_id=1, source_target_pairs={{0,4},{1,5},{2,6},{3,7},{4,8},{5,9},{6,10},{7,11},{8,12},{9,13},{1... | collective-permute-start | bytes 3145736 | tf_op jit(solution)/shard_map/ppermute | solution.py:505
  175.0 1.3 collective-permute-start.13
  176.3 4.5 %collective-permute-start.11 = (f32[2,512,256]{2,1,0:T(8,128)}, f32[2,512,256]{2,1,0:T(8,128)}, u32[]{:S(2)}, u32[]{:S(2)}) collective-permute-start(f32[2,512,256]{2,1,0:T(8,128)} %get-tuple-element.20), channel_id=1, source_target_pairs={{4,5},{5,6},{6,7},{12,13},{13,14},{14,15},{20,21},{21,22},{22,23},... | collective-permute-start | bytes 3145736 | tf_op jit(solution)/shard_map/ppermute | solution.py:505
  180.8 14.1 %collective-permute-done.25 = f32[128,512]{1,0:T(8,128)S(1)} collective-permute-done((f32[128,512]{1,0:T(8,128)S(1)}, f32[128,512]{1,0:T(8,128)S(1)}, u32[]{:S(2)}, u32[]{:S(2)}) %collective-permute-start.25) | collective-permute-done | bytes 262176 | tf_op jit(solution)/shard_map/ppermute | solution.py:532
  195.1 9.5 %collective-permute-done.9 = f32[2,512,256]{2,1,0:T(8,128)S(1)} collective-permute-done((f32[2,512,256]{2,1,0:T(8,128)}, f32[2,512,256]{2,1,0:T(8,128)S(1)}, u32[]{:S(2)}, u32[]{:S(2)}) %collective-permute-start.9) | collective-permute-done | bytes 1048608 | tf_op jit(solution)/shard_map/ppermute | solution.py:505
  204.5 4.3 %collective-permute-start.8 = (f32[2,512,256]{2,1,0:T(8,128)}, f32[2,512,256]{2,1,0:T(8,128)}, u32[]{:S(2)}, u32[]{:S(2)}) collective-permute-start(f32[2,512,256]{2,1,0:T(8,128)} %get-tuple-element.16), channel_id=1, source_target_pairs={{0,4},{1,5},{2,6},{3,7},{4,8},{5,9},{6,10},{7,11},{8,12},{9,13},{1... | collective-permute-start | bytes 3145736 | tf_op jit(solution)/shard_map/ppermute | solution.py:505
  208.8 1.4 add.135
  210.2 4.1 %collective-permute-start.10 = (f32[2,512,256]{2,1,0:T(8,128)S(1)}, f32[2,512,256]{2,1,0:T(8,128)}, u32[]{:S(2)}, u32[]{:S(2)}) collective-permute-start(f32[2,512,256]{2,1,0:T(8,128)S(1)} %add.135), channel_id=1, source_target_pairs={{0,1},{1,2},{2,3},{4,5},{5,6},{6,7},{8,9},{9,10},{10,11},{12,13},{... | collective-permute-start | bytes 3145736 | tf_op jit(solution)/shard_map/ppermute | solution.py:505
  214.3 2.3 add.139
  216.6 2.4 collective-permute-start.14
  219.0 2.3 add.137
  221.3 3.7 %collective-permute-done.26 = f32[256,512]{1,0:T(8,128)S(1)} collective-permute-done((f32[256,512]{1,0:T(8,128)S(1)}, f32[256,512]{1,0:T(8,128)S(1)}, u32[]{:S(2)}, u32[]{:S(2)}) %collective-permute-start.26) | collective-permute-done | bytes 524320 | tf_op jit(solution)/shard_map/ppermute | solution.py:532
  225.0 1.9 collective-permute-start.12
  226.9 0.1 broadcast_select_fusion.3
  227.2 1.5 collective-permute-start.27
  228.7 2.9 %slice_add_fusion = f32[2,512,512]{2,1,0:T(8,128)S(1)} fusion(f32[2,512,512]{2,1,0:T(8,128)} %collective-permute-done.15, f32[2,512,1024]{2,1,0:T(8,128)} %get-tuple-element.15), kind=kLoop, calls=%fused_computation.2 | loop fusion | flops 524288 | bytes 6291456 | tf_op jit(solution)/shard_map/add | solution.py:630
  231.6 4.6 %collective-permute-done.10 = f32[2,512,256]{2,1,0:T(8,128)} collective-permute-done((f32[2,512,256]{2,1,0:T(8,128)S(1)}, f32[2,512,256]{2,1,0:T(8,128)}, u32[]{:S(2)}, u32[]{:S(2)}) %collective-permute-start.10) | collective-permute-done | bytes 1048608 | tf_op jit(solution)/shard_map/ppermute | solution.py:505
  236.2 22.2 %collective-permute-done.14 = f32[2,512,256]{2,1,0:T(8,128)} collective-permute-done((f32[2,512,256]{2,1,0:T(8,128)}, f32[2,512,256]{2,1,0:T(8,128)}, u32[]{:S(2)}, u32[]{:S(2)}) %collective-permute-start.14) | collective-permute-done | bytes 1048608 | tf_op jit(solution)/shard_map/ppermute | solution.py:505
  258.4 2.6 add_add_fusion.1
  261.0 2.5 pad_maximum_fusion
  263.5 1.4 broadcast_select_fusion.1
  264.9 1.5 pad_maximum_fusion.1
  (47 shorter events, 0.8 us)
Async XLA Ops:
  0.6 7.4 %copy-start = (f32[2,512,1024]{2,1,0:T(8,128)S(1)}, f32[2,512,1024]{2,1,0:T(8,128)}, u32[]{:S(2)}) copy-start(f32[2,512,1024]{2,1,0:T(8,128)} %tile_hbm.1) | copy-start | bytes 12582916
  3.5 17.6 %collective-permute-start.3 = (f32[2,512,256]{2,1,0:T(8,128)}, f32[2,512,256]{2,1,0:T(8,128)}, u32[]{:S(2)}, u32[]{:S(2)}) collective-permute-start(f32[2,512,256]{2,1,0:T(8,128)} %get-tuple-element.28), channel_id=1, source_target_pairs={{4,0},{5,1},{6,2},{7,3},{8,4},{9,5},{10,6},{11,7},{12,8},{13,9},{1... | collective-permute-start | bytes 3145736 | tf_op jit(solution)/shard_map/ppermute | solution.py:505
  5.5 28.4 %collective-permute-start = (f32[2,512,256]{2,1,0:T(8,128)S(1)}, f32[2,512,256]{2,1,0:T(8,128)}, u32[]{:S(2)}, u32[]{:S(2)}) collective-permute-start(f32[2,512,256]{2,1,0:T(8,128)S(1)} %get-tuple-element.29), channel_id=1, source_target_pairs={{1,0},{2,1},{3,2},{5,4},{6,5},{7,6},{9,8},{10,9},{11,10},{13,12},{... | collective-permute-start | bytes 3145736 | tf_op jit(solution)/shard_map/ppermute | solution.py:505
  6.8 48.9 %collective-permute-start.1 = (f32[2,512,256]{2,1,0:T(8,128)}, f32[2,512,256]{2,1,0:T(8,128)}, u32[]{:S(2)}, u32[]{:S(2)}) collective-permute-start(f32[2,512,256]{2,1,0:T(8,128)} %get-tuple-element.28), channel_id=1, source_target_pairs={{1,0},{2,1},{3,2},{5,4},{6,5},{7,6},{9,8},{10,9},{11,10},{13,12},{... | collective-permute-start | bytes 3145736 | tf_op jit(solution)/shard_map/ppermute | solution.py:505
  8.3 51.9 %copy-start.8 = (s32[3]{0:T(128)S(1)}, s32[3]{0:T(128)}, u32[]{:S(2)}) copy-start(s32[3]{0:T(128)} %param.15) | copy-start | bytes 40
  8.3 52.0 %copy-start.7 = (s32[3,2]{0,1:T(2,128)S(1)}, s32[3,2]{0,1:T(2,128)}, u32[]{:S(2)}) copy-start(s32[3,2]{0,1:T(2,128)} %param.14) | copy-start | bytes 76
  8.3 52.8 %collective-permute-start.4 = (f32[2,512,512]{2,1,0:T(8,128)S(1)}, f32[2,512,512]{2,1,0:T(8,128)}, u32[]{:S(2)}, u32[]{:S(2)}) collective-permute-start(f32[2,512,512]{2,1,0:T(8,128)S(1)} %slice.30), channel_id=1, source_target_pairs={{4,0},{5,1},{6,2},{7,3},{8,4},{9,5},{10,6},{11,7},{12,8},{13,9},{1... | collective-permute-start | bytes 6291464 | tf_op jit(solution)/shard_map/ppermute | solution.py:505
  10.3 50.9 %collective-permute-start.2 = (f32[2,512,256]{2,1,0:T(8,128)S(1)}, f32[2,512,256]{2,1,0:T(8,128)}, u32[]{:S(2)}, u32[]{:S(2)}) collective-permute-start(f32[2,512,256]{2,1,0:T(8,128)S(1)} %get-tuple-element.29), channel_id=1, source_target_pairs={{4,0},{5,1},{6,2},{7,3},{8,4},{9,5},{10,6},{11,7},{12,8},{13,9},{1... | collective-permute-start | bytes 3145736 | tf_op jit(solution)/shard_map/ppermute | solution.py:505
  33.9 31.9 %collective-permute-start.5 = (f32[2,512,256]{2,1,0:T(8,128)}, f32[2,512,256]{2,1,0:T(8,128)}, u32[]{:S(2)}, u32[]{:S(2)}) collective-permute-start(f32[2,512,256]{2,1,0:T(8,128)} %collective-permute-done.right_a_hbm), channel_id=1, source_target_pairs={{4,0},{5,1},{6,2},{7,3},{8,4},{9,5},{10,6},{11,7},{12,8},{13,9},{1... | collective-permute-start | bytes 3145736 | tf_op jit(solution)/shard_map/ppermute | solution.py:505
  55.7 10.1 %collective-permute-start.6 = (f32[2,512,256]{2,1,0:T(8,128)}, f32[2,512,256]{2,1,0:T(8,128)}, u32[]{:S(2)}, u32[]{:S(2)}) collective-permute-start(f32[2,512,256]{2,1,0:T(8,128)} %collective-permute-done.1.right_b_hbm), channel_id=1, source_target_pairs={{4,0},{5,1},{6,2},{7,3},{12,8},{13,9},{14,10},{15,11},{20,16},{21,... | collective-permute-start | bytes 3145736 | tf_op jit(solution)/shard_map/ppermute | solution.py:505
  58.9 16.3 %collective-permute-start.7 = (f32[2,512,256]{2,1,0:T(8,128)}, f32[2,512,256]{2,1,0:T(8,128)}, u32[]{:S(2)}, u32[]{:S(2)}) collective-permute-start(f32[2,512,256]{2,1,0:T(8,128)} %collective-permute-done.3.lower_b_hbm), channel_id=1, source_target_pairs={{5,4},{6,5},{7,6},{13,12},{14,13},{15,14},{21,20},{22,21},{23,22},... | collective-permute-start | bytes 3145736 | tf_op jit(solution)/shard_map/ppermute | solution.py:505
  96.0 4.3 %copy-start.2 = (f32[2,512,512]{2,1,0:T(8,128)S(1)}, f32[2,512,512]{2,1,0:T(8,128)}, u32[]{:S(2)}) copy-start(f32[2,512,512]{2,1,0:T(8,128)} %get-tuple-element.23) | copy-start | bytes 6291460
  97.5 2.9 %collective-permute-start.16 = (f32[512,512]{1,0:T(8,128)S(1)}, f32[512,512]{1,0:T(8,128)}, u32[]{:S(2)}, u32[]{:S(2)}) collective-permute-start(f32[512,512]{1,0:T(8,128)S(1)} %constant_dynamic-slice_fusion.6), channel_id=1, source_target_pairs={{0,4},{4,0},{8,12},{12,8},{16,20},{20,16},{24,28},{28,24},{1,5},{5... | collective-permute-start | bytes 3145736 | tf_op jit(solution)/shard_map/ppermute | solution.py:526
  102.6 35.3 %collective-permute-start.17 = (f32[256,512]{1,0:T(8,128)S(1)}, f32[256,512]{1,0:T(8,128)S(1)}, u32[]{:S(2)}, u32[]{:S(2)}) collective-permute-start(f32[256,512]{1,0:T(8,128)S(1)} %get-tuple-element.34), channel_id=1, source_target_pairs={{0,16},{4,20},{8,24},{12,28},{16,0},{20,4},{24,8},{28,12},{1,17},{... | collective-permute-start | bytes 1572872 | tf_op jit(solution)/shard_map/ppermute | solution.py:526
  137.9 0.8 copy-start.9
  141.8 7.2 %collective-permute-start.18 = (f32[128,512]{1,0:T(8,128)S(1)}, f32[128,512]{1,0:T(8,128)S(1)}, u32[]{:S(2)}, u32[]{:S(2)}) collective-permute-start(f32[128,512]{1,0:T(8,128)S(1)} %constant_dynamic-slice_fusion.3), channel_id=1, source_target_pairs={{0,8},{4,12},{8,0},{12,4},{16,24},{20,28},{24,16},{28,20},{1,9},{5... | collective-permute-start | bytes 786440 | tf_op jit(solution)/shard_map/ppermute | solution.py:526
  141.9 66.9 %copy-start.5 = (f32[2,512,256]{2,1,0:T(8,128)S(1)}, f32[2,512,256]{2,1,0:T(8,128)}, u32[]{:S(2)}) copy-start(f32[2,512,256]{2,1,0:T(8,128)} %get-tuple-element.17) | copy-start | bytes 3145732
  150.0 4.6 %collective-permute-start.21 = (f32[32,512]{1,0:T(8,128)S(1)}, f32[32,512]{1,0:T(8,128)S(1)}, u32[]{:S(2)}, u32[]{:S(2)}) collective-permute-start(f32[32,512]{1,0:T(8,128)S(1)} %get-tuple-element.39), channel_id=1, source_target_pairs={{0,3},{1,0},{2,1},{3,2},{4,7},{5,4},{6,5},{7,6},{8,11},{9,8},{10,9... | collective-permute-start | bytes 196616 | tf_op jit(solution)/shard_map/ppermute | solution.py:548
  152.2 5.2 %collective-permute-start.20 = (f32[32,512]{1,0:T(8,128)S(1)}, f32[32,512]{1,0:T(8,128)S(1)}, u32[]{:S(2)}, u32[]{:S(2)}) collective-permute-start(f32[32,512]{1,0:T(8,128)S(1)} %get-tuple-element.40), channel_id=1, source_target_pairs={{0,2},{1,3},{2,0},{3,1},{4,6},{5,7},{6,4},{7,5},{8,10},{9,11},{10,... | collective-permute-start | bytes 196616 | tf_op jit(solution)/shard_map/ppermute | solution.py:548
  153.2 5.7 %collective-permute-start.19 = (f32[32,512]{1,0:T(8,128)S(1)}, f32[32,512]{1,0:T(8,128)S(1)}, u32[]{:S(2)}, u32[]{:S(2)}) collective-permute-start(f32[32,512]{1,0:T(8,128)S(1)} %get-tuple-element.38), channel_id=1, source_target_pairs={{0,1},{1,2},{2,3},{3,0},{4,5},{5,6},{6,7},{7,4},{8,9},{9,10},{10,1... | collective-permute-start | bytes 196616 | tf_op jit(solution)/shard_map/ppermute | solution.py:548
  159.0 9.0 %collective-permute-start.22 = (f32[32,512]{1,0:T(8,128)S(1)}, f32[32,512]{1,0:T(8,128)S(1)}, u32[]{:S(2)}, u32[]{:S(2)}) collective-permute-start(f32[32,512]{1,0:T(8,128)S(1)} %get-tuple-element.25), channel_id=1, source_target_pairs={{0,1},{1,2},{2,3},{3,0},{4,5},{5,6},{6,7},{7,4},{8,9},{9,10},{10,1... | collective-permute-start | bytes 196616 | tf_op jit(solution)/shard_map/ppermute | solution.py:557
  159.1 68.0 %collective-permute-start.15 = (f32[2,512,512]{2,1,0:T(8,128)}, f32[2,512,512]{2,1,0:T(8,128)}, u32[]{:S(2)}, u32[]{:S(2)}) collective-permute-start(f32[2,512,512]{2,1,0:T(8,128)} %get-tuple-element.22), channel_id=1, source_target_pairs={{0,4},{1,5},{2,6},{3,7},{4,8},{5,9},{6,10},{7,11},{8,12},{9,13},{1... | collective-permute-start | bytes 6291464 | tf_op jit(solution)/shard_map/ppermute | solution.py:505
  164.4 6.4 %collective-permute-start.23 = (f32[32,512]{1,0:T(8,128)S(1)}, f32[32,512]{1,0:T(8,128)S(1)}, u32[]{:S(2)}, u32[]{:S(2)}) collective-permute-start(f32[32,512]{1,0:T(8,128)S(1)} %get-tuple-element.25), channel_id=1, source_target_pairs={{0,2},{1,3},{2,0},{3,1},{4,6},{5,7},{6,4},{7,5},{8,10},{9,11},{10,... | collective-permute-start | bytes 196616 | tf_op jit(solution)/shard_map/ppermute | solution.py:557
  165.7 5.3 %collective-permute-start.24 = (f32[32,512]{1,0:T(8,128)S(1)}, f32[32,512]{1,0:T(8,128)S(1)}, u32[]{:S(2)}, u32[]{:S(2)}) collective-permute-start(f32[32,512]{1,0:T(8,128)S(1)} %get-tuple-element.25), channel_id=1, source_target_pairs={{0,3},{1,0},{2,1},{3,2},{4,7},{5,4},{6,5},{7,6},{8,11},{9,8},{10,9... | collective-permute-start | bytes 196616 | tf_op jit(solution)/shard_map/ppermute | solution.py:557
  171.0 23.9 %collective-permute-start.25 = (f32[128,512]{1,0:T(8,128)S(1)}, f32[128,512]{1,0:T(8,128)S(1)}, u32[]{:S(2)}, u32[]{:S(2)}) collective-permute-start(f32[128,512]{1,0:T(8,128)S(1)} %constant_dynamic-update-slice_fusion), channel_id=1, source_target_pairs={{0,8},{4,12},{8,0},{12,4},{16,24},{20,28},{24,16},{28,20},{1,9},{5... | collective-permute-start | bytes 786440 | tf_op jit(solution)/shard_map/ppermute | solution.py:532
  172.1 32.4 %collective-permute-start.9 = (f32[2,512,256]{2,1,0:T(8,128)}, f32[2,512,256]{2,1,0:T(8,128)S(1)}, u32[]{:S(2)}, u32[]{:S(2)}) collective-permute-start(f32[2,512,256]{2,1,0:T(8,128)} %get-tuple-element.18), channel_id=1, source_target_pairs={{0,4},{1,5},{2,6},{3,7},{4,8},{5,9},{6,10},{7,11},{8,12},{9,13},{1... | collective-permute-start | bytes 3145736 | tf_op jit(solution)/shard_map/ppermute | solution.py:505
  175.0 35.2 %collective-permute-start.13 = (f32[2,512,256]{2,1,0:T(8,128)}, f32[2,512,256]{2,1,0:T(8,128)}, u32[]{:S(2)}, u32[]{:S(2)}) collective-permute-start(f32[2,512,256]{2,1,0:T(8,128)} %get-tuple-element.20), channel_id=1, source_target_pairs={{0,4},{1,5},{2,6},{3,7},{8,12},{9,13},{10,14},{11,15},{16,20},{17,... | collective-permute-start | bytes 3145736 | tf_op jit(solution)/shard_map/ppermute | solution.py:505
  176.3 40.3 %collective-permute-start.11 = (f32[2,512,256]{2,1,0:T(8,128)}, f32[2,512,256]{2,1,0:T(8,128)}, u32[]{:S(2)}, u32[]{:S(2)}) collective-permute-start(f32[2,512,256]{2,1,0:T(8,128)} %get-tuple-element.20), channel_id=1, source_target_pairs={{4,5},{5,6},{6,7},{12,13},{13,14},{14,15},{20,21},{21,22},{22,23},... | collective-permute-start | bytes 3145736 | tf_op jit(solution)/shard_map/ppermute | solution.py:505
  194.9 19.3 %copy-start.4 = (f32[2,512,256]{2,1,0:T(8,128)S(1)}, f32[2,512,256]{2,1,0:T(8,128)}, u32[]{:S(2)}) copy-start(f32[2,512,256]{2,1,0:T(8,128)} %get-tuple-element.21) | copy-start | bytes 3145732
  195.0 30.0 %collective-permute-start.26 = (f32[256,512]{1,0:T(8,128)S(1)}, f32[256,512]{1,0:T(8,128)S(1)}, u32[]{:S(2)}, u32[]{:S(2)}) collective-permute-start(f32[256,512]{1,0:T(8,128)S(1)} %pad_maximum_fusion.3), channel_id=1, source_target_pairs={{0,16},{4,20},{8,24},{12,28},{16,0},{20,4},{24,8},{28,12},{1,17},{... | collective-permute-start | bytes 1572872 | tf_op jit(solution)/shard_map/ppermute | solution.py:532
  204.5 4.3 %copy-start.6 = (f32[2,512,256]{2,1,0:T(8,128)}, f32[2,512,256]{2,1,0:T(8,128)S(1)}, u32[]{:S(2)}) copy-start(f32[2,512,256]{2,1,0:T(8,128)S(1)} %collective-permute-done.9) | copy-start | bytes 3145732
  204.5 27.0 %collective-permute-start.8 = (f32[2,512,256]{2,1,0:T(8,128)}, f32[2,512,256]{2,1,0:T(8,128)}, u32[]{:S(2)}, u32[]{:S(2)}) collective-permute-start(f32[2,512,256]{2,1,0:T(8,128)} %get-tuple-element.16), channel_id=1, source_target_pairs={{0,4},{1,5},{2,6},{3,7},{4,8},{5,9},{6,10},{7,11},{8,12},{9,13},{1... | collective-permute-start | bytes 3145736 | tf_op jit(solution)/shard_map/ppermute | solution.py:505
  210.2 8.8 %copy-start.3 = (f32[2,512,256]{2,1,0:T(8,128)S(1)}, f32[2,512,256]{2,1,0:T(8,128)}, u32[]{:S(2)}) copy-start(f32[2,512,256]{2,1,0:T(8,128)} %get-tuple-element.19) | copy-start | bytes 3145732
  210.2 26.0 %collective-permute-start.10 = (f32[2,512,256]{2,1,0:T(8,128)S(1)}, f32[2,512,256]{2,1,0:T(8,128)}, u32[]{:S(2)}, u32[]{:S(2)}) collective-permute-start(f32[2,512,256]{2,1,0:T(8,128)S(1)} %add.135), channel_id=1, source_target_pairs={{0,1},{1,2},{2,3},{4,5},{5,6},{6,7},{8,9},{9,10},{10,11},{12,13},{... | collective-permute-start | bytes 3145736 | tf_op jit(solution)/shard_map/ppermute | solution.py:505
  216.6 41.8 %collective-permute-start.14 = (f32[2,512,256]{2,1,0:T(8,128)}, f32[2,512,256]{2,1,0:T(8,128)}, u32[]{:S(2)}, u32[]{:S(2)}) collective-permute-start(f32[2,512,256]{2,1,0:T(8,128)} %add.139), channel_id=1, source_target_pairs={{0,1},{1,2},{2,3},{4,5},{5,6},{6,7},{8,9},{9,10},{10,11},{12,13},{... | collective-permute-start | bytes 3145736 | tf_op jit(solution)/shard_map/ppermute | solution.py:505
  225.0 33.4 %collective-permute-start.12 = (f32[2,512,256]{2,1,0:T(8,128)}, f32[2,512,256]{2,1,0:T(8,128)}, u32[]{:S(2)}, u32[]{:S(2)}) collective-permute-start(f32[2,512,256]{2,1,0:T(8,128)} %add.137), channel_id=1, source_target_pairs={{0,4},{1,5},{2,6},{3,7},{4,8},{5,9},{6,10},{7,11},{8,12},{9,13},{1... | collective-permute-start | bytes 3145736 | tf_op jit(solution)/shard_map/ppermute | solution.py:505
  227.2 36.3 %collective-permute-start.27 = (f32[512,512]{1,0:T(8,128)S(1)}, f32[512,512]{1,0:T(8,128)}, u32[]{:S(2)}, u32[]{:S(2)}) collective-permute-start(f32[512,512]{1,0:T(8,128)S(1)} %pad_maximum_fusion.2), channel_id=1, source_target_pairs={{0,4},{4,0},{8,12},{12,8},{16,20},{20,16},{24,28},{28,24},{1,5},{5... | collective-permute-start | bytes 3145736 | tf_op jit(solution)/shard_map/ppermute | solution.py:532
  228.7 29.7 %copy-start.1 = (f32[2,512,1024]{2,1,0:T(8,128)S(1)}, f32[2,512,1024]{2,1,0:T(8,128)}, u32[]{:S(2)}) copy-start(f32[2,512,1024]{2,1,0:T(8,128)} %get-tuple-element.15) | copy-start | bytes 12582916

commit v4 on v3

--- a/solution.py
+++ b/solution.py
@@ -1,3 +1,5 @@
+import functools
+import itertools
 import math
 
 import jax
@@ -252,7 +254,7 @@
         row_base = pl.multiple_of((row // 8) * 8, 8)
         row_shift = row - row_base
 
-        @pl.loop(0, side // 32)
+        @pl.loop(0, side // 32, unroll=2)
         def _(step):
             base = pl.multiple_of(step * 32, 32)
             for plane in range(2):
@@ -269,7 +271,7 @@
             for load in late_loads:
                 load.wait()
 
-        @pl.loop(0, short // 16)
+        @pl.loop(0, short // 16, unroll=2)
         def _(step):
             base = pl.multiple_of(step * 16, 16)
             for part in range(RADIX):
@@ -293,12 +295,7 @@
                 rows_f32[p, :, cols] = left_dot(
                     mat_hi[p], mat_lo[p], left_hi[p, :, cols], left_lo[p, :, cols]
                 )
-
-        for p in range(RADIX):
-
-            @pl.loop(0, short // 16, unroll=2)
-            def _(step):
-                base = pl.multiple_of(step * 16, 16)
+            for base in range(0, short, 16):
                 values = []
                 for q in range(RADIX):
                     cols = pl.ds(q * short, short)
@@ -329,10 +326,7 @@
                 cols_f32[t, rows, :] = right_dot(hi, lo, mat_hi[t], mat_lo[t])
 
         for p in range(RADIX):
-
-            @pl.loop(0, short // 16, unroll=2)
-            def _(step):
-                base = pl.multiple_of(step * 16, 16)
+            for base in range(0, short, 16):
                 rows = pl.ds(base + p * short, 16)
                 values = [
                     (cols_f32[t, rows, pl.ds(0, short)], cols_f32[t, rows, pl.ds(short, short)])
@@ -344,15 +338,13 @@
                         hi, lo = split(value)
                         left_hi[p, pl.ds(base + offset, 16), cols] = hi
                         left_lo[p, pl.ds(base + offset, 16), cols] = lo
-
-        for p in range(RADIX):
             for half in range(2):
                 cols = pl.ds(half * (side // 2), side // 2)
                 rows_f32[p, :, cols] = left_dot(
                     mat_t_hi[p], mat_t_lo[p], left_hi[p, :, cols], left_lo[p, :, cols]
                 )
 
-        @pl.loop(0, short // 8)
+        @pl.loop(0, short // 8, unroll=2)
         def _(step):
             base = pl.multiple_of(step * 8, 8)
             for part in range(RADIX):
@@ -505,26 +497,13 @@
     return lax.ppermute(array, ("ty", "tx"), along(rule, sizes))
 
 
-def add_kernel(left, right, out):
-    out[...] = left[...] + right[...]
-
-
-def add_beside_transfers(left, right):
-    return pl.pallas_call(
-        add_kernel,
-        out_shape=jax.ShapeDtypeStruct(left.shape, left.dtype),
-        cost_estimate=pl.CostEstimate(flops=60 * 10**9, bytes_accessed=2**27, transcendentals=0),
-        name="add_beside_transfers",
-    )(left, right)
-
-
-def halve(value, bit, beside=False):
+def halve(value, bit):
     rows = value.shape[0] // 2
     mine = lax.axis_index("ty") // bit % 2
     kept = lax.dynamic_slice_in_dim(value, mine * rows, rows, 0)
     sent = lax.dynamic_slice_in_dim(value, (1 - mine) * rows, rows, 0)
     received = lax.ppermute(sent, "ty", [(i, i ^ bit) for i in range(lax.axis_size("ty"))])
-    return add_beside_transfers(kept, received) if beside else kept + received
+    return kept + received
 
 
 def double(value, bit):
@@ -561,20 +540,26 @@
     return out
 
 
-def pupil_sum(dpup):
+def after(value, *arrivals):
+    return lax.optimization_barrier((value, *arrivals))[0]
+
+
+def pupil_sum(dpup, arrivals):
     n_ty, n_tx = lax.axis_size("ty"), lax.axis_size("tx")
     bits = [1]
     bit = n_ty // 2
     while bit > 1:
         bits.append(bit)
         bit //= 2
+    steps = [functools.partial(halve, bit=bit) for bit in bits]
+    steps.append(lambda part: scatter_tx(part) * (1.0 / math.sqrt(n_ty * n_tx)))
+    steps.append(gather_tx)
+    steps += [functools.partial(double, bit=bit) for bit in reversed(bits)]
     part = dpup.reshape(-1, dpup.shape[-1])
-    for number, bit in enumerate(bits):
-        part = halve(part, bit, number == 1)
-    part = scatter_tx(part) * (1.0 / math.sqrt(n_ty * n_tx))
-    part = gather_tx(part)
-    for bit in reversed(bits):
-        part = double(part, bit)
+    for step, before in itertools.zip_longest(steps, arrivals, fillvalue=()):
+        if before:
+            part = after(part, *before)
+        part = step(part)
     return part.reshape(dpup.shape)
 
 
@@ -603,7 +588,8 @@
     lower_b, amps = lax.optimization_barrier((lower_b, amps))
     corner_side = send(lower_b, lambda i, j: (i, j - 1) if i % 2 else None)
     corner_a = send(right_a[:, :side], up)
-    corner_up = send(right_b[:, :side], lambda i, j: (i - 1, j) if i % 2 else None)
+    right_b_again = after(right_b, corner_side)
+    corner_up = send(right_b_again[:, :side], lambda i, j: (i - 1, j) if i % 2 else None)
 
     parts = (right_a, right_b, lower_a, lower_b, lower_c, corner_a, corner_up, corner_side)
     own_g, *grads, dpup = slots_call(meta, spectrum, parts, amps, pupil)
@@ -631,7 +617,17 @@
         ],
         axis=2,
     )
-    return spec_grad, pupil_sum(dpup)
+    arrivals = [
+        (),
+        (),
+        (back_a, back_side, back_down),
+        (),
+        (right_b,),
+        (lower_c,),
+        (right_a, lower_b),
+        (lower_a,),
+    ]
+    return spec_grad, pupil_sum(dpup, arrivals)
 
 
 def solution(mesh):

time: 267 us -> 266 us (level)
  waiting for transfers between devices: 131 us -> 120 us
  starting transfers between devices: 75.5 us -> 83.8 us
  other arithmetic: 19.7 us -> 22.8 us
  Pallas kernels: 31.1 us -> 28.1 us
    ppermute x16, waiting for transfers between devices: 83.7 us -> 45.4 us  [send(): return lax.ppermute(array, ('ty', 'tx'), along(rule, sizes))]
    ppermute x3, starting transfers between devices: 23.2 us -> 0.15 us  [halve(): lax.ppermute(sent, 'ty', [(i, i ^ bit) for i in range(lax.axis_size('ty'))])]
    ppermute x16, starting transfers between devices: 41.3 us -> 64.4 us  [send(): return lax.ppermute(array, ('ty', 'tx'), along(rule, sizes))]
    ppermute x3, waiting for transfers between devices: 3.01 us -> 17.2 us  [gather_tx(): parts.append(lax.ppermute(value, 'tx', ring_pairs(size, step)))]
    ppermute x3, waiting for transfers between devices: 21.9 us -> 34.6 us  [halve(): lax.ppermute(sent, 'ty', [(i, i ^ bit) for i in range(lax.axis_size('ty'))])]
    ppermute x3, starting transfers between devices: 4.63 us -> 12.6 us  [scatter_tx(): total = total + lax.ppermute(piece, 'tx', ring_pairs(size, step))]
    ppermute x3, waiting for transfers between devices: 17.8 us -> 22.6 us  [double(): lax.ppermute(value, 'ty', [(i, i ^ bit) for i in range(lax.axis_size('ty'...]
    ppermute x3, waiting for transfers between devices: 4.33 us -> 0.01 us  [scatter_tx(): total = total + lax.ppermute(piece, 'tx', ring_pairs(size, step))]
  transfers between devices with their start and end apart: 28 -> 28, of which waited for: 17 -> 9; matrix products, arithmetic and copies ran while one was open for 6% -> 9% of each run, Pallas kernels for 3% -> 3%
where the time goes in v4:
time: 266 us; the launch traced here: 265 us
  waiting for transfers between devices  120 us (45%)
  starting transfers between devices  83.8 us (32%)
  Pallas kernels  28.1 us (11%)
  other arithmetic  22.8 us (9%)
  local copies, waits for them, and re-layouts  9.79 us (4%)
    ppermute x16, starting transfers between devices, send(): return lax.ppermute(array, ('ty', 'tx'), along(rule, sizes))  64.4 us
    ppermute x16, waiting for transfers between devices, send(): return lax.ppermute(array, ('ty', 'tx'), along(rule, sizes))  45.4 us
    ppermute x3, waiting for transfers between devices, halve(): lax.ppermute(sent, 'ty', [(i, i ^ bit) for i in range(lax.axis_size('ty'))])  34.6 us
    ppermute x3, waiting for transfers between devices, double(): lax.ppermute(value, 'ty', [(i, i ^ bit) for i in range(lax.axis_size('ty'...  22.6 us
    pallas_call x1, Pallas kernels, slots_call(): pl.pallas_call(slots_kernel, out_shape=[jax.ShapeDtypeStruct(x.shape, f32...  19.8 us
    ppermute x3, waiting for transfers between devices, gather_tx(): parts.append(lax.ppermute(value, 'tx', ring_pairs(size, step)))  17.2 us
    ppermute x3, starting transfers between devices, scatter_tx(): total = total + lax.ppermute(piece, 'tx', ring_pairs(size, step))  12.6 us
    pallas_call x1, Pallas kernels, ordered(): pl.pallas_call(order_kernel, grid=(slots,), out_shape=jax.ShapeDtypeStruc...  8.26 us
  transfers between devices with their start and end apart: 28, of which 9 were waited for; matrix products, arithmetic and copies ran while one was open for 9% of the time, Pallas kernels for 3%

profile of v4, /device:TPU:1, one launch (start us, length us, event | category | flops | bytes accessed | tf_op | source)
XLA Modules:
  0.0 265.4 jit_solution(17686409333365691357)
XLA Ops:
  0.6 2.7 %fusion = (f32[2,512,256]{2,1,0:T(8,128)}, f32[2,512,256]{2,1,0:T(8,128)S(1)}) fusion(f32[2,512,1024]{2,1,0:T(8,128)} %tile_hbm.1), kind=kLoop, calls=%fused_computation.30 | loop fusion | bytes 4194304 | tf_op jit(solution)/shard_map/slice | solution.py:584
  3.3 2.0 collective-permute-start.3
  5.3 1.3 collective-permute-start.1
  6.6 1.3 collective-permute-start
  7.9 8.3 %ordered.1.amps_hbm = f32[3,512,512]{2,1,0:T(8,128)} custom-call(f32[3,512,512]{2,1,0:T(8,128)} %amps.1, bf16[512,512]{1,0:T(8,128)(2,1)} %constant.141.clone.perm_rows, bf16[512,512]{1,0:T(8,128)(2,1)} %constant.142.clone.perm_cols), custom_call_target="tpu_custom_call" | custom-call | flops 4831838208 | bytes 6291456 | tf_op jit(solution)/shard_map/ordered/pallas_call | solution.py:471
  16.2 4.8 %collective-permute-done.3.lower_b_hbm = f32[2,512,256]{2,1,0:T(8,128)} collective-permute-done((f32[2,512,256]{2,1,0:T(8,128)}, f32[2,512,256]{2,1,0:T(8,128)}, u32[]{:S(2)}, u32[]{:S(2)}) %collective-permute-start.3) | collective-permute-done | bytes 1048608 | tf_op jit(solution)/shard_map/ppermute | solution.py:497
  20.9 1.3 collective-permute-start.6
  22.2 1.8 slice.30
  24.0 1.9 collective-permute-start.4
  25.9 1.9 collective-permute-start.2
  27.9 27.9 %collective-permute-done.right_a_hbm = f32[2,512,256]{2,1,0:T(8,128)} collective-permute-done((f32[2,512,256]{2,1,0:T(8,128)S(1)}, f32[2,512,256]{2,1,0:T(8,128)}, u32[]{:S(2)}, u32[]{:S(2)}) %collective-permute-start) | collective-permute-done | bytes 1048608 | tf_op jit(solution)/shard_map/ppermute | solution.py:497
  55.7 2.2 collective-permute-start.5
  58.0 0.0 collective-permute-done.1.right_b_hbm
  58.0 9.0 %collective-permute-done.6.corner_side_hbm = f32[2,512,256]{2,1,0:T(8,128)} collective-permute-done((f32[2,512,256]{2,1,0:T(8,128)}, f32[2,512,256]{2,1,0:T(8,128)}, u32[]{:S(2)}, u32[]{:S(2)}) %collective-permute-start.6) | collective-permute-done | bytes 1048608 | tf_op jit(solution)/shard_map/ppermute | solution.py:497
  67.0 2.3 collective-permute-start.7
  69.3 0.1 copy.15
  69.4 0.1 copy.17
  69.5 0.1 copy.16
  69.6 0.1 pad_add_fusion
  69.6 0.6 concatenate.15.meta
  70.2 3.7 %collective-permute-done.5.corner_a_hbm = f32[2,512,256]{2,1,0:T(8,128)} collective-permute-done((f32[2,512,256]{2,1,0:T(8,128)}, f32[2,512,256]{2,1,0:T(8,128)}, u32[]{:S(2)}, u32[]{:S(2)}) %collective-permute-start.5) | collective-permute-done | bytes 1048608 | tf_op jit(solution)/shard_map/ppermute | solution.py:497
  73.9 19.8 %slots.1 = (f32[2,512,1024]{2,1,0:T(8,128)}, f32[2,512,256]{2,1,0:T(8,128)}, f32[2,512,256]{2,1,0:T(8,128)}, f32[2,512,256]{2,1,0:T(8,128)}, f32[2,512,256]{2,1,...) custom-call(s32[4,3]{1,0:T(4,128)} %concatenate.15.meta, ...), custom_call_target="tpu_custom_call" | custom-call | flops 9663676416 | bytes 41943040 | tf_op jit(solution)/shard_map/slots/pallas_call | solution.py:417
  93.8 1.4 constant_dynamic-slice_fusion.5
  95.2 0.1 collective-permute-start.16
  95.3 1.3 collective-permute-start.13
  96.6 4.7 %collective-permute-start.11 = (f32[2,512,256]{2,1,0:T(8,128)}, f32[2,512,256]{2,1,0:T(8,128)}, u32[]{:S(2)}, u32[]{:S(2)}) collective-permute-start(f32[2,512,256]{2,1,0:T(8,128)} %get-tuple-element.27), channel_id=1, source_target_pairs={{4,5},{5,6},{6,7},{12,13},{13,14},{14,15},{20,21},{21,22},{22,23},... | collective-permute-start | bytes 3145736 | tf_op jit(solution)/shard_map/ppermute | solution.py:497
  101.3 21.8 %collective-permute-start.9 = (f32[2,512,256]{2,1,0:T(8,128)}, f32[2,512,256]{2,1,0:T(8,128)}, u32[]{:S(2)}, u32[]{:S(2)}) collective-permute-start(f32[2,512,256]{2,1,0:T(8,128)} %get-tuple-element.25), channel_id=1, source_target_pairs={{0,4},{1,5},{2,6},{3,7},{4,8},{5,9},{6,10},{7,11},{8,12},{9,13},{1... | collective-permute-start | bytes 3145736 | tf_op jit(solution)/shard_map/ppermute | solution.py:497
  123.2 1.4 dynamic-slice_add_fusion
  124.6 0.8 constant_dynamic-slice_fusion.4
  125.4 2.7 %collective-permute-start.15 = (f32[2,512,512]{2,1,0:T(8,128)}, f32[2,512,512]{2,1,0:T(8,128)S(1)}, u32[]{:S(2)}, u32[]{:S(2)}) collective-permute-start(f32[2,512,512]{2,1,0:T(8,128)} %get-tuple-element.29), channel_id=1, source_target_pairs={{0,4},{1,5},{2,6},{3,7},{4,8},{5,9},{6,10},{7,11},{8,12},{9,13},{1... | collective-permute-start | bytes 6291464 | tf_op jit(solution)/shard_map/ppermute | solution.py:497
  128.3 2.7 %add.142 = f32[2,512,256]{2,1,0:T(8,128)} add(f32[2,512,256]{2,1,0:T(8,128)} %get-tuple-element.28, f32[2,512,256]{2,1,0:T(8,128)} %collective-permute-done.13) | non-fusion elementwise | flops 262144 | bytes 3145728 | tf_op jit(solution)/shard_map/add | solution.py:609
  130.9 3.2 %collective-permute-start.14 = (f32[2,512,256]{2,1,0:T(8,128)}, f32[2,512,256]{2,1,0:T(8,128)}, u32[]{:S(2)}, u32[]{:S(2)}) collective-permute-start(f32[2,512,256]{2,1,0:T(8,128)} %add.142), channel_id=1, source_target_pairs={{0,1},{1,2},{2,3},{4,5},{5,6},{6,7},{8,9},{9,10},{10,11},{12,13},{... | collective-permute-start | bytes 3145736 | tf_op jit(solution)/shard_map/ppermute | solution.py:497
  134.1 29.3 %collective-permute-done.17 = f32[256,512]{1,0:T(8,128)} collective-permute-done((f32[256,512]{1,0:T(8,128)}, f32[256,512]{1,0:T(8,128)}, u32[]{:S(2)}, u32[]{:S(2)}) %collective-permute-start.17) | collective-permute-done | bytes 524320 | tf_op jit(solution)/shard_map/ppermute | solution.py:505
  163.4 1.1 dynamic-slice_add_fusion.1
  164.6 0.8 copy-done.2
  165.4 0.1 collective-permute-start.18
  165.5 5.3 %collective-permute-done.18 = f32[128,512]{1,0:T(8,128)} collective-permute-done((f32[128,512]{1,0:T(8,128)S(1)}, f32[128,512]{1,0:T(8,128)}, u32[]{:S(2)}, u32[]{:S(2)}) %collective-permute-start.18) | collective-permute-done | bytes 262176 | tf_op jit(solution)/shard_map/ppermute | solution.py:505
  170.8 1.1 dynamic-slice_add_fusion.2
  171.9 0.7 constant_dynamic-slice_fusion.2
  172.6 12.3 %collective-permute-start.21 = (f32[32,512]{1,0:T(8,128)}, f32[32,512]{1,0:T(8,128)S(1)}, u32[]{:S(2)}, u32[]{:S(2)}) collective-permute-start(f32[32,512]{1,0:T(8,128)} %get-tuple-element.47), channel_id=1, source_target_pairs={{0,3},{1,0},{2,1},{3,2},{4,7},{5,4},{6,5},{7,6},{8,11},{9,8},{10,9... | collective-permute-start | bytes 196616 | tf_op jit(solution)/shard_map/ppermute | solution.py:527
  184.9 0.3 collective-permute-start.19
  185.1 2.7 %add.138 = f32[2,512,256]{2,1,0:T(8,128)} add(f32[2,512,256]{2,1,0:T(8,128)} %get-tuple-element.24, f32[2,512,256]{2,1,0:T(8,128)} %collective-permute-done.9) | non-fusion elementwise | flops 262144 | bytes 3145728 | tf_op jit(solution)/shard_map/add | solution.py:610
  187.8 2.4 add.140
  190.2 5.3 %collective-permute-start.10 = (f32[2,512,256]{2,1,0:T(8,128)}, f32[2,512,256]{2,1,0:T(8,128)}, u32[]{:S(2)}, u32[]{:S(2)}) collective-permute-start(f32[2,512,256]{2,1,0:T(8,128)} %add.138), channel_id=1, source_target_pairs={{0,1},{1,2},{2,3},{4,5},{5,6},{6,7},{8,9},{9,10},{10,11},{12,13},{... | collective-permute-start | bytes 3145736 | tf_op jit(solution)/shard_map/ppermute | solution.py:497
  195.4 4.2 %collective-permute-start.12 = (f32[2,512,256]{2,1,0:T(8,128)}, f32[2,512,256]{2,1,0:T(8,128)}, u32[]{:S(2)}, u32[]{:S(2)}) collective-permute-start(f32[2,512,256]{2,1,0:T(8,128)} %add.140), channel_id=1, source_target_pairs={{0,4},{1,5},{2,6},{3,7},{4,8},{5,9},{6,10},{7,11},{8,12},{9,13},{1... | collective-permute-start | bytes 3145736 | tf_op jit(solution)/shard_map/ppermute | solution.py:497
  199.6 0.9 add_multiply_fusion
  200.5 0.1 collective-permute-start.22
  200.5 0.1 collective-permute-start.23
  200.7 15.7 %collective-permute-done.22 = f32[32,512]{1,0:T(8,128)S(1)} collective-permute-done((f32[32,512]{1,0:T(8,128)S(1)}, f32[32,512]{1,0:T(8,128)S(1)}, u32[]{:S(2)}, u32[]{:S(2)}) %collective-permute-start.22) | collective-permute-done | bytes 65568 | tf_op jit(solution)/shard_map/ppermute | solution.py:536
  216.4 3.2 %collective-permute-start.24 = (f32[32,512]{1,0:T(8,128)S(1)}, f32[32,512]{1,0:T(8,128)S(1)}, u32[]{:S(2)}, u32[]{:S(2)}) collective-permute-start(f32[32,512]{1,0:T(8,128)S(1)} %add_multiply_fusion), channel_id=1, source_target_pairs={{0,3},{1,0},{2,1},{3,2},{4,7},{5,4},{6,5},{7,6},{8,11},{9,8},{10,9... | collective-permute-start | bytes 196616 | tf_op jit(solution)/shard_map/ppermute | solution.py:536
  219.6 1.5 collective-permute-done.24
  221.2 0.5 collective-permute-start.25
  221.7 7.1 %collective-permute-start.8 = (f32[2,512,256]{2,1,0:T(8,128)}, f32[2,512,256]{2,1,0:T(8,128)}, u32[]{:S(2)}, u32[]{:S(2)}) collective-permute-start(f32[2,512,256]{2,1,0:T(8,128)} %get-tuple-element.23), channel_id=1, source_target_pairs={{0,4},{1,5},{2,6},{3,7},{4,8},{5,9},{6,10},{7,11},{8,12},{9,13},{1... | collective-permute-start | bytes 3145736 | tf_op jit(solution)/shard_map/ppermute | solution.py:497
  228.9 2.3 collective-permute-start.26
  231.1 22.6 %collective-permute-done.26 = f32[256,512]{1,0:T(8,128)S(1)} collective-permute-done((f32[256,512]{1,0:T(8,128)S(1)}, f32[256,512]{1,0:T(8,128)S(1)}, u32[]{:S(2)}, u32[]{:S(2)}) %collective-permute-start.26) | collective-permute-done | bytes 524320 | tf_op jit(solution)/shard_map/ppermute | solution.py:511
  253.8 0.1 broadcast_select_fusion.3
  253.9 0.1 pad_maximum_fusion.2
  254.0 0.6 collective-permute-start.27
  254.5 2.2 slice_add_fusion
  256.8 0.6 copy-done
  257.3 2.6 add_add_fusion.1
  259.9 2.5 pad_maximum_fusion
  262.4 1.5 broadcast_select_fusion.1
  263.9 1.5 pad_maximum_fusion.1
  (40 shorter events, 0.2 us)
Async XLA Ops:
  3.3 17.6 %collective-permute-start.3 = (f32[2,512,256]{2,1,0:T(8,128)}, f32[2,512,256]{2,1,0:T(8,128)}, u32[]{:S(2)}, u32[]{:S(2)}) collective-permute-start(f32[2,512,256]{2,1,0:T(8,128)} %get-tuple-element.38), channel_id=1, source_target_pairs={{4,0},{5,1},{6,2},{7,3},{8,4},{9,5},{10,6},{11,7},{12,8},{13,9},{1... | collective-permute-start | bytes 3145736 | tf_op jit(solution)/shard_map/ppermute | solution.py:497
  5.3 52.7 %collective-permute-start.1 = (f32[2,512,256]{2,1,0:T(8,128)}, f32[2,512,256]{2,1,0:T(8,128)}, u32[]{:S(2)}, u32[]{:S(2)}) collective-permute-start(f32[2,512,256]{2,1,0:T(8,128)} %get-tuple-element.38), channel_id=1, source_target_pairs={{1,0},{2,1},{3,2},{5,4},{6,5},{7,6},{9,8},{10,9},{11,10},{13,12},{... | collective-permute-start | bytes 3145736 | tf_op jit(solution)/shard_map/ppermute | solution.py:497
  6.6 49.1 %collective-permute-start = (f32[2,512,256]{2,1,0:T(8,128)S(1)}, f32[2,512,256]{2,1,0:T(8,128)}, u32[]{:S(2)}, u32[]{:S(2)}) collective-permute-start(f32[2,512,256]{2,1,0:T(8,128)S(1)} %get-tuple-element.39), channel_id=1, source_target_pairs={{1,0},{2,1},{3,2},{5,4},{6,5},{7,6},{9,8},{10,9},{11,10},{13,12},{... | collective-permute-start | bytes 3145736 | tf_op jit(solution)/shard_map/ppermute | solution.py:497
  16.2 53.1 %copy-start.5 = (s32[3]{0:T(128)S(1)}, s32[3]{0:T(128)}, u32[]{:S(2)}) copy-start(s32[3]{0:T(128)} %param.15) | copy-start | bytes 40
  16.2 53.2 %copy-start.4 = (s32[3,2]{0,1:T(2,128)S(1)}, s32[3,2]{0,1:T(2,128)}, u32[]{:S(2)}) copy-start(s32[3,2]{0,1:T(2,128)} %param.14) | copy-start | bytes 76
  20.9 46.0 %collective-permute-start.6 = (f32[2,512,256]{2,1,0:T(8,128)}, f32[2,512,256]{2,1,0:T(8,128)}, u32[]{:S(2)}, u32[]{:S(2)}) collective-permute-start(f32[2,512,256]{2,1,0:T(8,128)} %collective-permute-done.3.lower_b_hbm), channel_id=1, source_target_pairs={{5,4},{6,5},{7,6},{13,12},{14,13},{15,14},{21,20},{22,21},{23,22},... | collective-permute-start | bytes 3145736 | tf_op jit(solution)/shard_map/ppermute | solution.py:497
  24.0 46.2 %collective-permute-start.4 = (f32[2,512,512]{2,1,0:T(8,128)S(1)}, f32[2,512,512]{2,1,0:T(8,128)}, u32[]{:S(2)}, u32[]{:S(2)}) collective-permute-start(f32[2,512,512]{2,1,0:T(8,128)S(1)} %slice.30), channel_id=1, source_target_pairs={{4,0},{5,1},{6,2},{7,3},{8,4},{9,5},{10,6},{11,7},{12,8},{13,9},{1... | collective-permute-start | bytes 6291464 | tf_op jit(solution)/shard_map/ppermute | solution.py:497
  25.9 44.3 %collective-permute-start.2 = (f32[2,512,256]{2,1,0:T(8,128)S(1)}, f32[2,512,256]{2,1,0:T(8,128)}, u32[]{:S(2)}, u32[]{:S(2)}) collective-permute-start(f32[2,512,256]{2,1,0:T(8,128)S(1)} %get-tuple-element.39), channel_id=1, source_target_pairs={{4,0},{5,1},{6,2},{7,3},{8,4},{9,5},{10,6},{11,7},{12,8},{13,9},{1... | collective-permute-start | bytes 3145736 | tf_op jit(solution)/shard_map/ppermute | solution.py:497
  55.7 18.2 %collective-permute-start.5 = (f32[2,512,256]{2,1,0:T(8,128)}, f32[2,512,256]{2,1,0:T(8,128)}, u32[]{:S(2)}, u32[]{:S(2)}) collective-permute-start(f32[2,512,256]{2,1,0:T(8,128)} %collective-permute-done.right_a_hbm), channel_id=1, source_target_pairs={{4,0},{5,1},{6,2},{7,3},{8,4},{9,5},{10,6},{11,7},{12,8},{13,9},{1... | collective-permute-start | bytes 3145736 | tf_op jit(solution)/shard_map/ppermute | solution.py:497
  67.0 7.0 %collective-permute-start.7 = (f32[2,512,256]{2,1,0:T(8,128)}, f32[2,512,256]{2,1,0:T(8,128)}, u32[]{:S(2)}, u32[]{:S(2)}) collective-permute-start(f32[2,512,256]{2,1,0:T(8,128)} %collective-permute-done.1.right_b_hbm), channel_id=1, source_target_pairs={{4,0},{5,1},{6,2},{7,3},{12,8},{13,9},{14,10},{15,11},{20,16},{21,... | collective-permute-start | bytes 3145736 | tf_op jit(solution)/shard_map/ppermute | solution.py:497
  93.8 29.4 %copy-start.1 = (f32[2,512,512]{2,1,0:T(8,128)S(1)}, f32[2,512,512]{2,1,0:T(8,128)}, u32[]{:S(2)}) copy-start(f32[2,512,512]{2,1,0:T(8,128)} %get-tuple-element.30) | copy-start | bytes 6291460
  95.2 27.9 %collective-permute-start.16 = (f32[512,512]{1,0:T(8,128)S(1)}, f32[512,512]{1,0:T(8,128)}, u32[]{:S(2)}, u32[]{:S(2)}) collective-permute-start(f32[512,512]{1,0:T(8,128)S(1)} %constant_dynamic-slice_fusion.5), channel_id=1, source_target_pairs={{0,4},{4,0},{8,12},{12,8},{16,20},{20,16},{24,28},{28,24},{1,5},{5... | collective-permute-start | bytes 3145736 | tf_op jit(solution)/shard_map/ppermute | solution.py:505
  95.3 32.9 %collective-permute-start.13 = (f32[2,512,256]{2,1,0:T(8,128)}, f32[2,512,256]{2,1,0:T(8,128)}, u32[]{:S(2)}, u32[]{:S(2)}) collective-permute-start(f32[2,512,256]{2,1,0:T(8,128)} %get-tuple-element.27), channel_id=1, source_target_pairs={{0,4},{1,5},{2,6},{3,7},{8,12},{9,13},{10,14},{11,15},{16,20},{17,... | collective-permute-start | bytes 3145736 | tf_op jit(solution)/shard_map/ppermute | solution.py:497
  96.6 68.0 %collective-permute-start.11 = (f32[2,512,256]{2,1,0:T(8,128)}, f32[2,512,256]{2,1,0:T(8,128)}, u32[]{:S(2)}, u32[]{:S(2)}) collective-permute-start(f32[2,512,256]{2,1,0:T(8,128)} %get-tuple-element.27), channel_id=1, source_target_pairs={{4,5},{5,6},{6,7},{12,13},{13,14},{14,15},{20,21},{21,22},{22,23},... | collective-permute-start | bytes 3145736 | tf_op jit(solution)/shard_map/ppermute | solution.py:497
  101.3 63.3 %collective-permute-start.9 = (f32[2,512,256]{2,1,0:T(8,128)}, f32[2,512,256]{2,1,0:T(8,128)}, u32[]{:S(2)}, u32[]{:S(2)}) collective-permute-start(f32[2,512,256]{2,1,0:T(8,128)} %get-tuple-element.25), channel_id=1, source_target_pairs={{0,4},{1,5},{2,6},{3,7},{4,8},{5,9},{6,10},{7,11},{8,12},{9,13},{1... | collective-permute-start | bytes 3145736 | tf_op jit(solution)/shard_map/ppermute | solution.py:497
  125.4 38.0 %collective-permute-start.17 = (f32[256,512]{1,0:T(8,128)}, f32[256,512]{1,0:T(8,128)}, u32[]{:S(2)}, u32[]{:S(2)}) collective-permute-start(f32[256,512]{1,0:T(8,128)} %constant_dynamic-slice_fusion.4), channel_id=1, source_target_pairs={{0,16},{4,20},{8,24},{12,28},{16,0},{20,4},{24,8},{28,12},{1,17},{... | collective-permute-start | bytes 1572872 | tf_op jit(solution)/shard_map/ppermute | solution.py:505
  125.4 95.7 %collective-permute-start.15 = (f32[2,512,512]{2,1,0:T(8,128)}, f32[2,512,512]{2,1,0:T(8,128)S(1)}, u32[]{:S(2)}, u32[]{:S(2)}) collective-permute-start(f32[2,512,512]{2,1,0:T(8,128)} %get-tuple-element.29), channel_id=1, source_target_pairs={{0,4},{1,5},{2,6},{3,7},{4,8},{5,9},{6,10},{7,11},{8,12},{9,13},{1... | collective-permute-start | bytes 6291464 | tf_op jit(solution)/shard_map/ppermute | solution.py:497
  130.9 69.6 %collective-permute-start.14 = (f32[2,512,256]{2,1,0:T(8,128)}, f32[2,512,256]{2,1,0:T(8,128)}, u32[]{:S(2)}, u32[]{:S(2)}) collective-permute-start(f32[2,512,256]{2,1,0:T(8,128)} %add.142), channel_id=1, source_target_pairs={{0,1},{1,2},{2,3},{4,5},{5,6},{6,7},{8,9},{9,10},{10,11},{12,13},{... | collective-permute-start | bytes 3145736 | tf_op jit(solution)/shard_map/ppermute | solution.py:497
  164.6 0.8 copy-start.2
  165.4 5.4 %collective-permute-start.18 = (f32[128,512]{1,0:T(8,128)S(1)}, f32[128,512]{1,0:T(8,128)}, u32[]{:S(2)}, u32[]{:S(2)}) collective-permute-start(f32[128,512]{1,0:T(8,128)S(1)} %constant_dynamic-slice_fusion.3), channel_id=1, source_target_pairs={{0,8},{4,12},{8,0},{12,4},{16,24},{20,28},{24,16},{28,20},{1,9},{5... | collective-permute-start | bytes 786440 | tf_op jit(solution)/shard_map/ppermute | solution.py:505
  165.5 22.3 %copy-start.3 = (f32[2,512,256]{2,1,0:T(8,128)S(1)}, f32[2,512,256]{2,1,0:T(8,128)}, u32[]{:S(2)}) copy-start(f32[2,512,256]{2,1,0:T(8,128)} %get-tuple-element.26) | copy-start | bytes 3145732
  172.6 17.6 %collective-permute-start.21 = (f32[32,512]{1,0:T(8,128)}, f32[32,512]{1,0:T(8,128)S(1)}, u32[]{:S(2)}, u32[]{:S(2)}) collective-permute-start(f32[32,512]{1,0:T(8,128)} %get-tuple-element.47), channel_id=1, source_target_pairs={{0,3},{1,0},{2,1},{3,2},{4,7},{5,4},{6,5},{7,6},{8,11},{9,8},{10,9... | collective-permute-start | bytes 196616 | tf_op jit(solution)/shard_map/ppermute | solution.py:527
  184.9 10.6 %collective-permute-start.20 = (f32[32,512]{1,0:T(8,128)}, f32[32,512]{1,0:T(8,128)S(1)}, u32[]{:S(2)}, u32[]{:S(2)}) collective-permute-start(f32[32,512]{1,0:T(8,128)} %get-tuple-element.48), channel_id=1, source_target_pairs={{0,2},{1,3},{2,0},{3,1},{4,6},{5,7},{6,4},{7,5},{8,10},{9,11},{10,... | collective-permute-start | bytes 196616 | tf_op jit(solution)/shard_map/ppermute | solution.py:527
  184.9 14.7 %collective-permute-start.19 = (f32[32,512]{1,0:T(8,128)}, f32[32,512]{1,0:T(8,128)}, u32[]{:S(2)}, u32[]{:S(2)}) collective-permute-start(f32[32,512]{1,0:T(8,128)} %get-tuple-element.46), channel_id=1, source_target_pairs={{0,1},{1,2},{2,3},{3,0},{4,5},{5,6},{6,7},{7,4},{8,9},{9,10},{10,1... | collective-permute-start | bytes 196616 | tf_op jit(solution)/shard_map/ppermute | solution.py:527
  190.2 38.7 %collective-permute-start.10 = (f32[2,512,256]{2,1,0:T(8,128)}, f32[2,512,256]{2,1,0:T(8,128)}, u32[]{:S(2)}, u32[]{:S(2)}) collective-permute-start(f32[2,512,256]{2,1,0:T(8,128)} %add.138), channel_id=1, source_target_pairs={{0,1},{1,2},{2,3},{4,5},{5,6},{6,7},{8,9},{9,10},{10,11},{12,13},{... | collective-permute-start | bytes 3145736 | tf_op jit(solution)/shard_map/ppermute | solution.py:497
  195.4 33.4 %collective-permute-start.12 = (f32[2,512,256]{2,1,0:T(8,128)}, f32[2,512,256]{2,1,0:T(8,128)}, u32[]{:S(2)}, u32[]{:S(2)}) collective-permute-start(f32[2,512,256]{2,1,0:T(8,128)} %add.140), channel_id=1, source_target_pairs={{0,4},{1,5},{2,6},{3,7},{4,8},{5,9},{6,10},{7,11},{8,12},{9,13},{1... | collective-permute-start | bytes 3145736 | tf_op jit(solution)/shard_map/ppermute | solution.py:497
  200.5 15.9 %collective-permute-start.22 = (f32[32,512]{1,0:T(8,128)S(1)}, f32[32,512]{1,0:T(8,128)S(1)}, u32[]{:S(2)}, u32[]{:S(2)}) collective-permute-start(f32[32,512]{1,0:T(8,128)S(1)} %add_multiply_fusion), channel_id=1, source_target_pairs={{0,1},{1,2},{2,3},{3,0},{4,5},{5,6},{6,7},{7,4},{8,9},{9,10},{10,1... | collective-permute-start | bytes 196616 | tf_op jit(solution)/shard_map/ppermute | solution.py:536
  200.5 19.1 %collective-permute-start.23 = (f32[32,512]{1,0:T(8,128)S(1)}, f32[32,512]{1,0:T(8,128)S(1)}, u32[]{:S(2)}, u32[]{:S(2)}) collective-permute-start(f32[32,512]{1,0:T(8,128)S(1)} %add_multiply_fusion), channel_id=1, source_target_pairs={{0,2},{1,3},{2,0},{3,1},{4,6},{5,7},{6,4},{7,5},{8,10},{9,11},{10,... | collective-permute-start | bytes 196616 | tf_op jit(solution)/shard_map/ppermute | solution.py:536
  216.4 4.8 %collective-permute-start.24 = (f32[32,512]{1,0:T(8,128)S(1)}, f32[32,512]{1,0:T(8,128)S(1)}, u32[]{:S(2)}, u32[]{:S(2)}) collective-permute-start(f32[32,512]{1,0:T(8,128)S(1)} %add_multiply_fusion), channel_id=1, source_target_pairs={{0,3},{1,0},{2,1},{3,2},{4,7},{5,4},{6,5},{7,6},{8,11},{9,8},{10,9... | collective-permute-start | bytes 196616 | tf_op jit(solution)/shard_map/ppermute | solution.py:536
  221.2 7.6 %collective-permute-start.25 = (f32[128,512]{1,0:T(8,128)S(1)}, f32[128,512]{1,0:T(8,128)S(1)}, u32[]{:S(2)}, u32[]{:S(2)}) collective-permute-start(f32[128,512]{1,0:T(8,128)S(1)} %constant_dynamic-update-slice_fusion), channel_id=1, source_target_pairs={{0,8},{4,12},{8,0},{12,4},{16,24},{20,28},{24,16},{28,20},{1,9},{5... | collective-permute-start | bytes 786440 | tf_op jit(solution)/shard_map/ppermute | solution.py:511
  221.7 32.3 %collective-permute-start.8 = (f32[2,512,256]{2,1,0:T(8,128)}, f32[2,512,256]{2,1,0:T(8,128)}, u32[]{:S(2)}, u32[]{:S(2)}) collective-permute-start(f32[2,512,256]{2,1,0:T(8,128)} %get-tuple-element.23), channel_id=1, source_target_pairs={{0,4},{1,5},{2,6},{3,7},{4,8},{5,9},{6,10},{7,11},{8,12},{9,13},{1... | collective-permute-start | bytes 3145736 | tf_op jit(solution)/shard_map/ppermute | solution.py:497
  228.9 24.9 %collective-permute-start.26 = (f32[256,512]{1,0:T(8,128)S(1)}, f32[256,512]{1,0:T(8,128)S(1)}, u32[]{:S(2)}, u32[]{:S(2)}) collective-permute-start(f32[256,512]{1,0:T(8,128)S(1)} %pad_maximum_fusion.3), channel_id=1, source_target_pairs={{0,16},{4,20},{8,24},{12,28},{16,0},{20,4},{24,8},{28,12},{1,17},{... | collective-permute-start | bytes 1572872 | tf_op jit(solution)/shard_map/ppermute | solution.py:511
  254.0 8.5 %collective-permute-start.27 = (f32[512,512]{1,0:T(8,128)S(1)}, f32[512,512]{1,0:T(8,128)}, u32[]{:S(2)}, u32[]{:S(2)}) collective-permute-start(f32[512,512]{1,0:T(8,128)S(1)} %pad_maximum_fusion.2), channel_id=1, source_target_pairs={{0,4},{4,0},{8,12},{12,8},{16,20},{20,16},{24,28},{28,24},{1,5},{5... | collective-permute-start | bytes 3145736 | tf_op jit(solution)/shard_map/ppermute | solution.py:511
  254.5 2.8 %copy-start = (f32[2,512,1024]{2,1,0:T(8,128)S(1)}, f32[2,512,1024]{2,1,0:T(8,128)}, u32[]{:S(2)}) copy-start(f32[2,512,1024]{2,1,0:T(8,128)} %get-tuple-element.22) | copy-start | bytes 12582916

commit v5 on v4

--- a/solution.py
+++ b/solution.py
@@ -1,5 +1,3 @@
-import functools
-import itertools
 import math
 
 import jax
@@ -121,10 +119,8 @@
     mat_t_hi_hbm,
     mat_t_lo_hbm,
     own_out,
-    right_a_out,
-    right_b_out,
-    lower_a_out,
-    lower_b_out,
+    right_out,
+    lower_ab_out,
     lower_c_out,
     corner_a_out,
     corner_b_out,
@@ -206,23 +202,22 @@
     for load in late_loads:
         load.start()
 
+    top, bottom = pl.ds(0, tile_rows), pl.ds(tile_rows, side)
     outs = (
-        own_out,
-        right_a_out,
-        right_b_out,
-        lower_a_out,
-        lower_b_out,
-        lower_c_out,
-        corner_a_out,
-        corner_b_out,
+        (corner_a_out, bottom, pl.ds(tile_cols, half)),
+        (corner_b_out, bottom, pl.ds(tile_cols + half, half)),
+        (lower_c_out, bottom, pl.ds(side, tile_cols - side)),
+        (lower_ab_out, bottom, pl.ds(0, side)),
+        (right_out, top, pl.ds(tile_cols, side)),
+        (own_out, top, pl.ds(0, tile_cols)),
     )
     stores = [
-        pltpu.make_async_copy(src, dst, out_sems.at[n])
-        for n, (src, dst) in enumerate(zip(pieces(grads), outs))
+        pltpu.make_async_copy(grads.at[:, rows, cols], dst, out_sems.at[n])
+        for n, (dst, rows, cols) in enumerate(outs)
     ]
-    dpup_store = pltpu.make_async_copy(dpup, dpup_out, out_sems.at[8])
-    lower_stores = stores[3:]
-    upper_stores = stores[:3]
+    dpup_store = pltpu.make_async_copy(dpup, dpup_out, out_sems.at[6])
+    lower_stores = stores[:4]
+    upper_stores = stores[4:]
 
     zero_rows = 16
 
@@ -271,30 +266,29 @@
             for load in late_loads:
                 load.wait()
 
-        @pl.loop(0, short // 16, unroll=2)
-        def _(step):
-            base = pl.multiple_of(step * 16, 16)
-            for part in range(RADIX):
-                cols = pl.ds(part * short, short)
-                values = []
-                for q in range(RADIX):
-                    rows = pl.ds(base + q * short, 16)
-                    wr, wi = win[0, rows, cols], win[1, rows, cols]
-                    pr, pi = pupil[0, rows, cols], pupil[1, rows, cols]
-                    values.append((wr * pr - wi * pi, wr * pi + wi * pr))
-                for p, (re, im) in enumerate(butterfly(values, 1)):
-                    for offset, value in ((0, re), (short, im)):
-                        hi, lo = split(value)
-                        rows = pl.ds(base + offset, 16)
-                        left_hi[p, rows, cols] = hi
-                        left_lo[p, rows, cols] = lo
-
-        for p in range(RADIX):
-            for half in range(2):
-                cols = pl.ds(half * (side // 2), side // 2)
+        for start in (0, half):
+            for base in range(0, short, 16):
+                for col0 in range(start, start + half, short):
+                    cols = pl.ds(col0, short)
+                    values = []
+                    for q in range(RADIX):
+                        rows = pl.ds(base + q * short, 16)
+                        wr, wi = win[0, rows, cols], win[1, rows, cols]
+                        pr, pi = pupil[0, rows, cols], pupil[1, rows, cols]
+                        values.append((wr * pr - wi * pi, wr * pi + wi * pr))
+                    for p, (re, im) in enumerate(butterfly(values, 1)):
+                        for offset, value in ((0, re), (short, im)):
+                            hi, lo = split(value)
+                            rows = pl.ds(base + offset, 16)
+                            left_hi[p, rows, cols] = hi
+                            left_lo[p, rows, cols] = lo
+            cols = pl.ds(start, half)
+            for p in range(RADIX):
                 rows_f32[p, :, cols] = left_dot(
                     mat_hi[p], mat_lo[p], left_hi[p, :, cols], left_lo[p, :, cols]
                 )
+
+        for p in range(RADIX):
             for base in range(0, short, 16):
                 values = []
                 for q in range(RADIX):
@@ -313,8 +307,8 @@
                         right_lo[t, rows, pl.ds(offset, short)] = lo
 
         for t in range(RADIX):
-            for half in range(2):
-                rows = pl.ds(half * (side // 2), side // 2)
+            for start in (0, half):
+                rows = pl.ds(start, half)
                 field = right_dot(
                     right_hi[t, rows, :], right_lo[t, rows, :], mat_t_hi[t], mat_t_lo[t]
                 )
@@ -338,30 +332,32 @@
                         hi, lo = split(value)
                         left_hi[p, pl.ds(base + offset, 16), cols] = hi
                         left_lo[p, pl.ds(base + offset, 16), cols] = lo
-            for half in range(2):
-                cols = pl.ds(half * (side // 2), side // 2)
+
+        for start in (0, half):
+            cols = pl.ds(start, half)
+            for p in range(RADIX):
                 rows_f32[p, :, cols] = left_dot(
                     mat_t_hi[p], mat_t_lo[p], left_hi[p, :, cols], left_lo[p, :, cols]
                 )
-
-        @pl.loop(0, short // 8, unroll=2)
-        def _(step):
-            base = pl.multiple_of(step * 8, 8)
-            for part in range(RADIX):
-                cols = pl.ds(part * short, short)
-                values = [
-                    (rows_f32[p, pl.ds(base, 8), cols], rows_f32[p, pl.ds(base + short, 8), cols])
-                    for p in range(RADIX)
-                ]
-                for q, (re, im) in enumerate(butterfly(values, -1)):
-                    rows = pl.ds(base + q * short, 8)
-                    pr, pi = pupil[0, rows, cols], pupil[1, rows, cols]
-                    padded = pl.ds(base + q * short + 8, 8)
-                    dwin[0, padded, cols] = pr * re + pi * im
-                    dwin[1, padded, cols] = pr * im - pi * re
-                    wr, wi = win[0, rows, cols], win[1, rows, cols]
-                    dpup[0, rows, cols] += wr * re + wi * im
-                    dpup[1, rows, cols] += wr * im - wi * re
+            for base in range(0, short, 8):
+                for col0 in range(start, start + half, short):
+                    cols = pl.ds(col0, short)
+                    values = [
+                        (
+                            rows_f32[p, pl.ds(base, 8), cols],
+                            rows_f32[p, pl.ds(base + short, 8), cols],
+                        )
+                        for p in range(RADIX)
+                    ]
+                    for q, (re, im) in enumerate(butterfly(values, -1)):
+                        rows = pl.ds(base + q * short, 8)
+                        pr, pi = pupil[0, rows, cols], pupil[1, rows, cols]
+                        padded = pl.ds(base + q * short + 8, 8)
+                        dwin[0, padded, cols] = pr * re + pi * im
+                        dwin[1, padded, cols] = pr * im - pi * re
+                        wr, wi = win[0, rows, cols], win[1, rows, cols]
+                        dpup[0, rows, cols] += wr * re + wi * im
+                        dpup[1, rows, cols] += wr * im - wi * re
 
         last = slot == count - 1
         pl.when(last)(dpup_store.start)
@@ -412,7 +408,10 @@
     anywhere = pl.BlockSpec(memory_space=pl.ANY)
     f32, bf16 = jnp.float32, jnp.bfloat16
     region = (2, tile_rows + side, tile_cols + side)
-    outs = (tile, *parts[:-1], pupil)
+    _, _, _, _, lower_c, corner_a, corner_b, _ = parts
+    right = jax.ShapeDtypeStruct((2, tile_rows, side), f32)
+    lower_ab = jax.ShapeDtypeStruct((2, side, side), f32)
+    outs = (tile, right, lower_ab, lower_c, corner_a, corner_b, pupil)
     table = pltpu.VMEM(high.shape, bf16)
     return pl.pallas_call(
         slots_kernel,
@@ -438,7 +437,7 @@
             table,
             table,
             pltpu.SemaphoreType.DMA((14,)),
-            pltpu.SemaphoreType.DMA((9,)),
+            pltpu.SemaphoreType.DMA((7,)),
         ],
         compiler_params=pltpu.CompilerParams(vmem_limit_bytes=56 * 1024 * 1024),
         cost_estimate=pl.CostEstimate(
@@ -544,23 +543,22 @@
     return lax.optimization_barrier((value, *arrivals))[0]
 
 
-def pupil_sum(dpup, arrivals):
+def pupil_sum(part, first, middle, last):
     n_ty, n_tx = lax.axis_size("ty"), lax.axis_size("tx")
-    bits = [1]
+    bits = []
     bit = n_ty // 2
     while bit > 1:
         bits.append(bit)
         bit //= 2
-    steps = [functools.partial(halve, bit=bit) for bit in bits]
-    steps.append(lambda part: scatter_tx(part) * (1.0 / math.sqrt(n_ty * n_tx)))
-    steps.append(gather_tx)
-    steps += [functools.partial(double, bit=bit) for bit in reversed(bits)]
-    part = dpup.reshape(-1, dpup.shape[-1])
-    for step, before in itertools.zip_longest(steps, arrivals, fillvalue=()):
-        if before:
-            part = after(part, *before)
-        part = step(part)
-    return part.reshape(dpup.shape)
+    part = after(part, *first)
+    for bit in bits[1:]:
+        part = halve(part, bit)
+    part = scatter_tx(part) * (1.0 / math.sqrt(n_ty * n_tx))
+    part = gather_tx(part)
+    for bit in reversed(bits[1:]):
+        part = double(part, bit)
+    part = double(after(part, *middle), bits[0])
+    return double(after(part, *last), 1)
 
 
 def body(spectrum, pupil, amplitudes, offsets, live):
@@ -581,7 +579,7 @@
 
     lower_b = send(spectrum[:, :side, half:side], up)
     right_a = send(spectrum[:, :, :half], left)
-    right_b = send(spectrum[:, :, half:side], left)
+    right_b = send(after(spectrum[:, :, half:side], lower_b), left)
     lower_a = send(spectrum[:, :side, :half], up)
     lower_c = send(spectrum[:, :side, side:], up)
     amps = ordered(amplitudes)
@@ -592,8 +590,9 @@
     corner_up = send(right_b_again[:, :side], lambda i, j: (i - 1, j) if i % 2 else None)
 
     parts = (right_a, right_b, lower_a, lower_b, lower_c, corner_a, corner_up, corner_side)
-    own_g, *grads, dpup = slots_call(meta, spectrum, parts, amps, pupil)
-    right_a_g, right_b_g, lower_a_g, lower_b_g, lower_c_g, corner_a_g, corner_b_g = grads
+    own_g, right_g, lower_ab_g, lower_c_g, corner_a_g, corner_b_g, dpup = slots_call(
+        meta, spectrum, parts, amps, pupil
+    )
 
     def down(i, j):
         return (i + 1, j)
@@ -604,30 +603,21 @@
     back_side = send(corner_b_g, lambda i, j: (i, j + 1) if i % 2 else None)
     back_a = send(corner_a_g, down)
     back_down = send(corner_b_g, lambda i, j: None if i % 2 else (i + 1, j))
-    lower_a = send(lower_a_g, down)
-    lower_c = send(lower_c_g, down)
-    right_b = send(right_b_g + back_down, right)
-    right_a = send(right_a_g + back_a, right)
-    lower_b = send(lower_b_g + back_side, down)
+    halved = halve(halve(dpup.reshape(-1, side), 1), lax.axis_size("ty") // 2)
+    lower_c = send(after(lower_c_g, halved), down)
+    right_back = send(right_g + jnp.concatenate([back_a, back_down], axis=2), right)
+    lower_ab = send(lower_ab_g.at[:, :, half:].add(back_side), down)
     spec_grad = jnp.concatenate(
         [
-            own_g[:, :, :half] + lower_a + right_a,
-            own_g[:, :, half:side] + lower_b + right_b,
+            own_g[:, :, :side] + lower_ab + right_back,
             own_g[:, :, side:] + lower_c,
         ],
         axis=2,
     )
-    arrivals = [
-        (),
-        (),
-        (back_a, back_side, back_down),
-        (),
-        (right_b,),
-        (lower_c,),
-        (right_a, lower_b),
-        (lower_a,),
-    ]
-    return spec_grad, pupil_sum(dpup, arrivals)
+    pupil_grad = pupil_sum(
+        halved, (back_a, back_down, back_side), (lower_c,), (right_back, lower_ab)
+    )
+    return spec_grad, pupil_grad.reshape(pupil.shape)
 
 
 def solution(mesh):

time: 266 us -> 260 us (0.977)
  starting transfers between devices: 83.8 us -> 62.7 us
  waiting for transfers between devices: 120 us -> 141 us
  other arithmetic: 22.8 us -> 19.1 us
    ppermute x3, waiting for transfers between devices: 0.01 us -> 16.9 us  [scatter_tx(): total = total + lax.ppermute(piece, 'tx', ring_pairs(size, step))]
    ppermute x16 -> x14, starting transfers between devices: 64.4 us -> 47.9 us  [send(): return lax.ppermute(array, ('ty', 'tx'), along(rule, sizes))]
    ppermute x3, waiting for transfers between devices: 17.2 us -> 3.93 us  [gather_tx(): parts.append(lax.ppermute(value, 'tx', ring_pairs(size, step)))]
    ppermute x3, waiting for transfers between devices: 34.6 us -> 45.1 us  [halve(): lax.ppermute(sent, 'ty', [(i, i ^ bit) for i in range(lax.axis_size('ty'))])]
    ppermute x3, starting transfers between devices: 12.6 us -> 4.21 us  [scatter_tx(): total = total + lax.ppermute(piece, 'tx', ring_pairs(size, step))]
    ppermute x3, waiting for transfers between devices: 22.6 us -> 27.8 us  [double(): lax.ppermute(value, 'ty', [(i, i ^ bit) for i in range(lax.axis_size('ty'...]
    add x5 -> x2, other arithmetic: 12.5 us -> 8.04 us  [the longest x1 4.76 us: body(): own_g[:, :, :side] + lower_ab + right_back]
    ppermute x3, starting transfers between devices: 0.15 us -> 4.42 us  [halve(): lax.ppermute(sent, 'ty', [(i, i ^ bit) for i in range(lax.axis_size('ty'))])]
  transfers between devices with their start and end apart: 28 -> 26, of which waited for: 9 -> 13; matrix products, arithmetic and copies ran while one was open for 9% -> 8% of each run, Pallas kernels for 3% -> 3%
where the time goes in v5:
time: 260 us; the launch traced here: 259 us
  waiting for transfers between devices  141 us (54%)
  starting transfers between devices  62.7 us (24%)
  Pallas kernels  27.5 us (11%)
  other arithmetic  19.1 us (7%)
  local copies, waits for them, and re-layouts  7.76 us (3%)
    ppermute x14, starting transfers between devices, send(): return lax.ppermute(array, ('ty', 'tx'), along(rule, sizes))  47.9 us
    ppermute x14, waiting for transfers between devices, send(): return lax.ppermute(array, ('ty', 'tx'), along(rule, sizes))  47 us
    ppermute x3, waiting for transfers between devices, halve(): lax.ppermute(sent, 'ty', [(i, i ^ bit) for i in range(lax.axis_size('ty'))])  45.1 us
    ppermute x3, waiting for transfers between devices, double(): lax.ppermute(value, 'ty', [(i, i ^ bit) for i in range(lax.axis_size('ty'...  27.8 us
    pallas_call x1, Pallas kernels, slots_call(): pl.pallas_call(slots_kernel, out_shape=[jax.ShapeDtypeStruct(x.shape, f32...  19.3 us
    ppermute x3, waiting for transfers between devices, scatter_tx(): total = total + lax.ppermute(piece, 'tx', ring_pairs(size, step))  16.9 us
    pallas_call x1, Pallas kernels, ordered(): pl.pallas_call(order_kernel, grid=(slots,), out_shape=jax.ShapeDtypeStruc...  8.24 us
    ppermute x3, starting transfers between devices, gather_tx(): parts.append(lax.ppermute(value, 'tx', ring_pairs(size, step)))  5.93 us
  transfers between devices with their start and end apart: 26, of which 13 were waited for; matrix products, arithmetic and copies ran while one was open for 8% of the time, Pallas kernels for 3%

profile of v5, /device:TPU:1, one launch (start us, length us, event | category | flops | bytes accessed | tf_op | source)
XLA Modules:
  0.0 258.9 jit_solution(10307027249678039357)
XLA Ops:
  0.6 2.7 %fusion = (f32[2,512,256]{2,1,0:T(8,128)}, f32[2,512,256]{2,1,0:T(8,128)S(1)}) fusion(f32[2,512,1024]{2,1,0:T(8,128)} %tile_hbm.1), kind=kLoop, calls=%fused_computation.31 | loop fusion | bytes 4194304 | tf_op jit(solution)/shard_map/slice | solution.py:582
  3.3 2.0 collective-permute-start.1
  5.3 1.3 collective-permute-start
  6.6 8.2 %ordered.1.amps_hbm = f32[3,512,512]{2,1,0:T(8,128)} custom-call(f32[3,512,512]{2,1,0:T(8,128)} %amps.1, bf16[512,512]{1,0:T(8,128)(2,1)} %constant.168.clone.perm_rows, bf16[512,512]{1,0:T(8,128)(2,1)} %constant.169.clone.perm_cols), custom_call_target="tpu_custom_call" | custom-call | flops 4831838208 | bytes 6291456 | tf_op jit(solution)/shard_map/ordered/pallas_call | solution.py:470
  14.9 6.1 %collective-permute-done.1.lower_b_hbm = f32[2,512,256]{2,1,0:T(8,128)} collective-permute-done((f32[2,512,256]{2,1,0:T(8,128)}, f32[2,512,256]{2,1,0:T(8,128)}, u32[]{:S(2)}, u32[]{:S(2)}) %collective-permute-start.1) | collective-permute-done | bytes 1048608 | tf_op jit(solution)/shard_map/ppermute | solution.py:496
  20.9 1.3 collective-permute-start.2
  22.2 1.3 collective-permute-start.6
  23.5 1.8 slice.51
  25.3 1.9 collective-permute-start.4
  27.2 1.9 collective-permute-start.3
  29.2 4.5 %collective-permute-done.right_a_hbm = f32[2,512,256]{2,1,0:T(8,128)} collective-permute-done((f32[2,512,256]{2,1,0:T(8,128)S(1)}, f32[2,512,256]{2,1,0:T(8,128)}, u32[]{:S(2)}, u32[]{:S(2)}) %collective-permute-start) | collective-permute-done | bytes 1048608 | tf_op jit(solution)/shard_map/ppermute | solution.py:496
  33.7 1.9 collective-permute-start.5
  35.6 19.9 %collective-permute-done.2.right_b_hbm = f32[2,512,256]{2,1,0:T(8,128)} collective-permute-done((f32[2,512,256]{2,1,0:T(8,128)}, f32[2,512,256]{2,1,0:T(8,128)}, u32[]{:S(2)}, u32[]{:S(2)}) %collective-permute-start.2) | collective-permute-done | bytes 1048608 | tf_op jit(solution)/shard_map/ppermute | solution.py:496
  55.5 11.2 %collective-permute-done.6.corner_side_hbm = f32[2,512,256]{2,1,0:T(8,128)} collective-permute-done((f32[2,512,256]{2,1,0:T(8,128)}, f32[2,512,256]{2,1,0:T(8,128)}, u32[]{:S(2)}, u32[]{:S(2)}) %collective-permute-start.6) | collective-permute-done | bytes 1048608 | tf_op jit(solution)/shard_map/ppermute | solution.py:496
  66.8 2.3 collective-permute-start.7
  69.0 0.1 copy.15
  69.1 0.1 copy.17
  69.2 0.1 copy.16
  69.3 0.1 pad_add_fusion
  69.4 0.6 concatenate.20.meta
  70.0 0.0 collective-permute-done.3.lower_a_hbm
  70.0 5.2 %collective-permute-done.5.corner_a_hbm = f32[2,512,256]{2,1,0:T(8,128)} collective-permute-done((f32[2,512,256]{2,1,0:T(8,128)}, f32[2,512,256]{2,1,0:T(8,128)}, u32[]{:S(2)}, u32[]{:S(2)}) %collective-permute-start.5) | collective-permute-done | bytes 1048608 | tf_op jit(solution)/shard_map/ppermute | solution.py:496
  75.2 0.0 collective-permute-done.7.corner_up_hbm
  75.2 19.3 %slots.1 = (f32[2,512,1024]{2,1,0:T(8,128)}, f32[2,512,512]{2,1,0:T(8,128)}, f32[2,512,512]{2,1,0:T(8,128)}, f32[2,512,512]{2,1,0:T(8,128)}, f32[2,512,256]{2,1,...) custom-call(s32[4,3]{1,0:T(4,128)} %concatenate.20.meta, f32[2,512,1024]{2,1,0:T(8,128)} %tile_hbm.1, ...), custom_call_target="tpu_custom_call" | custom-call | flops 9663676416 | bytes 41943040 | tf_op jit(solution)/shard_map/slots/pallas_call | solution.py:416
  94.5 1.4 constant_dynamic-slice_fusion.5
  95.9 0.1 collective-permute-start.13
  96.1 1.3 collective-permute-start.11
  97.4 5.1 %collective-permute-start.8 = (f32[2,512,256]{2,1,0:T(8,128)}, f32[2,512,256]{2,1,0:T(8,128)}, u32[]{:S(2)}, u32[]{:S(2)}) collective-permute-start(f32[2,512,256]{2,1,0:T(8,128)} %get-tuple-element.35), channel_id=1, source_target_pairs={{4,5},{5,6},{6,7},{12,13},{13,14},{14,15},{20,21},{21,22},{22,23},... | collective-permute-start | bytes 3145736 | tf_op jit(solution)/shard_map/ppermute | solution.py:496
  102.5 20.5 %collective-permute-start.10 = (f32[2,512,256]{2,1,0:T(8,128)}, f32[2,512,256]{2,1,0:T(8,128)}, u32[]{:S(2)}, u32[]{:S(2)}) collective-permute-start(f32[2,512,256]{2,1,0:T(8,128)} %get-tuple-element.37), channel_id=1, source_target_pairs={{0,4},{1,5},{2,6},{3,7},{4,8},{5,9},{6,10},{7,11},{8,12},{9,13},{1... | collective-permute-start | bytes 3145736 | tf_op jit(solution)/shard_map/ppermute | solution.py:496
  123.0 0.0 collective-permute-done.13
  123.1 1.4 dynamic-slice_add_fusion
  124.5 0.0 copy-start
  124.5 0.8 constant_dynamic-slice_fusion.4
  125.3 0.5 collective-permute-start.14
  125.9 22.0 %collective-permute-done.14 = f32[256,512]{1,0:T(8,128)} collective-permute-done((f32[256,512]{1,0:T(8,128)}, f32[256,512]{1,0:T(8,128)}, u32[]{:S(2)}, u32[]{:S(2)}) %collective-permute-start.14) | collective-permute-done | bytes 524320 | tf_op jit(solution)/shard_map/ppermute | solution.py:504
  147.9 1.1 dynamic-slice_add_fusion.1
  149.0 1.9 collective-permute-start.15
  151.0 3.8 %collective-permute-start.16 = (f32[128,512]{1,0:T(8,128)S(1)}, f32[128,512]{1,0:T(8,128)S(1)}, u32[]{:S(2)}, u32[]{:S(2)}) collective-permute-start(f32[128,512]{1,0:T(8,128)S(1)} %constant_dynamic-slice_fusion.3), channel_id=1, source_target_pairs={{0,8},{4,12},{8,0},{12,4},{16,24},{20,28},{24,16},{28,20},{1,9},{5... | collective-permute-start | bytes 786440 | tf_op jit(solution)/shard_map/ppermute | solution.py:504
  154.8 3.3 %maximum_add_fusion = f32[2,512,512]{2,1,0:T(8,128)} fusion(f32[2,512,512]{2,1,0:T(8,128)S(1)} %copy-done, f32[2,512,256]{2,1,0:T(8,128)} %collective-permute-done.11, f32[2,512,256]{2,1,0:T(8,128)} %collective-permute-done.10), kind=kLoop, calls=%fused_computation.1 | loop fusion | flops 1048576 | bytes 6291456 | tf_op jit(solution)/shard_map/add | solution.py:608
  158.1 2.7 %collective-permute-start.12 = (f32[2,512,512]{2,1,0:T(8,128)}, f32[2,512,512]{2,1,0:T(8,128)S(1)}, u32[]{:S(2)}, u32[]{:S(2)}) collective-permute-start(f32[2,512,512]{2,1,0:T(8,128)} %maximum_add_fusion), channel_id=1, source_target_pairs={{0,1},{1,2},{2,3},{4,5},{5,6},{6,7},{8,9},{9,10},{10,11},{12,13},{... | collective-permute-start | bytes 6291464 | tf_op jit(solution)/shard_map/ppermute | solution.py:496
  160.8 23.0 %collective-permute-done.16 = f32[128,512]{1,0:T(8,128)S(1)} collective-permute-done((f32[128,512]{1,0:T(8,128)S(1)}, f32[128,512]{1,0:T(8,128)S(1)}, u32[]{:S(2)}, u32[]{:S(2)}) %collective-permute-start.16) | collective-permute-done | bytes 262176 | tf_op jit(solution)/shard_map/ppermute | solution.py:504
  184.0 0.1 collective-permute-start.19
  184.0 2.8 %collective-permute-start.18 = (f32[32,512]{1,0:T(8,128)S(1)}, f32[32,512]{1,0:T(8,128)S(1)}, u32[]{:S(2)}, u32[]{:S(2)}) collective-permute-start(f32[32,512]{1,0:T(8,128)S(1)} %get-tuple-element.58), channel_id=1, source_target_pairs={{0,2},{1,3},{2,0},{3,1},{4,6},{5,7},{6,4},{7,5},{8,10},{9,11},{10,... | collective-permute-start | bytes 196616 | tf_op jit(solution)/shard_map/ppermute | solution.py:526
  186.8 1.4 collective-permute-start.17
  188.2 2.7 %add_dynamic-update-slice_fusion = f32[2,512,512]{2,1,0:T(8,128)} fusion(f32[2,512,512]{2,1,0:T(8,128)} %get-tuple-element.34, f32[2,512,256]{2,1,0:T(8,128)} %collective-permute-done.8), kind=kLoop, calls=%fused_computation.7 | loop fusion | flops 262144 | bytes 3145728 | tf_op jit(solution)/shard_map/scatter-add | solution.py:609
  190.9 16.9 %collective-permute-done.19 = f32[32,512]{1,0:T(8,128)S(1)} collective-permute-done((f32[32,512]{1,0:T(8,128)S(1)}, f32[32,512]{1,0:T(8,128)S(1)}, u32[]{:S(2)}, u32[]{:S(2)}) %collective-permute-start.19) | collective-permute-done | bytes 65568 | tf_op jit(solution)/shard_map/ppermute | solution.py:526
  207.8 2.5 collective-permute-start.9
  210.4 2.4 collective-permute-start.20
  212.8 2.1 collective-permute-start.21
  214.9 1.4 collective-permute-done.20
  216.3 1.4 collective-permute-start.22
  217.7 2.0 collective-permute-done.21
  219.7 0.5 collective-permute-done.22
  220.3 0.1 collective-permute-start.23
  220.4 19.8 %collective-permute-done.23 = f32[128,512]{1,0:T(8,128)S(1)} collective-permute-done((f32[128,512]{1,0:T(8,128)S(1)}, f32[128,512]{1,0:T(8,128)S(1)}, u32[]{:S(2)}, u32[]{:S(2)}) %collective-permute-start.23) | collective-permute-done | bytes 262176 | tf_op jit(solution)/shard_map/ppermute | solution.py:510
  240.3 0.1 collective-permute-start.24
  240.4 8.0 %collective-permute-done.24 = f32[256,512]{1,0:T(8,128)S(1)} collective-permute-done((f32[256,512]{1,0:T(8,128)S(1)}, f32[256,512]{1,0:T(8,128)S(1)}, u32[]{:S(2)}, u32[]{:S(2)}) %collective-permute-start.24) | collective-permute-done | bytes 524320 | tf_op jit(solution)/shard_map/ppermute | solution.py:510
  248.4 0.1 broadcast_select_fusion.3
  248.5 0.1 pad_maximum_fusion.2
  248.6 0.1 collective-permute-start.25
  248.7 4.8 %add_add_fusion = (f32[2,512,512]{2,1,0:T(8,128)S(1)}, f32[2,512,512]{2,1,0:T(8,128)S(1)}) fusion(f32[2,512,512]{2,1,0:T(8,128)S(1)} %collective-permute-done.12, f32[2,512,512]{2,1,0:T(8,128)} %collective-permute-done.9, f32[2,512,1024]{2,1,0:T(8,128)} %get-tuple-element.33, f32[2,512,512]{2,1,0:T(8,128)} %collective-permute-done.15), kind=kLoop, calls=%fused_computation.4 | loop fusion | flops 1572864 | bytes 14680064 | tf_op jit(solution)/shard_map/add | solution.py:612
  253.5 2.5 pad_maximum_fusion
  255.9 1.4 broadcast_select_fusion.1
  257.4 1.5 pad_maximum_fusion.1
  (29 shorter events, 0.3 us)
Async XLA Ops:
  3.3 17.6 %collective-permute-start.1 = (f32[2,512,256]{2,1,0:T(8,128)}, f32[2,512,256]{2,1,0:T(8,128)}, u32[]{:S(2)}, u32[]{:S(2)}) collective-permute-start(f32[2,512,256]{2,1,0:T(8,128)} %get-tuple-element.29), channel_id=1, source_target_pairs={{4,0},{5,1},{6,2},{7,3},{8,4},{9,5},{10,6},{11,7},{12,8},{13,9},{1... | collective-permute-start | bytes 3145736 | tf_op jit(solution)/shard_map/ppermute | solution.py:496
  5.3 28.4 %collective-permute-start = (f32[2,512,256]{2,1,0:T(8,128)S(1)}, f32[2,512,256]{2,1,0:T(8,128)}, u32[]{:S(2)}, u32[]{:S(2)}) collective-permute-start(f32[2,512,256]{2,1,0:T(8,128)S(1)} %get-tuple-element.49), channel_id=1, source_target_pairs={{1,0},{2,1},{3,2},{5,4},{6,5},{7,6},{9,8},{10,9},{11,10},{13,12},{... | collective-permute-start | bytes 3145736 | tf_op jit(solution)/shard_map/ppermute | solution.py:496
  14.9 54.2 %copy-start.3 = (s32[3]{0:T(128)S(1)}, s32[3]{0:T(128)}, u32[]{:S(2)}) copy-start(s32[3]{0:T(128)} %param.17) | copy-start | bytes 40
  14.9 54.3 %copy-start.2 = (s32[3,2]{0,1:T(2,128)S(1)}, s32[3,2]{0,1:T(2,128)}, u32[]{:S(2)}) copy-start(s32[3,2]{0,1:T(2,128)} %param.16) | copy-start | bytes 76
  20.9 34.6 %collective-permute-start.2 = (f32[2,512,256]{2,1,0:T(8,128)}, f32[2,512,256]{2,1,0:T(8,128)}, u32[]{:S(2)}, u32[]{:S(2)}) collective-permute-start(f32[2,512,256]{2,1,0:T(8,128)} %get-tuple-element.29), channel_id=1, source_target_pairs={{1,0},{2,1},{3,2},{5,4},{6,5},{7,6},{9,8},{10,9},{11,10},{13,12},{... | collective-permute-start | bytes 3145736 | tf_op jit(solution)/shard_map/ppermute | solution.py:496
  22.2 44.5 %collective-permute-start.6 = (f32[2,512,256]{2,1,0:T(8,128)}, f32[2,512,256]{2,1,0:T(8,128)}, u32[]{:S(2)}, u32[]{:S(2)}) collective-permute-start(f32[2,512,256]{2,1,0:T(8,128)} %collective-permute-done.1.lower_b_hbm), channel_id=1, source_target_pairs={{5,4},{6,5},{7,6},{13,12},{14,13},{15,14},{21,20},{22,21},{23,22},... | collective-permute-start | bytes 3145736 | tf_op jit(solution)/shard_map/ppermute | solution.py:496
  25.3 44.7 %collective-permute-start.4 = (f32[2,512,512]{2,1,0:T(8,128)S(1)}, f32[2,512,512]{2,1,0:T(8,128)}, u32[]{:S(2)}, u32[]{:S(2)}) collective-permute-start(f32[2,512,512]{2,1,0:T(8,128)S(1)} %slice.51), channel_id=1, source_target_pairs={{4,0},{5,1},{6,2},{7,3},{8,4},{9,5},{10,6},{11,7},{12,8},{13,9},{1... | collective-permute-start | bytes 6291464 | tf_op jit(solution)/shard_map/ppermute | solution.py:496
  27.2 42.8 %collective-permute-start.3 = (f32[2,512,256]{2,1,0:T(8,128)S(1)}, f32[2,512,256]{2,1,0:T(8,128)}, u32[]{:S(2)}, u32[]{:S(2)}) collective-permute-start(f32[2,512,256]{2,1,0:T(8,128)S(1)} %get-tuple-element.49), channel_id=1, source_target_pairs={{4,0},{5,1},{6,2},{7,3},{8,4},{9,5},{10,6},{11,7},{12,8},{13,9},{1... | collective-permute-start | bytes 3145736 | tf_op jit(solution)/shard_map/ppermute | solution.py:496
  33.7 41.5 %collective-permute-start.5 = (f32[2,512,256]{2,1,0:T(8,128)}, f32[2,512,256]{2,1,0:T(8,128)}, u32[]{:S(2)}, u32[]{:S(2)}) collective-permute-start(f32[2,512,256]{2,1,0:T(8,128)} %collective-permute-done.right_a_hbm), channel_id=1, source_target_pairs={{4,0},{5,1},{6,2},{7,3},{8,4},{9,5},{10,6},{11,7},{12,8},{13,9},{1... | collective-permute-start | bytes 3145736 | tf_op jit(solution)/shard_map/ppermute | solution.py:496
  66.8 8.5 %collective-permute-start.7 = (f32[2,512,256]{2,1,0:T(8,128)}, f32[2,512,256]{2,1,0:T(8,128)}, u32[]{:S(2)}, u32[]{:S(2)}) collective-permute-start(f32[2,512,256]{2,1,0:T(8,128)} %collective-permute-done.2.right_b_hbm), channel_id=1, source_target_pairs={{4,0},{5,1},{6,2},{7,3},{12,8},{13,9},{14,10},{15,11},{20,16},{21,... | collective-permute-start | bytes 3145736 | tf_op jit(solution)/shard_map/ppermute | solution.py:496
  94.5 28.6 %copy-start.1 = (f32[2,512,512]{2,1,0:T(8,128)S(1)}, f32[2,512,512]{2,1,0:T(8,128)}, u32[]{:S(2)}) copy-start(f32[2,512,512]{2,1,0:T(8,128)} %get-tuple-element.39) | copy-start | bytes 6291460
  95.9 27.1 %collective-permute-start.13 = (f32[512,512]{1,0:T(8,128)S(1)}, f32[512,512]{1,0:T(8,128)}, u32[]{:S(2)}, u32[]{:S(2)}) collective-permute-start(f32[512,512]{1,0:T(8,128)S(1)} %constant_dynamic-slice_fusion.5), channel_id=1, source_target_pairs={{0,4},{4,0},{8,12},{12,8},{16,20},{20,16},{24,28},{28,24},{1,5},{5... | collective-permute-start | bytes 3145736 | tf_op jit(solution)/shard_map/ppermute | solution.py:504
  96.1 54.9 %collective-permute-start.11 = (f32[2,512,256]{2,1,0:T(8,128)}, f32[2,512,256]{2,1,0:T(8,128)}, u32[]{:S(2)}, u32[]{:S(2)}) collective-permute-start(f32[2,512,256]{2,1,0:T(8,128)} %get-tuple-element.35), channel_id=1, source_target_pairs={{0,4},{1,5},{2,6},{3,7},{8,12},{9,13},{10,14},{11,15},{16,20},{17,... | collective-permute-start | bytes 3145736 | tf_op jit(solution)/shard_map/ppermute | solution.py:496
  97.4 53.6 %collective-permute-start.8 = (f32[2,512,256]{2,1,0:T(8,128)}, f32[2,512,256]{2,1,0:T(8,128)}, u32[]{:S(2)}, u32[]{:S(2)}) collective-permute-start(f32[2,512,256]{2,1,0:T(8,128)} %get-tuple-element.35), channel_id=1, source_target_pairs={{4,5},{5,6},{6,7},{12,13},{13,14},{14,15},{20,21},{21,22},{22,23},... | collective-permute-start | bytes 3145736 | tf_op jit(solution)/shard_map/ppermute | solution.py:496
  102.5 48.5 %collective-permute-start.10 = (f32[2,512,256]{2,1,0:T(8,128)}, f32[2,512,256]{2,1,0:T(8,128)}, u32[]{:S(2)}, u32[]{:S(2)}) collective-permute-start(f32[2,512,256]{2,1,0:T(8,128)} %get-tuple-element.37), channel_id=1, source_target_pairs={{0,4},{1,5},{2,6},{3,7},{4,8},{5,9},{6,10},{7,11},{8,12},{9,13},{1... | collective-permute-start | bytes 3145736 | tf_op jit(solution)/shard_map/ppermute | solution.py:496
  124.5 30.3 %copy-start = (f32[2,512,512]{2,1,0:T(8,128)S(1)}, f32[2,512,512]{2,1,0:T(8,128)}, u32[]{:S(2)}) copy-start(f32[2,512,512]{2,1,0:T(8,128)} %get-tuple-element.36) | copy-start | bytes 6291460
  125.3 22.6 %collective-permute-start.14 = (f32[256,512]{1,0:T(8,128)}, f32[256,512]{1,0:T(8,128)}, u32[]{:S(2)}, u32[]{:S(2)}) collective-permute-start(f32[256,512]{1,0:T(8,128)} %constant_dynamic-slice_fusion.4), channel_id=1, source_target_pairs={{0,16},{4,20},{8,24},{12,28},{16,0},{20,4},{24,8},{28,12},{1,17},{... | collective-permute-start | bytes 1572872 | tf_op jit(solution)/shard_map/ppermute | solution.py:504
  149.0 91.3 %collective-permute-start.15 = (f32[2,512,512]{2,1,0:T(8,128)}, f32[2,512,512]{2,1,0:T(8,128)}, u32[]{:S(2)}, u32[]{:S(2)}) collective-permute-start(f32[2,512,512]{2,1,0:T(8,128)} %get-tuple-element.40), channel_id=1, source_target_pairs={{0,4},{1,5},{2,6},{3,7},{4,8},{5,9},{6,10},{7,11},{8,12},{9,13},{1... | collective-permute-start | bytes 6291464 | tf_op jit(solution)/shard_map/ppermute | solution.py:496
  151.0 32.9 %collective-permute-start.16 = (f32[128,512]{1,0:T(8,128)S(1)}, f32[128,512]{1,0:T(8,128)S(1)}, u32[]{:S(2)}, u32[]{:S(2)}) collective-permute-start(f32[128,512]{1,0:T(8,128)S(1)} %constant_dynamic-slice_fusion.3), channel_id=1, source_target_pairs={{0,8},{4,12},{8,0},{12,4},{16,24},{20,28},{24,16},{28,20},{1,9},{5... | collective-permute-start | bytes 786440 | tf_op jit(solution)/shard_map/ppermute | solution.py:504
  158.1 90.5 %collective-permute-start.12 = (f32[2,512,512]{2,1,0:T(8,128)}, f32[2,512,512]{2,1,0:T(8,128)S(1)}, u32[]{:S(2)}, u32[]{:S(2)}) collective-permute-start(f32[2,512,512]{2,1,0:T(8,128)} %maximum_add_fusion), channel_id=1, source_target_pairs={{0,1},{1,2},{2,3},{4,5},{5,6},{6,7},{8,9},{9,10},{10,11},{12,13},{... | collective-permute-start | bytes 6291464 | tf_op jit(solution)/shard_map/ppermute | solution.py:496
  184.0 23.8 %collective-permute-start.19 = (f32[32,512]{1,0:T(8,128)S(1)}, f32[32,512]{1,0:T(8,128)S(1)}, u32[]{:S(2)}, u32[]{:S(2)}) collective-permute-start(f32[32,512]{1,0:T(8,128)S(1)} %get-tuple-element.57), channel_id=1, source_target_pairs={{0,3},{1,0},{2,1},{3,2},{4,7},{5,4},{6,5},{7,6},{8,11},{9,8},{10,9... | collective-permute-start | bytes 196616 | tf_op jit(solution)/shard_map/ppermute | solution.py:526
  184.0 26.3 %collective-permute-start.18 = (f32[32,512]{1,0:T(8,128)S(1)}, f32[32,512]{1,0:T(8,128)S(1)}, u32[]{:S(2)}, u32[]{:S(2)}) collective-permute-start(f32[32,512]{1,0:T(8,128)S(1)} %get-tuple-element.58), channel_id=1, source_target_pairs={{0,2},{1,3},{2,0},{3,1},{4,6},{5,7},{6,4},{7,5},{8,10},{9,11},{10,... | collective-permute-start | bytes 196616 | tf_op jit(solution)/shard_map/ppermute | solution.py:526
  186.8 23.5 %collective-permute-start.17 = (f32[32,512]{1,0:T(8,128)S(1)}, f32[32,512]{1,0:T(8,128)S(1)}, u32[]{:S(2)}, u32[]{:S(2)}) collective-permute-start(f32[32,512]{1,0:T(8,128)S(1)} %get-tuple-element.56), channel_id=1, source_target_pairs={{0,1},{1,2},{2,3},{3,0},{4,5},{5,6},{6,7},{7,4},{8,9},{9,10},{10,1... | collective-permute-start | bytes 196616 | tf_op jit(solution)/shard_map/ppermute | solution.py:526
  207.8 40.8 %collective-permute-start.9 = (f32[2,512,512]{2,1,0:T(8,128)}, f32[2,512,512]{2,1,0:T(8,128)}, u32[]{:S(2)}, u32[]{:S(2)}) collective-permute-start(f32[2,512,512]{2,1,0:T(8,128)} %add_dynamic-update-slice_fusion), channel_id=1, source_target_pairs={{0,4},{1,5},{2,6},{3,7},{4,8},{5,9},{6,10},{7,11},{8,12},{9,13},{1... | collective-permute-start | bytes 6291464 | tf_op jit(solution)/shard_map/ppermute | solution.py:496
  210.4 5.9 %collective-permute-start.20 = (f32[32,512]{1,0:T(8,128)S(1)}, f32[32,512]{1,0:T(8,128)S(1)}, u32[]{:S(2)}, u32[]{:S(2)}) collective-permute-start(f32[32,512]{1,0:T(8,128)S(1)} %get-tuple-element.45), channel_id=1, source_target_pairs={{0,1},{1,2},{2,3},{3,0},{4,5},{5,6},{6,7},{7,4},{8,9},{9,10},{10,1... | collective-permute-start | bytes 196616 | tf_op jit(solution)/shard_map/ppermute | solution.py:535
  212.8 7.0 %collective-permute-start.21 = (f32[32,512]{1,0:T(8,128)S(1)}, f32[32,512]{1,0:T(8,128)S(1)}, u32[]{:S(2)}, u32[]{:S(2)}) collective-permute-start(f32[32,512]{1,0:T(8,128)S(1)} %get-tuple-element.45), channel_id=1, source_target_pairs={{0,2},{1,3},{2,0},{3,1},{4,6},{5,7},{6,4},{7,5},{8,10},{9,11},{10,... | collective-permute-start | bytes 196616 | tf_op jit(solution)/shard_map/ppermute | solution.py:535
  216.3 4.0 %collective-permute-start.22 = (f32[32,512]{1,0:T(8,128)S(1)}, f32[32,512]{1,0:T(8,128)S(1)}, u32[]{:S(2)}, u32[]{:S(2)}) collective-permute-start(f32[32,512]{1,0:T(8,128)S(1)} %get-tuple-element.45), channel_id=1, source_target_pairs={{0,3},{1,0},{2,1},{3,2},{4,7},{5,4},{6,5},{7,6},{8,11},{9,8},{10,9... | collective-permute-start | bytes 196616 | tf_op jit(solution)/shard_map/ppermute | solution.py:535
  220.3 19.9 %collective-permute-start.23 = (f32[128,512]{1,0:T(8,128)S(1)}, f32[128,512]{1,0:T(8,128)S(1)}, u32[]{:S(2)}, u32[]{:S(2)}) collective-permute-start(f32[128,512]{1,0:T(8,128)S(1)} %constant_dynamic-update-slice_fusion), channel_id=1, source_target_pairs={{0,8},{4,12},{8,0},{12,4},{16,24},{20,28},{24,16},{28,20},{1,9},{5... | collective-permute-start | bytes 786440 | tf_op jit(solution)/shard_map/ppermute | solution.py:510
  240.3 8.1 %collective-permute-start.24 = (f32[256,512]{1,0:T(8,128)S(1)}, f32[256,512]{1,0:T(8,128)S(1)}, u32[]{:S(2)}, u32[]{:S(2)}) collective-permute-start(f32[256,512]{1,0:T(8,128)S(1)} %pad_maximum_fusion.3), channel_id=1, source_target_pairs={{0,16},{4,20},{8,24},{12,28},{16,0},{20,4},{24,8},{28,12},{1,17},{... | collective-permute-start | bytes 1572872 | tf_op jit(solution)/shard_map/ppermute | solution.py:510
  248.6 7.3 %collective-permute-start.25 = (f32[512,512]{1,0:T(8,128)S(1)}, f32[512,512]{1,0:T(8,128)}, u32[]{:S(2)}, u32[]{:S(2)}) collective-permute-start(f32[512,512]{1,0:T(8,128)S(1)} %pad_maximum_fusion.2), channel_id=1, source_target_pairs={{0,4},{4,0},{8,12},{12,8},{16,20},{20,16},{24,28},{28,24},{1,5},{5... | collective-permute-start | bytes 3145736 | tf_op jit(solution)/shard_map/ppermute | solution.py:510

commit v6 on v5

--- a/solution.py
+++ b/solution.py
@@ -39,14 +39,16 @@
     return jnp.dot(lhs, rhs, preferred_element_type=jnp.float32)
 
 
-def left_dot(mat_hi, mat_lo, val_hi, val_lo):
-    lhs = jnp.concatenate([mat_hi, mat_hi, mat_lo], axis=1)
-    return dot(lhs, jnp.concatenate([val_hi, val_lo, val_hi], axis=0))
+def left_dot(mats, val_hi, val_lo):
+    rows = mats.shape[0] // 2
+    both = dot(mats, val_hi)
+    return both[:rows] + (both[rows:] + dot(mats[:rows], val_lo))
 
 
 def right_dot(val_hi, val_lo, mat_hi, mat_lo):
-    lhs = jnp.concatenate([val_hi, val_lo, val_hi], axis=1)
-    return dot(lhs, jnp.concatenate([mat_hi, mat_hi, mat_lo], axis=0))
+    rows = val_hi.shape[0]
+    both = dot(jnp.concatenate([val_hi, val_lo], axis=0), mat_hi)
+    return both[:rows] + (both[rows:] + dot(val_hi, mat_lo))
 
 
 def butterfly(parts, sign):
@@ -285,7 +287,9 @@
             cols = pl.ds(start, half)
             for p in range(RADIX):
                 rows_f32[p, :, cols] = left_dot(
-                    mat_hi[p], mat_lo[p], left_hi[p, :, cols], left_lo[p, :, cols]
+                    jnp.concatenate([mat_hi[p], mat_lo[p]], axis=0),
+                    left_hi[p, :, cols],
+                    left_lo[p, :, cols],
                 )
 
         for p in range(RADIX):
@@ -307,17 +311,13 @@
                         right_lo[t, rows, pl.ds(offset, short)] = lo
 
         for t in range(RADIX):
-            for start in (0, half):
-                rows = pl.ds(start, half)
-                field = right_dot(
-                    right_hi[t, rows, :], right_lo[t, rows, :], mat_t_hi[t], mat_t_lo[t]
-                )
-                fre, fim = field[:, :short], field[:, short:]
-                measured = amps[slot, rows, pl.ds(t * short, short)]
-                factor = 1.0 - measured * lax.rsqrt(fre * fre + fim * fim + 1.0)
-                residual = jnp.concatenate([factor * fre, factor * fim], axis=1)
-                hi, lo = split(residual)
-                cols_f32[t, rows, :] = right_dot(hi, lo, mat_hi[t], mat_lo[t])
+            field = right_dot(right_hi[t], right_lo[t], mat_t_hi[t], mat_t_lo[t])
+            fre, fim = field[:, :short], field[:, short:]
+            measured = amps[slot, :, pl.ds(t * short, short)]
+            factor = 1.0 - measured * lax.rsqrt(fre * fre + fim * fim + 1.0)
+            residual = jnp.concatenate([factor * fre, factor * fim], axis=1)
+            hi, lo = split(residual)
+            cols_f32[t] = right_dot(hi, lo, mat_hi[t], mat_lo[t])
 
         for p in range(RADIX):
             for base in range(0, short, 16):
@@ -337,7 +337,9 @@
             cols = pl.ds(start, half)
             for p in range(RADIX):
                 rows_f32[p, :, cols] = left_dot(
-                    mat_t_hi[p], mat_t_lo[p], left_hi[p, :, cols], left_lo[p, :, cols]
+                    jnp.concatenate([mat_t_hi[p], mat_t_lo[p]], axis=0),
+                    left_hi[p, :, cols],
+                    left_lo[p, :, cols],
                 )
             for base in range(0, short, 8):
                 for col0 in range(start, start + half, short):
@@ -496,69 +498,16 @@
     return lax.ppermute(array, ("ty", "tx"), along(rule, sizes))
 
 
-def halve(value, bit):
-    rows = value.shape[0] // 2
-    mine = lax.axis_index("ty") // bit % 2
-    kept = lax.dynamic_slice_in_dim(value, mine * rows, rows, 0)
-    sent = lax.dynamic_slice_in_dim(value, (1 - mine) * rows, rows, 0)
-    received = lax.ppermute(sent, "ty", [(i, i ^ bit) for i in range(lax.axis_size("ty"))])
-    return kept + received
-
-
-def double(value, bit):
-    mine = lax.axis_index("ty") // bit % 2
-    other = lax.ppermute(value, "ty", [(i, i ^ bit) for i in range(lax.axis_size("ty"))])
-    first = jnp.where(mine == 0, value, other)
-    second = jnp.where(mine == 0, other, value)
-    return jnp.concatenate([first, second], axis=0)
-
-
-def ring_pairs(size, step):
-    return [(i, (i + step) % size) for i in range(size)]
-
-
-def scatter_tx(value):
-    size, own = lax.axis_size("tx"), lax.axis_index("tx")
-    rows = value.shape[0] // size
-    total = lax.dynamic_slice_in_dim(value, own * rows, rows, 0)
-    for step in range(1, size):
-        piece = lax.dynamic_slice_in_dim(value, (own + step) % size * rows, rows, 0)
-        total = total + lax.ppermute(piece, "tx", ring_pairs(size, step))
-    return total
-
-
-def gather_tx(value):
-    size, own = lax.axis_size("tx"), lax.axis_index("tx")
-    rows = value.shape[0]
-    parts = [value]
-    for step in range(1, size):
-        parts.append(lax.ppermute(value, "tx", ring_pairs(size, step)))
-    out = jnp.zeros((size * rows,) + value.shape[1:], value.dtype)
-    for step, part in enumerate(parts):
-        out = lax.dynamic_update_slice_in_dim(out, part, (own - step) % size * rows, 0)
-    return out
-
-
 def after(value, *arrivals):
     return lax.optimization_barrier((value, *arrivals))[0]
 
 
-def pupil_sum(part, first, middle, last):
-    n_ty, n_tx = lax.axis_size("ty"), lax.axis_size("tx")
-    bits = []
-    bit = n_ty // 2
-    while bit > 1:
-        bits.append(bit)
-        bit //= 2
-    part = after(part, *first)
-    for bit in bits[1:]:
-        part = halve(part, bit)
-    part = scatter_tx(part) * (1.0 / math.sqrt(n_ty * n_tx))
-    part = gather_tx(part)
-    for bit in reversed(bits[1:]):
-        part = double(part, bit)
-    part = double(after(part, *middle), bits[0])
-    return double(after(part, *last), 1)
+def pupil_sum(dpup):
+    axes = ("ty", "tx")
+    flat = dpup.reshape(-1, dpup.shape[-1])
+    part = lax.psum_scatter(flat, axes, scatter_dimension=0, tiled=True)
+    part = part * (1.0 / math.sqrt(lax.axis_size("ty") * lax.axis_size("tx")))
+    return lax.all_gather(part, axes, axis=0, tiled=True).reshape(dpup.shape)
 
 
 def body(spectrum, pupil, amplitudes, offsets, live):
@@ -603,8 +552,7 @@
     back_side = send(corner_b_g, lambda i, j: (i, j + 1) if i % 2 else None)
     back_a = send(corner_a_g, down)
     back_down = send(corner_b_g, lambda i, j: None if i % 2 else (i + 1, j))
-    halved = halve(halve(dpup.reshape(-1, side), 1), lax.axis_size("ty") // 2)
-    lower_c = send(after(lower_c_g, halved), down)
+    lower_c = send(lower_c_g, down)
     right_back = send(right_g + jnp.concatenate([back_a, back_down], axis=2), right)
     lower_ab = send(lower_ab_g.at[:, :, half:].add(back_side), down)
     spec_grad = jnp.concatenate(
@@ -614,10 +562,7 @@
         ],
         axis=2,
     )
-    pupil_grad = pupil_sum(
-        halved, (back_a, back_down, back_side), (lower_c,), (right_back, lower_ab)
-    )
-    return spec_grad, pupil_grad.reshape(pupil.shape)
+    return spec_grad, pupil_sum(dpup)
 
 
 def solution(mesh):

time: 260 us -> 345 us (1.33)
  waiting for transfers between devices: 141 us -> 237 us
  starting transfers between devices: 62.7 us -> 43 us
  between operations: 1.04 us -> 14.2 us
  other arithmetic: 19.1 us -> 9.84 us
    reduce_scatter x0 -> x1, waiting for transfers between devices: none -> 135 us  [pupil_sum(): part = lax.psum_scatter(flat, axes, scatter_dimension=0, tiled=True)]
    ppermute x12 -> x0, waiting for transfers between devices: 93.8 us -> none  [the longest x3 45.1 us: halve(): lax.ppermute(sent, 'ty', [(i, i ^ bit) for i in range(lax.axis_size('ty'))])]
    ppermute x14, waiting for transfers between devices: 47 us -> 101 us  [send(): return lax.ppermute(array, ('ty', 'tx'), along(rule, sizes))]
    ppermute x12 -> x0, starting transfers between devices: 14.8 us -> none  [the longest x3 5.93 us: gather_tx(): parts.append(lax.ppermute(value, 'tx', ring_pairs(size, step)))]
    ppermute x14, starting transfers between devices: 47.9 us -> 43 us  [send(): return lax.ppermute(array, ('ty', 'tx'), along(rule, sizes))]
    add x1, other arithmetic: 4.76 us -> 1.29 us  [body(): own_g[:, :, :side] + lower_ab + right_back]
  transfers between devices with their start and end apart: 26 -> 16, of which waited for: 13 -> 9; matrix products, arithmetic and copies ran while one was open for 8% -> 4% of each run, Pallas kernels for 3% -> 2%
where the time goes in v6:
time: 345 us; the launch traced here: 341 us
  waiting for transfers between devices  237 us (69%)
  starting transfers between devices  43 us (12%)
  Pallas kernels  28.5 us (8%)
  between operations  14.2 us (4%)
  other arithmetic  9.84 us (3%)
  local copies, waits for them, and re-layouts  8.46 us (2%)
    reduce_scatter x1, waiting for transfers between devices, pupil_sum(): part = lax.psum_scatter(flat, axes, scatter_dimension=0, tiled=True)  135 us
    ppermute x14, waiting for transfers between devices, send(): return lax.ppermute(array, ('ty', 'tx'), along(rule, sizes))  101 us
    ppermute x14, starting transfers between devices, send(): return lax.ppermute(array, ('ty', 'tx'), along(rule, sizes))  43 us
    pallas_call x1, Pallas kernels, slots_call(): pl.pallas_call(slots_kernel, out_shape=[jax.ShapeDtypeStruct(x.shape, f32...  20.3 us
    pallas_call x1, Pallas kernels, ordered(): pl.pallas_call(order_kernel, grid=(slots,), out_shape=jax.ShapeDtypeStruc...  8.24 us
  transfers between devices with their start and end apart: 16, of which 9 were waited for; matrix products, arithmetic and copies ran while one was open for 4% of the time, Pallas kernels for 2%

profile of v6, /device:TPU:1, one launch (start us, length us, event | category | flops | bytes accessed | tf_op | source)
XLA Modules:
  0.0 340.6 jit_solution(2944033095658296657)
XLA Ops:
  7.2 0.0 reduce-scatter.2.cloned.1.call-start
  7.2 2.7 fusion
  9.9 2.0 collective-permute-start.1
  11.9 1.3 collective-permute-start
  13.2 8.2 %ordered.1.amps_hbm = f32[3,512,512]{2,1,0:T(8,128)} custom-call(f32[3,512,512]{2,1,0:T(8,128)} %amps.1, bf16[512,512]{1,0:T(8,128)(2,1)} %constant.68.clone.perm_rows, bf16[512,512]{1,0:T(8,128)(2,1)} %constant.69.clone.perm_cols), custom_call_target="tpu_custom_call" | custom-call | flops 4831838208 | bytes 6291456 | tf_op jit(solution)/shard_map/ordered/pallas_call | solution.py:472
  21.4 0.0 copy-start.2
  21.4 0.0 copy-start.3
  21.4 6.1 %collective-permute-done.1.lower_b_hbm = f32[2,512,256]{2,1,0:T(8,128)} collective-permute-done((f32[2,512,256]{2,1,0:T(8,128)}, f32[2,512,256]{2,1,0:T(8,128)}, u32[]{:S(2)}, u32[]{:S(2)}) %collective-permute-start.1) | collective-permute-done | bytes 1048608 | tf_op jit(solution)/shard_map/ppermute | solution.py:498
  27.5 1.3 collective-permute-start.2
  28.8 1.3 collective-permute-start.6
  30.1 1.8 slice.51
  31.9 1.9 collective-permute-start.4
  33.8 1.9 collective-permute-start.3
  35.7 4.5 %collective-permute-done.right_a_hbm = f32[2,512,256]{2,1,0:T(8,128)} collective-permute-done((f32[2,512,256]{2,1,0:T(8,128)S(1)}, f32[2,512,256]{2,1,0:T(8,128)}, u32[]{:S(2)}, u32[]{:S(2)}) %collective-permute-start) | collective-permute-done | bytes 1048608 | tf_op jit(solution)/shard_map/ppermute | solution.py:498
  40.3 1.9 collective-permute-start.5
  42.2 19.9 %collective-permute-done.2.right_b_hbm = f32[2,512,256]{2,1,0:T(8,128)} collective-permute-done((f32[2,512,256]{2,1,0:T(8,128)}, f32[2,512,256]{2,1,0:T(8,128)}, u32[]{:S(2)}, u32[]{:S(2)}) %collective-permute-start.2) | collective-permute-done | bytes 1048608 | tf_op jit(solution)/shard_map/ppermute | solution.py:498
  62.1 11.2 %collective-permute-done.6.corner_side_hbm = f32[2,512,256]{2,1,0:T(8,128)} collective-permute-done((f32[2,512,256]{2,1,0:T(8,128)}, f32[2,512,256]{2,1,0:T(8,128)}, u32[]{:S(2)}, u32[]{:S(2)}) %collective-permute-start.6) | collective-permute-done | bytes 1048608 | tf_op jit(solution)/shard_map/ppermute | solution.py:498
  73.3 2.3 collective-permute-start.7
  75.6 0.0 copy-done.2
  75.6 0.1 copy.16
  75.7 0.1 copy.17
  75.8 0.0 copy-done.3
  75.8 0.1 copy.15
  75.9 0.1 pad_add_fusion
  76.0 0.6 concatenate.11.meta
  76.6 0.0 collective-permute-done.3.lower_a_hbm
  76.6 5.2 %collective-permute-done.5.corner_a_hbm = f32[2,512,256]{2,1,0:T(8,128)} collective-permute-done((f32[2,512,256]{2,1,0:T(8,128)}, f32[2,512,256]{2,1,0:T(8,128)}, u32[]{:S(2)}, u32[]{:S(2)}) %collective-permute-start.5) | collective-permute-done | bytes 1048608 | tf_op jit(solution)/shard_map/ppermute | solution.py:498
  81.8 0.0 collective-permute-done.4.lower_c_hbm
  81.8 0.0 collective-permute-done.7.corner_up_hbm
  81.8 20.3 %slots.1 = (f32[2,512,1024]{2,1,0:T(8,128)}, f32[2,512,512]{2,1,0:T(8,128)}, f32[2,512,512]{2,1,0:T(8,128)}, f32[2,512,512]{2,1,0:T(8,128)}, f32[2,512,256]{2,1,...) custom-call(s32[4,3]{1,0:T(4,128)} %concatenate.11.meta, f32[2,512,1024]{2,1,0:T(8,128)} %tile_hbm.1, ...), custom_call_target="tpu_custom_call" | custom-call | flops 9663676416 | bytes 41943040 | tf_op jit(solution)/shard_map/slots/pallas_call | solution.py:418
  102.1 0.0 reduce-scatter.2.cloned.1.call-update
  102.1 0.0 copy-start.1
  102.2 0.0 all-gather.2.cloned.1.call-start
  102.2 3.8 %collective-permute-start.8 = (f32[2,512,256]{2,1,0:T(8,128)}, f32[2,512,256]{2,1,0:T(8,128)S(1)}, u32[]{:S(2)}, u32[]{:S(2)}) collective-permute-start(f32[2,512,256]{2,1,0:T(8,128)} %get-tuple-element.31), channel_id=1, source_target_pairs={{4,5},{5,6},{6,7},{12,13},{13,14},{14,15},{20,21},{21,22},{22,23},... | collective-permute-start | bytes 3145736 | tf_op jit(solution)/shard_map/ppermute | solution.py:498
  106.0 1.3 collective-permute-start.11
  107.3 16.0 %collective-permute-start.10 = (f32[2,512,256]{2,1,0:T(8,128)}, f32[2,512,256]{2,1,0:T(8,128)}, u32[]{:S(2)}, u32[]{:S(2)}) collective-permute-start(f32[2,512,256]{2,1,0:T(8,128)} %get-tuple-element.33), channel_id=1, source_target_pairs={{0,4},{1,5},{2,6},{3,7},{4,8},{5,9},{6,10},{7,11},{8,12},{9,13},{1... | collective-permute-start | bytes 3145736 | tf_op jit(solution)/shard_map/ppermute | solution.py:498
  123.3 135.4 %reduce-scatter.2.cloned.1.call-done = f32[32,512]{1,0:T(8,128)} async-done(((f32[1024,512]{1,0:T(8,128)}), f32[32,512]{1,0:T(8,128)}) %reduce-scatter.2.cloned.1.call-update) | async-done | bytes 65552 | tf_op jit(solution)/shard_map/reduce_scatter | solution.py:508
  258.7 1.5 broadcast_multiply_fusion
  260.2 0.0 all-gather.2.cloned.1.call-update
  260.2 1.9 collective-permute-start.13
  262.1 0.0 collective-permute-done.8
  262.2 2.4 add_dynamic-update-slice_fusion
  264.6 1.9 collective-permute-start.9
  266.5 0.0 collective-permute-done.10
  266.5 0.0 collective-permute-done.11
  266.5 0.0 copy-done.1
  266.5 0.0 copy-start
  266.5 2.1 maximum_add_fusion
  268.7 4.2 %collective-permute-start.12 = (f32[2,512,512]{2,1,0:T(8,128)S(1)}, f32[2,512,512]{2,1,0:T(8,128)S(1)}, u32[]{:S(2)}, u32[]{:S(2)}) collective-permute-start(f32[2,512,512]{2,1,0:T(8,128)S(1)} %maximum_add_fusion), channel_id=1, source_target_pairs={{0,1},{1,2},{2,3},{4,5},{5,6},{6,7},{8,9},{9,10},{10,11},{12,13},{... | collective-permute-start | bytes 6291464 | tf_op jit(solution)/shard_map/ppermute | solution.py:498
  272.9 13.0 %collective-permute-done.13 = f32[2,512,512]{2,1,0:T(8,128)S(1)} collective-permute-done((f32[2,512,512]{2,1,0:T(8,128)}, f32[2,512,512]{2,1,0:T(8,128)S(1)}, u32[]{:S(2)}, u32[]{:S(2)}) %collective-permute-start.13) | collective-permute-done | bytes 2097184 | tf_op jit(solution)/shard_map/ppermute | solution.py:498
  285.9 28.0 %collective-permute-done.9 = f32[2,512,512]{2,1,0:T(8,128)S(1)} collective-permute-done((f32[2,512,512]{2,1,0:T(8,128)}, f32[2,512,512]{2,1,0:T(8,128)S(1)}, u32[]{:S(2)}, u32[]{:S(2)}) %collective-permute-start.9) | collective-permute-done | bytes 2097184 | tf_op jit(solution)/shard_map/ppermute | solution.py:498
  313.9 13.0 %collective-permute-done.12 = f32[2,512,512]{2,1,0:T(8,128)S(1)} collective-permute-done((f32[2,512,512]{2,1,0:T(8,128)S(1)}, f32[2,512,512]{2,1,0:T(8,128)S(1)}, u32[]{:S(2)}, u32[]{:S(2)}) %collective-permute-start.12) | collective-permute-done | bytes 2097184 | tf_op jit(solution)/shard_map/ppermute | solution.py:498
  326.9 0.0 copy-done
  326.9 1.3 add_add_fusion
  328.2 2.5 pad_maximum_fusion
  330.7 0.0 all-gather.2.cloned.1.call-done
  330.7 3.1 copy.20
  (2 shorter events, 0.0 us)
Async XLA Ops:
  7.2 251.6 %reduce-scatter.2.cloned.1.call-start = ((), (), s32[]{:S(2)}) async-start(), calls=%async_computation.1 | async-start | bytes 2162688 | tf_op jit(solution)/shard_map/reduce_scatter | solution.py:508
  9.9 17.6 %collective-permute-start.1 = (f32[2,512,256]{2,1,0:T(8,128)}, f32[2,512,256]{2,1,0:T(8,128)}, u32[]{:S(2)}, u32[]{:S(2)}) collective-permute-start(f32[2,512,256]{2,1,0:T(8,128)} %get-tuple-element.25), channel_id=1, source_target_pairs={{4,0},{5,1},{6,2},{7,3},{8,4},{9,5},{10,6},{11,7},{12,8},{13,9},{1... | collective-permute-start | bytes 3145736 | tf_op jit(solution)/shard_map/ppermute | solution.py:498
  11.9 28.4 %collective-permute-start = (f32[2,512,256]{2,1,0:T(8,128)S(1)}, f32[2,512,256]{2,1,0:T(8,128)}, u32[]{:S(2)}, u32[]{:S(2)}) collective-permute-start(f32[2,512,256]{2,1,0:T(8,128)S(1)} %get-tuple-element.39), channel_id=1, source_target_pairs={{1,0},{2,1},{3,2},{5,4},{6,5},{7,6},{9,8},{10,9},{11,10},{13,12},{... | collective-permute-start | bytes 3145736 | tf_op jit(solution)/shard_map/ppermute | solution.py:498
  21.4 54.2 %copy-start.2 = (s32[3,2]{0,1:T(2,128)S(1)}, s32[3,2]{0,1:T(2,128)}, u32[]{:S(2)}) copy-start(s32[3,2]{0,1:T(2,128)} %param.16) | copy-start | bytes 76
  21.4 54.4 %copy-start.3 = (s32[3]{0:T(128)S(1)}, s32[3]{0:T(128)}, u32[]{:S(2)}) copy-start(s32[3]{0:T(128)} %param.17) | copy-start | bytes 40
  27.5 34.6 %collective-permute-start.2 = (f32[2,512,256]{2,1,0:T(8,128)}, f32[2,512,256]{2,1,0:T(8,128)}, u32[]{:S(2)}, u32[]{:S(2)}) collective-permute-start(f32[2,512,256]{2,1,0:T(8,128)} %get-tuple-element.25), channel_id=1, source_target_pairs={{1,0},{2,1},{3,2},{5,4},{6,5},{7,6},{9,8},{10,9},{11,10},{13,12},{... | collective-permute-start | bytes 3145736 | tf_op jit(solution)/shard_map/ppermute | solution.py:498
  28.8 44.5 %collective-permute-start.6 = (f32[2,512,256]{2,1,0:T(8,128)}, f32[2,512,256]{2,1,0:T(8,128)}, u32[]{:S(2)}, u32[]{:S(2)}) collective-permute-start(f32[2,512,256]{2,1,0:T(8,128)} %collective-permute-done.1.lower_b_hbm), channel_id=1, source_target_pairs={{5,4},{6,5},{7,6},{13,12},{14,13},{15,14},{21,20},{22,21},{23,22},... | collective-permute-start | bytes 3145736 | tf_op jit(solution)/shard_map/ppermute | solution.py:498
  31.9 49.9 %collective-permute-start.4 = (f32[2,512,512]{2,1,0:T(8,128)S(1)}, f32[2,512,512]{2,1,0:T(8,128)}, u32[]{:S(2)}, u32[]{:S(2)}) collective-permute-start(f32[2,512,512]{2,1,0:T(8,128)S(1)} %slice.51), channel_id=1, source_target_pairs={{4,0},{5,1},{6,2},{7,3},{8,4},{9,5},{10,6},{11,7},{12,8},{13,9},{1... | collective-permute-start | bytes 6291464 | tf_op jit(solution)/shard_map/ppermute | solution.py:498
  33.8 42.8 %collective-permute-start.3 = (f32[2,512,256]{2,1,0:T(8,128)S(1)}, f32[2,512,256]{2,1,0:T(8,128)}, u32[]{:S(2)}, u32[]{:S(2)}) collective-permute-start(f32[2,512,256]{2,1,0:T(8,128)S(1)} %get-tuple-element.39), channel_id=1, source_target_pairs={{4,0},{5,1},{6,2},{7,3},{8,4},{9,5},{10,6},{11,7},{12,8},{13,9},{1... | collective-permute-start | bytes 3145736 | tf_op jit(solution)/shard_map/ppermute | solution.py:498
  40.3 41.5 %collective-permute-start.5 = (f32[2,512,256]{2,1,0:T(8,128)}, f32[2,512,256]{2,1,0:T(8,128)}, u32[]{:S(2)}, u32[]{:S(2)}) collective-permute-start(f32[2,512,256]{2,1,0:T(8,128)} %collective-permute-done.right_a_hbm), channel_id=1, source_target_pairs={{4,0},{5,1},{6,2},{7,3},{8,4},{9,5},{10,6},{11,7},{12,8},{13,9},{1... | collective-permute-start | bytes 3145736 | tf_op jit(solution)/shard_map/ppermute | solution.py:498
  73.3 8.5 %collective-permute-start.7 = (f32[2,512,256]{2,1,0:T(8,128)}, f32[2,512,256]{2,1,0:T(8,128)}, u32[]{:S(2)}, u32[]{:S(2)}) collective-permute-start(f32[2,512,256]{2,1,0:T(8,128)} %collective-permute-done.2.right_b_hbm), channel_id=1, source_target_pairs={{4,0},{5,1},{6,2},{7,3},{12,8},{13,9},{14,10},{15,11},{20,16},{21,... | collective-permute-start | bytes 3145736 | tf_op jit(solution)/shard_map/ppermute | solution.py:498
  102.1 164.4 %copy-start.1 = (f32[2,512,512]{2,1,0:T(8,128)S(1)}, f32[2,512,512]{2,1,0:T(8,128)}, u32[]{:S(2)}) copy-start(f32[2,512,512]{2,1,0:T(8,128)} %get-tuple-element.32) | copy-start | bytes 6291460
  102.2 228.5 %all-gather.2.cloned.1.call-start = ((), (), s32[]{:S(2)}) async-start(), calls=%async_computation.2 | async-start | bytes 2162688 | tf_op jit(solution)/shard_map/all_gather | solution.py:510
  102.2 159.9 %collective-permute-start.8 = (f32[2,512,256]{2,1,0:T(8,128)}, f32[2,512,256]{2,1,0:T(8,128)S(1)}, u32[]{:S(2)}, u32[]{:S(2)}) collective-permute-start(f32[2,512,256]{2,1,0:T(8,128)} %get-tuple-element.31), channel_id=1, source_target_pairs={{4,5},{5,6},{6,7},{12,13},{13,14},{14,15},{20,21},{21,22},{22,23},... | collective-permute-start | bytes 3145736 | tf_op jit(solution)/shard_map/ppermute | solution.py:498
  106.0 160.5 %collective-permute-start.11 = (f32[2,512,256]{2,1,0:T(8,128)}, f32[2,512,256]{2,1,0:T(8,128)}, u32[]{:S(2)}, u32[]{:S(2)}) collective-permute-start(f32[2,512,256]{2,1,0:T(8,128)} %get-tuple-element.31), channel_id=1, source_target_pairs={{0,4},{1,5},{2,6},{3,7},{8,12},{9,13},{10,14},{11,15},{16,20},{17,... | collective-permute-start | bytes 3145736 | tf_op jit(solution)/shard_map/ppermute | solution.py:498
  107.3 159.2 %collective-permute-start.10 = (f32[2,512,256]{2,1,0:T(8,128)}, f32[2,512,256]{2,1,0:T(8,128)}, u32[]{:S(2)}, u32[]{:S(2)}) collective-permute-start(f32[2,512,256]{2,1,0:T(8,128)} %get-tuple-element.33), channel_id=1, source_target_pairs={{0,4},{1,5},{2,6},{3,7},{4,8},{5,9},{6,10},{7,11},{8,12},{9,13},{1... | collective-permute-start | bytes 3145736 | tf_op jit(solution)/shard_map/ppermute | solution.py:498
  260.2 25.7 %collective-permute-start.13 = (f32[2,512,512]{2,1,0:T(8,128)}, f32[2,512,512]{2,1,0:T(8,128)S(1)}, u32[]{:S(2)}, u32[]{:S(2)}) collective-permute-start(f32[2,512,512]{2,1,0:T(8,128)} %get-tuple-element.34), channel_id=1, source_target_pairs={{0,4},{1,5},{2,6},{3,7},{4,8},{5,9},{6,10},{7,11},{8,12},{9,13},{1... | collective-permute-start | bytes 6291464 | tf_op jit(solution)/shard_map/ppermute | solution.py:498
  264.6 49.3 %collective-permute-start.9 = (f32[2,512,512]{2,1,0:T(8,128)}, f32[2,512,512]{2,1,0:T(8,128)S(1)}, u32[]{:S(2)}, u32[]{:S(2)}) collective-permute-start(f32[2,512,512]{2,1,0:T(8,128)} %add_dynamic-update-slice_fusion), channel_id=1, source_target_pairs={{0,4},{1,5},{2,6},{3,7},{4,8},{5,9},{6,10},{7,11},{8,12},{9,13},{1... | collective-permute-start | bytes 6291464 | tf_op jit(solution)/shard_map/ppermute | solution.py:498
  266.5 60.4 %copy-start = (f32[2,512,1024]{2,1,0:T(8,128)S(1)}, f32[2,512,1024]{2,1,0:T(8,128)}, u32[]{:S(2)}) copy-start(f32[2,512,1024]{2,1,0:T(8,128)} %get-tuple-element.29) | copy-start | bytes 12582916
  268.7 58.3 %collective-permute-start.12 = (f32[2,512,512]{2,1,0:T(8,128)S(1)}, f32[2,512,512]{2,1,0:T(8,128)S(1)}, u32[]{:S(2)}, u32[]{:S(2)}) collective-permute-start(f32[2,512,512]{2,1,0:T(8,128)S(1)} %maximum_add_fusion), channel_id=1, source_target_pairs={{0,1},{1,2},{2,3},{4,5},{5,6},{6,7},{8,9},{9,10},{10,11},{12,13},{... | collective-permute-start | bytes 6291464 | tf_op jit(solution)/shard_map/ppermute | solution.py:498
Sparse Core Ops, SparseCore 0:
  102.3 156.4 reduce-scatter.1
  262.1 61.7 all-gather.1

commit v7 on v5

--- a/solution.py
+++ b/solution.py
@@ -70,35 +70,48 @@
     return [tile[:, i : i + 128] for i in range(0, tile.shape[1], 128)]
 
 
-def pull_lanes(tile, shift):
-    rolled = [pltpu.roll(part, (128 - shift) % 128, 1) for part in lane_tiles(tile)]
-    keep = lane_index() < 128 - shift
-    return [jnp.where(keep, a, b) for a, b in zip(rolled, rolled[1:])]
-
-
-def pull_rows(tiles, shift):
-    rolled = [[pltpu.roll(part, (8 - shift) % 8, 0) for part in tile] for tile in tiles]
-    keep = row_index() < 8 - shift
+def rolled(tiles, amount, axis):
+    return [[pltpu.roll(part, amount, axis) for part in tile] for tile in tiles]
+
+
+def shift_on(tiles, row_shift, col_shift):
+    keep = lane_index() >= col_shift
+    tiles = rolled([lane_tiles(tile) for tile in tiles], col_shift, 1)
+    tiles = [[jnp.where(keep, x, y) for x, y in zip(t, t[-1:] + t[:-1])] for t in tiles]
+    keep = row_index() >= row_shift
+    tiles = rolled(tiles, row_shift, 0)
+    return [
+        jnp.concatenate([jnp.where(keep, y, x) for x, y in zip(a, b)], axis=1)
+        for a, b in zip(tiles, tiles[1:])
+    ]
+
+
+def shift_back(tiles, row_shift, col_shift):
+    keep = lane_index() < 128 - col_shift
+    tiles = rolled([lane_tiles(tile) for tile in tiles], (128 - col_shift) % 128, 1)
+    tiles = [[jnp.where(keep, x, y) for x, y in zip(t, t[1:] + t[:1])] for t in tiles]
+    keep = row_index() < 8 - row_shift
+    tiles = rolled(tiles, (8 - row_shift) % 8, 0)
     return [
         jnp.concatenate([jnp.where(keep, x, y) for x, y in zip(a, b)], axis=1)
-        for a, b in zip(rolled, rolled[1:])
+        for a, b in zip(tiles, tiles[1:])
     ]
 
 
-def push_lanes(tile, shift):
-    rolled = [pltpu.roll(part, shift, 1) for part in lane_tiles(tile)]
-    zero = jnp.zeros((8, 128), jnp.float32)
-    keep = lane_index() >= shift
-    return [jnp.where(keep, b, a) for a, b in zip([zero] + rolled, rolled + [zero])]
-
-
-def push_rows(tiles, shift):
-    rolled = [[pltpu.roll(part, shift, 0) for part in tile] for tile in tiles]
-    keep = row_index() >= shift
-    return [
-        jnp.concatenate([jnp.where(keep, y, x) for x, y in zip(a, b)], axis=1)
-        for a, b in zip(rolled, rolled[1:])
-    ]
+def wrap_lanes(block, col_shift):
+    rows = block.shape[0]
+    keep = lax.broadcasted_iota(jnp.int32, (rows, 128), 1) >= col_shift
+    first = jnp.where(keep, block[:, :128], block[:, -128:])
+    return jnp.concatenate([first, block[:, 128:-128]], axis=1)
+
+
+def unwrap_lanes(block, col_shift):
+    rows = block.shape[0]
+    keep = lax.broadcasted_iota(jnp.int32, (rows, 128), 1) >= col_shift
+    zero = jnp.zeros((rows, 128), jnp.float32)
+    first = jnp.where(keep, block[:, :128], zero)
+    last = jnp.where(keep, zero, block[:, :128])
+    return jnp.concatenate([first, block[:, 128:], last], axis=1)
 
 
 def slots_kernel(
@@ -231,9 +244,6 @@
         rows = pl.ds(pl.multiple_of(step * zero_rows, zero_rows), zero_rows)
         dpup[:, rows, :] = jnp.zeros((2, zero_rows, side), jnp.float32)
 
-    for start in (0, side + 8):
-        dwin[:, pl.ds(start, 8), :] = jnp.zeros((2, 8, side), jnp.float32)
-
     for load in loads:
         load.wait()
 
@@ -252,14 +262,17 @@
         @pl.loop(0, side // 32, unroll=2)
         def _(step):
             base = pl.multiple_of(step * 32, 32)
+            rows = pl.ds(pl.multiple_of(row_base + base, 8), 32)
             for plane in range(2):
-                tiles = []
-                for i in range(5):
-                    start = pl.multiple_of(row_base + base + 8 * i, 8)
-                    tiles.append(region[plane, pl.ds(start, 8), pl.ds(col_base, wide)])
-                tiles = [pull_lanes(tile, col_shift) for tile in tiles]
-                for i, tile in enumerate(pull_rows(tiles, row_shift)):
-                    win[plane, pl.ds(base + 8 * i, 8), :] = tile
+                block = region[plane, rows, pl.ds(col_base, wide)]
+                win[plane, pl.ds(base, 32), :] = wrap_lanes(block, col_shift)
+
+        first_keep = lax.broadcasted_iota(jnp.int32, (8, side), 0) >= row_shift
+        last_rows = pl.ds(pl.multiple_of(row_base + side, 8), 8)
+        for plane in range(2):
+            block = region[plane, last_rows, pl.ds(col_base, wide)]
+            block = wrap_lanes(block, col_shift)
+            win[plane, :8, :] = jnp.where(first_keep, win[plane, :8, :], block)
 
         @pl.when(slot == 0)
         def _():
@@ -274,7 +287,7 @@
                     for q in range(RADIX):
                         rows = pl.ds(base + q * short, 16)
                         wr, wi = win[0, rows, cols], win[1, rows, cols]
-                        pr, pi = pupil[0, rows, cols], pupil[1, rows, cols]
+                        pr, pi = pupil[slot, 0, rows, cols], pupil[slot, 1, rows, cols]
                         values.append((wr * pr - wi * pi, wr * pi + wi * pr))
                     for p, (re, im) in enumerate(butterfly(values, 1)):
                         for offset, value in ((0, re), (short, im)):
@@ -351,26 +364,39 @@
                     ]
                     for q, (re, im) in enumerate(butterfly(values, -1)):
                         rows = pl.ds(base + q * short, 8)
-                        pr, pi = pupil[0, rows, cols], pupil[1, rows, cols]
-                        padded = pl.ds(base + q * short + 8, 8)
-                        dwin[0, padded, cols] = pr * re + pi * im
-                        dwin[1, padded, cols] = pr * im - pi * re
+                        pr, pi = pupil[slot, 0, rows, cols], pupil[slot, 1, rows, cols]
+                        dwin[0, rows, cols] = pr * re + pi * im
+                        dwin[1, rows, cols] = pr * im - pi * re
                         wr, wi = win[0, rows, cols], win[1, rows, cols]
-                        dpup[0, rows, cols] += wr * re + wi * im
-                        dpup[1, rows, cols] += wr * im - wi * re
+                        win[0, rows, cols] = wr * re + wi * im
+                        win[1, rows, cols] = wr * im - wi * re
+
+        @pl.loop(0, side // 32, unroll=2)
+        def _(step):
+            base = pl.multiple_of(step * 32, 32)
+            after = pl.multiple_of((base + 32) % side, 8)
+            for plane in range(2):
+                tiles = [win[plane, pl.ds(base + 8 * i, 8), :] for i in range(4)]
+                tiles.append(win[plane, pl.ds(after, 8), :])
+                for i, tile in enumerate(shift_back(tiles, row_shift, col_shift)):
+                    dpup[plane, pl.ds(base + 8 * i, 8), :] += tile
 
         last = slot == count - 1
         pl.when(last)(dpup_store.start)
 
+        zero = jnp.zeros((8, side), jnp.float32)
+        for plane in range(2):
+            block = dwin[plane, :8, :]
+            dwin[plane, :8, :] = jnp.where(first_keep, block, zero)
+            dwin[plane, pl.ds(side, 8), :] = jnp.where(first_keep, zero, block)
+
         def place(step):
             base = pl.multiple_of(step * 40, 8)
+            rows = pl.ds(pl.multiple_of(row_base + base, 8), 40)
             for plane in range(2):
-                tiles = [dwin[plane, pl.ds(base + 8 * i, 8), :] for i in range(6)]
-                tiles = [push_lanes(tile, col_shift) for tile in tiles]
-                for i, tile in enumerate(push_rows(tiles, row_shift)):
-                    start = pl.multiple_of(row_base + base + 8 * i, 8)
-                    target = (plane, pl.ds(start, 8), pl.ds(col_base, wide))
-                    grads[target] = grads[target] + tile
+                block = unwrap_lanes(dwin[plane, pl.ds(base, 40), :], col_shift)
+                target = (plane, rows, pl.ds(col_base, wide))
+                grads[target] = grads[target] + block
 
         steps = (side + 8) // 40
         above = (tile_rows - row_base) // 40
@@ -398,8 +424,8 @@
         store.wait()
 
 
-def slots_call(meta, tile, parts, amps, pupil):
-    side = pupil.shape[-1]
+def slots_call(meta, tile, parts, amps, pupils):
+    side = pupils.shape[-1]
     short = side // RADIX
     slots = amps.shape[0]
     tile_rows, tile_cols = tile.shape[1:]
@@ -411,7 +437,7 @@
     _, _, _, _, lower_c, corner_a, corner_b, _ = parts
     right = jax.ShapeDtypeStruct((2, tile_rows, side), f32)
     lower_ab = jax.ShapeDtypeStruct((2, side, side), f32)
-    outs = (tile, right, lower_ab, lower_c, corner_a, corner_b, pupil)
+    outs = (tile, right, lower_ab, lower_c, corner_a, corner_b, jax.ShapeDtypeStruct(pupils.shape[1:], f32))
     table = pltpu.VMEM(high.shape, bf16)
     return pl.pallas_call(
         slots_kernel,
@@ -428,10 +454,10 @@
             pltpu.VMEM((RADIX, side, 2 * short), bf16),
             pltpu.VMEM((RADIX, side, 2 * short), f32),
             pltpu.VMEM((RADIX, 2 * short, side), f32),
-            pltpu.VMEM((2, side + 16, side), f32),
+            pltpu.VMEM((2, side + 8, side), f32),
             pltpu.VMEM((2, side, side), f32),
             pltpu.VMEM(amps.shape, f32),
-            pltpu.VMEM(pupil.shape, f32),
+            pltpu.VMEM(pupils.shape, f32),
             table,
             table,
             table,
@@ -446,7 +472,7 @@
             transcendentals=slots * side * side,
         ),
         name="slots",
-    )(meta, tile, *parts, amps, pupil, *tables)
+    )(meta, tile, *parts, amps, pupils, *tables)
 
 
 def exact_parts(value):
@@ -455,12 +481,27 @@
     return (hi, *split(rest))
 
 
-def order_kernel(amps, perm_rows, perm_cols, out):
+def prepare_kernel(meta, amps, pupil, perm_rows, perm_cols, amps_out, pupil_out):
     value = sum(dot(part, perm_cols[...]) for part in exact_parts(amps[0]))
-    out[0] = sum(dot(perm_rows[...], part) for part in exact_parts(value))
-
-
-def ordered(amps):
+    amps_out[0] = sum(dot(perm_rows[...], part) for part in exact_parts(value))
+
+    slot = pl.program_id(0)
+    row_shift = meta[slot, 0] % 8
+    col_shift = meta[slot, 1] % 128
+    side = pupil.shape[-1]
+
+    @pl.loop(0, side // 32, unroll=2)
+    def _(step):
+        base = pl.multiple_of(step * 32, 32)
+        before = pl.multiple_of((base + side - 8) % side, 8)
+        for plane in range(2):
+            tiles = [pupil[plane, pl.ds(before, 8), :]]
+            tiles += [pupil[plane, pl.ds(base + 8 * i, 8), :] for i in range(4)]
+            for i, tile in enumerate(shift_on(tiles, row_shift, col_shift)):
+                pupil_out[0, plane, pl.ds(base + 8 * i, 8), :] = tile
+
+
+def prepare(meta, amps, pupil):
     slots, side, _ = amps.shape
     index = np.arange(side)
     perm = np.zeros((side, side), ml_dtypes.bfloat16)
@@ -468,16 +509,26 @@
     block = pl.BlockSpec((1, side, side), lambda s: (s, 0, 0))
     table = pl.BlockSpec((side, side), lambda s: (0, 0))
     return pl.pallas_call(
-        order_kernel,
+        prepare_kernel,
         grid=(slots,),
-        out_shape=jax.ShapeDtypeStruct(amps.shape, amps.dtype),
-        in_specs=[block, table, table],
-        out_specs=block,
+        out_shape=[
+            jax.ShapeDtypeStruct(amps.shape, amps.dtype),
+            jax.ShapeDtypeStruct((slots, 2, side, side), pupil.dtype),
+        ],
+        in_specs=[
+            pl.BlockSpec(memory_space=pltpu.SMEM),
+            block,
+            pl.BlockSpec((2, side, side), lambda s: (0, 0, 0)),
+            table,
+            table,
+        ],
+        out_specs=[block, pl.BlockSpec((1, 2, side, side), lambda s: (s, 0, 0, 0))],
+        compiler_params=pltpu.CompilerParams(vmem_limit_bytes=32 * 1024 * 1024),
         cost_estimate=pl.CostEstimate(
-            flops=slots * 12 * side**3, bytes_accessed=8 * slots * side**2, transcendentals=0
+            flops=slots * 12 * side**3, bytes_accessed=24 * slots * side**2, transcendentals=0
         ),
-        name="ordered",
-    )(amps, jnp.asarray(perm.T), jnp.asarray(perm))
+        name="prepare",
+    )(meta, amps, pupil, jnp.asarray(perm.T), jnp.asarray(perm))
 
 
 def along(axis_pairs, members):
@@ -513,52 +564,20 @@
     return jnp.concatenate([first, second], axis=0)
 
 
-def ring_pairs(size, step):
-    return [(i, (i + step) % size) for i in range(size)]
-
-
-def scatter_tx(value):
-    size, own = lax.axis_size("tx"), lax.axis_index("tx")
-    rows = value.shape[0] // size
+def scatter(value, axis, inner):
+    size, own = lax.axis_size(axis), lax.axis_index(axis) // inner
+    members = size // inner
+    rows = value.shape[0] // members
     total = lax.dynamic_slice_in_dim(value, own * rows, rows, 0)
-    for step in range(1, size):
-        piece = lax.dynamic_slice_in_dim(value, (own + step) % size * rows, rows, 0)
-        total = total + lax.ppermute(piece, "tx", ring_pairs(size, step))
+    for step in range(1, members):
+        pairs = [(i, (i + step * inner) % size) for i in range(size)]
+        piece = lax.dynamic_slice_in_dim(value, (own + step) % members * rows, rows, 0)
+        total = total + lax.ppermute(piece, axis, pairs)
     return total
-
-
-def gather_tx(value):
-    size, own = lax.axis_size("tx"), lax.axis_index("tx")
-    rows = value.shape[0]
-    parts = [value]
-    for step in range(1, size):
-        parts.append(lax.ppermute(value, "tx", ring_pairs(size, step)))
-    out = jnp.zeros((size * rows,) + value.shape[1:], value.dtype)
-    for step, part in enumerate(parts):
-        out = lax.dynamic_update_slice_in_dim(out, part, (own - step) % size * rows, 0)
-    return out
 
 
 def after(value, *arrivals):
     return lax.optimization_barrier((value, *arrivals))[0]
-
-
-def pupil_sum(part, first, middle, last):
-    n_ty, n_tx = lax.axis_size("ty"), lax.axis_size("tx")
-    bits = []
-    bit = n_ty // 2
-    while bit > 1:
-        bits.append(bit)
-        bit //= 2
-    part = after(part, *first)
-    for bit in bits[1:]:
-        part = halve(part, bit)
-    part = scatter_tx(part) * (1.0 / math.sqrt(n_ty * n_tx))
-    part = gather_tx(part)
-    for bit in reversed(bits[1:]):
-        part = double(part, bit)
-    part = double(after(part, *middle), bits[0])
-    return double(after(part, *last), 1)
 
 
 def body(spectrum, pupil, amplitudes, offsets, live):
@@ -582,7 +601,7 @@
     right_b = send(after(spectrum[:, :, half:side], lower_b), left)
     lower_a = send(spectrum[:, :side, :half], up)
     lower_c = send(spectrum[:, :side, side:], up)
-    amps = ordered(amplitudes)
+    amps, pupils = prepare(meta, amplitudes, pupil)
     lower_b, amps = lax.optimization_barrier((lower_b, amps))
     corner_side = send(lower_b, lambda i, j: (i, j - 1) if i % 2 else None)
     corner_a = send(right_a[:, :side], up)
@@ -591,7 +610,7 @@
 
     parts = (right_a, right_b, lower_a, lower_b, lower_c, corner_a, corner_up, corner_side)
     own_g, right_g, lower_ab_g, lower_c_g, corner_a_g, corner_b_g, dpup = slots_call(
-        meta, spectrum, parts, amps, pupil
+        meta, spectrum, parts, amps, pupils
     )
 
     def down(i, j):
@@ -603,10 +622,20 @@
     back_side = send(corner_b_g, lambda i, j: (i, j + 1) if i % 2 else None)
     back_a = send(corner_a_g, down)
     back_down = send(corner_b_g, lambda i, j: None if i % 2 else (i + 1, j))
-    halved = halve(halve(dpup.reshape(-1, side), 1), lax.axis_size("ty") // 2)
-    lower_c = send(after(lower_c_g, halved), down)
-    right_back = send(right_g + jnp.concatenate([back_a, back_down], axis=2), right)
-    lower_ab = send(lower_ab_g.at[:, :, half:].add(back_side), down)
+    n_ty, n_tx = lax.axis_size("ty"), lax.axis_size("tx")
+    over_cores = halve(dpup.reshape(-1, side), 1)
+    over_ty = scatter(over_cores, "ty", 2)
+    lower_c = send(after(lower_c_g, over_ty), down)
+    over_ty = after(over_ty, back_a, back_down, back_side)
+    part = scatter(over_ty, "tx", 1) * (1.0 / math.sqrt(n_ty * n_tx))
+    right_total = right_g + jnp.concatenate([back_a, back_down], axis=2)
+    right_back = send(after(right_total, part), right)
+    lower_ab = send(lower_ab_g.at[:, :, half:].add(after(back_side, part)), down)
+    groups = [
+        [(2 * k + core) * n_tx + j for k in range(n_ty // 2) for j in range(n_tx)]
+        for core in range(2)
+    ]
+    part = lax.all_gather(part, ("ty", "tx"), axis_index_groups=groups, axis=0, tiled=True)
     spec_grad = jnp.concatenate(
         [
             own_g[:, :, :side] + lower_ab + right_back,
@@ -614,10 +643,7 @@
         ],
         axis=2,
     )
-    pupil_grad = pupil_sum(
-        halved, (back_a, back_down, back_side), (lower_c,), (right_back, lower_ab)
-    )
-    return spec_grad, pupil_grad.reshape(pupil.shape)
+    return spec_grad, double(part, 1).reshape(pupil.shape)
 
 
 def solution(mesh):

time: 260 us -> 255 us (0.981)
  waiting for transfers between devices: 141 us -> 102 us
  between operations: 1.04 us -> 14.5 us
  starting transfers between devices: 62.7 us -> 74.7 us
  local copies, waits for them, and re-layouts: 7.76 us -> 13 us
  Pallas kernels: 27.5 us -> 31.3 us
    ppermute x3 -> x1, waiting for transfers between devices: 45.1 us -> 0.01 us  [halve(): lax.ppermute(sent, 'ty', [(i, i ^ bit) for i in range(lax.axis_size('ty'))])]
    all_gather x0 -> x1, waiting for transfers between devices: none -> 44.4 us  [body(): lax.all_gather(part, ('ty', 'tx'), axis_index_groups=groups, axis=0, tile...]
    ppermute x3 -> x1, waiting for transfers between devices: 27.8 us -> 0.01 us  [double(): lax.ppermute(value, 'ty', [(i, i ^ bit) for i in range(lax.axis_size('ty'...]
    ppermute x6, starting transfers between devices: 10.1 us -> 30.1 us  [scatter(): total = total + lax.ppermute(piece, axis, pairs)]
    ppermute x6, waiting for transfers between devices: 20.9 us -> 8.49 us  [scatter(): total = total + lax.ppermute(piece, axis, pairs)]
    unnamed x10 -> x32, local copies, waits for them, and re-layouts: 0.21 us -> 7.28 us
    ppermute x14, starting transfers between devices: 47.9 us -> 43.1 us  [send(): return lax.ppermute(array, ('ty', 'tx'), along(rule, sizes))]
    ppermute x3 -> x1, starting transfers between devices: 4.42 us -> 0.07 us  [halve(): lax.ppermute(sent, 'ty', [(i, i ^ bit) for i in range(lax.axis_size('ty'))])]
  transfers between devices with their start and end apart: 26 -> 23, of which waited for: 13 -> 9; matrix products, arithmetic and copies ran while one was open for 8% -> 7% of each run, Pallas kernels for 3% -> 4%
where the time goes in v7:
time: 255 us; the launch traced here: 254 us
  waiting for transfers between devices  102 us (40%)
  starting transfers between devices  74.7 us (29%)
  Pallas kernels  31.3 us (12%)
  other arithmetic  18.3 us (7%)
  between operations  14.5 us (6%)
  local copies, waits for them, and re-layouts  13 us (5%)
    ppermute x14, waiting for transfers between devices, send(): return lax.ppermute(array, ('ty', 'tx'), along(rule, sizes))  49.5 us
    all_gather x1, waiting for transfers between devices, body(): lax.all_gather(part, ('ty', 'tx'), axis_index_groups=groups, axis=0, tile...  44.4 us
    ppermute x14, starting transfers between devices, send(): return lax.ppermute(array, ('ty', 'tx'), along(rule, sizes))  43.1 us
    ppermute x6, starting transfers between devices, scatter(): total = total + lax.ppermute(piece, axis, pairs)  30.1 us
    pallas_call x1, Pallas kernels, slots_call(): pl.pallas_call(slots_kernel, out_shape=[jax.ShapeDtypeStruct(x.shape, f32...  21.2 us
    pallas_call x1, Pallas kernels, prepare(): pl.pallas_call(prepare_kernel, grid=(slots,), out_shape=[jax.ShapeDtypeSt...  10.1 us
    ppermute x6, waiting for transfers between devices, scatter(): total = total + lax.ppermute(piece, axis, pairs)  8.49 us
    unnamed x32, local copies, waits for them, and re-layouts  7.28 us
  transfers between devices with their start and end apart: 23, of which 9 were waited for; matrix products, arithmetic and copies ran while one was open for 7% of the time, Pallas kernels for 4%

profile of v7, /device:TPU:1, one launch (start us, length us, event | category | flops | bytes accessed | tf_op | source)
XLA Modules:
  0.0 254.2 jit_solution(4945059050523074220)
XLA Ops:
  7.2 0.0 all-gather.2.cloned.1.call-start
  7.2 3.2 %fusion = (f32[2,512,256]{2,1,0:T(8,128)}, f32[2,512,256]{2,1,0:T(8,128)}) fusion(f32[2,512,1024]{2,1,0:T(8,128)} %tile_hbm.1), kind=kLoop, calls=%fused_computation.21 | loop fusion | bytes 4194304 | tf_op jit(solution)/shard_map/slice | solution.py:601
  10.4 2.0 collective-permute-start.1
  12.4 1.3 collective-permute-start
  13.7 0.1 copy.16
  13.8 0.1 copy.17
  13.9 0.1 copy.15
  14.0 0.1 pad_add_fusion
  14.1 0.0 copy-start.2
  14.1 1.6 copy-done.2
  15.7 1.0 copy-done.3
  16.7 1.0 copy-done.4
  17.7 10.1 %prepare.1 = (f32[3,512,512]{2,1,0:T(8,128)S(1)}, f32[3,2,512,512]{3,2,1,0:T(8,128)S(1)}) custom-call(s32[4,3]{1,0:T(4,128)S(1)} %concatenate.14.meta, f32[3,512,512]{2,1,0:T(8,128)S(1)} %copy-done.1, f32[2,512,512]{2,1,0:T(8,128)S(1)} %copy-done.2, bf16[512,512]{1,0:T(8,128)(2,1)S(1)} %copy-done.3, bf16[512,512]{1,0:T(8,128)(2,1)S(1)} %copy-done.4), custom_call_target="tpu_custom_call" | custom-call | flops 4831838208 | bytes 18874368 | tf_op jit(solution)/shard_map/prepare/pallas_call | solution.py:511
  27.9 2.7 %copy-done.5 = f32[3,2,512,512]{3,2,1,0:T(8,128)} copy-done((f32[3,2,512,512]{3,2,1,0:T(8,128)}, f32[3,2,512,512]{3,2,1,0:T(8,128)S(1)}, u32[]{:S(2)}) %copy-start.5) | copy-done | bytes 6291480
  30.5 1.3 collective-permute-start.6
  31.8 1.3 collective-permute-start.2
  33.1 0.2 slice.51
  33.4 1.9 collective-permute-start.4
  35.3 1.9 collective-permute-start.3
  37.3 3.7 %collective-permute-done.right_a_hbm = f32[2,512,256]{2,1,0:T(8,128)} collective-permute-done((f32[2,512,256]{2,1,0:T(8,128)}, f32[2,512,256]{2,1,0:T(8,128)}, u32[]{:S(2)}, u32[]{:S(2)}) %collective-permute-start) | collective-permute-done | bytes 1048608 | tf_op jit(solution)/shard_map/ppermute | solution.py:547
  40.9 1.9 collective-permute-start.5
  42.9 19.8 %collective-permute-done.6.corner_side_hbm = f32[2,512,256]{2,1,0:T(8,128)S(1)} collective-permute-done((f32[2,512,256]{2,1,0:T(8,128)}, f32[2,512,256]{2,1,0:T(8,128)S(1)}, u32[]{:S(2)}, u32[]{:S(2)}) %collective-permute-start.6) | collective-permute-done | bytes 1048608 | tf_op jit(solution)/shard_map/ppermute | solution.py:547
  62.7 11.3 %collective-permute-done.2.right_b_hbm = f32[2,512,256]{2,1,0:T(8,128)} collective-permute-done((f32[2,512,256]{2,1,0:T(8,128)}, f32[2,512,256]{2,1,0:T(8,128)}, u32[]{:S(2)}, u32[]{:S(2)}) %collective-permute-start.2) | collective-permute-done | bytes 1048608 | tf_op jit(solution)/shard_map/ppermute | solution.py:547
  74.0 2.3 collective-permute-start.7
  76.3 0.0 collective-permute-done.3.lower_a_hbm
  76.3 7.3 %collective-permute-done.5.corner_a_hbm = f32[2,512,256]{2,1,0:T(8,128)} collective-permute-done((f32[2,512,256]{2,1,0:T(8,128)}, f32[2,512,256]{2,1,0:T(8,128)}, u32[]{:S(2)}, u32[]{:S(2)}) %collective-permute-start.5) | collective-permute-done | bytes 1048608 | tf_op jit(solution)/shard_map/ppermute | solution.py:547
  83.6 0.0 collective-permute-done.4.lower_c_hbm
  83.6 0.0 collective-permute-done.7.corner_up_hbm
  83.6 21.2 %slots.1 = (f32[2,512,1024]{2,1,0:T(8,128)}, f32[2,512,512]{2,1,0:T(8,128)}, f32[2,512,512]{2,1,0:T(8,128)}, f32[2,512,512]{2,1,0:T(8,128)}, f32[2,512,256]{2,1,...) custom-call(s32[4,3]{1,0:T(4,128)} %copy-done, f32[2,512,1024]{2,1,0:T(8,128)} %tile_hbm.1, ...), custom_call_target="tpu_custom_call" | custom-call | flops 9663676416 | bytes 41943040 | tf_op jit(solution)/shard_map/slots/pallas_call | solution.py:442
  104.8 1.4 constant_dynamic-slice_fusion.6
  106.3 0.1 collective-permute-start.9
  106.4 1.3 collective-permute-start.14
  107.7 7.3 %collective-permute-start.8 = (f32[2,512,256]{2,1,0:T(8,128)}, f32[2,512,256]{2,1,0:T(8,128)}, u32[]{:S(2)}, u32[]{:S(2)}) collective-permute-start(f32[2,512,256]{2,1,0:T(8,128)} %get-tuple-element.39), channel_id=1, source_target_pairs={{4,5},{5,6},{6,7},{12,13},{13,14},{14,15},{20,21},{21,22},{22,23},... | collective-permute-start | bytes 3145736 | tf_op jit(solution)/shard_map/ppermute | solution.py:547
  115.0 9.2 %collective-permute-start.13 = (f32[2,512,256]{2,1,0:T(8,128)}, f32[2,512,256]{2,1,0:T(8,128)}, u32[]{:S(2)}, u32[]{:S(2)}) collective-permute-start(f32[2,512,256]{2,1,0:T(8,128)} %get-tuple-element.41), channel_id=1, source_target_pairs={{0,4},{1,5},{2,6},{3,7},{4,8},{5,9},{6,10},{7,11},{8,12},{9,13},{1... | collective-permute-start | bytes 3145736 | tf_op jit(solution)/shard_map/ppermute | solution.py:547
  124.2 0.0 collective-permute-done.9
  124.3 1.4 dynamic-slice_add_fusion
  125.7 0.0 copy-start.8
  125.7 0.8 constant_dynamic-slice_fusion.5
  126.5 10.3 %collective-permute-start.10 = (f32[128,512]{1,0:T(8,128)S(1)}, f32[128,512]{1,0:T(8,128)S(1)}, u32[]{:S(2)}, u32[]{:S(2)}) collective-permute-start(f32[128,512]{1,0:T(8,128)S(1)} %get-tuple-element.54), channel_id=1, source_target_pairs={{0,8},{4,12},{8,16},{12,20},{16,24},{20,28},{24,0},{28,4},{1,9},{5... | collective-permute-start | bytes 786440 | tf_op jit(solution)/shard_map/ppermute | solution.py:575
  136.8 5.2 %collective-permute-done.10 = f32[128,512]{1,0:T(8,128)S(1)} collective-permute-done((f32[128,512]{1,0:T(8,128)S(1)}, f32[128,512]{1,0:T(8,128)S(1)}, u32[]{:S(2)}, u32[]{:S(2)}) %collective-permute-start.10) | collective-permute-done | bytes 262176 | tf_op jit(solution)/shard_map/ppermute | solution.py:575
  142.0 0.7 copy-done.11
  142.7 13.6 %collective-permute-start.12 = (f32[128,512]{1,0:T(8,128)S(1)}, f32[128,512]{1,0:T(8,128)}, u32[]{:S(2)}, u32[]{:S(2)}) collective-permute-start(f32[128,512]{1,0:T(8,128)S(1)} %get-tuple-element.55), channel_id=1, source_target_pairs={{0,24},{4,28},{8,0},{12,4},{16,8},{20,12},{24,16},{28,20},{1,25},{... | collective-permute-start | bytes 786440 | tf_op jit(solution)/shard_map/ppermute | solution.py:575
  156.3 1.1 collective-permute-done.11
  157.4 2.2 collective-permute-done.12
  159.6 1.2 add_add_fusion.1
  160.8 0.0 collective-permute-done.13
  160.8 0.0 collective-permute-done.8
  160.9 2.6 %collective-permute-start.15 = (f32[32,512]{1,0:T(8,128)S(1)}, f32[32,512]{1,0:T(8,128)S(1)}, u32[]{:S(2)}, u32[]{:S(2)}) collective-permute-start(f32[32,512]{1,0:T(8,128)S(1)} %get-tuple-element.57), channel_id=1, source_target_pairs={{0,1},{1,2},{2,3},{3,0},{4,5},{5,6},{6,7},{7,4},{8,9},{9,10},{10,1... | collective-permute-start | bytes 196616 | tf_op jit(solution)/shard_map/ppermute | solution.py:575
  163.4 3.6 %collective-permute-start.16 = (f32[32,512]{1,0:T(8,128)S(1)}, f32[32,512]{1,0:T(8,128)S(1)}, u32[]{:S(2)}, u32[]{:S(2)}) collective-permute-start(f32[32,512]{1,0:T(8,128)S(1)} %get-tuple-element.59), channel_id=1, source_target_pairs={{0,2},{1,3},{2,0},{3,1},{4,6},{5,7},{6,4},{7,5},{8,10},{9,11},{10,... | collective-permute-start | bytes 196616 | tf_op jit(solution)/shard_map/ppermute | solution.py:575
  167.0 0.0 collective-permute-start.17
  167.0 3.3 %maximum_add_fusion = f32[2,512,512]{2,1,0:T(8,128)} fusion(f32[2,512,512]{2,1,0:T(8,128)S(1)} %copy-done.8, f32[2,512,256]{2,1,0:T(8,128)} %collective-permute-done.14, f32[2,512,256]{2,1,0:T(8,128)} %collective-permute-done.13), kind=kLoop, calls=%fused_computation.1 | loop fusion | flops 1048576 | bytes 6291456 | tf_op jit(solution)/shard_map/add | solution.py:631
  170.3 1.9 collective-permute-start.20
  172.2 0.7 add_multiply_fusion
  172.9 0.0 all-gather.2.cloned.1.call-update
  172.9 2.7 %add_dynamic-update-slice_fusion = f32[2,512,512]{2,1,0:T(8,128)} fusion(f32[2,512,512]{2,1,0:T(8,128)} %get-tuple-element.38, f32[2,512,256]{2,1,0:T(8,128)} %collective-permute-done.8), kind=kLoop, calls=%fused_computation.5 | loop fusion | flops 262144 | bytes 3145728 | tf_op jit(solution)/shard_map/scatter-add | solution.py:633
  175.6 4.8 %collective-permute-start.18 = (f32[2,512,512]{2,1,0:T(8,128)}, f32[2,512,512]{2,1,0:T(8,128)}, u32[]{:S(2)}, u32[]{:S(2)}) collective-permute-start(f32[2,512,512]{2,1,0:T(8,128)} %add_dynamic-update-slice_fusion), channel_id=1, source_target_pairs={{0,4},{1,5},{2,6},{3,7},{4,8},{5,9},{6,10},{7,11},{8,12},{9,13},{1... | collective-permute-start | bytes 6291464 | tf_op jit(solution)/shard_map/ppermute | solution.py:547
  180.4 4.7 %collective-permute-start.19 = (f32[2,512,512]{2,1,0:T(8,128)}, f32[2,512,512]{2,1,0:T(8,128)}, u32[]{:S(2)}, u32[]{:S(2)}) collective-permute-start(f32[2,512,512]{2,1,0:T(8,128)} %maximum_add_fusion), channel_id=1, source_target_pairs={{0,1},{1,2},{2,3},{4,5},{5,6},{6,7},{8,9},{9,10},{10,11},{12,13},{... | collective-permute-start | bytes 6291464 | tf_op jit(solution)/shard_map/ppermute | solution.py:547
  185.2 44.4 %all-gather.2.cloned.1.call-done = f32[512,512]{1,0:T(8,128)} async-done(((f32[32,512]{1,0:T(8,128)}), f32[512,512]{1,0:T(8,128)}) %all-gather.2.cloned.1.call-update) | async-done | bytes 1048592 | tf_op jit(solution)/shard_map/all_gather | solution.py:638
  229.6 1.5 collective-permute-start.21
  231.1 7.3 %collective-permute-done.19 = f32[2,512,512]{2,1,0:T(8,128)} collective-permute-done((f32[2,512,512]{2,1,0:T(8,128)}, f32[2,512,512]{2,1,0:T(8,128)}, u32[]{:S(2)}, u32[]{:S(2)}) %collective-permute-start.19) | collective-permute-done | bytes 2097184 | tf_op jit(solution)/shard_map/ppermute | solution.py:547
  238.4 4.8 %add_add_fusion = (f32[2,512,512]{2,1,0:T(8,128)S(1)}, f32[2,512,512]{2,1,0:T(8,128)S(1)}) fusion(f32[2,512,512]{2,1,0:T(8,128)} %collective-permute-done.19, f32[2,512,512]{2,1,0:T(8,128)} %collective-permute-done.18, f32[2,512,1024]{2,1,0:T(8,128)} %get-tuple-element.37, f32[2,512,512]{2,1,0:T(8,128)S(1)} %collective-permute-done.20), kind=kLoop, calls=%fused_computation.4 | loop fusion | flops 1572864 | bytes 14680064 | tf_op jit(solution)/shard_map/add | solution.py:641
  243.2 2.5 pad_maximum_fusion
  245.6 0.2 broadcast_select_fusion.1
  245.9 1.5 pad_maximum_fusion.1
  (36 shorter events, 0.1 us)
Async XLA Ops:
  7.2 6.5 %copy-start.12 = (s32[3,2]{0,1:T(2,128)S(1)}, s32[3,2]{0,1:T(2,128)}, u32[]{:S(2)}) copy-start(s32[3,2]{0,1:T(2,128)} %param.16) | copy-start | bytes 76
  7.2 6.7 %copy-start.13 = (s32[3]{0:T(128)S(1)}, s32[3]{0:T(128)}, u32[]{:S(2)}) copy-start(s32[3]{0:T(128)} %param.17) | copy-start | bytes 40
  7.2 6.9 %copy-start.1 = (f32[3,512,512]{2,1,0:T(8,128)S(1)}, f32[3,512,512]{2,1,0:T(8,128)}, u32[]{:S(2)}) copy-start(f32[3,512,512]{2,1,0:T(8,128)} %amps.1) | copy-start | bytes 9437188
  7.2 222.4 %all-gather.2.cloned.1.call-start = ((), (), s32[]{:S(2)}) async-start(), calls=%async_computation | async-start | bytes 1114112 | tf_op jit(solution)/shard_map/all_gather | solution.py:638
  10.4 20.1 %collective-permute-start.1 = (f32[2,512,256]{2,1,0:T(8,128)}, f32[2,512,256]{2,1,0:T(8,128)}, u32[]{:S(2)}, u32[]{:S(2)}) collective-permute-start(f32[2,512,256]{2,1,0:T(8,128)} %get-tuple-element.31), channel_id=1, source_target_pairs={{4,0},{5,1},{6,2},{7,3},{8,4},{9,5},{10,6},{11,7},{12,8},{13,9},{1... | collective-permute-start | bytes 3145736 | tf_op jit(solution)/shard_map/ppermute | solution.py:547
  12.4 28.6 %collective-permute-start = (f32[2,512,256]{2,1,0:T(8,128)}, f32[2,512,256]{2,1,0:T(8,128)}, u32[]{:S(2)}, u32[]{:S(2)}) collective-permute-start(f32[2,512,256]{2,1,0:T(8,128)} %get-tuple-element.51), channel_id=1, source_target_pairs={{1,0},{2,1},{3,2},{5,4},{6,5},{7,6},{9,8},{10,9},{11,10},{13,12},{... | collective-permute-start | bytes 3145736 | tf_op jit(solution)/shard_map/ppermute | solution.py:547
  14.1 1.6 copy-start.2
  15.7 1.0 copy-start.3
  16.7 1.0 copy-start.4
  17.7 10.1 %copy-start = (s32[4,3]{1,0:T(4,128)}, s32[4,3]{1,0:T(4,128)S(1)}, u32[]{:S(2)}) copy-start(s32[4,3]{1,0:T(4,128)S(1)} %concatenate.14.meta) | copy-start | bytes 148
  17.7 15.4 %copy-start.7 = (f32[2,512,1024]{2,1,0:T(8,128)S(1)}, f32[2,512,1024]{2,1,0:T(8,128)}, u32[]{:S(2)}) copy-start(f32[2,512,1024]{2,1,0:T(8,128)} %tile_hbm.1) | copy-start | bytes 12582916
  27.9 2.7 %copy-start.5 = (f32[3,2,512,512]{3,2,1,0:T(8,128)}, f32[3,2,512,512]{3,2,1,0:T(8,128)S(1)}, u32[]{:S(2)}) copy-start(f32[3,2,512,512]{3,2,1,0:T(8,128)S(1)} %get-tuple-element.36.pupil_hbm) | copy-start | bytes 18874372
  30.5 2.9 %copy-start.6 = (f32[3,512,512]{2,1,0:T(8,128)}, f32[3,512,512]{2,1,0:T(8,128)S(1)}, u32[]{:S(2)}) copy-start(f32[3,512,512]{2,1,0:T(8,128)S(1)} %get-tuple-element.35.amps_hbm) | copy-start | bytes 9437188
  30.5 32.2 %collective-permute-start.6 = (f32[2,512,256]{2,1,0:T(8,128)}, f32[2,512,256]{2,1,0:T(8,128)S(1)}, u32[]{:S(2)}, u32[]{:S(2)}) collective-permute-start(f32[2,512,256]{2,1,0:T(8,128)} %collective-permute-done.1.lower_b_hbm), channel_id=1, source_target_pairs={{5,4},{6,5},{7,6},{13,12},{14,13},{15,14},{21,20},{22,21},{23,22},... | collective-permute-start | bytes 3145736 | tf_op jit(solution)/shard_map/ppermute | solution.py:547
  31.8 42.2 %collective-permute-start.2 = (f32[2,512,256]{2,1,0:T(8,128)}, f32[2,512,256]{2,1,0:T(8,128)}, u32[]{:S(2)}, u32[]{:S(2)}) collective-permute-start(f32[2,512,256]{2,1,0:T(8,128)} %get-tuple-element.31), channel_id=1, source_target_pairs={{1,0},{2,1},{3,2},{5,4},{6,5},{7,6},{9,8},{10,9},{11,10},{13,12},{... | collective-permute-start | bytes 3145736 | tf_op jit(solution)/shard_map/ppermute | solution.py:547
  33.4 50.2 %collective-permute-start.4 = (f32[2,512,512]{2,1,0:T(8,128)S(1)}, f32[2,512,512]{2,1,0:T(8,128)}, u32[]{:S(2)}, u32[]{:S(2)}) collective-permute-start(f32[2,512,512]{2,1,0:T(8,128)S(1)} %slice.51), channel_id=1, source_target_pairs={{4,0},{5,1},{6,2},{7,3},{8,4},{9,5},{10,6},{11,7},{12,8},{13,9},{1... | collective-permute-start | bytes 6291464 | tf_op jit(solution)/shard_map/ppermute | solution.py:547
  35.3 41.0 %collective-permute-start.3 = (f32[2,512,256]{2,1,0:T(8,128)}, f32[2,512,256]{2,1,0:T(8,128)}, u32[]{:S(2)}, u32[]{:S(2)}) collective-permute-start(f32[2,512,256]{2,1,0:T(8,128)} %get-tuple-element.51), channel_id=1, source_target_pairs={{4,0},{5,1},{6,2},{7,3},{8,4},{9,5},{10,6},{11,7},{12,8},{13,9},{1... | collective-permute-start | bytes 3145736 | tf_op jit(solution)/shard_map/ppermute | solution.py:547
  40.9 42.6 %collective-permute-start.5 = (f32[2,512,256]{2,1,0:T(8,128)}, f32[2,512,256]{2,1,0:T(8,128)}, u32[]{:S(2)}, u32[]{:S(2)}) collective-permute-start(f32[2,512,256]{2,1,0:T(8,128)} %collective-permute-done.right_a_hbm), channel_id=1, source_target_pairs={{4,0},{5,1},{6,2},{7,3},{8,4},{9,5},{10,6},{11,7},{12,8},{13,9},{1... | collective-permute-start | bytes 3145736 | tf_op jit(solution)/shard_map/ppermute | solution.py:547
  62.7 20.9 %copy-start.14 = (f32[2,512,256]{2,1,0:T(8,128)}, f32[2,512,256]{2,1,0:T(8,128)S(1)}, u32[]{:S(2)}) copy-start(f32[2,512,256]{2,1,0:T(8,128)S(1)} %collective-permute-done.6.corner_side_hbm) | copy-start | bytes 3145732
  74.0 9.6 %collective-permute-start.7 = (f32[2,512,256]{2,1,0:T(8,128)}, f32[2,512,256]{2,1,0:T(8,128)}, u32[]{:S(2)}, u32[]{:S(2)}) collective-permute-start(f32[2,512,256]{2,1,0:T(8,128)} %collective-permute-done.2.right_b_hbm), channel_id=1, source_target_pairs={{4,0},{5,1},{6,2},{7,3},{12,8},{13,9},{14,10},{15,11},{20,16},{21,... | collective-permute-start | bytes 3145736 | tf_op jit(solution)/shard_map/ppermute | solution.py:547
  104.8 19.4 %copy-start.9 = (f32[2,512,512]{2,1,0:T(8,128)S(1)}, f32[2,512,512]{2,1,0:T(8,128)}, u32[]{:S(2)}) copy-start(f32[2,512,512]{2,1,0:T(8,128)} %get-tuple-element.40) | copy-start | bytes 6291460
  106.3 18.0 %collective-permute-start.9 = (f32[512,512]{1,0:T(8,128)S(1)}, f32[512,512]{1,0:T(8,128)}, u32[]{:S(2)}, u32[]{:S(2)}) collective-permute-start(f32[512,512]{1,0:T(8,128)S(1)} %constant_dynamic-slice_fusion.6), channel_id=1, source_target_pairs={{0,4},{4,0},{8,12},{12,8},{16,20},{20,16},{24,28},{28,24},{1,5},{5... | collective-permute-start | bytes 3145736 | tf_op jit(solution)/shard_map/ppermute | solution.py:555
  106.4 54.4 %collective-permute-start.14 = (f32[2,512,256]{2,1,0:T(8,128)}, f32[2,512,256]{2,1,0:T(8,128)}, u32[]{:S(2)}, u32[]{:S(2)}) collective-permute-start(f32[2,512,256]{2,1,0:T(8,128)} %get-tuple-element.39), channel_id=1, source_target_pairs={{0,4},{1,5},{2,6},{3,7},{8,12},{9,13},{10,14},{11,15},{16,20},{17,... | collective-permute-start | bytes 3145736 | tf_op jit(solution)/shard_map/ppermute | solution.py:547
  107.7 53.1 %collective-permute-start.8 = (f32[2,512,256]{2,1,0:T(8,128)}, f32[2,512,256]{2,1,0:T(8,128)}, u32[]{:S(2)}, u32[]{:S(2)}) collective-permute-start(f32[2,512,256]{2,1,0:T(8,128)} %get-tuple-element.39), channel_id=1, source_target_pairs={{4,5},{5,6},{6,7},{12,13},{13,14},{14,15},{20,21},{21,22},{22,23},... | collective-permute-start | bytes 3145736 | tf_op jit(solution)/shard_map/ppermute | solution.py:547
  115.0 45.8 %collective-permute-start.13 = (f32[2,512,256]{2,1,0:T(8,128)}, f32[2,512,256]{2,1,0:T(8,128)}, u32[]{:S(2)}, u32[]{:S(2)}) collective-permute-start(f32[2,512,256]{2,1,0:T(8,128)} %get-tuple-element.41), channel_id=1, source_target_pairs={{0,4},{1,5},{2,6},{3,7},{4,8},{5,9},{6,10},{7,11},{8,12},{9,13},{1... | collective-permute-start | bytes 3145736 | tf_op jit(solution)/shard_map/ppermute | solution.py:547
  125.7 41.3 %copy-start.8 = (f32[2,512,512]{2,1,0:T(8,128)S(1)}, f32[2,512,512]{2,1,0:T(8,128)}, u32[]{:S(2)}) copy-start(f32[2,512,512]{2,1,0:T(8,128)} %get-tuple-element.44) | copy-start | bytes 6291460
  126.5 15.5 %collective-permute-start.10 = (f32[128,512]{1,0:T(8,128)S(1)}, f32[128,512]{1,0:T(8,128)S(1)}, u32[]{:S(2)}, u32[]{:S(2)}) collective-permute-start(f32[128,512]{1,0:T(8,128)S(1)} %get-tuple-element.54), channel_id=1, source_target_pairs={{0,8},{4,12},{8,16},{12,20},{16,24},{20,28},{24,0},{28,4},{1,9},{5... | collective-permute-start | bytes 786440 | tf_op jit(solution)/shard_map/ppermute | solution.py:575
  136.8 20.6 %collective-permute-start.11 = (f32[128,512]{1,0:T(8,128)}, f32[128,512]{1,0:T(8,128)}, u32[]{:S(2)}, u32[]{:S(2)}) collective-permute-start(f32[128,512]{1,0:T(8,128)} %get-tuple-element.56), channel_id=1, source_target_pairs={{0,16},{4,20},{8,24},{12,28},{16,0},{20,4},{24,8},{28,12},{1,17},{... | collective-permute-start | bytes 786440 | tf_op jit(solution)/shard_map/ppermute | solution.py:575
  142.0 0.7 copy-start.11
  142.7 16.9 %collective-permute-start.12 = (f32[128,512]{1,0:T(8,128)S(1)}, f32[128,512]{1,0:T(8,128)}, u32[]{:S(2)}, u32[]{:S(2)}) collective-permute-start(f32[128,512]{1,0:T(8,128)S(1)} %get-tuple-element.55), channel_id=1, source_target_pairs={{0,24},{4,28},{8,0},{12,4},{16,8},{20,12},{24,16},{28,20},{1,25},{... | collective-permute-start | bytes 786440 | tf_op jit(solution)/shard_map/ppermute | solution.py:575
  160.9 11.4 %collective-permute-start.15 = (f32[32,512]{1,0:T(8,128)S(1)}, f32[32,512]{1,0:T(8,128)S(1)}, u32[]{:S(2)}, u32[]{:S(2)}) collective-permute-start(f32[32,512]{1,0:T(8,128)S(1)} %get-tuple-element.57), channel_id=1, source_target_pairs={{0,1},{1,2},{2,3},{3,0},{4,5},{5,6},{6,7},{7,4},{8,9},{9,10},{10,1... | collective-permute-start | bytes 196616 | tf_op jit(solution)/shard_map/ppermute | solution.py:575
  163.4 8.8 %collective-permute-start.16 = (f32[32,512]{1,0:T(8,128)S(1)}, f32[32,512]{1,0:T(8,128)S(1)}, u32[]{:S(2)}, u32[]{:S(2)}) collective-permute-start(f32[32,512]{1,0:T(8,128)S(1)} %get-tuple-element.59), channel_id=1, source_target_pairs={{0,2},{1,3},{2,0},{3,1},{4,6},{5,7},{6,4},{7,5},{8,10},{9,11},{10,... | collective-permute-start | bytes 196616 | tf_op jit(solution)/shard_map/ppermute | solution.py:575
  167.0 5.2 %collective-permute-start.17 = (f32[32,512]{1,0:T(8,128)S(1)}, f32[32,512]{1,0:T(8,128)S(1)}, u32[]{:S(2)}, u32[]{:S(2)}) collective-permute-start(f32[32,512]{1,0:T(8,128)S(1)} %get-tuple-element.58), channel_id=1, source_target_pairs={{0,3},{1,0},{2,1},{3,2},{4,7},{5,4},{6,5},{7,6},{8,11},{9,8},{10,9... | collective-permute-start | bytes 196616 | tf_op jit(solution)/shard_map/ppermute | solution.py:575
  170.3 60.8 %collective-permute-start.20 = (f32[2,512,512]{2,1,0:T(8,128)}, f32[2,512,512]{2,1,0:T(8,128)S(1)}, u32[]{:S(2)}, u32[]{:S(2)}) collective-permute-start(f32[2,512,512]{2,1,0:T(8,128)} %get-tuple-element.47), channel_id=1, source_target_pairs={{0,4},{1,5},{2,6},{3,7},{4,8},{5,9},{6,10},{7,11},{8,12},{9,13},{1... | collective-permute-start | bytes 6291464 | tf_op jit(solution)/shard_map/ppermute | solution.py:547
  175.6 55.5 %collective-permute-start.18 = (f32[2,512,512]{2,1,0:T(8,128)}, f32[2,512,512]{2,1,0:T(8,128)}, u32[]{:S(2)}, u32[]{:S(2)}) collective-permute-start(f32[2,512,512]{2,1,0:T(8,128)} %add_dynamic-update-slice_fusion), channel_id=1, source_target_pairs={{0,4},{1,5},{2,6},{3,7},{4,8},{5,9},{6,10},{7,11},{8,12},{9,13},{1... | collective-permute-start | bytes 6291464 | tf_op jit(solution)/shard_map/ppermute | solution.py:547
  180.4 58.0 %collective-permute-start.19 = (f32[2,512,512]{2,1,0:T(8,128)}, f32[2,512,512]{2,1,0:T(8,128)}, u32[]{:S(2)}, u32[]{:S(2)}) collective-permute-start(f32[2,512,512]{2,1,0:T(8,128)} %maximum_add_fusion), channel_id=1, source_target_pairs={{0,1},{1,2},{2,3},{4,5},{5,6},{6,7},{8,9},{9,10},{10,11},{12,13},{... | collective-permute-start | bytes 6291464 | tf_op jit(solution)/shard_map/ppermute | solution.py:547
  229.6 16.0 %collective-permute-start.21 = (f32[512,512]{1,0:T(8,128)}, f32[512,512]{1,0:T(8,128)S(1)}, u32[]{:S(2)}, u32[]{:S(2)}) collective-permute-start(f32[512,512]{1,0:T(8,128)} %all-gather.2.cloned.1.call-done), channel_id=1, source_target_pairs={{0,4},{4,0},{8,12},{12,8},{16,20},{20,16},{24,28},{28,24},{1,5},{5... | collective-permute-start | bytes 3145736 | tf_op jit(solution)/shard_map/ppermute | solution.py:561
  243.2 2.5 copy-start.10
Sparse Core Ops, SparseCore 0:
  173.0 56.5 all-gather.1

commit v8 on v7

--- a/solution.py
+++ b/solution.py
@@ -120,8 +120,7 @@
     right_a_hbm,
     right_b_hbm,
     lower_a_hbm,
-    lower_b_hbm,
-    lower_c_hbm,
+    lower_bc_hbm,
     corner_a_hbm,
     corner_up_hbm,
     corner_side_hbm,
@@ -156,6 +155,7 @@
     mat_t_hi,
     mat_t_lo,
     in_sems,
+    slot_sems,
     out_sems,
 ):
     side = pupil.shape[-1]
@@ -165,18 +165,18 @@
     lanes = 128
     wide = side + lanes
     half = side // 2
+    cut = corner_a_hbm.shape[-1]
 
     def pieces(buffer):
         top, bottom = pl.ds(0, tile_rows), pl.ds(tile_rows, side)
         return (
             buffer.at[:, top, pl.ds(0, tile_cols)],
-            buffer.at[:, top, pl.ds(tile_cols, half)],
-            buffer.at[:, top, pl.ds(tile_cols + half, half)],
-            buffer.at[:, bottom, pl.ds(0, half)],
-            buffer.at[:, bottom, pl.ds(half, half)],
-            buffer.at[:, bottom, pl.ds(side, tile_cols - side)],
-            buffer.at[:, bottom, pl.ds(tile_cols, half)],
-            buffer.at[:, bottom, pl.ds(tile_cols + half, half)],
+            buffer.at[:, top, pl.ds(tile_cols, cut)],
+            buffer.at[:, top, pl.ds(tile_cols + cut, side - cut)],
+            buffer.at[:, bottom, pl.ds(0, cut)],
+            buffer.at[:, bottom, pl.ds(cut, tile_cols - cut)],
+            buffer.at[:, bottom, pl.ds(tile_cols, cut)],
+            buffer.at[:, bottom, pl.ds(tile_cols + cut, side - cut)],
         )
 
     odd = meta[slots, 0]
@@ -186,8 +186,7 @@
         right_a_hbm,
         right_b_hbm,
         lower_a_hbm,
-        lower_b_hbm,
-        lower_c_hbm,
+        lower_bc_hbm,
         corner_a_hbm,
     )
     loads = [
@@ -196,29 +195,41 @@
     ]
     for load in loads:
         load.start()
-    from_side = pltpu.make_async_copy(corner_side_hbm, targets[7], in_sems.at[7])
-    from_below = pltpu.make_async_copy(corner_up_hbm, targets[7], in_sems.at[7])
+    from_side = pltpu.make_async_copy(corner_side_hbm, targets[6], in_sems.at[6])
+    from_below = pltpu.make_async_copy(corner_up_hbm, targets[6], in_sems.at[6])
     pl.when(odd == 1)(from_side.start)
     pl.when(odd != 1)(from_below.start)
     loads.append(from_side)
     late = (
-        (pupil_hbm, pupil),
         (mat_hi_hbm, mat_hi),
         (mat_lo_hbm, mat_lo),
         (mat_t_hi_hbm, mat_t_hi),
         (mat_t_lo_hbm, mat_t_lo),
-        (amps_hbm, amps),
     )
     late_loads = [
-        pltpu.make_async_copy(src, dst, in_sems.at[8 + n]) for n, (src, dst) in enumerate(late)
+        pltpu.make_async_copy(src, dst, in_sems.at[7 + n]) for n, (src, dst) in enumerate(late)
     ]
     for load in late_loads:
         load.start()
+    count = meta[0, 2]
+    for slot in range(1, slots):
+        count = count + meta[slot, 2]
+
+    def slot_loads(slot):
+        return (
+            pltpu.make_async_copy(pupil_hbm.at[slot], pupil.at[slot], slot_sems.at[0, slot]),
+            pltpu.make_async_copy(amps_hbm.at[slot], amps.at[slot], slot_sems.at[1, slot]),
+        )
+
+    @pl.loop(0, count)
+    def _(slot):
+        for load in slot_loads(slot):
+            load.start()
 
     top, bottom = pl.ds(0, tile_rows), pl.ds(tile_rows, side)
     outs = (
-        (corner_a_out, bottom, pl.ds(tile_cols, half)),
-        (corner_b_out, bottom, pl.ds(tile_cols + half, half)),
+        (corner_a_out, bottom, pl.ds(tile_cols, cut)),
+        (corner_b_out, bottom, pl.ds(tile_cols + cut, side - cut)),
         (lower_c_out, bottom, pl.ds(side, tile_cols - side)),
         (lower_ab_out, bottom, pl.ds(0, side)),
         (right_out, top, pl.ds(tile_cols, side)),
@@ -247,10 +258,6 @@
     for load in loads:
         load.wait()
 
-    count = meta[0, 2]
-    for slot in range(1, slots):
-        count = count + meta[slot, 2]
-
     def one_slot(slot):
         row = meta[slot, 0]
         col = meta[slot, 1]
@@ -273,6 +280,9 @@
             block = region[plane, last_rows, pl.ds(col_base, wide)]
             block = wrap_lanes(block, col_shift)
             win[plane, :8, :] = jnp.where(first_keep, win[plane, :8, :], block)
+
+        pupil_load, amps_load = slot_loads(slot)
+        pupil_load.wait()
 
         @pl.when(slot == 0)
         def _():
@@ -318,6 +328,8 @@
                         rows = pl.ds(base + p * short, 16)
                         right_hi[t, rows, pl.ds(offset, short)] = hi
                         right_lo[t, rows, pl.ds(offset, short)] = lo
+
+        amps_load.wait()
 
         for t in range(RADIX):
             for start in (0, half):
@@ -434,7 +446,8 @@
     anywhere = pl.BlockSpec(memory_space=pl.ANY)
     f32, bf16 = jnp.float32, jnp.bfloat16
     region = (2, tile_rows + side, tile_cols + side)
-    _, _, _, _, lower_c, corner_a, corner_b, _ = parts
+    corner_a, corner_b, _ = parts[-3:]
+    lower_c = jax.ShapeDtypeStruct((2, side, tile_cols - side), f32)
     right = jax.ShapeDtypeStruct((2, tile_rows, side), f32)
     lower_ab = jax.ShapeDtypeStruct((2, side, side), f32)
     outs = (tile, right, lower_ab, lower_c, corner_a, corner_b, jax.ShapeDtypeStruct(pupils.shape[1:], f32))
@@ -462,7 +475,8 @@
             table,
             table,
             table,
-            pltpu.SemaphoreType.DMA((14,)),
+            pltpu.SemaphoreType.DMA((11,)),
+            pltpu.SemaphoreType.DMA((2, slots)),
             pltpu.SemaphoreType.DMA((7,)),
         ],
         compiler_params=pltpu.CompilerParams(vmem_limit_bytes=56 * 1024 * 1024),
@@ -582,7 +596,7 @@
 
 def body(spectrum, pupil, amplitudes, offsets, live):
     side = pupil.shape[-1]
-    half = side // 2
+    cut = 3 * side // 4
     tile_rows, tile_cols = spectrum.shape[1:]
     own_ty, own_tx = lax.axis_index("ty"), lax.axis_index("tx")
     rows_local = offsets[:, 0] - own_ty * tile_rows
@@ -596,19 +610,17 @@
     def up(i, j):
         return (i - 1, j)
 
-    lower_b = send(spectrum[:, :side, half:side], up)
-    right_a = send(spectrum[:, :, :half], left)
-    right_b = send(after(spectrum[:, :, half:side], lower_b), left)
-    lower_a = send(spectrum[:, :side, :half], up)
-    lower_c = send(spectrum[:, :side, side:], up)
+    lower_bc = send(spectrum[:, :side, cut:], up)
+    right_a = send(spectrum[:, :, :cut], left)
+    right_b = send(spectrum[:, :, cut:side], left)
+    lower_a = send(spectrum[:, :side, :cut], up)
     amps, pupils = prepare(meta, amplitudes, pupil)
-    lower_b, amps = lax.optimization_barrier((lower_b, amps))
-    corner_side = send(lower_b, lambda i, j: (i, j - 1) if i % 2 else None)
     corner_a = send(right_a[:, :side], up)
+    corner_side = send(lower_bc[:, :, : side - cut], lambda i, j: (i, j - 1) if i % 2 else None)
     right_b_again = after(right_b, corner_side)
     corner_up = send(right_b_again[:, :side], lambda i, j: (i - 1, j) if i % 2 else None)
 
-    parts = (right_a, right_b, lower_a, lower_b, lower_c, corner_a, corner_up, corner_side)
+    parts = (right_a, right_b, lower_a, lower_bc, corner_a, corner_up, corner_side)
     own_g, right_g, lower_ab_g, lower_c_g, corner_a_g, corner_b_g, dpup = slots_call(
         meta, spectrum, parts, amps, pupils
     )
@@ -623,26 +635,24 @@
     back_a = send(corner_a_g, down)
     back_down = send(corner_b_g, lambda i, j: None if i % 2 else (i + 1, j))
     n_ty, n_tx = lax.axis_size("ty"), lax.axis_size("tx")
-    over_cores = halve(dpup.reshape(-1, side), 1)
-    over_ty = scatter(over_cores, "ty", 2)
-    lower_c = send(after(lower_c_g, over_ty), down)
-    over_ty = after(over_ty, back_a, back_down, back_side)
-    part = scatter(over_ty, "tx", 1) * (1.0 / math.sqrt(n_ty * n_tx))
+    part = halve(dpup.reshape(-1, side), 1)
+    part, lower_c_g, back_a, back_down, back_side = lax.optimization_barrier(
+        (part, lower_c_g, back_a, back_down, back_side)
+    )
+    lower_c = send(lower_c_g, down)
+    over_tx = scatter(part, "tx", 1)
     right_total = right_g + jnp.concatenate([back_a, back_down], axis=2)
-    right_back = send(after(right_total, part), right)
-    lower_ab = send(lower_ab_g.at[:, :, half:].add(after(back_side, part)), down)
+    right_back = send(after(right_total, over_tx), right)
+    part = scatter(after(over_tx, lower_c), "ty", 2)
+    part = part * (1.0 / math.sqrt(n_ty * n_tx))
+    lower_ab = send(lower_ab_g.at[:, :, cut:].add(after(back_side, part)), down)
     groups = [
-        [(2 * k + core) * n_tx + j for k in range(n_ty // 2) for j in range(n_tx)]
+        [(2 * k + core) * n_tx + j for j in range(n_tx) for k in range(n_ty // 2)]
         for core in range(2)
     ]
     part = lax.all_gather(part, ("ty", "tx"), axis_index_groups=groups, axis=0, tiled=True)
-    spec_grad = jnp.concatenate(
-        [
-            own_g[:, :, :side] + lower_ab + right_back,
-            own_g[:, :, side:] + lower_c,
-        ],
-        axis=2,
-    )
+    spec_grad = own_g.at[:, :, side:].add(lower_c)
+    spec_grad = spec_grad.at[:, :, :side].add(lower_ab + right_back)
     return spec_grad, double(part, 1).reshape(pupil.shape)
 
 

time: 255 us -> 267 us (1.047)
  waiting for transfers between devices: 102 us -> 128 us
  starting transfers between devices: 74.7 us -> 56.5 us
  local copies, waits for them, and re-layouts: 13 us -> 17.9 us
    ppermute x6, starting transfers between devices: 30.1 us -> 6.47 us  [scatter(): total = total + lax.ppermute(piece, axis, pairs)]
    ppermute x14 -> x13, waiting for transfers between devices: 49.5 us -> 64.2 us  [send(): return lax.ppermute(array, ('ty', 'tx'), along(rule, sizes))]
    ppermute x6, waiting for transfers between devices: 8.49 us -> 19.5 us  [scatter(): total = total + lax.ppermute(piece, axis, pairs)]
    scatter-add x1 -> x3, other arithmetic: 2.69 us -> 10.5 us  [the longest x1 4.38 us: body(): spec_grad = spec_grad.at[:, :, :side].add(lower_ab + right_back)]
    ppermute x14 -> x13, starting transfers between devices: 43.1 us -> 47.9 us  [send(): return lax.ppermute(array, ('ty', 'tx'), along(rule, sizes))]
    add x1 -> x0, other arithmetic: 4.76 us -> none  [body(): own_g[:, :, :side] + lower_ab + right_back]
    unnamed x32, local copies, waits for them, and re-layouts: 7.28 us -> 10.5 us
  transfers between devices with their start and end apart: 23 -> 22, of which waited for: 9 -> 11; matrix products, arithmetic and copies ran while one was open for 7% -> 8% of each run, Pallas kernels for 4% -> 4%
where the time goes in v8:
time: 267 us; the launch traced here: 265 us
  waiting for transfers between devices  128 us (48%)
  starting transfers between devices  56.5 us (21%)
  Pallas kernels  29.4 us (11%)
  other arithmetic  18.8 us (7%)
  local copies, waits for them, and re-layouts  17.9 us (7%)
  between operations  14.4 us (5%)
    ppermute x13, waiting for transfers between devices, send(): return lax.ppermute(array, ('ty', 'tx'), along(rule, sizes))  64.2 us
    ppermute x13, starting transfers between devices, send(): return lax.ppermute(array, ('ty', 'tx'), along(rule, sizes))  47.9 us
    all_gather x1, waiting for transfers between devices, body(): lax.all_gather(part, ('ty', 'tx'), axis_index_groups=groups, axis=0, tile...  44.3 us
    ppermute x6, waiting for transfers between devices, scatter(): total = total + lax.ppermute(piece, axis, pairs)  19.5 us
    pallas_call x1, Pallas kernels, slots_call(): pl.pallas_call(slots_kernel, out_shape=[jax.ShapeDtypeStruct(x.shape, f32...  19.3 us
    unnamed x32, local copies, waits for them, and re-layouts  10.5 us
    pallas_call x1, Pallas kernels, prepare(): pl.pallas_call(prepare_kernel, grid=(slots,), out_shape=[jax.ShapeDtypeSt...  10.1 us
    ppermute x6, starting transfers between devices, scatter(): total = total + lax.ppermute(piece, axis, pairs)  6.47 us
  transfers between devices with their start and end apart: 22, of which 11 were waited for; matrix products, arithmetic and copies ran while one was open for 8% of the time, Pallas kernels for 4%

profile of v8, /device:TPU:1, one launch (start us, length us, event | category | flops | bytes accessed | tf_op | source)
XLA Modules:
  0.0 265.1 jit_solution(482562571721027674)
XLA Ops:
  7.2 0.0 all-gather.2.cloned.1.call-start
  7.2 0.0 copy-start.7
  7.2 2.1 slice.95
  9.3 0.0 copy-start.13
  9.3 0.0 copy-start.1
  9.3 2.2 collective-permute-start.3
  11.6 1.3 slice.93
  12.9 1.3 collective-permute-start
  14.2 1.9 collective-permute-start.2
  16.1 36.0 %collective-permute-done.right_a_hbm = f32[2,512,384]{2,1,0:T(8,128)} collective-permute-done((f32[2,512,384]{2,1,0:T(8,128)}, f32[2,512,384]{2,1,0:T(8,128)}, u32[]{:S(2)}, u32[]{:S(2)}) %collective-permute-start) | collective-permute-done | bytes 1572896 | tf_op jit(solution)/shard_map/ppermute | solution.py:561
  52.0 2.2 collective-permute-start.4
  54.3 0.9 slice.94
  55.1 1.3 collective-permute-start.1
  56.5 1.5 copy-done.11
  57.9 0.9 slice.100
  58.8 1.3 collective-permute-start.5
  60.1 0.1 copy.16
  60.2 0.1 copy.17
  60.3 0.1 copy.15
  60.4 10.6 %collective-permute-done.1.right_b_hbm = f32[2,512,128]{2,1,0:T(8,128)} collective-permute-done((f32[2,512,128]{2,1,0:T(8,128)}, f32[2,512,128]{2,1,0:T(8,128)}, u32[]{:S(2)}, u32[]{:S(2)}) %collective-permute-start.1) | collective-permute-done | bytes 524320 | tf_op jit(solution)/shard_map/ppermute | solution.py:561
  71.0 5.6 %collective-permute-done.5.corner_side_hbm = f32[2,512,128]{2,1,0:T(8,128)} collective-permute-done((f32[2,512,128]{2,1,0:T(8,128)}, f32[2,512,128]{2,1,0:T(8,128)}, u32[]{:S(2)}, u32[]{:S(2)}) %collective-permute-start.5) | collective-permute-done | bytes 524320 | tf_op jit(solution)/shard_map/ppermute | solution.py:561
  76.7 1.3 collective-permute-start.6
  78.0 0.1 pad_add_fusion
  78.1 1.6 copy-done.2
  79.7 1.0 copy-done.3
  80.7 1.0 copy-done.4
  81.7 10.1 %prepare.1 = (f32[3,512,512]{2,1,0:T(8,128)S(1)}, f32[3,2,512,512]{3,2,1,0:T(8,128)S(1)}) custom-call(s32[4,3]{1,0:T(4,128)S(1)} %concatenate.15.meta, f32[3,512,512]{2,1,0:T(8,128)S(1)} %copy-done.1, f32[2,512,512]{2,1,0:T(8,128)S(1)} %copy-done.2, bf16[512,512]{1,0:T(8,128)(2,1)S(1)} %copy-done.3, bf16[512,512]{1,0:T(8,128)(2,1)S(1)} %copy-done.4), custom_call_target="tpu_custom_call" | custom-call | flops 4831838208 | bytes 18874368 | tf_op jit(solution)/shard_map/prepare/pallas_call | solution.py:525
  91.9 2.7 %copy-done.5 = f32[3,2,512,512]{3,2,1,0:T(8,128)} copy-done((f32[3,2,512,512]{3,2,1,0:T(8,128)}, f32[3,2,512,512]{3,2,1,0:T(8,128)S(1)}, u32[]{:S(2)}) %copy-start.5) | copy-done | bytes 6291480
  94.5 1.7 copy-done.6
  96.2 0.8 copy-done.14
  97.0 19.3 %slots.1 = (f32[2,512,1024]{2,1,0:T(8,128)}, f32[2,512,512]{2,1,0:T(8,128)}, f32[2,512,512]{2,1,0:T(8,128)}, f32[2,512,512]{2,1,0:T(8,128)}, f32[2,512,384]{2,1,...) custom-call(s32[4,3]{1,0:T(4,128)} %copy-done, f32[2,512,1024]{2,1,0:T(8,128)} %tile_hbm.1, ...), custom_call_target="tpu_custom_call" | custom-call | flops 9663676416 | bytes 41943040 | tf_op jit(solution)/shard_map/slots/pallas_call | solution.py:455
  116.3 15.2 %collective-permute-start.8 = (f32[2,512,384]{2,1,0:T(8,128)}, f32[2,512,384]{2,1,0:T(8,128)}, u32[]{:S(2)}, u32[]{:S(2)}) collective-permute-start(f32[2,512,384]{2,1,0:T(8,128)} %get-tuple-element.62), channel_id=1, source_target_pairs={{0,4},{1,5},{2,6},{3,7},{4,8},{5,9},{6,10},{7,11},{8,12},{9,13},{1... | collective-permute-start | bytes 4718600 | tf_op jit(solution)/shard_map/ppermute | solution.py:561
  131.5 1.3 constant_dynamic-slice_fusion.6
  132.8 0.1 collective-permute-start.7
  132.9 2.1 collective-permute-start.10
  135.0 1.3 collective-permute-start.9
  136.3 1.4 dynamic-slice_add_fusion
  137.7 0.0 copy-start.8
  137.8 2.9 %collective-permute-done.10 = f32[2,512,128]{2,1,0:T(8,128)} collective-permute-done((f32[2,512,128]{2,1,0:T(8,128)}, f32[2,512,128]{2,1,0:T(8,128)}, u32[]{:S(2)}, u32[]{:S(2)}) %collective-permute-start.10) | collective-permute-done | bytes 524320 | tf_op jit(solution)/shard_map/ppermute | solution.py:561
  140.6 8.5 %collective-permute-done.8 = f32[2,512,384]{2,1,0:T(8,128)} collective-permute-done((f32[2,512,384]{2,1,0:T(8,128)}, f32[2,512,384]{2,1,0:T(8,128)}, u32[]{:S(2)}, u32[]{:S(2)}) %collective-permute-start.8) | collective-permute-done | bytes 1572896 | tf_op jit(solution)/shard_map/ppermute | solution.py:561
  149.2 4.4 %collective-permute-start.11 = (f32[2,512,512]{2,1,0:T(8,128)}, f32[2,512,512]{2,1,0:T(8,128)}, u32[]{:S(2)}, u32[]{:S(2)}) collective-permute-start(f32[2,512,512]{2,1,0:T(8,128)} %get-tuple-element.64), channel_id=1, source_target_pairs={{0,4},{1,5},{2,6},{3,7},{4,8},{5,9},{6,10},{7,11},{8,12},{9,13},{1... | collective-permute-start | bytes 6291464 | tf_op jit(solution)/shard_map/ppermute | solution.py:561
  153.6 0.9 constant_dynamic-slice_fusion.5
  154.5 1.6 collective-permute-start.13
  156.0 1.7 collective-permute-start.14
  157.7 7.0 %collective-permute-done.12 = f32[128,512]{1,0:T(8,128)} collective-permute-done((f32[128,512]{1,0:T(8,128)}, f32[128,512]{1,0:T(8,128)}, u32[]{:S(2)}, u32[]{:S(2)}) %collective-permute-start.12) | collective-permute-done | bytes 262176 | tf_op jit(solution)/shard_map/ppermute | solution.py:589
  164.8 10.2 %collective-permute-done.13 = f32[128,512]{1,0:T(8,128)} collective-permute-done((f32[128,512]{1,0:T(8,128)}, f32[128,512]{1,0:T(8,128)}, u32[]{:S(2)}, u32[]{:S(2)}) %collective-permute-start.13) | collective-permute-done | bytes 262176 | tf_op jit(solution)/shard_map/ppermute | solution.py:589
  175.0 1.2 add_add_fusion
  176.2 0.6 collective-permute-done.11
  176.8 1.7 collective-permute-start.15
  178.6 1.5 collective-permute-start.17
  180.1 1.7 collective-permute-done.15
  181.8 0.5 collective-permute-done.16
  182.3 0.6 add_multiply_fusion
  183.0 0.0 all-gather.2.cloned.1.call-update
  183.0 3.2 %maximum_add_fusion = f32[2,512,512]{2,1,0:T(8,128)} fusion(f32[2,512,512]{2,1,0:T(8,128)S(1)} %copy-done.8, f32[2,512,128]{2,1,0:T(8,128)} %collective-permute-done.9, f32[2,512,384]{2,1,0:T(8,128)} %collective-permute-done.8), kind=kLoop, calls=%fused_computation.2 | loop fusion | flops 1048576 | bytes 6291456 | tf_op jit(solution)/shard_map/add | solution.py:644
  186.2 9.4 %collective-permute-start.19 = (f32[2,512,512]{2,1,0:T(8,128)}, f32[2,512,512]{2,1,0:T(8,128)S(1)}, u32[]{:S(2)}, u32[]{:S(2)}) collective-permute-start(f32[2,512,512]{2,1,0:T(8,128)} %maximum_add_fusion), channel_id=1, source_target_pairs={{0,1},{1,2},{2,3},{4,5},{5,6},{6,7},{8,9},{9,10},{10,11},{12,13},{... | collective-permute-start | bytes 6291464 | tf_op jit(solution)/shard_map/ppermute | solution.py:561
  195.6 2.1 add_dynamic-update-slice_fusion.1
  197.7 4.0 %collective-permute-start.18 = (f32[2,512,512]{2,1,0:T(8,128)}, f32[2,512,512]{2,1,0:T(8,128)}, u32[]{:S(2)}, u32[]{:S(2)}) collective-permute-start(f32[2,512,512]{2,1,0:T(8,128)} %add_dynamic-update-slice_fusion.1), channel_id=1, source_target_pairs={{0,4},{1,5},{2,6},{3,7},{4,8},{5,9},{6,10},{7,11},{8,12},{9,13},{1... | collective-permute-start | bytes 6291464 | tf_op jit(solution)/shard_map/ppermute | solution.py:561
  201.8 44.3 %all-gather.2.cloned.1.call-done = f32[512,512]{1,0:T(8,128)} async-done(((f32[32,512]{1,0:T(8,128)}), f32[512,512]{1,0:T(8,128)}) %all-gather.2.cloned.1.call-update) | async-done | bytes 1048592 | tf_op jit(solution)/shard_map/all_gather | solution.py:653
  246.0 2.0 collective-permute-start.20
  248.1 4.0 %add_dynamic-update-slice_fusion = f32[2,512,1024]{2,1,0:T(8,128)} fusion(f32[2,512,1024]{2,1,0:T(8,128)} %get-tuple-element.59, f32[2,512,512]{2,1,0:T(8,128)} %collective-permute-done.11), kind=kLoop, calls=%fused_computation.4 | loop fusion | flops 524288 | bytes 6291456 | tf_op jit(solution)/shard_map/scatter-add | solution.py:654
  252.1 4.4 %fusion = f32[2,512,1024]{2,1,0:T(8,128)} fusion(f32[2,512,1024]{2,1,0:T(8,128)} %add_dynamic-update-slice_fusion, f32[2,512,512]{2,1,0:T(8,128)} %collective-permute-done.18, f32[2,512,512]{2,1,0:T(8,128)S(1)} %collective-permute-done.19), kind=kLoop, calls=%fused_computation.1 | loop fusion | flops 1048576 | bytes 8388608 | tf_op jit(solution)/shard_map/scatter-add | solution.py:655
  256.5 0.2 broadcast_select_fusion.1
  256.7 1.5 pad_maximum_fusion
  (36 shorter events, 0.1 us)
Async XLA Ops:
  7.2 238.9 %all-gather.2.cloned.1.call-start = ((), (), s32[]{:S(2)}) async-start(), calls=%async_computation | async-start | bytes 1114112 | tf_op jit(solution)/shard_map/all_gather | solution.py:653
  7.2 4.4 %copy-start.7 = (f32[2,512,1024]{2,1,0:T(8,128)S(1)}, f32[2,512,1024]{2,1,0:T(8,128)}, u32[]{:S(2)}) copy-start(f32[2,512,1024]{2,1,0:T(8,128)} %tile_hbm.1) | copy-start | bytes 12582916
  9.3 50.8 %copy-start.12 = (s32[3,2]{0,1:T(2,128)S(1)}, s32[3,2]{0,1:T(2,128)}, u32[]{:S(2)}) copy-start(s32[3,2]{0,1:T(2,128)} %param.20) | copy-start | bytes 76
  9.3 51.0 %copy-start.13 = (s32[3]{0:T(128)S(1)}, s32[3]{0:T(128)}, u32[]{:S(2)}) copy-start(s32[3]{0:T(128)} %param.21) | copy-start | bytes 40
  9.3 68.8 %copy-start.1 = (f32[3,512,512]{2,1,0:T(8,128)S(1)}, f32[3,512,512]{2,1,0:T(8,128)}, u32[]{:S(2)}) copy-start(f32[3,512,512]{2,1,0:T(8,128)} %amps.1) | copy-start | bytes 9437188
  9.3 47.1 %collective-permute-start.3 = (f32[2,512,640]{2,1,0:T(8,128)S(1)}, f32[2,512,640]{2,1,0:T(8,128)S(1)}, u32[]{:S(2)}, u32[]{:S(2)}) collective-permute-start(f32[2,512,640]{2,1,0:T(8,128)S(1)} %slice.95), channel_id=1, source_target_pairs={{4,0},{5,1},{6,2},{7,3},{8,4},{9,5},{10,6},{11,7},{12,8},{13,9},{1... | collective-permute-start | bytes 7864328 | tf_op jit(solution)/shard_map/ppermute | solution.py:561
  12.9 39.2 %collective-permute-start = (f32[2,512,384]{2,1,0:T(8,128)}, f32[2,512,384]{2,1,0:T(8,128)}, u32[]{:S(2)}, u32[]{:S(2)}) collective-permute-start(f32[2,512,384]{2,1,0:T(8,128)} %slice.93), channel_id=1, source_target_pairs={{1,0},{2,1},{3,2},{5,4},{6,5},{7,6},{9,8},{10,9},{11,10},{13,12},{... | collective-permute-start | bytes 4718600 | tf_op jit(solution)/shard_map/ppermute | solution.py:561
  14.2 82.1 %collective-permute-start.2 = (f32[2,512,384]{2,1,0:T(8,128)}, f32[2,512,384]{2,1,0:T(8,128)}, u32[]{:S(2)}, u32[]{:S(2)}) collective-permute-start(f32[2,512,384]{2,1,0:T(8,128)} %slice.93), channel_id=1, source_target_pairs={{4,0},{5,1},{6,2},{7,3},{8,4},{9,5},{10,6},{11,7},{12,8},{13,9},{1... | collective-permute-start | bytes 4718600 | tf_op jit(solution)/shard_map/ppermute | solution.py:561
  52.0 44.2 %collective-permute-start.4 = (f32[2,512,384]{2,1,0:T(8,128)}, f32[2,512,384]{2,1,0:T(8,128)}, u32[]{:S(2)}, u32[]{:S(2)}) collective-permute-start(f32[2,512,384]{2,1,0:T(8,128)} %collective-permute-done.right_a_hbm), channel_id=1, source_target_pairs={{4,0},{5,1},{6,2},{7,3},{8,4},{9,5},{10,6},{11,7},{12,8},{13,9},{1... | collective-permute-start | bytes 4718600 | tf_op jit(solution)/shard_map/ppermute | solution.py:561
  55.1 15.9 %collective-permute-start.1 = (f32[2,512,128]{2,1,0:T(8,128)}, f32[2,512,128]{2,1,0:T(8,128)}, u32[]{:S(2)}, u32[]{:S(2)}) collective-permute-start(f32[2,512,128]{2,1,0:T(8,128)} %slice.94), channel_id=1, source_target_pairs={{1,0},{2,1},{3,2},{5,4},{6,5},{7,6},{9,8},{10,9},{11,10},{13,12},{... | collective-permute-start | bytes 1572872 | tf_op jit(solution)/shard_map/ppermute | solution.py:561
  56.4 1.5 copy-start.11
  58.8 17.8 %collective-permute-start.5 = (f32[2,512,128]{2,1,0:T(8,128)}, f32[2,512,128]{2,1,0:T(8,128)}, u32[]{:S(2)}, u32[]{:S(2)}) collective-permute-start(f32[2,512,128]{2,1,0:T(8,128)} %slice.100), channel_id=1, source_target_pairs={{5,4},{6,5},{7,6},{13,12},{14,13},{15,14},{21,20},{22,21},{23,22},... | collective-permute-start | bytes 1572872 | tf_op jit(solution)/shard_map/ppermute | solution.py:561
  76.7 19.6 %collective-permute-start.6 = (f32[2,512,128]{2,1,0:T(8,128)}, f32[2,512,128]{2,1,0:T(8,128)S(1)}, u32[]{:S(2)}, u32[]{:S(2)}) collective-permute-start(f32[2,512,128]{2,1,0:T(8,128)} %collective-permute-done.1.right_b_hbm), channel_id=1, source_target_pairs={{4,0},{5,1},{6,2},{7,3},{12,8},{13,9},{14,10},{15,11},{20,16},{21,... | collective-permute-start | bytes 1572872 | tf_op jit(solution)/shard_map/ppermute | solution.py:561
  78.1 1.6 copy-start.2
  79.7 1.0 copy-start.3
  80.7 1.0 copy-start.4
  81.7 10.1 %copy-start = (s32[4,3]{1,0:T(4,128)}, s32[4,3]{1,0:T(4,128)S(1)}, u32[]{:S(2)}) copy-start(s32[4,3]{1,0:T(4,128)S(1)} %concatenate.15.meta) | copy-start | bytes 148
  91.9 2.7 %copy-start.5 = (f32[3,2,512,512]{3,2,1,0:T(8,128)}, f32[3,2,512,512]{3,2,1,0:T(8,128)S(1)}, u32[]{:S(2)}) copy-start(f32[3,2,512,512]{3,2,1,0:T(8,128)S(1)} %get-tuple-element.58.pupil_hbm) | copy-start | bytes 18874372
  94.5 1.7 copy-start.6
  96.2 0.8 copy-start.14
  116.3 20.0 %copy-start.9 = (f32[2,512,512]{2,1,0:T(8,128)S(1)}, f32[2,512,512]{2,1,0:T(8,128)}, u32[]{:S(2)}) copy-start(f32[2,512,512]{2,1,0:T(8,128)} %get-tuple-element.60) | copy-start | bytes 6291460
  116.3 32.8 %collective-permute-start.8 = (f32[2,512,384]{2,1,0:T(8,128)}, f32[2,512,384]{2,1,0:T(8,128)}, u32[]{:S(2)}, u32[]{:S(2)}) collective-permute-start(f32[2,512,384]{2,1,0:T(8,128)} %get-tuple-element.62), channel_id=1, source_target_pairs={{0,4},{1,5},{2,6},{3,7},{4,8},{5,9},{6,10},{7,11},{8,12},{9,13},{1... | collective-permute-start | bytes 4718600 | tf_op jit(solution)/shard_map/ppermute | solution.py:561
  132.8 3.5 %collective-permute-start.7 = (f32[512,512]{1,0:T(8,128)S(1)}, f32[512,512]{1,0:T(8,128)}, u32[]{:S(2)}, u32[]{:S(2)}) collective-permute-start(f32[512,512]{1,0:T(8,128)S(1)} %constant_dynamic-slice_fusion.6), channel_id=1, source_target_pairs={{0,4},{4,0},{8,12},{12,8},{16,20},{20,16},{24,28},{28,24},{1,5},{5... | collective-permute-start | bytes 3145736 | tf_op jit(solution)/shard_map/ppermute | solution.py:569
  132.9 7.7 %collective-permute-start.10 = (f32[2,512,128]{2,1,0:T(8,128)}, f32[2,512,128]{2,1,0:T(8,128)}, u32[]{:S(2)}, u32[]{:S(2)}) collective-permute-start(f32[2,512,128]{2,1,0:T(8,128)} %get-tuple-element.63), channel_id=1, source_target_pairs={{4,5},{5,6},{6,7},{12,13},{13,14},{14,15},{20,21},{21,22},{22,23},... | collective-permute-start | bytes 1572872 | tf_op jit(solution)/shard_map/ppermute | solution.py:561
  135.0 5.6 %collective-permute-start.9 = (f32[2,512,128]{2,1,0:T(8,128)}, f32[2,512,128]{2,1,0:T(8,128)}, u32[]{:S(2)}, u32[]{:S(2)}) collective-permute-start(f32[2,512,128]{2,1,0:T(8,128)} %get-tuple-element.63), channel_id=1, source_target_pairs={{0,4},{1,5},{2,6},{3,7},{8,12},{9,13},{10,14},{11,15},{16,20},{17,... | collective-permute-start | bytes 1572872 | tf_op jit(solution)/shard_map/ppermute | solution.py:561
  137.7 45.2 %copy-start.8 = (f32[2,512,512]{2,1,0:T(8,128)S(1)}, f32[2,512,512]{2,1,0:T(8,128)}, u32[]{:S(2)}) copy-start(f32[2,512,512]{2,1,0:T(8,128)} %get-tuple-element.70) | copy-start | bytes 6291460
  149.2 27.7 %collective-permute-start.11 = (f32[2,512,512]{2,1,0:T(8,128)}, f32[2,512,512]{2,1,0:T(8,128)}, u32[]{:S(2)}, u32[]{:S(2)}) collective-permute-start(f32[2,512,512]{2,1,0:T(8,128)} %get-tuple-element.64), channel_id=1, source_target_pairs={{0,4},{1,5},{2,6},{3,7},{4,8},{5,9},{6,10},{7,11},{8,12},{9,13},{1... | collective-permute-start | bytes 6291464 | tf_op jit(solution)/shard_map/ppermute | solution.py:561
  154.5 10.3 %collective-permute-start.12 = (f32[128,512]{1,0:T(8,128)}, f32[128,512]{1,0:T(8,128)}, u32[]{:S(2)}, u32[]{:S(2)}) collective-permute-start(f32[128,512]{1,0:T(8,128)} %get-tuple-element.76), channel_id=1, source_target_pairs={{0,1},{1,2},{2,3},{3,0},{4,5},{5,6},{6,7},{7,4},{8,9},{9,10},{10,1... | collective-permute-start | bytes 786440 | tf_op jit(solution)/shard_map/ppermute | solution.py:589
  154.5 20.5 %collective-permute-start.13 = (f32[128,512]{1,0:T(8,128)}, f32[128,512]{1,0:T(8,128)}, u32[]{:S(2)}, u32[]{:S(2)}) collective-permute-start(f32[128,512]{1,0:T(8,128)} %get-tuple-element.78), channel_id=1, source_target_pairs={{0,2},{1,3},{2,0},{3,1},{4,6},{5,7},{6,4},{7,5},{8,10},{9,11},{10,... | collective-permute-start | bytes 786440 | tf_op jit(solution)/shard_map/ppermute | solution.py:589
  156.0 19.0 %collective-permute-start.14 = (f32[128,512]{1,0:T(8,128)S(1)}, f32[128,512]{1,0:T(8,128)}, u32[]{:S(2)}, u32[]{:S(2)}) collective-permute-start(f32[128,512]{1,0:T(8,128)S(1)} %get-tuple-element.77), channel_id=1, source_target_pairs={{0,3},{1,0},{2,1},{3,2},{4,7},{5,4},{6,5},{7,6},{8,11},{9,8},{10,9... | collective-permute-start | bytes 786440 | tf_op jit(solution)/shard_map/ppermute | solution.py:589
  176.8 4.9 %collective-permute-start.15 = (f32[32,512]{1,0:T(8,128)S(1)}, f32[32,512]{1,0:T(8,128)S(1)}, u32[]{:S(2)}, u32[]{:S(2)}) collective-permute-start(f32[32,512]{1,0:T(8,128)S(1)} %get-tuple-element.79), channel_id=1, source_target_pairs={{0,8},{4,12},{8,16},{12,20},{16,24},{20,28},{24,0},{28,4},{1,9},{5... | collective-permute-start | bytes 196616 | tf_op jit(solution)/shard_map/ppermute | solution.py:589
  178.6 3.7 %collective-permute-start.16 = (f32[32,512]{1,0:T(8,128)S(1)}, f32[32,512]{1,0:T(8,128)S(1)}, u32[]{:S(2)}, u32[]{:S(2)}) collective-permute-start(f32[32,512]{1,0:T(8,128)S(1)} %get-tuple-element.81), channel_id=1, source_target_pairs={{0,16},{4,20},{8,24},{12,28},{16,0},{20,4},{24,8},{28,12},{1,17},{... | collective-permute-start | bytes 196616 | tf_op jit(solution)/shard_map/ppermute | solution.py:589
  178.6 3.7 %collective-permute-start.17 = (f32[32,512]{1,0:T(8,128)S(1)}, f32[32,512]{1,0:T(8,128)S(1)}, u32[]{:S(2)}, u32[]{:S(2)}) collective-permute-start(f32[32,512]{1,0:T(8,128)S(1)} %get-tuple-element.80), channel_id=1, source_target_pairs={{0,24},{4,28},{8,0},{12,4},{16,8},{20,12},{24,16},{28,20},{1,25},{... | collective-permute-start | bytes 196616 | tf_op jit(solution)/shard_map/ppermute | solution.py:589
  186.2 65.9 %collective-permute-start.19 = (f32[2,512,512]{2,1,0:T(8,128)}, f32[2,512,512]{2,1,0:T(8,128)S(1)}, u32[]{:S(2)}, u32[]{:S(2)}) collective-permute-start(f32[2,512,512]{2,1,0:T(8,128)} %maximum_add_fusion), channel_id=1, source_target_pairs={{0,1},{1,2},{2,3},{4,5},{5,6},{6,7},{8,9},{9,10},{10,11},{12,13},{... | collective-permute-start | bytes 6291464 | tf_op jit(solution)/shard_map/ppermute | solution.py:561
  197.7 54.4 %collective-permute-start.18 = (f32[2,512,512]{2,1,0:T(8,128)}, f32[2,512,512]{2,1,0:T(8,128)}, u32[]{:S(2)}, u32[]{:S(2)}) collective-permute-start(f32[2,512,512]{2,1,0:T(8,128)} %add_dynamic-update-slice_fusion.1), channel_id=1, source_target_pairs={{0,4},{1,5},{2,6},{3,7},{4,8},{5,9},{6,10},{7,11},{8,12},{9,13},{1... | collective-permute-start | bytes 6291464 | tf_op jit(solution)/shard_map/ppermute | solution.py:561
  246.0 10.5 %collective-permute-start.20 = (f32[512,512]{1,0:T(8,128)}, f32[512,512]{1,0:T(8,128)S(1)}, u32[]{:S(2)}, u32[]{:S(2)}) collective-permute-start(f32[512,512]{1,0:T(8,128)} %all-gather.2.cloned.1.call-done), channel_id=1, source_target_pairs={{0,4},{4,0},{8,12},{12,8},{16,20},{20,16},{24,28},{28,24},{1,5},{5... | collective-permute-start | bytes 3145736 | tf_op jit(solution)/shard_map/ppermute | solution.py:575
  252.1 4.4 %copy-start.10 = (f32[512,512]{1,0:T(8,128)S(1)}, f32[512,512]{1,0:T(8,128)}, u32[]{:S(2)}) copy-start(f32[512,512]{1,0:T(8,128)} %all-gather.2.cloned.1.call-done) | copy-start | bytes 3145732
Sparse Core Ops, SparseCore 0:
  183.1 62.8 all-gather.1

commit v9 on v8

--- a/solution.py
+++ b/solution.py
@@ -120,9 +120,11 @@
     right_a_hbm,
     right_b_hbm,
     lower_a_hbm,
-    lower_bc_hbm,
+    lower_b_hbm,
+    lower_c_hbm,
     corner_a_hbm,
-    corner_up_hbm,
+    corner_up_a_hbm,
+    corner_up_b_hbm,
     corner_side_hbm,
     amps_hbm,
     pupil_hbm,
@@ -132,7 +134,8 @@
     mat_t_lo_hbm,
     own_out,
     right_out,
-    lower_ab_out,
+    lower_a_out,
+    lower_b_out,
     lower_c_out,
     corner_a_out,
     corner_b_out,
@@ -165,40 +168,34 @@
     lanes = 128
     wide = side + lanes
     half = side // 2
-    cut = corner_a_hbm.shape[-1]
-
-    def pieces(buffer):
-        top, bottom = pl.ds(0, tile_rows), pl.ds(tile_rows, side)
-        return (
-            buffer.at[:, top, pl.ds(0, tile_cols)],
-            buffer.at[:, top, pl.ds(tile_cols, cut)],
-            buffer.at[:, top, pl.ds(tile_cols + cut, side - cut)],
-            buffer.at[:, bottom, pl.ds(0, cut)],
-            buffer.at[:, bottom, pl.ds(cut, tile_cols - cut)],
-            buffer.at[:, bottom, pl.ds(tile_cols, cut)],
-            buffer.at[:, bottom, pl.ds(tile_cols + cut, side - cut)],
-        )
-
-    odd = meta[slots, 0]
-    targets = pieces(region)
-    sources = (
-        tile_hbm,
-        right_a_hbm,
-        right_b_hbm,
-        lower_a_hbm,
-        lower_bc_hbm,
-        corner_a_hbm,
-    )
+    top, bottom = pl.ds(0, tile_rows), pl.ds(tile_rows, side)
+
+    def copy_in(src, row_range, start, sem):
+        dst = region.at[:, row_range, pl.ds(start, src.shape[-1])]
+        return pltpu.make_async_copy(src, dst, in_sems.at[sem])
+
     loads = [
-        pltpu.make_async_copy(src, dst, in_sems.at[n])
-        for n, (src, dst) in enumerate(zip(sources, targets))
+        copy_in(tile_hbm, top, 0, 0),
+        copy_in(right_a_hbm, top, tile_cols, 1),
+        copy_in(right_b_hbm, top, tile_cols + half, 2),
+        copy_in(lower_a_hbm, bottom, 0, 3),
+        copy_in(lower_b_hbm, bottom, half, 4),
+        copy_in(lower_c_hbm, bottom, side, 5),
+        copy_in(corner_a_hbm, bottom, tile_cols, 6),
     ]
     for load in loads:
         load.start()
-    from_side = pltpu.make_async_copy(corner_side_hbm, targets[6], in_sems.at[6])
-    from_below = pltpu.make_async_copy(corner_up_hbm, targets[6], in_sems.at[6])
+    from_side = copy_in(corner_side_hbm, bottom, tile_cols + half, 7)
+    from_below_a = copy_in(corner_up_a_hbm, bottom, tile_cols + half, 7)
+    from_below_b = copy_in(corner_up_b_hbm, bottom, tile_cols + half + half // 2, 7)
+    odd = meta[slots, 0]
     pl.when(odd == 1)(from_side.start)
-    pl.when(odd != 1)(from_below.start)
+
+    @pl.when(odd != 1)
+    def _():
+        from_below_a.start()
+        from_below_b.start()
+
     loads.append(from_side)
     late = (
         (mat_hi_hbm, mat_hi),
@@ -207,7 +204,7 @@
         (mat_t_lo_hbm, mat_t_lo),
     )
     late_loads = [
-        pltpu.make_async_copy(src, dst, in_sems.at[7 + n]) for n, (src, dst) in enumerate(late)
+        pltpu.make_async_copy(src, dst, in_sems.at[8 + n]) for n, (src, dst) in enumerate(late)
     ]
     for load in late_loads:
         load.start()
@@ -226,22 +223,24 @@
         for load in slot_loads(slot):
             load.start()
 
-    top, bottom = pl.ds(0, tile_rows), pl.ds(tile_rows, side)
     outs = (
-        (corner_a_out, bottom, pl.ds(tile_cols, cut)),
-        (corner_b_out, bottom, pl.ds(tile_cols + cut, side - cut)),
-        (lower_c_out, bottom, pl.ds(side, tile_cols - side)),
-        (lower_ab_out, bottom, pl.ds(0, side)),
-        (right_out, top, pl.ds(tile_cols, side)),
-        (own_out, top, pl.ds(0, tile_cols)),
+        (corner_a_out, bottom, tile_cols),
+        (corner_b_out, bottom, tile_cols + half),
+        (lower_a_out, bottom, 0),
+        (lower_b_out, bottom, half),
+        (lower_c_out, bottom, side),
+        (right_out, top, tile_cols),
+        (own_out, top, 0),
     )
     stores = [
-        pltpu.make_async_copy(grads.at[:, rows, cols], dst, out_sems.at[n])
-        for n, (dst, rows, cols) in enumerate(outs)
+        pltpu.make_async_copy(
+            grads.at[:, rows, pl.ds(start, dst.shape[-1])], dst, out_sems.at[n]
+        )
+        for n, (dst, rows, start) in enumerate(outs)
     ]
-    dpup_store = pltpu.make_async_copy(dpup, dpup_out, out_sems.at[6])
-    lower_stores = stores[:4]
-    upper_stores = stores[4:]
+    dpup_store = pltpu.make_async_copy(dpup, dpup_out, out_sems.at[7])
+    lower_stores = stores[:5]
+    upper_stores = stores[5:]
 
     zero_rows = 16
 
@@ -446,11 +445,10 @@
     anywhere = pl.BlockSpec(memory_space=pl.ANY)
     f32, bf16 = jnp.float32, jnp.bfloat16
     region = (2, tile_rows + side, tile_cols + side)
-    corner_a, corner_b, _ = parts[-3:]
-    lower_c = jax.ShapeDtypeStruct((2, side, tile_cols - side), f32)
+    lower_a, lower_b, lower_c, corner_a = parts[2:6]
     right = jax.ShapeDtypeStruct((2, tile_rows, side), f32)
-    lower_ab = jax.ShapeDtypeStruct((2, side, side), f32)
-    outs = (tile, right, lower_ab, lower_c, corner_a, corner_b, jax.ShapeDtypeStruct(pupils.shape[1:], f32))
+    dpup = jax.ShapeDtypeStruct(pupils.shape[1:], f32)
+    outs = (tile, right, lower_a, lower_b, lower_c, corner_a, corner_a, dpup)
     table = pltpu.VMEM(high.shape, bf16)
     return pl.pallas_call(
         slots_kernel,
@@ -475,9 +473,9 @@
             table,
             table,
             table,
-            pltpu.SemaphoreType.DMA((11,)),
+            pltpu.SemaphoreType.DMA((12,)),
             pltpu.SemaphoreType.DMA((2, slots)),
-            pltpu.SemaphoreType.DMA((7,)),
+            pltpu.SemaphoreType.DMA((8,)),
         ],
         compiler_params=pltpu.CompilerParams(vmem_limit_bytes=56 * 1024 * 1024),
         cost_estimate=pl.CostEstimate(
@@ -578,16 +576,37 @@
     return jnp.concatenate([first, second], axis=0)
 
 
+def stepped(value, axis, inner, step):
+    size = lax.axis_size(axis)
+    return lax.ppermute(value, axis, [(i, (i + step * inner) % size) for i in range(size)])
+
+
 def scatter(value, axis, inner):
-    size, own = lax.axis_size(axis), lax.axis_index(axis) // inner
-    members = size // inner
+    members, own = lax.axis_size(axis) // inner, lax.axis_index(axis) // inner
     rows = value.shape[0] // members
     total = lax.dynamic_slice_in_dim(value, own * rows, rows, 0)
     for step in range(1, members):
-        pairs = [(i, (i + step * inner) % size) for i in range(size)]
         piece = lax.dynamic_slice_in_dim(value, (own + step) % members * rows, rows, 0)
-        total = total + lax.ppermute(piece, axis, pairs)
+        total = total + stepped(piece, axis, inner, step)
     return total
+
+
+def gather(value, axis, inner):
+    members, own = lax.axis_size(axis) // inner, lax.axis_index(axis) // inner
+    rows = value.shape[0]
+    parts = [value] + [stepped(value, axis, inner, step) for step in range(1, members)]
+    out = jnp.zeros((members * rows,) + value.shape[1:], value.dtype)
+    for step, part in enumerate(parts):
+        out = lax.dynamic_update_slice_in_dim(out, part, (own - step) % members * rows, 0)
+    return out
+
+
+def sum_all(value, axis):
+    parts = [value] + [stepped(value, axis, 1, step) for step in range(1, lax.axis_size(axis))]
+    while len(parts) > 1:
+        middle = len(parts) // 2
+        parts = [a + b for a, b in zip(parts[:middle], parts[middle:])]
+    return parts[0]
 
 
 def after(value, *arrivals):
@@ -596,8 +615,9 @@
 
 def body(spectrum, pupil, amplitudes, offsets, live):
     side = pupil.shape[-1]
-    cut = 3 * side // 4
+    half = side // 2
     tile_rows, tile_cols = spectrum.shape[1:]
+    n_ty, n_tx = lax.axis_size("ty"), lax.axis_size("tx")
     own_ty, own_tx = lax.axis_index("ty"), lax.axis_index("tx")
     rows_local = offsets[:, 0] - own_ty * tile_rows
     cols_local = offsets[:, 1] - own_tx * tile_cols
@@ -610,19 +630,34 @@
     def up(i, j):
         return (i - 1, j)
 
-    lower_bc = send(spectrum[:, :side, cut:], up)
-    right_a = send(spectrum[:, :, :cut], left)
-    right_b = send(spectrum[:, :, cut:side], left)
-    lower_a = send(spectrum[:, :side, :cut], up)
+    def up_odd(i, j):
+        return (i - 1, j) if i % 2 else None
+
+    lower_b = send(spectrum[:, :side, half:side], up)
+    right_a = send(spectrum[:, :, :half], left)
+    right_b = send(spectrum[:, :, half:side], left)
+    lower_a = send(spectrum[:, :side, :half], up)
+    lower_c = send(spectrum[:, :side, side:], up)
     amps, pupils = prepare(meta, amplitudes, pupil)
+    lower_b, amps = lax.optimization_barrier((lower_b, amps))
+    corner_side = send(lower_b, lambda i, j: (i, j - 1) if i % 2 else None)
     corner_a = send(right_a[:, :side], up)
-    corner_side = send(lower_bc[:, :, : side - cut], lambda i, j: (i, j - 1) if i % 2 else None)
-    right_b_again = after(right_b, corner_side)
-    corner_up = send(right_b_again[:, :side], lambda i, j: (i - 1, j) if i % 2 else None)
-
-    parts = (right_a, right_b, lower_a, lower_bc, corner_a, corner_up, corner_side)
-    own_g, right_g, lower_ab_g, lower_c_g, corner_a_g, corner_b_g, dpup = slots_call(
-        meta, spectrum, parts, amps, pupils
+    corner_up_a = send(right_b[:, :side, : half // 2], up_odd)
+    corner_up_b = send(right_b[:, :side, half // 2 :], up_odd)
+
+    parts = (
+        right_a,
+        right_b,
+        lower_a,
+        lower_b,
+        lower_c,
+        corner_a,
+        corner_up_a,
+        corner_up_b,
+        corner_side,
+    )
+    own_g, right_g, lower_a_g, lower_b_g, lower_c_g, corner_a_g, corner_b_g, dpup = (
+        slots_call(meta, spectrum, parts, amps, pupils)
     )
 
     def down(i, j):
@@ -631,28 +666,25 @@
     def right(i, j):
         return (i, j + 1)
 
+    part = halve(dpup.reshape(-1, side), 1)
+    back_a = send(corner_a_g, down)
     back_side = send(corner_b_g, lambda i, j: (i, j + 1) if i % 2 else None)
-    back_a = send(corner_a_g, down)
     back_down = send(corner_b_g, lambda i, j: None if i % 2 else (i + 1, j))
-    n_ty, n_tx = lax.axis_size("ty"), lax.axis_size("tx")
-    part = halve(dpup.reshape(-1, side), 1)
-    part, lower_c_g, back_a, back_down, back_side = lax.optimization_barrier(
-        (part, lower_c_g, back_a, back_down, back_side)
+    part, back_a, back_side, back_down = lax.optimization_barrier(
+        (part, back_a, back_side, back_down)
     )
-    lower_c = send(lower_c_g, down)
-    over_tx = scatter(part, "tx", 1)
-    right_total = right_g + jnp.concatenate([back_a, back_down], axis=2)
-    right_back = send(after(right_total, over_tx), right)
-    part = scatter(after(over_tx, lower_c), "ty", 2)
-    part = part * (1.0 / math.sqrt(n_ty * n_tx))
-    lower_ab = send(lower_ab_g.at[:, :, cut:].add(after(back_side, part)), down)
-    groups = [
-        [(2 * k + core) * n_tx + j for j in range(n_tx) for k in range(n_ty // 2)]
-        for core in range(2)
-    ]
-    part = lax.all_gather(part, ("ty", "tx"), axis_index_groups=groups, axis=0, tiled=True)
+    part = scatter(part, "ty", 2)
+    lower_a = send(after(lower_a_g, part), down)
+    lower_c = send(after(lower_c_g, part), down)
+    part = sum_all(part, "tx") * (1.0 / math.sqrt(n_ty * n_tx))
+    right_g = right_g + jnp.concatenate([back_a, back_down], axis=2)
+    right_back = send(after(right_g, part), right)
+    part = gather(after(part, lower_a, lower_c), "ty", 2)
+    lower_b = send(after(lower_b_g + back_side, part), down)
     spec_grad = own_g.at[:, :, side:].add(lower_c)
-    spec_grad = spec_grad.at[:, :, :side].add(lower_ab + right_back)
+    spec_grad = spec_grad.at[:, :, :half].add(lower_a)
+    part, spec_grad = lax.optimization_barrier((part, spec_grad))
+    spec_grad = spec_grad.at[:, :, :side].add(right_back.at[:, :, half:].add(lower_b))
     return spec_grad, double(part, 1).reshape(pupil.shape)
 
 

time: 267 us -> 227 us (0.85)
  waiting for transfers between devices: 128 us -> 74.5 us
  starting transfers between devices: 56.5 us -> 76.7 us
  between operations: 14.4 us -> 1.2 us
  other arithmetic: 18.8 us -> 22.9 us
    all_gather x1 -> x0, waiting for transfers between devices: 44.3 us -> none  [body(): lax.all_gather(part, ('ty', 'tx'), axis_index_groups=groups, axis=0, tile...]
    ppermute x13 -> x16, waiting for transfers between devices: 64.2 us -> 52.9 us  [send(): return lax.ppermute(array, ('ty', 'tx'), along(rule, sizes))]
    ppermute x13 -> x16, starting transfers between devices: 47.9 us -> 58.8 us  [send(): return lax.ppermute(array, ('ty', 'tx'), along(rule, sizes))]
    ppermute x6 -> x9, starting transfers between devices: 6.47 us -> 17.2 us  [stepped(): lax.ppermute(value, axis, [(i, (i + step * inner) % size) for i in range(...]
    add x2 -> x3, other arithmetic: 4.4 us -> 6.82 us  [the longest x1 3.3 us: body(): right_g = right_g + jnp.concatenate([back_a, back_down], axis=2)]
    ppermute x6 -> x9, waiting for transfers between devices: 19.5 us -> 21.6 us  [stepped(): lax.ppermute(value, axis, [(i, (i + step * inner) % size) for i in range(...]
    scatter-add x2 -> x3, other arithmetic: 6.48 us -> 7.54 us  [the longest x1 3.39 us: body(): spec_grad.at[:, :, :side].add(right_back.at[:, :, half:].add(lower_b))]
    slice x4 -> x3, local copies, waits for them, and re-layouts: 5.09 us -> 5.96 us  [the longest x1 3.15 us: body(): right_b = send(spectrum[:, :, half:side], left)]
  transfers between devices with their start and end apart: 22 -> 27, of which waited for: 11 -> 10; matrix products, arithmetic and copies ran while one was open for 8% -> 9% of each run, Pallas kernels for 4% -> 5%
where the time goes in v9:
time: 227 us; the launch traced here: 223 us
  starting transfers between devices  76.7 us (34%)
  waiting for transfers between devices  74.5 us (33%)
  Pallas kernels  29.4 us (13%)
  other arithmetic  22.9 us (10%)
  local copies, waits for them, and re-layouts  18.2 us (8%)
    ppermute x16, starting transfers between devices, send(): return lax.ppermute(array, ('ty', 'tx'), along(rule, sizes))  58.8 us
    ppermute x16, waiting for transfers between devices, send(): return lax.ppermute(array, ('ty', 'tx'), along(rule, sizes))  52.9 us
    ppermute x9, waiting for transfers between devices, stepped(): lax.ppermute(value, axis, [(i, (i + step * inner) % size) for i in range(...  21.6 us
    pallas_call x1, Pallas kernels, slots_call(): pl.pallas_call(slots_kernel, out_shape=[jax.ShapeDtypeStruct(x.shape, f32...  19.3 us
    ppermute x9, starting transfers between devices, stepped(): lax.ppermute(value, axis, [(i, (i + step * inner) % size) for i in range(...  17.2 us
    pallas_call x1, Pallas kernels, prepare(): pl.pallas_call(prepare_kernel, grid=(slots,), out_shape=[jax.ShapeDtypeSt...  10.1 us
    unnamed x32, local copies, waits for them, and re-layouts  9.65 us
  transfers between devices with their start and end apart: 27, of which 10 were waited for; matrix products, arithmetic and copies ran while one was open for 9% of the time, Pallas kernels for 5%

profile of v9, /device:TPU:1, one launch (start us, length us, event | category | flops | bytes accessed | tf_op | source)
XLA Modules:
  0.0 223.0 jit_solution(8003067881560014043)
XLA Ops:
  0.6 3.2 %fusion.2 = (f32[2,512,256]{2,1,0:T(8,128)}, f32[2,512,256]{2,1,0:T(8,128)}) fusion(f32[2,512,1024]{2,1,0:T(8,128)} %tile_hbm.1), kind=kLoop, calls=%fused_computation.24 | loop fusion | bytes 4194304 | tf_op jit(solution)/shard_map/slice | solution.py:638
  3.8 2.0 collective-permute-start.3
  5.8 1.6 collective-permute-start
  7.4 1.5 slice.123
  8.9 1.9 collective-permute-start.4
  10.8 1.3 collective-permute-start.1
  12.1 1.9 collective-permute-start.2
  14.1 0.1 copy.16
  14.2 0.1 copy.17
  14.3 0.1 copy.15
  14.4 0.1 pad_add_fusion
  14.5 1.6 copy-done.2
  16.1 1.0 copy-done.3
  17.1 1.0 copy-done.4
  18.1 10.1 %prepare.1 = (f32[3,512,512]{2,1,0:T(8,128)S(1)}, f32[3,2,512,512]{3,2,1,0:T(8,128)S(1)}) custom-call(s32[4,3]{1,0:T(4,128)S(1)} %concatenate.17.meta, f32[3,512,512]{2,1,0:T(8,128)S(1)} %copy-done.1, f32[2,512,512]{2,1,0:T(8,128)S(1)} %copy-done.2, bf16[512,512]{1,0:T(8,128)(2,1)S(1)} %copy-done.3, bf16[512,512]{1,0:T(8,128)(2,1)S(1)} %copy-done.4), custom_call_target="tpu_custom_call" | custom-call | flops 4831838208 | bytes 18874368 | tf_op jit(solution)/shard_map/prepare/pallas_call | solution.py:523
  28.3 2.7 %copy-done.5 = f32[3,2,512,512]{3,2,1,0:T(8,128)} copy-done((f32[3,2,512,512]{3,2,1,0:T(8,128)}, f32[3,2,512,512]{3,2,1,0:T(8,128)S(1)}, u32[]{:S(2)}) %copy-start.5) | copy-done | bytes 6291480
  30.9 1.7 copy-done.6
  32.7 1.3 collective-permute-start.8
  33.9 0.7 collective-permute-done.right_a_hbm
  34.6 1.9 collective-permute-start.5
  36.6 19.9 %collective-permute-done.1.right_b_hbm = f32[2,512,256]{2,1,0:T(8,128)} collective-permute-done((f32[2,512,256]{2,1,0:T(8,128)}, f32[2,512,256]{2,1,0:T(8,128)}, u32[]{:S(2)}, u32[]{:S(2)}) %collective-permute-start.1) | collective-permute-done | bytes 1048608 | tf_op jit(solution)/shard_map/ppermute | solution.py:559
  56.5 1.3 fusion.3
  57.8 3.1 %collective-permute-start.6 = (f32[2,512,128]{2,1,0:T(8,128)S(1)}, f32[2,512,128]{2,1,0:T(8,128)}, u32[]{:S(2)}, u32[]{:S(2)}) collective-permute-start(f32[2,512,128]{2,1,0:T(8,128)S(1)} %get-tuple-element.104), channel_id=1, source_target_pairs={{4,0},{5,1},{6,2},{7,3},{12,8},{13,9},{14,10},{15,11},{20,16},{21,... | collective-permute-start | bytes 1572872 | tf_op jit(solution)/shard_map/ppermute | solution.py:559
  60.8 2.1 collective-permute-start.7
  62.9 0.8 collective-permute-done.7.corner_up_b_hbm
  63.8 3.8 %collective-permute-done.8.corner_side_hbm = f32[2,512,256]{2,1,0:T(8,128)S(1)} collective-permute-done((f32[2,512,256]{2,1,0:T(8,128)}, f32[2,512,256]{2,1,0:T(8,128)S(1)}, u32[]{:S(2)}, u32[]{:S(2)}) %collective-permute-start.8) | collective-permute-done | bytes 1048608 | tf_op jit(solution)/shard_map/ppermute | solution.py:559
  67.6 1.0 copy-done.13
  68.6 0.4 copy-done.14
  69.0 19.3 %slots.1 = (f32[2,512,1024]{2,1,0:T(8,128)}, f32[2,512,512]{2,1,0:T(8,128)}, f32[2,512,256]{2,1,0:T(8,128)}, f32[2,512,256]{2,1,0:T(8,128)}, f32[2,512,512]{2,1,...) custom-call(s32[4,3]{1,0:T(4,128)} %copy-done, f32[2,512,1024]{2,1,0:T(8,128)} %tile_hbm.1, ...), custom_call_target="tpu_custom_call" | custom-call | flops 9663676416 | bytes 41943040 | tf_op jit(solution)/shard_map/slots/pallas_call | solution.py:453
  88.3 1.4 constant_dynamic-slice_fusion.3
  89.8 11.9 %collective-permute-start.10 = (f32[2,512,256]{2,1,0:T(8,128)}, f32[2,512,256]{2,1,0:T(8,128)}, u32[]{:S(2)}, u32[]{:S(2)}) collective-permute-start(f32[2,512,256]{2,1,0:T(8,128)} %get-tuple-element.78), channel_id=1, source_target_pairs={{0,4},{1,5},{2,6},{3,7},{4,8},{5,9},{6,10},{7,11},{8,12},{9,13},{1... | collective-permute-start | bytes 3145736 | tf_op jit(solution)/shard_map/ppermute | solution.py:559
  101.8 12.1 %collective-permute-start.11 = (f32[2,512,256]{2,1,0:T(8,128)}, f32[2,512,256]{2,1,0:T(8,128)}, u32[]{:S(2)}, u32[]{:S(2)}) collective-permute-start(f32[2,512,256]{2,1,0:T(8,128)} %get-tuple-element.79), channel_id=1, source_target_pairs={{4,5},{5,6},{6,7},{12,13},{13,14},{14,15},{20,21},{21,22},{22,23},... | collective-permute-start | bytes 3145736 | tf_op jit(solution)/shard_map/ppermute | solution.py:559
  113.8 1.3 collective-permute-start.12
  115.2 1.4 dynamic-slice_add_fusion
  116.7 8.2 %collective-permute-done.11 = f32[2,512,256]{2,1,0:T(8,128)} collective-permute-done((f32[2,512,256]{2,1,0:T(8,128)}, f32[2,512,256]{2,1,0:T(8,128)}, u32[]{:S(2)}, u32[]{:S(2)}) %collective-permute-start.11) | collective-permute-done | bytes 1048608 | tf_op jit(solution)/shard_map/ppermute | solution.py:559
  124.9 0.9 constant_dynamic-slice_fusion.2
  125.8 1.2 collective-permute-start.13
  126.9 1.2 collective-permute-start.15
  128.1 4.2 %collective-permute-done.13 = f32[128,512]{1,0:T(8,128)} collective-permute-done((f32[128,512]{1,0:T(8,128)}, f32[128,512]{1,0:T(8,128)}, u32[]{:S(2)}, u32[]{:S(2)}) %collective-permute-start.13) | collective-permute-done | bytes 262176 | tf_op jit(solution)/shard_map/ppermute | solution.py:581
  132.4 2.7 %collective-permute-done.14 = f32[128,512]{1,0:T(8,128)} collective-permute-done((f32[128,512]{1,0:T(8,128)}, f32[128,512]{1,0:T(8,128)}, u32[]{:S(2)}, u32[]{:S(2)}) %collective-permute-start.14) | collective-permute-done | bytes 262176 | tf_op jit(solution)/shard_map/ppermute | solution.py:581
  135.1 1.2 add_add_fusion
  136.3 1.9 collective-permute-start.20
  138.2 3.4 %collective-permute-start.19 = (f32[2,512,256]{2,1,0:T(8,128)}, f32[2,512,256]{2,1,0:T(8,128)}, u32[]{:S(2)}, u32[]{:S(2)}) collective-permute-start(f32[2,512,256]{2,1,0:T(8,128)} %get-tuple-element.82), channel_id=1, source_target_pairs={{0,4},{1,5},{2,6},{3,7},{4,8},{5,9},{6,10},{7,11},{8,12},{9,13},{1... | collective-permute-start | bytes 3145736 | tf_op jit(solution)/shard_map/ppermute | solution.py:559
  141.7 7.9 %collective-permute-start.16 = (f32[128,512]{1,0:T(8,128)S(1)}, f32[128,512]{1,0:T(8,128)S(1)}, u32[]{:S(2)}, u32[]{:S(2)}) collective-permute-start(f32[128,512]{1,0:T(8,128)S(1)} %add_add_fusion), channel_id=1, source_target_pairs={{0,2},{1,3},{2,0},{3,1},{4,6},{5,7},{6,4},{7,5},{8,10},{9,11},{10,... | collective-permute-start | bytes 786440 | tf_op jit(solution)/shard_map/ppermute | solution.py:581
  149.6 3.3 %collective-permute-start.18 = (f32[128,512]{1,0:T(8,128)S(1)}, f32[128,512]{1,0:T(8,128)S(1)}, u32[]{:S(2)}, u32[]{:S(2)}) collective-permute-start(f32[128,512]{1,0:T(8,128)S(1)} %add_add_fusion), channel_id=1, source_target_pairs={{0,3},{1,0},{2,1},{3,2},{4,7},{5,4},{6,5},{7,6},{8,11},{9,8},{10,9... | collective-permute-start | bytes 786440 | tf_op jit(solution)/shard_map/ppermute | solution.py:581
  152.9 3.3 %maximum_add_fusion = f32[2,512,512]{2,1,0:T(8,128)} fusion(f32[2,512,512]{2,1,0:T(8,128)S(1)} %copy-done.8, f32[2,512,256]{2,1,0:T(8,128)} %collective-permute-done.12, f32[2,512,256]{2,1,0:T(8,128)} %collective-permute-done.10), kind=kLoop, calls=%fused_computation | loop fusion | flops 1048576 | bytes 6291456 | tf_op jit(solution)/shard_map/add | solution.py:680
  156.2 10.4 %collective-permute-done.16 = f32[128,512]{1,0:T(8,128)S(1)} collective-permute-done((f32[128,512]{1,0:T(8,128)S(1)}, f32[128,512]{1,0:T(8,128)S(1)}, u32[]{:S(2)}, u32[]{:S(2)}) %collective-permute-start.16) | collective-permute-done | bytes 262176 | tf_op jit(solution)/shard_map/ppermute | solution.py:581
  166.5 0.1 add_multiply_fusion
  166.7 7.9 %collective-permute-start.24 = (f32[2,512,512]{2,1,0:T(8,128)}, f32[2,512,512]{2,1,0:T(8,128)S(1)}, u32[]{:S(2)}, u32[]{:S(2)}) collective-permute-start(f32[2,512,512]{2,1,0:T(8,128)} %maximum_add_fusion), channel_id=1, source_target_pairs={{0,1},{1,2},{2,3},{4,5},{5,6},{6,7},{8,9},{9,10},{10,11},{12,13},{... | collective-permute-start | bytes 6291464 | tf_op jit(solution)/shard_map/ppermute | solution.py:559
  174.6 1.1 collective-permute-start.21
  175.7 0.3 collective-permute-start.22
  176.0 2.3 %collective-permute-start.23 = (f32[128,512]{1,0:T(8,128)S(1)}, f32[128,512]{1,0:T(8,128)S(1)}, u32[]{:S(2)}, u32[]{:S(2)}) collective-permute-start(f32[128,512]{1,0:T(8,128)S(1)} %add_multiply_fusion), channel_id=1, source_target_pairs={{0,24},{4,28},{8,0},{12,4},{16,8},{20,12},{24,16},{28,20},{1,25},{... | collective-permute-start | bytes 786440 | tf_op jit(solution)/shard_map/ppermute | solution.py:581
  178.3 4.0 %add_dynamic-update-slice_fusion.1 = f32[2,512,1024]{2,1,0:T(8,128)} fusion(f32[2,512,1024]{2,1,0:T(8,128)} %get-tuple-element.86, f32[2,512,512]{2,1,0:T(8,128)} %collective-permute-done.20), kind=kLoop, calls=%fused_computation.3 | loop fusion | flops 524288 | bytes 6291456 | tf_op jit(solution)/shard_map/scatter-add | solution.py:684
  182.3 2.7 %fusion.1 = f32[2,512,1024]{2,1,0:T(8,128)} fusion(f32[2,512,1024]{2,1,0:T(8,128)} %add_dynamic-update-slice_fusion.1, f32[2,512,256]{2,1,0:T(8,128)} %collective-permute-done.19), kind=kLoop, calls=%fused_computation.7 | loop fusion | flops 262144 | bytes 3145728 | tf_op jit(solution)/shard_map/scatter-add | solution.py:685
  185.0 0.1 broadcast_in_dim.4
  185.2 4.2 %collective-permute-done.22 = f32[128,512]{1,0:T(8,128)S(1)} collective-permute-done((f32[128,512]{1,0:T(8,128)S(1)}, f32[128,512]{1,0:T(8,128)S(1)}, u32[]{:S(2)}, u32[]{:S(2)}) %collective-permute-start.22) | collective-permute-done | bytes 262176 | tf_op jit(solution)/shard_map/ppermute | solution.py:581
  189.5 0.6 collective-permute-start.26
  190.1 2.3 %add.159 = f32[2,512,256]{2,1,0:T(8,128)} add(f32[2,512,256]{2,1,0:T(8,128)S(1)} %copy-done.10, f32[2,512,256]{2,1,0:T(8,128)} %collective-permute-done.11) | non-fusion elementwise | flops 262144 | bytes 3145728 | tf_op jit(solution)/shard_map/add | solution.py:683
  192.5 3.3 %collective-permute-start.25 = (f32[2,512,256]{2,1,0:T(8,128)}, f32[2,512,256]{2,1,0:T(8,128)}, u32[]{:S(2)}, u32[]{:S(2)}) collective-permute-start(f32[2,512,256]{2,1,0:T(8,128)} %add.159), channel_id=1, source_target_pairs={{0,4},{1,5},{2,6},{3,7},{4,8},{5,9},{6,10},{7,11},{8,12},{9,13},{1... | collective-permute-start | bytes 3145736 | tf_op jit(solution)/shard_map/ppermute | solution.py:559
  195.8 1.5 broadcast_select_fusion.1
  197.2 1.5 pad_maximum_fusion
  198.7 19.4 %collective-permute-done.24 = f32[2,512,512]{2,1,0:T(8,128)S(1)} collective-permute-done((f32[2,512,512]{2,1,0:T(8,128)}, f32[2,512,512]{2,1,0:T(8,128)S(1)}, u32[]{:S(2)}, u32[]{:S(2)}) %collective-permute-start.24) | collective-permute-done | bytes 2097184 | tf_op jit(solution)/shard_map/ppermute | solution.py:559
  218.1 1.5 fusion
  219.6 3.4 %add_dynamic-update-slice_fusion = f32[2,512,1024]{2,1,0:T(8,128)} fusion(f32[2,512,1024]{2,1,0:T(8,128)} %fusion.1, f32[2,512,512]{2,1,0:T(8,128)S(1)} %fusion), kind=kLoop, calls=%fused_computation.2 | loop fusion | flops 524288 | bytes 6291456 | tf_op jit(solution)/shard_map/scatter-add | solution.py:687
  (50 shorter events, 0.3 us)
Async XLA Ops:
  0.6 6.7 %copy-start.7 = (f32[2,512,1024]{2,1,0:T(8,128)S(1)}, f32[2,512,1024]{2,1,0:T(8,128)}, u32[]{:S(2)}) copy-start(f32[2,512,1024]{2,1,0:T(8,128)} %tile_hbm.1) | copy-start | bytes 12582916
  3.8 28.9 %collective-permute-start.3 = (f32[2,512,256]{2,1,0:T(8,128)}, f32[2,512,256]{2,1,0:T(8,128)}, u32[]{:S(2)}, u32[]{:S(2)}) collective-permute-start(f32[2,512,256]{2,1,0:T(8,128)} %get-tuple-element.96), channel_id=1, source_target_pairs={{4,0},{5,1},{6,2},{7,3},{8,4},{9,5},{10,6},{11,7},{12,8},{13,9},{1... | collective-permute-start | bytes 3145736 | tf_op jit(solution)/shard_map/ppermute | solution.py:559
  5.8 8.3 %copy-start.11 = (s32[3,2]{0,1:T(2,128)S(1)}, s32[3,2]{0,1:T(2,128)}, u32[]{:S(2)}) copy-start(s32[3,2]{0,1:T(2,128)} %param.22) | copy-start | bytes 76
  5.8 8.5 %copy-start.12 = (s32[3]{0:T(128)S(1)}, s32[3]{0:T(128)}, u32[]{:S(2)}) copy-start(s32[3]{0:T(128)} %param.23) | copy-start | bytes 40
  5.8 8.7 %copy-start.1 = (f32[3,512,512]{2,1,0:T(8,128)S(1)}, f32[3,512,512]{2,1,0:T(8,128)}, u32[]{:S(2)}) copy-start(f32[3,512,512]{2,1,0:T(8,128)} %amps.1) | copy-start | bytes 9437188
  5.8 28.9 %collective-permute-start = (f32[2,512,256]{2,1,0:T(8,128)}, f32[2,512,256]{2,1,0:T(8,128)}, u32[]{:S(2)}, u32[]{:S(2)}) collective-permute-start(f32[2,512,256]{2,1,0:T(8,128)} %get-tuple-element.97), channel_id=1, source_target_pairs={{1,0},{2,1},{3,2},{5,4},{6,5},{7,6},{9,8},{10,9},{11,10},{13,12},{... | collective-permute-start | bytes 3145736 | tf_op jit(solution)/shard_map/ppermute | solution.py:559
  8.9 58.7 %collective-permute-start.4 = (f32[2,512,512]{2,1,0:T(8,128)}, f32[2,512,512]{2,1,0:T(8,128)}, u32[]{:S(2)}, u32[]{:S(2)}) collective-permute-start(f32[2,512,512]{2,1,0:T(8,128)} %slice.123), channel_id=1, source_target_pairs={{4,0},{5,1},{6,2},{7,3},{8,4},{9,5},{10,6},{11,7},{12,8},{13,9},{1... | collective-permute-start | bytes 6291464 | tf_op jit(solution)/shard_map/ppermute | solution.py:559
  10.8 45.6 %collective-permute-start.1 = (f32[2,512,256]{2,1,0:T(8,128)}, f32[2,512,256]{2,1,0:T(8,128)}, u32[]{:S(2)}, u32[]{:S(2)}) collective-permute-start(f32[2,512,256]{2,1,0:T(8,128)} %get-tuple-element.96), channel_id=1, source_target_pairs={{1,0},{2,1},{3,2},{5,4},{6,5},{7,6},{9,8},{10,9},{11,10},{13,12},{... | collective-permute-start | bytes 3145736 | tf_op jit(solution)/shard_map/ppermute | solution.py:559
  12.1 48.7 %collective-permute-start.2 = (f32[2,512,256]{2,1,0:T(8,128)}, f32[2,512,256]{2,1,0:T(8,128)}, u32[]{:S(2)}, u32[]{:S(2)}) collective-permute-start(f32[2,512,256]{2,1,0:T(8,128)} %get-tuple-element.97), channel_id=1, source_target_pairs={{4,0},{5,1},{6,2},{7,3},{8,4},{9,5},{10,6},{11,7},{12,8},{13,9},{1... | collective-permute-start | bytes 3145736 | tf_op jit(solution)/shard_map/ppermute | solution.py:559
  14.5 1.6 copy-start.2
  16.1 1.0 copy-start.3
  17.1 1.0 copy-start.4
  18.1 10.1 %copy-start = (s32[4,3]{1,0:T(4,128)}, s32[4,3]{1,0:T(4,128)S(1)}, u32[]{:S(2)}) copy-start(s32[4,3]{1,0:T(4,128)S(1)} %concatenate.17.meta) | copy-start | bytes 148
  28.2 2.7 %copy-start.5 = (f32[3,2,512,512]{3,2,1,0:T(8,128)}, f32[3,2,512,512]{3,2,1,0:T(8,128)S(1)}, u32[]{:S(2)}) copy-start(f32[3,2,512,512]{3,2,1,0:T(8,128)S(1)} %get-tuple-element.76.pupil_hbm) | copy-start | bytes 18874372
  30.9 1.7 copy-start.6
  32.7 35.0 %collective-permute-start.8 = (f32[2,512,256]{2,1,0:T(8,128)}, f32[2,512,256]{2,1,0:T(8,128)S(1)}, u32[]{:S(2)}, u32[]{:S(2)}) collective-permute-start(f32[2,512,256]{2,1,0:T(8,128)} %collective-permute-done.3.lower_b_hbm), channel_id=1, source_target_pairs={{5,4},{6,5},{7,6},{13,12},{14,13},{15,14},{21,20},{22,21},{23,22},... | collective-permute-start | bytes 3145736 | tf_op jit(solution)/shard_map/ppermute | solution.py:559
  34.6 33.0 %collective-permute-start.5 = (f32[2,512,256]{2,1,0:T(8,128)}, f32[2,512,256]{2,1,0:T(8,128)S(1)}, u32[]{:S(2)}, u32[]{:S(2)}) collective-permute-start(f32[2,512,256]{2,1,0:T(8,128)} %collective-permute-done.right_a_hbm), channel_id=1, source_target_pairs={{4,0},{5,1},{6,2},{7,3},{8,4},{9,5},{10,6},{11,7},{12,8},{13,9},{1... | collective-permute-start | bytes 3145736 | tf_op jit(solution)/shard_map/ppermute | solution.py:559
  57.8 5.2 %collective-permute-start.6 = (f32[2,512,128]{2,1,0:T(8,128)S(1)}, f32[2,512,128]{2,1,0:T(8,128)}, u32[]{:S(2)}, u32[]{:S(2)}) collective-permute-start(f32[2,512,128]{2,1,0:T(8,128)S(1)} %get-tuple-element.104), channel_id=1, source_target_pairs={{4,0},{5,1},{6,2},{7,3},{12,8},{13,9},{14,10},{15,11},{20,16},{21,... | collective-permute-start | bytes 1572872 | tf_op jit(solution)/shard_map/ppermute | solution.py:559
  60.8 2.9 %collective-permute-start.7 = (f32[2,512,128]{2,1,0:T(8,128)S(1)}, f32[2,512,128]{2,1,0:T(8,128)}, u32[]{:S(2)}, u32[]{:S(2)}) collective-permute-start(f32[2,512,128]{2,1,0:T(8,128)S(1)} %get-tuple-element.103), channel_id=1, source_target_pairs={{4,0},{5,1},{6,2},{7,3},{12,8},{13,9},{14,10},{15,11},{20,16},{21,... | collective-permute-start | bytes 1572872 | tf_op jit(solution)/shard_map/ppermute | solution.py:559
  67.6 1.0 copy-start.13
  67.6 1.4 copy-start.14
  88.3 26.9 %copy-start.9 = (f32[2,512,512]{2,1,0:T(8,128)S(1)}, f32[2,512,512]{2,1,0:T(8,128)}, u32[]{:S(2)}) copy-start(f32[2,512,512]{2,1,0:T(8,128)} %get-tuple-element.77) | copy-start | bytes 6291460
  89.8 25.4 %collective-permute-start.9 = (f32[512,512]{1,0:T(8,128)S(1)}, f32[512,512]{1,0:T(8,128)}, u32[]{:S(2)}, u32[]{:S(2)}) collective-permute-start(f32[512,512]{1,0:T(8,128)S(1)} %constant_dynamic-slice_fusion.3), channel_id=1, source_target_pairs={{0,4},{4,0},{8,12},{12,8},{16,20},{20,16},{24,28},{28,24},{1,5},{5... | collective-permute-start | bytes 3145736 | tf_op jit(solution)/shard_map/ppermute | solution.py:567
  89.8 26.8 %collective-permute-start.10 = (f32[2,512,256]{2,1,0:T(8,128)}, f32[2,512,256]{2,1,0:T(8,128)}, u32[]{:S(2)}, u32[]{:S(2)}) collective-permute-start(f32[2,512,256]{2,1,0:T(8,128)} %get-tuple-element.78), channel_id=1, source_target_pairs={{0,4},{1,5},{2,6},{3,7},{4,8},{5,9},{6,10},{7,11},{8,12},{9,13},{1... | collective-permute-start | bytes 3145736 | tf_op jit(solution)/shard_map/ppermute | solution.py:559
  101.8 23.1 %collective-permute-start.11 = (f32[2,512,256]{2,1,0:T(8,128)}, f32[2,512,256]{2,1,0:T(8,128)}, u32[]{:S(2)}, u32[]{:S(2)}) collective-permute-start(f32[2,512,256]{2,1,0:T(8,128)} %get-tuple-element.79), channel_id=1, source_target_pairs={{4,5},{5,6},{6,7},{12,13},{13,14},{14,15},{20,21},{21,22},{22,23},... | collective-permute-start | bytes 3145736 | tf_op jit(solution)/shard_map/ppermute | solution.py:559
  113.8 11.1 %collective-permute-start.12 = (f32[2,512,256]{2,1,0:T(8,128)}, f32[2,512,256]{2,1,0:T(8,128)}, u32[]{:S(2)}, u32[]{:S(2)}) collective-permute-start(f32[2,512,256]{2,1,0:T(8,128)} %get-tuple-element.79), channel_id=1, source_target_pairs={{0,4},{1,5},{2,6},{3,7},{8,12},{9,13},{10,14},{11,15},{16,20},{17,... | collective-permute-start | bytes 3145736 | tf_op jit(solution)/shard_map/ppermute | solution.py:559
  116.7 36.2 %copy-start.8 = (f32[2,512,512]{2,1,0:T(8,128)S(1)}, f32[2,512,512]{2,1,0:T(8,128)}, u32[]{:S(2)}) copy-start(f32[2,512,512]{2,1,0:T(8,128)} %get-tuple-element.88) | copy-start | bytes 6291460
  125.8 6.6 %collective-permute-start.13 = (f32[128,512]{1,0:T(8,128)}, f32[128,512]{1,0:T(8,128)}, u32[]{:S(2)}, u32[]{:S(2)}) collective-permute-start(f32[128,512]{1,0:T(8,128)} %get-tuple-element.100), channel_id=1, source_target_pairs={{0,8},{4,12},{8,16},{12,20},{16,24},{20,28},{24,0},{28,4},{1,9},{5... | collective-permute-start | bytes 786440 | tf_op jit(solution)/shard_map/ppermute | solution.py:581
  126.9 8.1 %collective-permute-start.14 = (f32[128,512]{1,0:T(8,128)}, f32[128,512]{1,0:T(8,128)}, u32[]{:S(2)}, u32[]{:S(2)}) collective-permute-start(f32[128,512]{1,0:T(8,128)} %get-tuple-element.102), channel_id=1, source_target_pairs={{0,16},{4,20},{8,24},{12,28},{16,0},{20,4},{24,8},{28,12},{1,17},{... | collective-permute-start | bytes 786440 | tf_op jit(solution)/shard_map/ppermute | solution.py:581
  126.9 8.1 %collective-permute-start.15 = (f32[128,512]{1,0:T(8,128)S(1)}, f32[128,512]{1,0:T(8,128)}, u32[]{:S(2)}, u32[]{:S(2)}) collective-permute-start(f32[128,512]{1,0:T(8,128)S(1)} %get-tuple-element.101), channel_id=1, source_target_pairs={{0,24},{4,28},{8,0},{12,4},{16,8},{20,12},{24,16},{28,20},{1,25},{... | collective-permute-start | bytes 786440 | tf_op jit(solution)/shard_map/ppermute | solution.py:581
  136.3 38.3 %collective-permute-start.20 = (f32[2,512,512]{2,1,0:T(8,128)}, f32[2,512,512]{2,1,0:T(8,128)}, u32[]{:S(2)}, u32[]{:S(2)}) collective-permute-start(f32[2,512,512]{2,1,0:T(8,128)} %get-tuple-element.84), channel_id=1, source_target_pairs={{0,4},{1,5},{2,6},{3,7},{4,8},{5,9},{6,10},{7,11},{8,12},{9,13},{1... | collective-permute-start | bytes 6291464 | tf_op jit(solution)/shard_map/ppermute | solution.py:559
  138.2 36.4 %collective-permute-start.19 = (f32[2,512,256]{2,1,0:T(8,128)}, f32[2,512,256]{2,1,0:T(8,128)}, u32[]{:S(2)}, u32[]{:S(2)}) collective-permute-start(f32[2,512,256]{2,1,0:T(8,128)} %get-tuple-element.82), channel_id=1, source_target_pairs={{0,4},{1,5},{2,6},{3,7},{4,8},{5,9},{6,10},{7,11},{8,12},{9,13},{1... | collective-permute-start | bytes 3145736 | tf_op jit(solution)/shard_map/ppermute | solution.py:559
  141.7 24.8 %collective-permute-start.16 = (f32[128,512]{1,0:T(8,128)S(1)}, f32[128,512]{1,0:T(8,128)S(1)}, u32[]{:S(2)}, u32[]{:S(2)}) collective-permute-start(f32[128,512]{1,0:T(8,128)S(1)} %add_add_fusion), channel_id=1, source_target_pairs={{0,2},{1,3},{2,0},{3,1},{4,6},{5,7},{6,4},{7,5},{8,10},{9,11},{10,... | collective-permute-start | bytes 786440 | tf_op jit(solution)/shard_map/ppermute | solution.py:581
  149.6 16.9 %collective-permute-start.17 = (f32[128,512]{1,0:T(8,128)S(1)}, f32[128,512]{1,0:T(8,128)S(1)}, u32[]{:S(2)}, u32[]{:S(2)}) collective-permute-start(f32[128,512]{1,0:T(8,128)S(1)} %add_add_fusion), channel_id=1, source_target_pairs={{0,1},{1,2},{2,3},{3,0},{4,5},{5,6},{6,7},{7,4},{8,9},{9,10},{10,1... | collective-permute-start | bytes 786440 | tf_op jit(solution)/shard_map/ppermute | solution.py:581
  149.6 16.9 %collective-permute-start.18 = (f32[128,512]{1,0:T(8,128)S(1)}, f32[128,512]{1,0:T(8,128)S(1)}, u32[]{:S(2)}, u32[]{:S(2)}) collective-permute-start(f32[128,512]{1,0:T(8,128)S(1)} %add_add_fusion), channel_id=1, source_target_pairs={{0,3},{1,0},{2,1},{3,2},{4,7},{5,4},{6,5},{7,6},{8,11},{9,8},{10,9... | collective-permute-start | bytes 786440 | tf_op jit(solution)/shard_map/ppermute | solution.py:581
  166.7 51.4 %collective-permute-start.24 = (f32[2,512,512]{2,1,0:T(8,128)}, f32[2,512,512]{2,1,0:T(8,128)S(1)}, u32[]{:S(2)}, u32[]{:S(2)}) collective-permute-start(f32[2,512,512]{2,1,0:T(8,128)} %maximum_add_fusion), channel_id=1, source_target_pairs={{0,1},{1,2},{2,3},{4,5},{5,6},{6,7},{8,9},{9,10},{10,11},{12,13},{... | collective-permute-start | bytes 6291464 | tf_op jit(solution)/shard_map/ppermute | solution.py:559
  174.6 10.5 %collective-permute-start.21 = (f32[128,512]{1,0:T(8,128)S(1)}, f32[128,512]{1,0:T(8,128)S(1)}, u32[]{:S(2)}, u32[]{:S(2)}) collective-permute-start(f32[128,512]{1,0:T(8,128)S(1)} %add_multiply_fusion), channel_id=1, source_target_pairs={{0,8},{4,12},{8,16},{12,20},{16,24},{20,28},{24,0},{28,4},{1,9},{5... | collective-permute-start | bytes 786440 | tf_op jit(solution)/shard_map/ppermute | solution.py:581
  175.7 13.7 %collective-permute-start.22 = (f32[128,512]{1,0:T(8,128)S(1)}, f32[128,512]{1,0:T(8,128)S(1)}, u32[]{:S(2)}, u32[]{:S(2)}) collective-permute-start(f32[128,512]{1,0:T(8,128)S(1)} %add_multiply_fusion), channel_id=1, source_target_pairs={{0,16},{4,20},{8,24},{12,28},{16,0},{20,4},{24,8},{28,12},{1,17},{... | collective-permute-start | bytes 786440 | tf_op jit(solution)/shard_map/ppermute | solution.py:581
  176.0 13.4 %collective-permute-start.23 = (f32[128,512]{1,0:T(8,128)S(1)}, f32[128,512]{1,0:T(8,128)S(1)}, u32[]{:S(2)}, u32[]{:S(2)}) collective-permute-start(f32[128,512]{1,0:T(8,128)S(1)} %add_multiply_fusion), channel_id=1, source_target_pairs={{0,24},{4,28},{8,0},{12,4},{16,8},{20,12},{24,16},{28,20},{1,25},{... | collective-permute-start | bytes 786440 | tf_op jit(solution)/shard_map/ppermute | solution.py:581
  185.0 5.2 %copy-start.10 = (f32[2,512,256]{2,1,0:T(8,128)S(1)}, f32[2,512,256]{2,1,0:T(8,128)}, u32[]{:S(2)}) copy-start(f32[2,512,256]{2,1,0:T(8,128)} %get-tuple-element.92) | copy-start | bytes 3145732
  189.5 6.3 %collective-permute-start.26 = (f32[512,512]{1,0:T(8,128)S(1)}, f32[512,512]{1,0:T(8,128)}, u32[]{:S(2)}, u32[]{:S(2)}) collective-permute-start(f32[512,512]{1,0:T(8,128)S(1)} %constant_dynamic-update-slice_fusion), channel_id=1, source_target_pairs={{0,4},{4,0},{8,12},{12,8},{16,20},{20,16},{24,28},{28,24},{1,5},{5... | collective-permute-start | bytes 3145736 | tf_op jit(solution)/shard_map/ppermute | solution.py:573
  192.5 25.6 %collective-permute-start.25 = (f32[2,512,256]{2,1,0:T(8,128)}, f32[2,512,256]{2,1,0:T(8,128)}, u32[]{:S(2)}, u32[]{:S(2)}) collective-permute-start(f32[2,512,256]{2,1,0:T(8,128)} %add.159), channel_id=1, source_target_pairs={{0,4},{1,5},{2,6},{3,7},{4,8},{5,9},{6,10},{7,11},{8,12},{9,13},{1... | collective-permute-start | bytes 3145736 | tf_op jit(solution)/shard_map/ppermute | solution.py:559

commit v10 on v9

--- a/solution.py
+++ b/solution.py
@@ -133,7 +133,8 @@
     mat_t_hi_hbm,
     mat_t_lo_hbm,
     own_out,
-    right_out,
+    right_a_out,
+    right_b_out,
     lower_a_out,
     lower_b_out,
     lower_c_out,
@@ -229,7 +230,8 @@
         (lower_a_out, bottom, 0),
         (lower_b_out, bottom, half),
         (lower_c_out, bottom, side),
-        (right_out, top, tile_cols),
+        (right_a_out, top, tile_cols),
+        (right_b_out, top, tile_cols + half),
         (own_out, top, 0),
     )
     stores = [
@@ -238,7 +240,7 @@
         )
         for n, (dst, rows, start) in enumerate(outs)
     ]
-    dpup_store = pltpu.make_async_copy(dpup, dpup_out, out_sems.at[7])
+    dpup_store = pltpu.make_async_copy(dpup, dpup_out, out_sems.at[8])
     lower_stores = stores[:5]
     upper_stores = stores[5:]
 
@@ -253,9 +255,6 @@
     def _(step):
         rows = pl.ds(pl.multiple_of(step * zero_rows, zero_rows), zero_rows)
         dpup[:, rows, :] = jnp.zeros((2, zero_rows, side), jnp.float32)
-
-    for load in loads:
-        load.wait()
 
     def one_slot(slot):
         row = meta[slot, 0]
@@ -265,13 +264,28 @@
         row_base = pl.multiple_of((row // 8) * 8, 8)
         row_shift = row - row_base
 
-        @pl.loop(0, side // 32, unroll=2)
-        def _(step):
+        def cut(step):
             base = pl.multiple_of(step * 32, 32)
             rows = pl.ds(pl.multiple_of(row_base + base, 8), 32)
             for plane in range(2):
                 block = region[plane, rows, pl.ds(col_base, wide)]
                 win[plane, pl.ds(base, 32), :] = wrap_lanes(block, col_shift)
+
+        above = (tile_rows - row_base) // 32
+
+        @pl.when(slot == 0)
+        def _():
+            for load in loads[:3]:
+                load.wait()
+
+        pl.loop(0, above)(cut)
+
+        @pl.when(slot == 0)
+        def _():
+            for load in loads[3:]:
+                load.wait()
+
+        pl.loop(above, side // 32)(cut)
 
         first_keep = lax.broadcasted_iota(jnp.int32, (8, side), 0) >= row_shift
         last_rows = pl.ds(pl.multiple_of(row_base + side, 8), 8)
@@ -426,7 +440,7 @@
     def _():
         for store in [dpup_store] + lower_stores:
             store.start()
-        for load in late_loads:
+        for load in loads + late_loads:
             load.wait()
 
     for store in upper_stores:
@@ -445,10 +459,9 @@
     anywhere = pl.BlockSpec(memory_space=pl.ANY)
     f32, bf16 = jnp.float32, jnp.bfloat16
     region = (2, tile_rows + side, tile_cols + side)
-    lower_a, lower_b, lower_c, corner_a = parts[2:6]
-    right = jax.ShapeDtypeStruct((2, tile_rows, side), f32)
+    right_a, right_b, lower_a, lower_b, lower_c, corner_a = parts[:6]
     dpup = jax.ShapeDtypeStruct(pupils.shape[1:], f32)
-    outs = (tile, right, lower_a, lower_b, lower_c, corner_a, corner_a, dpup)
+    outs = (tile, right_a, right_b, lower_a, lower_b, lower_c, corner_a, corner_a, dpup)
     table = pltpu.VMEM(high.shape, bf16)
     return pl.pallas_call(
         slots_kernel,
@@ -475,7 +488,7 @@
             table,
             pltpu.SemaphoreType.DMA((12,)),
             pltpu.SemaphoreType.DMA((2, slots)),
-            pltpu.SemaphoreType.DMA((8,)),
+            pltpu.SemaphoreType.DMA((9,)),
         ],
         compiler_params=pltpu.CompilerParams(vmem_limit_bytes=56 * 1024 * 1024),
         cost_estimate=pl.CostEstimate(
@@ -656,7 +669,7 @@
         corner_up_b,
         corner_side,
     )
-    own_g, right_g, lower_a_g, lower_b_g, lower_c_g, corner_a_g, corner_b_g, dpup = (
+    own_g, right_a_g, right_b_g, lower_a_g, lower_b_g, lower_c_g, corner_a_g, corner_b_g, dpup = (
         slots_call(meta, spectrum, parts, amps, pupils)
     )
 
@@ -670,21 +683,21 @@
     back_a = send(corner_a_g, down)
     back_side = send(corner_b_g, lambda i, j: (i, j + 1) if i % 2 else None)
     back_down = send(corner_b_g, lambda i, j: None if i % 2 else (i + 1, j))
+    part = scatter(part, "ty", 2)
+    lower_a = send(after(lower_a_g, part), down)
+    lower_c = send(after(lower_c_g, part), down)
     part, back_a, back_side, back_down = lax.optimization_barrier(
         (part, back_a, back_side, back_down)
     )
-    part = scatter(part, "ty", 2)
-    lower_a = send(after(lower_a_g, part), down)
-    lower_c = send(after(lower_c_g, part), down)
     part = sum_all(part, "tx") * (1.0 / math.sqrt(n_ty * n_tx))
-    right_g = right_g + jnp.concatenate([back_a, back_down], axis=2)
-    right_back = send(after(right_g, part), right)
+    right_a = send(after(right_a_g + back_a, part), right)
+    right_b = send(after(right_b_g + back_down, part), right)
     part = gather(after(part, lower_a, lower_c), "ty", 2)
     lower_b = send(after(lower_b_g + back_side, part), down)
     spec_grad = own_g.at[:, :, side:].add(lower_c)
-    spec_grad = spec_grad.at[:, :, :half].add(lower_a)
+    spec_grad = spec_grad.at[:, :, :half].add(lower_a + right_a)
     part, spec_grad = lax.optimization_barrier((part, spec_grad))
-    spec_grad = spec_grad.at[:, :, :side].add(right_back.at[:, :, half:].add(lower_b))
+    spec_grad = spec_grad.at[:, :, half:side].add(lower_b + right_b)
     return spec_grad, double(part, 1).reshape(pupil.shape)
 
 

time: 227 us -> 225 us (level)
  the two profiles are of different devices: /device:TPU:1 before, /device:TPU:10 now
where the time goes in v10:
time: 225 us; the launch traced here: 224 us
  waiting for transfers between devices  92.5 us (41%)
  starting transfers between devices  48.2 us (21%)
  Pallas kernels  45.2 us (20%)
  other arithmetic  18.6 us (8%)
  local copies, waits for them, and re-layouts  18 us (8%)
    ppermute x17, waiting for transfers between devices, send(): return lax.ppermute(array, ('ty', 'tx'), along(rule, sizes))  68.4 us
    ppermute x17, starting transfers between devices, send(): return lax.ppermute(array, ('ty', 'tx'), along(rule, sizes))  37.3 us
    pallas_call x1, Pallas kernels, slots_call(): pl.pallas_call(slots_kernel, out_shape=[jax.ShapeDtypeStruct(x.shape, f32...  35.1 us
    ppermute x9, waiting for transfers between devices, stepped(): lax.ppermute(value, axis, [(i, (i + step * inner) % size) for i in range(...  21.8 us
    pallas_call x1, Pallas kernels, prepare(): pl.pallas_call(prepare_kernel, grid=(slots,), out_shape=[jax.ShapeDtypeSt...  10.1 us
    unnamed x30, local copies, waits for them, and re-layouts  9.63 us
    ppermute x9, starting transfers between devices, stepped(): lax.ppermute(value, axis, [(i, (i + step * inner) % size) for i in range(...  7.53 us
  transfers between devices with their start and end apart: 28, of which 13 were waited for; matrix products, arithmetic and copies ran while one was open for 8% of the time, Pallas kernels for 5%

profile of v10, /device:TPU:10, one launch (start us, length us, event | category | flops | bytes accessed | tf_op | source)
XLA Modules:
  0.0 223.6 jit_solution(12415342686830438324)
XLA Ops:
  0.6 3.2 %fusion.1 = (f32[2,512,256]{2,1,0:T(8,128)}, f32[2,512,256]{2,1,0:T(8,128)}) fusion(f32[2,512,1024]{2,1,0:T(8,128)} %tile_hbm.1), kind=kLoop, calls=%fused_computation.21 | loop fusion | bytes 4194304 | tf_op jit(solution)/shard_map/slice | solution.py:651
  3.9 2.2 collective-permute-start.3
  6.1 2.4 %collective-permute-start = (f32[2,512,256]{2,1,0:T(8,128)}, f32[2,512,256]{2,1,0:T(8,128)}, u32[]{:S(2)}, u32[]{:S(2)}) collective-permute-start(f32[2,512,256]{2,1,0:T(8,128)} %get-tuple-element.89), channel_id=1, source_target_pairs={{1,0},{2,1},{3,2},{5,4},{6,5},{7,6},{9,8},{10,9},{11,10},{13,12},{... | collective-permute-start | bytes 3145736 | tf_op jit(solution)/shard_map/ppermute | solution.py:572
  8.4 1.5 slice.99
  10.0 2.1 collective-permute-start.4
  12.1 1.9 collective-permute-start.1
  14.0 1.9 collective-permute-start.2
  16.0 0.1 copy.16
  16.1 0.1 copy.17
  16.2 0.1 copy.15
  16.4 1.6 copy-done.2
  17.9 1.0 copy-done.3
  19.0 1.0 copy-done.4
  20.0 10.1 %prepare.1 = (f32[3,512,512]{2,1,0:T(8,128)S(1)}, f32[3,2,512,512]{3,2,1,0:T(8,128)S(1)}) custom-call(s32[4,3]{1,0:T(4,128)S(1)} %concatenate.12.meta, f32[3,512,512]{2,1,0:T(8,128)S(1)} %copy-done.1, f32[2,512,512]{2,1,0:T(8,128)S(1)} %copy-done.2, bf16[512,512]{1,0:T(8,128)(2,1)S(1)} %copy-done.3, bf16[512,512]{1,0:T(8,128)(2,1)S(1)} %copy-done.4), custom_call_target="tpu_custom_call" | custom-call | flops 4831838208 | bytes 18874368 | tf_op jit(solution)/shard_map/prepare/pallas_call | solution.py:536
  30.1 2.7 %copy-done.5 = f32[3,2,512,512]{3,2,1,0:T(8,128)} copy-done((f32[3,2,512,512]{3,2,1,0:T(8,128)}, f32[3,2,512,512]{3,2,1,0:T(8,128)S(1)}, u32[]{:S(2)}) %copy-start.5) | copy-done | bytes 6291480
  32.8 1.7 copy-done.6
  34.5 0.7 collective-permute-start.8
  35.3 3.1 %collective-permute-start.5 = (f32[2,512,256]{2,1,0:T(8,128)}, f32[2,512,256]{2,1,0:T(8,128)S(1)}, u32[]{:S(2)}, u32[]{:S(2)}) collective-permute-start(f32[2,512,256]{2,1,0:T(8,128)} %collective-permute-done.right_a_hbm), channel_id=1, source_target_pairs={{4,0},{5,1},{6,2},{7,3},{8,4},{9,5},{10,6},{11,7},{12,8},{13,9},{1... | collective-permute-start | bytes 3145736 | tf_op jit(solution)/shard_map/ppermute | solution.py:572
  38.4 18.3 %collective-permute-done.1.right_b_hbm = f32[2,512,256]{2,1,0:T(8,128)} collective-permute-done((f32[2,512,256]{2,1,0:T(8,128)}, f32[2,512,256]{2,1,0:T(8,128)}, u32[]{:S(2)}, u32[]{:S(2)}) %collective-permute-start.1) | collective-permute-done | bytes 1048608 | tf_op jit(solution)/shard_map/ppermute | solution.py:572
  56.7 1.3 fusion.2
  58.0 1.3 collective-permute-start.6
  59.3 1.3 collective-permute-start.7
  60.6 1.3 collective-permute-done.6.corner_up_a_hbm
  61.9 2.1 collective-permute-done.7.corner_up_b_hbm
  64.1 0.9 copy-done.12
  65.0 0.4 copy-done.13
  65.4 35.1 %slots.1 = (f32[2,512,1024]{2,1,0:T(8,128)}, f32[2,512,256]{2,1,0:T(8,128)}, f32[2,512,256]{2,1,0:T(8,128)}, f32[2,512,256]{2,1,0:T(8,128)}, f32[2,512,256]{2,1,...) custom-call(s32[4,3]{1,0:T(4,128)} %copy-done, ...), custom_call_target="tpu_custom_call" | custom-call | flops 9663676416 | bytes 41943040 | tf_op jit(solution)/shard_map/slots/pallas_call | solution.py:466
  100.5 1.3 constant_dynamic-slice_fusion.3
  101.8 3.3 %collective-permute-start.9 = (f32[512,512]{1,0:T(8,128)S(1)}, f32[512,512]{1,0:T(8,128)S(1)}, u32[]{:S(2)}, u32[]{:S(2)}) collective-permute-start(f32[512,512]{1,0:T(8,128)S(1)} %constant_dynamic-slice_fusion.3), channel_id=1, source_target_pairs={{0,4},{4,0},{8,12},{12,8},{16,20},{20,16},{24,28},{28,24},{1,5},{5... | collective-permute-start | bytes 3145736 | tf_op jit(solution)/shard_map/ppermute | solution.py:580
  105.1 2.3 %collective-permute-done.9 = f32[512,512]{1,0:T(8,128)S(1)} collective-permute-done((f32[512,512]{1,0:T(8,128)S(1)}, f32[512,512]{1,0:T(8,128)S(1)}, u32[]{:S(2)}, u32[]{:S(2)}) %collective-permute-start.9) | collective-permute-done | bytes 1048608 | tf_op jit(solution)/shard_map/ppermute | solution.py:580
  107.4 1.4 dynamic-slice_add_fusion
  108.8 0.8 constant_dynamic-slice_fusion.2
  109.6 2.0 collective-permute-start.12
  111.6 0.7 collective-permute-start.14
  112.4 5.2 %collective-permute-start.15 = (f32[2,512,256]{2,1,0:T(8,128)}, f32[2,512,256]{2,1,0:T(8,128)}, u32[]{:S(2)}, u32[]{:S(2)}) collective-permute-start(f32[2,512,256]{2,1,0:T(8,128)} %get-tuple-element.69), channel_id=1, source_target_pairs={{0,4},{1,5},{2,6},{3,7},{8,12},{9,13},{10,14},{11,15},{16,20},{17,... | collective-permute-start | bytes 3145736 | tf_op jit(solution)/shard_map/ppermute | solution.py:572
  117.6 1.4 collective-permute-done.10
  118.9 1.9 collective-permute-start.13
  120.9 2.9 %collective-permute-done.11 = f32[128,512]{1,0:T(8,128)S(1)} collective-permute-done((f32[128,512]{1,0:T(8,128)S(1)}, f32[128,512]{1,0:T(8,128)S(1)}, u32[]{:S(2)}, u32[]{:S(2)}) %collective-permute-start.11) | collective-permute-done | bytes 262176 | tf_op jit(solution)/shard_map/ppermute | solution.py:594
  123.9 1.9 collective-permute-start.20
  125.8 9.4 %collective-permute-done.13 = f32[2,512,256]{2,1,0:T(8,128)S(1)} collective-permute-done((f32[2,512,256]{2,1,0:T(8,128)}, f32[2,512,256]{2,1,0:T(8,128)S(1)}, u32[]{:S(2)}, u32[]{:S(2)}) %collective-permute-start.13) | collective-permute-done | bytes 1048608 | tf_op jit(solution)/shard_map/ppermute | solution.py:572
  135.3 0.1 collective-permute-start.16
  135.4 1.5 collective-permute-start.17
  136.9 1.4 collective-permute-start.18
  138.3 1.9 collective-permute-start.19
  140.2 2.3 %add.159 = f32[2,512,256]{2,1,0:T(8,128)} add(f32[2,512,256]{2,1,0:T(8,128)} %get-tuple-element.77, f32[2,512,256]{2,1,0:T(8,128)S(1)} %collective-permute-done.13) | non-fusion elementwise | flops 262144 | bytes 3145728 | tf_op jit(solution)/shard_map/add | solution.py:693
  142.6 6.6 %collective-permute-done.16 = f32[128,512]{1,0:T(8,128)S(1)} collective-permute-done((f32[128,512]{1,0:T(8,128)S(1)}, f32[128,512]{1,0:T(8,128)S(1)}, u32[]{:S(2)}, u32[]{:S(2)}) %collective-permute-start.16) | collective-permute-done | bytes 262176 | tf_op jit(solution)/shard_map/ppermute | solution.py:594
  149.2 9.7 %collective-permute-done.17 = f32[128,512]{1,0:T(8,128)S(1)} collective-permute-done((f32[128,512]{1,0:T(8,128)S(1)}, f32[128,512]{1,0:T(8,128)S(1)}, u32[]{:S(2)}, u32[]{:S(2)}) %collective-permute-start.17) | collective-permute-done | bytes 262176 | tf_op jit(solution)/shard_map/ppermute | solution.py:594
  158.9 1.1 collective-permute-done.18
  160.1 3.3 %collective-permute-start.24 = (f32[2,512,256]{2,1,0:T(8,128)}, f32[2,512,256]{2,1,0:T(8,128)}, u32[]{:S(2)}, u32[]{:S(2)}) collective-permute-start(f32[2,512,256]{2,1,0:T(8,128)} %add.159), channel_id=1, source_target_pairs={{0,1},{1,2},{2,3},{4,5},{5,6},{6,7},{8,9},{9,10},{10,11},{12,13},{... | collective-permute-start | bytes 3145736 | tf_op jit(solution)/shard_map/ppermute | solution.py:572
  163.5 5.6 %collective-permute-done.19 = f32[2,512,256]{2,1,0:T(8,128)} collective-permute-done((f32[2,512,256]{2,1,0:T(8,128)}, f32[2,512,256]{2,1,0:T(8,128)}, u32[]{:S(2)}, u32[]{:S(2)}) %collective-permute-start.19) | collective-permute-done | bytes 1048608 | tf_op jit(solution)/shard_map/ppermute | solution.py:572
  169.1 1.9 collective-permute-start.21
  171.0 0.6 collective-permute-start.23
  171.5 3.4 %add_dynamic-update-slice_fusion = f32[2,512,1024]{2,1,0:T(8,128)} fusion(f32[2,512,1024]{2,1,0:T(8,128)} %get-tuple-element.76, f32[2,512,512]{2,1,0:T(8,128)S(1)} %collective-permute-done.20), kind=kLoop, calls=%fused_computation.1 | loop fusion | flops 524288 | bytes 6291456 | tf_op jit(solution)/shard_map/scatter-add | solution.py:697
  174.9 12.6 %collective-permute-done.24 = f32[2,512,256]{2,1,0:T(8,128)} collective-permute-done((f32[2,512,256]{2,1,0:T(8,128)}, f32[2,512,256]{2,1,0:T(8,128)}, u32[]{:S(2)}, u32[]{:S(2)}) %collective-permute-start.24) | collective-permute-done | bytes 1048608 | tf_op jit(solution)/shard_map/ppermute | solution.py:572
  187.6 3.0 %fusion = f32[2,512,1024]{2,1,0:T(8,128)} fusion(f32[2,512,1024]{2,1,0:T(8,128)} %add_dynamic-update-slice_fusion, f32[2,512,256]{2,1,0:T(8,128)} %collective-permute-done.19, f32[2,512,256]{2,1,0:T(8,128)} %collective-permute-done.24), kind=kLoop, calls=%fused_computation.3 | loop fusion | flops 524288 | bytes 4194304 | tf_op jit(solution)/shard_map/scatter-add | solution.py:698
  190.6 0.1 broadcast_in_dim.4
  191.0 1.4 add.163
  192.3 1.1 add.162
  193.5 3.3 %collective-permute-start.26 = (f32[2,512,256]{2,1,0:T(8,128)S(1)}, f32[2,512,256]{2,1,0:T(8,128)S(1)}, u32[]{:S(2)}, u32[]{:S(2)}) collective-permute-start(f32[2,512,256]{2,1,0:T(8,128)S(1)} %add.163), channel_id=1, source_target_pairs={{0,1},{1,2},{2,3},{4,5},{5,6},{6,7},{8,9},{9,10},{10,11},{12,13},{... | collective-permute-start | bytes 3145736 | tf_op jit(solution)/shard_map/ppermute | solution.py:572
  196.8 2.1 collective-permute-start.25
  199.0 1.5 broadcast_select_fusion.1
  200.4 1.5 pad_maximum_fusion
  201.9 19.0 %collective-permute-done.26 = f32[2,512,256]{2,1,0:T(8,128)S(1)} collective-permute-done((f32[2,512,256]{2,1,0:T(8,128)S(1)}, f32[2,512,256]{2,1,0:T(8,128)S(1)}, u32[]{:S(2)}, u32[]{:S(2)}) %collective-permute-start.26) | collective-permute-done | bytes 1048608 | tf_op jit(solution)/shard_map/ppermute | solution.py:572
  220.9 2.7 %add_dynamic-update-slice_fusion.1 = f32[2,512,1024]{2,1,0:T(8,128)} fusion(f32[2,512,1024]{2,1,0:T(8,128)} %fusion, f32[2,512,256]{2,1,0:T(8,128)} %collective-permute-done.25, f32[2,512,256]{2,1,0:T(8,128)S(1)} %collective-permute-done.26), kind=kLoop, calls=%fused_computation.4 | loop fusion | flops 524288 | bytes 4194304 | tf_op jit(solution)/shard_map/scatter-add | solution.py:700
  (50 shorter events, 0.5 us)
Async XLA Ops:
  0.6 7.8 %copy-start.7 = (f32[2,512,1024]{2,1,0:T(8,128)S(1)}, f32[2,512,1024]{2,1,0:T(8,128)}, u32[]{:S(2)}) copy-start(f32[2,512,1024]{2,1,0:T(8,128)} %tile_hbm.1) | copy-start | bytes 12582916
  3.9 12.1 %copy-start.10 = (s32[3,2]{0,1:T(2,128)S(1)}, s32[3,2]{0,1:T(2,128)}, u32[]{:S(2)}) copy-start(s32[3,2]{0,1:T(2,128)} %param.20) | copy-start | bytes 76
  3.9 12.3 %copy-start.11 = (s32[3]{0:T(128)S(1)}, s32[3]{0:T(128)}, u32[]{:S(2)}) copy-start(s32[3]{0:T(128)} %param.21) | copy-start | bytes 40
  3.9 12.5 %copy-start.1 = (f32[3,512,512]{2,1,0:T(8,128)S(1)}, f32[3,512,512]{2,1,0:T(8,128)}, u32[]{:S(2)}) copy-start(f32[3,512,512]{2,1,0:T(8,128)} %amps.1) | copy-start | bytes 9437188
  3.9 30.7 %collective-permute-start.3 = (f32[2,512,256]{2,1,0:T(8,128)}, f32[2,512,256]{2,1,0:T(8,128)}, u32[]{:S(2)}, u32[]{:S(2)}) collective-permute-start(f32[2,512,256]{2,1,0:T(8,128)} %get-tuple-element.88), channel_id=1, source_target_pairs={{4,0},{5,1},{6,2},{7,3},{8,4},{9,5},{10,6},{11,7},{12,8},{13,9},{1... | collective-permute-start | bytes 3145736 | tf_op jit(solution)/shard_map/ppermute | solution.py:572
  6.1 29.2 %collective-permute-start = (f32[2,512,256]{2,1,0:T(8,128)}, f32[2,512,256]{2,1,0:T(8,128)}, u32[]{:S(2)}, u32[]{:S(2)}) collective-permute-start(f32[2,512,256]{2,1,0:T(8,128)} %get-tuple-element.89), channel_id=1, source_target_pairs={{1,0},{2,1},{3,2},{5,4},{6,5},{7,6},{9,8},{10,9},{11,10},{13,12},{... | collective-permute-start | bytes 3145736 | tf_op jit(solution)/shard_map/ppermute | solution.py:572
  10.0 54.1 %collective-permute-start.4 = (f32[2,512,512]{2,1,0:T(8,128)}, f32[2,512,512]{2,1,0:T(8,128)}, u32[]{:S(2)}, u32[]{:S(2)}) collective-permute-start(f32[2,512,512]{2,1,0:T(8,128)} %slice.99), channel_id=1, source_target_pairs={{4,0},{5,1},{6,2},{7,3},{8,4},{9,5},{10,6},{11,7},{12,8},{13,9},{1... | collective-permute-start | bytes 6291464 | tf_op jit(solution)/shard_map/ppermute | solution.py:572
  12.1 44.6 %collective-permute-start.1 = (f32[2,512,256]{2,1,0:T(8,128)}, f32[2,512,256]{2,1,0:T(8,128)}, u32[]{:S(2)}, u32[]{:S(2)}) collective-permute-start(f32[2,512,256]{2,1,0:T(8,128)} %get-tuple-element.88), channel_id=1, source_target_pairs={{1,0},{2,1},{3,2},{5,4},{6,5},{7,6},{9,8},{10,9},{11,10},{13,12},{... | collective-permute-start | bytes 3145736 | tf_op jit(solution)/shard_map/ppermute | solution.py:572
  14.0 45.3 %collective-permute-start.2 = (f32[2,512,256]{2,1,0:T(8,128)}, f32[2,512,256]{2,1,0:T(8,128)}, u32[]{:S(2)}, u32[]{:S(2)}) collective-permute-start(f32[2,512,256]{2,1,0:T(8,128)} %get-tuple-element.89), channel_id=1, source_target_pairs={{4,0},{5,1},{6,2},{7,3},{8,4},{9,5},{10,6},{11,7},{12,8},{13,9},{1... | collective-permute-start | bytes 3145736 | tf_op jit(solution)/shard_map/ppermute | solution.py:572
  16.3 1.6 copy-start.2
  17.9 1.0 copy-start.3
  19.0 1.0 copy-start.4
  20.0 10.1 %copy-start = (s32[4,3]{1,0:T(4,128)}, s32[4,3]{1,0:T(4,128)S(1)}, u32[]{:S(2)}) copy-start(s32[4,3]{1,0:T(4,128)S(1)} %concatenate.12.meta) | copy-start | bytes 148
  30.1 2.7 %copy-start.5 = (f32[3,2,512,512]{3,2,1,0:T(8,128)}, f32[3,2,512,512]{3,2,1,0:T(8,128)S(1)}, u32[]{:S(2)}) copy-start(f32[3,2,512,512]{3,2,1,0:T(8,128)S(1)} %get-tuple-element.66.pupil_hbm) | copy-start | bytes 18874372
  32.8 1.7 copy-start.6
  34.5 29.5 %collective-permute-start.8 = (f32[2,512,256]{2,1,0:T(8,128)}, f32[2,512,256]{2,1,0:T(8,128)S(1)}, u32[]{:S(2)}, u32[]{:S(2)}) collective-permute-start(f32[2,512,256]{2,1,0:T(8,128)} %collective-permute-done.3.lower_b_hbm), channel_id=1, source_target_pairs={{5,4},{6,5},{7,6},{13,12},{14,13},{15,14},{21,20},{22,21},{23,22},... | collective-permute-start | bytes 3145736 | tf_op jit(solution)/shard_map/ppermute | solution.py:572
  35.3 28.8 %collective-permute-start.5 = (f32[2,512,256]{2,1,0:T(8,128)}, f32[2,512,256]{2,1,0:T(8,128)S(1)}, u32[]{:S(2)}, u32[]{:S(2)}) collective-permute-start(f32[2,512,256]{2,1,0:T(8,128)} %collective-permute-done.right_a_hbm), channel_id=1, source_target_pairs={{4,0},{5,1},{6,2},{7,3},{8,4},{9,5},{10,6},{11,7},{12,8},{13,9},{1... | collective-permute-start | bytes 3145736 | tf_op jit(solution)/shard_map/ppermute | solution.py:572
  58.0 3.9 %collective-permute-start.6 = (f32[2,512,128]{2,1,0:T(8,128)S(1)}, f32[2,512,128]{2,1,0:T(8,128)}, u32[]{:S(2)}, u32[]{:S(2)}) collective-permute-start(f32[2,512,128]{2,1,0:T(8,128)S(1)} %get-tuple-element.96), channel_id=1, source_target_pairs={{4,0},{5,1},{6,2},{7,3},{12,8},{13,9},{14,10},{15,11},{20,16},{21,... | collective-permute-start | bytes 1572872 | tf_op jit(solution)/shard_map/ppermute | solution.py:572
  59.3 4.7 %collective-permute-start.7 = (f32[2,512,128]{2,1,0:T(8,128)S(1)}, f32[2,512,128]{2,1,0:T(8,128)}, u32[]{:S(2)}, u32[]{:S(2)}) collective-permute-start(f32[2,512,128]{2,1,0:T(8,128)S(1)} %get-tuple-element.95), channel_id=1, source_target_pairs={{4,0},{5,1},{6,2},{7,3},{12,8},{13,9},{14,10},{15,11},{20,16},{21,... | collective-permute-start | bytes 1572872 | tf_op jit(solution)/shard_map/ppermute | solution.py:572
  64.0 1.0 copy-start.12
  64.0 1.4 copy-start.13
  101.8 5.6 %collective-permute-start.9 = (f32[512,512]{1,0:T(8,128)S(1)}, f32[512,512]{1,0:T(8,128)S(1)}, u32[]{:S(2)}, u32[]{:S(2)}) collective-permute-start(f32[512,512]{1,0:T(8,128)S(1)} %constant_dynamic-slice_fusion.3), channel_id=1, source_target_pairs={{0,4},{4,0},{8,12},{12,8},{16,20},{20,16},{24,28},{28,24},{1,5},{5... | collective-permute-start | bytes 3145736 | tf_op jit(solution)/shard_map/ppermute | solution.py:580
  109.6 9.3 %collective-permute-start.10 = (f32[128,512]{1,0:T(8,128)}, f32[128,512]{1,0:T(8,128)S(1)}, u32[]{:S(2)}, u32[]{:S(2)}) collective-permute-start(f32[128,512]{1,0:T(8,128)} %get-tuple-element.92), channel_id=1, source_target_pairs={{0,8},{4,12},{8,16},{12,20},{16,24},{20,28},{24,0},{28,4},{1,9},{5... | collective-permute-start | bytes 786440 | tf_op jit(solution)/shard_map/ppermute | solution.py:594
  109.6 14.2 %collective-permute-start.11 = (f32[128,512]{1,0:T(8,128)S(1)}, f32[128,512]{1,0:T(8,128)S(1)}, u32[]{:S(2)}, u32[]{:S(2)}) collective-permute-start(f32[128,512]{1,0:T(8,128)S(1)} %get-tuple-element.94), channel_id=1, source_target_pairs={{0,16},{4,20},{8,24},{12,28},{16,0},{20,4},{24,8},{28,12},{1,17},{... | collective-permute-start | bytes 786440 | tf_op jit(solution)/shard_map/ppermute | solution.py:594
  109.6 14.2 %collective-permute-start.12 = (f32[128,512]{1,0:T(8,128)S(1)}, f32[128,512]{1,0:T(8,128)S(1)}, u32[]{:S(2)}, u32[]{:S(2)}) collective-permute-start(f32[128,512]{1,0:T(8,128)S(1)} %get-tuple-element.93), channel_id=1, source_target_pairs={{0,24},{4,28},{8,0},{12,4},{16,8},{20,12},{24,16},{28,20},{1,25},{... | collective-permute-start | bytes 786440 | tf_op jit(solution)/shard_map/ppermute | solution.py:594
  111.6 23.6 %collective-permute-start.14 = (f32[2,512,256]{2,1,0:T(8,128)}, f32[2,512,256]{2,1,0:T(8,128)S(1)}, u32[]{:S(2)}, u32[]{:S(2)}) collective-permute-start(f32[2,512,256]{2,1,0:T(8,128)} %get-tuple-element.69), channel_id=1, source_target_pairs={{4,5},{5,6},{6,7},{12,13},{13,14},{14,15},{20,21},{21,22},{22,23},... | collective-permute-start | bytes 3145736 | tf_op jit(solution)/shard_map/ppermute | solution.py:572
  112.4 22.9 %collective-permute-start.15 = (f32[2,512,256]{2,1,0:T(8,128)}, f32[2,512,256]{2,1,0:T(8,128)}, u32[]{:S(2)}, u32[]{:S(2)}) collective-permute-start(f32[2,512,256]{2,1,0:T(8,128)} %get-tuple-element.69), channel_id=1, source_target_pairs={{0,4},{1,5},{2,6},{3,7},{8,12},{9,13},{10,14},{11,15},{16,20},{17,... | collective-permute-start | bytes 3145736 | tf_op jit(solution)/shard_map/ppermute | solution.py:572
  118.9 16.3 %collective-permute-start.13 = (f32[2,512,256]{2,1,0:T(8,128)}, f32[2,512,256]{2,1,0:T(8,128)S(1)}, u32[]{:S(2)}, u32[]{:S(2)}) collective-permute-start(f32[2,512,256]{2,1,0:T(8,128)} %get-tuple-element.68), channel_id=1, source_target_pairs={{0,4},{1,5},{2,6},{3,7},{4,8},{5,9},{6,10},{7,11},{8,12},{9,13},{1... | collective-permute-start | bytes 3145736 | tf_op jit(solution)/shard_map/ppermute | solution.py:572
  123.9 45.2 %collective-permute-start.20 = (f32[2,512,512]{2,1,0:T(8,128)}, f32[2,512,512]{2,1,0:T(8,128)S(1)}, u32[]{:S(2)}, u32[]{:S(2)}) collective-permute-start(f32[2,512,512]{2,1,0:T(8,128)} %get-tuple-element.74), channel_id=1, source_target_pairs={{0,4},{1,5},{2,6},{3,7},{4,8},{5,9},{6,10},{7,11},{8,12},{9,13},{1... | collective-permute-start | bytes 6291464 | tf_op jit(solution)/shard_map/ppermute | solution.py:572
  135.3 13.9 %collective-permute-start.16 = (f32[128,512]{1,0:T(8,128)S(1)}, f32[128,512]{1,0:T(8,128)S(1)}, u32[]{:S(2)}, u32[]{:S(2)}) collective-permute-start(f32[128,512]{1,0:T(8,128)S(1)} %add_add_fusion), channel_id=1, source_target_pairs={{0,2},{1,3},{2,0},{3,1},{4,6},{5,7},{6,4},{7,5},{8,10},{9,11},{10,... | collective-permute-start | bytes 786440 | tf_op jit(solution)/shard_map/ppermute | solution.py:594
  135.4 23.5 %collective-permute-start.17 = (f32[128,512]{1,0:T(8,128)S(1)}, f32[128,512]{1,0:T(8,128)S(1)}, u32[]{:S(2)}, u32[]{:S(2)}) collective-permute-start(f32[128,512]{1,0:T(8,128)S(1)} %add_add_fusion), channel_id=1, source_target_pairs={{0,1},{1,2},{2,3},{3,0},{4,5},{5,6},{6,7},{7,4},{8,9},{9,10},{10,1... | collective-permute-start | bytes 786440 | tf_op jit(solution)/shard_map/ppermute | solution.py:594
  136.9 23.1 %collective-permute-start.18 = (f32[128,512]{1,0:T(8,128)S(1)}, f32[128,512]{1,0:T(8,128)S(1)}, u32[]{:S(2)}, u32[]{:S(2)}) collective-permute-start(f32[128,512]{1,0:T(8,128)S(1)} %add_add_fusion), channel_id=1, source_target_pairs={{0,3},{1,0},{2,1},{3,2},{4,7},{5,4},{6,5},{7,6},{8,11},{9,8},{10,9... | collective-permute-start | bytes 786440 | tf_op jit(solution)/shard_map/ppermute | solution.py:594
  138.3 30.8 %collective-permute-start.19 = (f32[2,512,256]{2,1,0:T(8,128)}, f32[2,512,256]{2,1,0:T(8,128)}, u32[]{:S(2)}, u32[]{:S(2)}) collective-permute-start(f32[2,512,256]{2,1,0:T(8,128)} %get-tuple-element.72), channel_id=1, source_target_pairs={{0,4},{1,5},{2,6},{3,7},{4,8},{5,9},{6,10},{7,11},{8,12},{9,13},{1... | collective-permute-start | bytes 3145736 | tf_op jit(solution)/shard_map/ppermute | solution.py:572
  160.1 27.5 %collective-permute-start.24 = (f32[2,512,256]{2,1,0:T(8,128)}, f32[2,512,256]{2,1,0:T(8,128)}, u32[]{:S(2)}, u32[]{:S(2)}) collective-permute-start(f32[2,512,256]{2,1,0:T(8,128)} %add.159), channel_id=1, source_target_pairs={{0,1},{1,2},{2,3},{4,5},{5,6},{6,7},{8,9},{9,10},{10,11},{12,13},{... | collective-permute-start | bytes 3145736 | tf_op jit(solution)/shard_map/ppermute | solution.py:572
  169.1 21.7 %collective-permute-start.21 = (f32[128,512]{1,0:T(8,128)S(1)}, f32[128,512]{1,0:T(8,128)S(1)}, u32[]{:S(2)}, u32[]{:S(2)}) collective-permute-start(f32[128,512]{1,0:T(8,128)S(1)} %add_multiply_fusion), channel_id=1, source_target_pairs={{0,8},{4,12},{8,16},{12,20},{16,24},{20,28},{24,0},{28,4},{1,9},{5... | collective-permute-start | bytes 786440 | tf_op jit(solution)/shard_map/ppermute | solution.py:594
  171.0 19.8 %collective-permute-start.22 = (f32[128,512]{1,0:T(8,128)S(1)}, f32[128,512]{1,0:T(8,128)S(1)}, u32[]{:S(2)}, u32[]{:S(2)}) collective-permute-start(f32[128,512]{1,0:T(8,128)S(1)} %add_multiply_fusion), channel_id=1, source_target_pairs={{0,16},{4,20},{8,24},{12,28},{16,0},{20,4},{24,8},{28,12},{1,17},{... | collective-permute-start | bytes 786440 | tf_op jit(solution)/shard_map/ppermute | solution.py:594
  171.0 19.9 %collective-permute-start.23 = (f32[128,512]{1,0:T(8,128)S(1)}, f32[128,512]{1,0:T(8,128)S(1)}, u32[]{:S(2)}, u32[]{:S(2)}) collective-permute-start(f32[128,512]{1,0:T(8,128)S(1)} %add_multiply_fusion), channel_id=1, source_target_pairs={{0,24},{4,28},{8,0},{12,4},{16,8},{20,12},{24,16},{28,20},{1,25},{... | collective-permute-start | bytes 786440 | tf_op jit(solution)/shard_map/ppermute | solution.py:594
  174.9 16.0 %copy-start.9 = (f32[2,512,256]{2,1,0:T(8,128)S(1)}, f32[2,512,256]{2,1,0:T(8,128)}, u32[]{:S(2)}) copy-start(f32[2,512,256]{2,1,0:T(8,128)} %get-tuple-element.84) | copy-start | bytes 3145732
  190.6 1.7 copy-start.8
  190.9 8.1 %collective-permute-start.27 = (f32[512,512]{1,0:T(8,128)S(1)}, f32[512,512]{1,0:T(8,128)}, u32[]{:S(2)}, u32[]{:S(2)}) collective-permute-start(f32[512,512]{1,0:T(8,128)S(1)} %constant_dynamic-update-slice_fusion), channel_id=1, source_target_pairs={{0,4},{4,0},{8,12},{12,8},{16,20},{20,16},{24,28},{28,24},{1,5},{5... | collective-permute-start | bytes 3145736 | tf_op jit(solution)/shard_map/ppermute | solution.py:586
  193.5 27.4 %collective-permute-start.26 = (f32[2,512,256]{2,1,0:T(8,128)S(1)}, f32[2,512,256]{2,1,0:T(8,128)S(1)}, u32[]{:S(2)}, u32[]{:S(2)}) collective-permute-start(f32[2,512,256]{2,1,0:T(8,128)S(1)} %add.163), channel_id=1, source_target_pairs={{0,1},{1,2},{2,3},{4,5},{5,6},{6,7},{8,9},{9,10},{10,11},{12,13},{... | collective-permute-start | bytes 3145736 | tf_op jit(solution)/shard_map/ppermute | solution.py:572
  196.8 24.1 %collective-permute-start.25 = (f32[2,512,256]{2,1,0:T(8,128)}, f32[2,512,256]{2,1,0:T(8,128)}, u32[]{:S(2)}, u32[]{:S(2)}) collective-permute-start(f32[2,512,256]{2,1,0:T(8,128)} %add.162), channel_id=1, source_target_pairs={{0,4},{1,5},{2,6},{3,7},{4,8},{5,9},{6,10},{7,11},{8,12},{9,13},{1... | collective-permute-start | bytes 3145736 | tf_op jit(solution)/shard_map/ppermute | solution.py:572

commit v11 on v10

--- a/solution.py
+++ b/solution.py
@@ -133,11 +133,9 @@
     mat_t_hi_hbm,
     mat_t_lo_hbm,
     own_out,
-    right_a_out,
-    right_b_out,
-    lower_a_out,
+    right_out,
+    lower_ca_out,
     lower_b_out,
-    lower_c_out,
     corner_a_out,
     corner_b_out,
     dpup_out,
@@ -224,14 +222,15 @@
         for load in slot_loads(slot):
             load.start()
 
+    lower_c_out = lower_ca_out.at[:, :, pl.ds(0, tile_cols - side)]
+    lower_a_out = lower_ca_out.at[:, :, pl.ds(tile_cols - side, half)]
     outs = (
         (corner_a_out, bottom, tile_cols),
         (corner_b_out, bottom, tile_cols + half),
+        (lower_c_out, bottom, side),
         (lower_a_out, bottom, 0),
         (lower_b_out, bottom, half),
-        (lower_c_out, bottom, side),
-        (right_a_out, top, tile_cols),
-        (right_b_out, top, tile_cols + half),
+        (right_out, top, tile_cols),
         (own_out, top, 0),
     )
     stores = [
@@ -240,7 +239,7 @@
         )
         for n, (dst, rows, start) in enumerate(outs)
     ]
-    dpup_store = pltpu.make_async_copy(dpup, dpup_out, out_sems.at[8])
+    dpup_store = pltpu.make_async_copy(dpup, dpup_out, out_sems.at[7])
     lower_stores = stores[:5]
     upper_stores = stores[5:]
 
@@ -459,9 +458,11 @@
     anywhere = pl.BlockSpec(memory_space=pl.ANY)
     f32, bf16 = jnp.float32, jnp.bfloat16
     region = (2, tile_rows + side, tile_cols + side)
-    right_a, right_b, lower_a, lower_b, lower_c, corner_a = parts[:6]
+    corner = parts[5]
+    right = jax.ShapeDtypeStruct((2, tile_rows, side), f32)
+    lower_ca = jax.ShapeDtypeStruct((2, side, tile_cols - side // 2), f32)
     dpup = jax.ShapeDtypeStruct(pupils.shape[1:], f32)
-    outs = (tile, right_a, right_b, lower_a, lower_b, lower_c, corner_a, corner_a, dpup)
+    outs = (tile, right, lower_ca, corner, corner, corner, dpup)
     table = pltpu.VMEM(high.shape, bf16)
     return pl.pallas_call(
         slots_kernel,
@@ -488,7 +489,7 @@
             table,
             pltpu.SemaphoreType.DMA((12,)),
             pltpu.SemaphoreType.DMA((2, slots)),
-            pltpu.SemaphoreType.DMA((9,)),
+            pltpu.SemaphoreType.DMA((8,)),
         ],
         compiler_params=pltpu.CompilerParams(vmem_limit_bytes=56 * 1024 * 1024),
         cost_estimate=pl.CostEstimate(
@@ -669,8 +670,8 @@
         corner_up_b,
         corner_side,
     )
-    own_g, right_a_g, right_b_g, lower_a_g, lower_b_g, lower_c_g, corner_a_g, corner_b_g, dpup = (
-        slots_call(meta, spectrum, parts, amps, pupils)
+    own_g, right_g, lower_ca_g, lower_b_g, corner_a_g, corner_b_g, dpup = slots_call(
+        meta, spectrum, parts, amps, pupils
     )
 
     def down(i, j):
@@ -683,21 +684,22 @@
     back_a = send(corner_a_g, down)
     back_side = send(corner_b_g, lambda i, j: (i, j + 1) if i % 2 else None)
     back_down = send(corner_b_g, lambda i, j: None if i % 2 else (i + 1, j))
+    part, back_down = lax.optimization_barrier((part, back_down))
     part = scatter(part, "ty", 2)
-    lower_a = send(after(lower_a_g, part), down)
-    lower_c = send(after(lower_c_g, part), down)
-    part, back_a, back_side, back_down = lax.optimization_barrier(
-        (part, back_a, back_side, back_down)
+    part, lower_ca_g, back_a, back_side = lax.optimization_barrier(
+        (part, lower_ca_g, back_a, back_side)
     )
+    lower_ca = send(lower_ca_g, down)
     part = sum_all(part, "tx") * (1.0 / math.sqrt(n_ty * n_tx))
-    right_a = send(after(right_a_g + back_a, part), right)
-    right_b = send(after(right_b_g + back_down, part), right)
-    part = gather(after(part, lower_a, lower_c), "ty", 2)
+    right_g = right_g + jnp.concatenate([back_a, back_down], axis=2)
+    right_back = send(after(right_g, part), right)
+    part = gather(after(part, lower_ca), "ty", 2)
     lower_b = send(after(lower_b_g + back_side, part), down)
-    spec_grad = own_g.at[:, :, side:].add(lower_c)
-    spec_grad = spec_grad.at[:, :, :half].add(lower_a + right_a)
+    split_at = tile_cols - side
+    spec_grad = own_g.at[:, :, side:].add(lower_ca[:, :, :split_at])
+    spec_grad = spec_grad.at[:, :, :half].add(lower_ca[:, :, split_at:])
     part, spec_grad = lax.optimization_barrier((part, spec_grad))
-    spec_grad = spec_grad.at[:, :, half:side].add(lower_b + right_b)
+    spec_grad = spec_grad.at[:, :, :side].add(right_back.at[:, :, half:].add(lower_b))
     return spec_grad, double(part, 1).reshape(pupil.shape)
 
 

time: 225 us -> 218 us (0.969)
  the two profiles are of different devices: /device:TPU:10 before, /device:TPU:1 now
where the time goes in v11:
time: 218 us; the launch traced here: 215 us
  starting transfers between devices  78.3 us (36%)
  waiting for transfers between devices  65.4 us (30%)
  Pallas kernels  29.4 us (13%)
  other arithmetic  23 us (11%)
  local copies, waits for them, and re-layouts  18.3 us (8%)
    ppermute x15, starting transfers between devices, send(): return lax.ppermute(array, ('ty', 'tx'), along(rule, sizes))  51.5 us
    ppermute x15, waiting for transfers between devices, send(): return lax.ppermute(array, ('ty', 'tx'), along(rule, sizes))  45.2 us
    ppermute x9, starting transfers between devices, stepped(): lax.ppermute(value, axis, [(i, (i + step * inner) % size) for i in range(...  25.5 us
    ppermute x9, waiting for transfers between devices, stepped(): lax.ppermute(value, axis, [(i, (i + step * inner) % size) for i in range(...  20.2 us
    pallas_call x1, Pallas kernels, slots_call(): pl.pallas_call(slots_kernel, out_shape=[jax.ShapeDtypeStruct(x.shape, f32...  19.3 us
    pallas_call x1, Pallas kernels, prepare(): pl.pallas_call(prepare_kernel, grid=(slots,), out_shape=[jax.ShapeDtypeSt...  10.1 us
    unnamed x32, local copies, waits for them, and re-layouts  9.65 us
  transfers between devices with their start and end apart: 26, of which 12 were waited for; matrix products, arithmetic and copies ran while one was open for 10% of the time, Pallas kernels for 5%

profile of v11, /device:TPU:1, one launch (start us, length us, event | category | flops | bytes accessed | tf_op | source)
XLA Modules:
  0.0 215.5 jit_solution(16668740007757259974)
XLA Ops:
  0.6 3.2 %fusion.3 = (f32[2,512,256]{2,1,0:T(8,128)}, f32[2,512,256]{2,1,0:T(8,128)}) fusion(f32[2,512,1024]{2,1,0:T(8,128)} %tile_hbm.1), kind=kLoop, calls=%fused_computation.25 | loop fusion | bytes 4194304 | tf_op jit(solution)/shard_map/slice | solution.py:652
  3.8 2.0 collective-permute-start.3
  5.8 1.6 collective-permute-start
  7.4 1.5 slice.129
  8.9 1.9 collective-permute-start.4
  10.8 1.3 collective-permute-start.1
  12.1 1.9 collective-permute-start.2
  14.1 0.1 copy.16
  14.2 0.1 copy.17
  14.5 1.6 copy-done.2
  16.1 1.0 copy-done.3
  17.1 1.0 copy-done.4
  18.1 10.1 %prepare.1 = (f32[3,512,512]{2,1,0:T(8,128)S(1)}, f32[3,2,512,512]{3,2,1,0:T(8,128)S(1)}) custom-call(s32[4,3]{1,0:T(4,128)S(1)} %concatenate.17.meta, f32[3,512,512]{2,1,0:T(8,128)S(1)} %copy-done.1, f32[2,512,512]{2,1,0:T(8,128)S(1)} %copy-done.2, bf16[512,512]{1,0:T(8,128)(2,1)S(1)} %copy-done.3, bf16[512,512]{1,0:T(8,128)(2,1)S(1)} %copy-done.4), custom_call_target="tpu_custom_call" | custom-call | flops 4831838208 | bytes 18874368 | tf_op jit(solution)/shard_map/prepare/pallas_call | solution.py:537
  28.3 2.7 %copy-done.5 = f32[3,2,512,512]{3,2,1,0:T(8,128)} copy-done((f32[3,2,512,512]{3,2,1,0:T(8,128)}, f32[3,2,512,512]{3,2,1,0:T(8,128)S(1)}, u32[]{:S(2)}) %copy-start.5) | copy-done | bytes 6291480
  30.9 1.7 copy-done.6
  32.7 1.3 collective-permute-start.8
  34.0 0.7 collective-permute-done.right_a_hbm
  34.6 1.9 collective-permute-start.5
  36.6 19.9 %collective-permute-done.1.right_b_hbm = f32[2,512,256]{2,1,0:T(8,128)} collective-permute-done((f32[2,512,256]{2,1,0:T(8,128)}, f32[2,512,256]{2,1,0:T(8,128)}, u32[]{:S(2)}, u32[]{:S(2)}) %collective-permute-start.1) | collective-permute-done | bytes 1048608 | tf_op jit(solution)/shard_map/ppermute | solution.py:573
  56.5 1.3 fusion.4
  57.8 3.1 %collective-permute-start.6 = (f32[2,512,128]{2,1,0:T(8,128)S(1)}, f32[2,512,128]{2,1,0:T(8,128)}, u32[]{:S(2)}, u32[]{:S(2)}) collective-permute-start(f32[2,512,128]{2,1,0:T(8,128)S(1)} %get-tuple-element.102), channel_id=1, source_target_pairs={{4,0},{5,1},{6,2},{7,3},{12,8},{13,9},{14,10},{15,11},{20,16},{21,... | collective-permute-start | bytes 1572872 | tf_op jit(solution)/shard_map/ppermute | solution.py:573
  60.8 2.1 collective-permute-start.7
  62.9 0.8 collective-permute-done.7.corner_up_b_hbm
  63.8 3.8 %collective-permute-done.8.corner_side_hbm = f32[2,512,256]{2,1,0:T(8,128)S(1)} collective-permute-done((f32[2,512,256]{2,1,0:T(8,128)}, f32[2,512,256]{2,1,0:T(8,128)S(1)}, u32[]{:S(2)}, u32[]{:S(2)}) %collective-permute-start.8) | collective-permute-done | bytes 1048608 | tf_op jit(solution)/shard_map/ppermute | solution.py:573
  67.6 1.0 copy-done.13
  68.6 0.4 copy-done.14
  69.0 19.3 %slots.1 = (f32[2,512,1024]{2,1,0:T(8,128)}, f32[2,512,512]{2,1,0:T(8,128)}, f32[2,512,768]{2,1,0:T(8,128)}, f32[2,512,256]{2,1,0:T(8,128)}, f32[2,512,256]{2,1,...) custom-call(s32[4,3]{1,0:T(4,128)} %copy-done, f32[2,512,1024]{2,1,0:T(8,128)} %tile_hbm.1, ...), custom_call_target="tpu_custom_call" | custom-call | flops 9663676416 | bytes 41943040 | tf_op jit(solution)/shard_map/slots/pallas_call | solution.py:467
  88.3 1.4 constant_dynamic-slice_fusion.3
  89.9 1.3 collective-permute-start.10
  91.2 13.6 %collective-permute-start.14 = (f32[2,512,256]{2,1,0:T(8,128)}, f32[2,512,256]{2,1,0:T(8,128)}, u32[]{:S(2)}, u32[]{:S(2)}) collective-permute-start(f32[2,512,256]{2,1,0:T(8,128)} %get-tuple-element.80), channel_id=1, source_target_pairs={{0,4},{1,5},{2,6},{3,7},{4,8},{5,9},{6,10},{7,11},{8,12},{9,13},{1... | collective-permute-start | bytes 3145736 | tf_op jit(solution)/shard_map/ppermute | solution.py:573
  104.8 4.2 %collective-permute-start.15 = (f32[2,512,256]{2,1,0:T(8,128)}, f32[2,512,256]{2,1,0:T(8,128)}, u32[]{:S(2)}, u32[]{:S(2)}) collective-permute-start(f32[2,512,256]{2,1,0:T(8,128)} %get-tuple-element.77), channel_id=1, source_target_pairs={{4,5},{5,6},{6,7},{12,13},{13,14},{14,15},{20,21},{21,22},{22,23},... | collective-permute-start | bytes 3145736 | tf_op jit(solution)/shard_map/ppermute | solution.py:573
  109.0 1.4 dynamic-slice_add_fusion
  110.4 0.9 constant_dynamic-slice_fusion.2
  111.3 9.1 %collective-permute-start.11 = (f32[128,512]{1,0:T(8,128)}, f32[128,512]{1,0:T(8,128)}, u32[]{:S(2)}, u32[]{:S(2)}) collective-permute-start(f32[128,512]{1,0:T(8,128)} %get-tuple-element.98), channel_id=1, source_target_pairs={{0,8},{4,12},{8,16},{12,20},{16,24},{20,28},{24,0},{28,4},{1,9},{5... | collective-permute-start | bytes 786440 | tf_op jit(solution)/shard_map/ppermute | solution.py:595
  120.4 1.2 collective-permute-start.13
  121.6 3.7 %collective-permute-done.11 = f32[128,512]{1,0:T(8,128)} collective-permute-done((f32[128,512]{1,0:T(8,128)}, f32[128,512]{1,0:T(8,128)}, u32[]{:S(2)}, u32[]{:S(2)}) %collective-permute-start.11) | collective-permute-done | bytes 262176 | tf_op jit(solution)/shard_map/ppermute | solution.py:595
  125.2 3.7 %collective-permute-done.12 = f32[128,512]{1,0:T(8,128)} collective-permute-done((f32[128,512]{1,0:T(8,128)}, f32[128,512]{1,0:T(8,128)}, u32[]{:S(2)}, u32[]{:S(2)}) %collective-permute-start.12) | collective-permute-done | bytes 262176 | tf_op jit(solution)/shard_map/ppermute | solution.py:595
  129.0 0.8 collective-permute-done.13
  129.7 1.2 add_add_fusion
  130.9 1.9 collective-permute-start.19
  133.0 8.5 %collective-permute-start.16 = (f32[128,512]{1,0:T(8,128)S(1)}, f32[128,512]{1,0:T(8,128)S(1)}, u32[]{:S(2)}, u32[]{:S(2)}) collective-permute-start(f32[128,512]{1,0:T(8,128)S(1)} %add_add_fusion), channel_id=1, source_target_pairs={{0,2},{1,3},{2,0},{3,1},{4,6},{5,7},{6,4},{7,5},{8,10},{9,11},{10,... | collective-permute-start | bytes 786440 | tf_op jit(solution)/shard_map/ppermute | solution.py:595
  141.5 0.8 collective-permute-start.17
  142.3 2.5 %collective-permute-start.18 = (f32[128,512]{1,0:T(8,128)S(1)}, f32[128,512]{1,0:T(8,128)S(1)}, u32[]{:S(2)}, u32[]{:S(2)}) collective-permute-start(f32[128,512]{1,0:T(8,128)S(1)} %add_add_fusion), channel_id=1, source_target_pairs={{0,3},{1,0},{2,1},{3,2},{4,7},{5,4},{6,5},{7,6},{8,11},{9,8},{10,9... | collective-permute-start | bytes 786440 | tf_op jit(solution)/shard_map/ppermute | solution.py:595
  144.7 3.3 %maximum_add_fusion = f32[2,512,512]{2,1,0:T(8,128)} fusion(f32[2,512,512]{2,1,0:T(8,128)S(1)} %copy-done.8, f32[2,512,256]{2,1,0:T(8,128)} %collective-permute-done.10, f32[2,512,256]{2,1,0:T(8,128)} %collective-permute-done.14), kind=kLoop, calls=%fused_computation.2 | loop fusion | flops 1048576 | bytes 6291456 | tf_op jit(solution)/shard_map/add | solution.py:694
  148.1 7.4 %collective-permute-done.16 = f32[128,512]{1,0:T(8,128)S(1)} collective-permute-done((f32[128,512]{1,0:T(8,128)S(1)}, f32[128,512]{1,0:T(8,128)S(1)}, u32[]{:S(2)}, u32[]{:S(2)}) %collective-permute-start.16) | collective-permute-done | bytes 262176 | tf_op jit(solution)/shard_map/ppermute | solution.py:595
  155.4 1.0 collective-permute-done.18
  156.4 0.1 add_multiply_fusion
  156.5 10.2 %collective-permute-start.23 = (f32[2,512,512]{2,1,0:T(8,128)}, f32[2,512,512]{2,1,0:T(8,128)S(1)}, u32[]{:S(2)}, u32[]{:S(2)}) collective-permute-start(f32[2,512,512]{2,1,0:T(8,128)} %maximum_add_fusion), channel_id=1, source_target_pairs={{0,1},{1,2},{2,3},{4,5},{5,6},{6,7},{8,9},{9,10},{10,11},{12,13},{... | collective-permute-start | bytes 6291464 | tf_op jit(solution)/shard_map/ppermute | solution.py:573
  166.8 0.6 collective-permute-done.19
  167.4 0.6 collective-permute-start.20
  168.0 0.6 collective-permute-start.21
  168.6 2.3 %collective-permute-start.22 = (f32[128,512]{1,0:T(8,128)S(1)}, f32[128,512]{1,0:T(8,128)S(1)}, u32[]{:S(2)}, u32[]{:S(2)}) collective-permute-start(f32[128,512]{1,0:T(8,128)S(1)} %add_multiply_fusion), channel_id=1, source_target_pairs={{0,24},{4,28},{8,0},{12,4},{16,8},{20,12},{24,16},{28,20},{1,25},{... | collective-permute-start | bytes 786440 | tf_op jit(solution)/shard_map/ppermute | solution.py:595
  170.9 4.0 %fusion = f32[2,512,1024]{2,1,0:T(8,128)} fusion(f32[2,512,1024]{2,1,0:T(8,128)} %get-tuple-element.84, f32[2,512,768]{2,1,0:T(8,128)} %collective-permute-done.19), kind=kLoop, calls=%fused_computation.1 | loop fusion | flops 524288 | bytes 6291456 | tf_op jit(solution)/shard_map/scatter-add | solution.py:699
  174.9 2.7 %fusion.2 = f32[2,512,1024]{2,1,0:T(8,128)} fusion(f32[2,512,1024]{2,1,0:T(8,128)} %fusion, f32[2,512,768]{2,1,0:T(8,128)} %collective-permute-done.19), kind=kLoop, calls=%fused_computation.8 | loop fusion | flops 262144 | bytes 3145728 | tf_op jit(solution)/shard_map/scatter-add | solution.py:700
  177.6 0.1 broadcast_in_dim.4
  177.8 3.7 %collective-permute-done.21 = f32[128,512]{1,0:T(8,128)S(1)} collective-permute-done((f32[128,512]{1,0:T(8,128)S(1)}, f32[128,512]{1,0:T(8,128)S(1)}, u32[]{:S(2)}, u32[]{:S(2)}) %collective-permute-start.21) | collective-permute-done | bytes 262176 | tf_op jit(solution)/shard_map/ppermute | solution.py:595
  181.5 1.2 collective-permute-start.25
  182.7 2.4 %add.159 = f32[2,512,256]{2,1,0:T(8,128)} add(f32[2,512,256]{2,1,0:T(8,128)S(1)} %copy-done.10, f32[2,512,256]{2,1,0:T(8,128)} %collective-permute-done.15) | non-fusion elementwise | flops 262144 | bytes 3145728 | tf_op jit(solution)/shard_map/add | solution.py:697
  185.1 3.3 %collective-permute-start.24 = (f32[2,512,256]{2,1,0:T(8,128)}, f32[2,512,256]{2,1,0:T(8,128)}, u32[]{:S(2)}, u32[]{:S(2)}) collective-permute-start(f32[2,512,256]{2,1,0:T(8,128)} %add.159), channel_id=1, source_target_pairs={{0,4},{1,5},{2,6},{3,7},{4,8},{5,9},{6,10},{7,11},{8,12},{9,13},{1... | collective-permute-start | bytes 3145736 | tf_op jit(solution)/shard_map/ppermute | solution.py:573
  188.4 1.5 broadcast_select_fusion.1
  189.8 1.5 pad_maximum_fusion
  191.3 19.2 %collective-permute-done.23 = f32[2,512,512]{2,1,0:T(8,128)S(1)} collective-permute-done((f32[2,512,512]{2,1,0:T(8,128)}, f32[2,512,512]{2,1,0:T(8,128)S(1)}, u32[]{:S(2)}, u32[]{:S(2)}) %collective-permute-start.23) | collective-permute-done | bytes 2097184 | tf_op jit(solution)/shard_map/ppermute | solution.py:573
  210.6 1.5 fusion.1
  212.1 3.4 %add_dynamic-update-slice_fusion = f32[2,512,1024]{2,1,0:T(8,128)} fusion(f32[2,512,1024]{2,1,0:T(8,128)} %fusion.2, f32[2,512,512]{2,1,0:T(8,128)S(1)} %fusion.1), kind=kLoop, calls=%fused_computation.4 | loop fusion | flops 524288 | bytes 6291456 | tf_op jit(solution)/shard_map/scatter-add | solution.py:702
  (48 shorter events, 0.5 us)
Async XLA Ops:
  0.6 6.7 %copy-start.7 = (f32[2,512,1024]{2,1,0:T(8,128)S(1)}, f32[2,512,1024]{2,1,0:T(8,128)}, u32[]{:S(2)}) copy-start(f32[2,512,1024]{2,1,0:T(8,128)} %tile_hbm.1) | copy-start | bytes 12582916
  3.8 28.9 %collective-permute-start.3 = (f32[2,512,256]{2,1,0:T(8,128)}, f32[2,512,256]{2,1,0:T(8,128)}, u32[]{:S(2)}, u32[]{:S(2)}) collective-permute-start(f32[2,512,256]{2,1,0:T(8,128)} %get-tuple-element.94), channel_id=1, source_target_pairs={{4,0},{5,1},{6,2},{7,3},{8,4},{9,5},{10,6},{11,7},{12,8},{13,9},{1... | collective-permute-start | bytes 3145736 | tf_op jit(solution)/shard_map/ppermute | solution.py:573
  5.8 8.3 %copy-start.11 = (s32[3,2]{0,1:T(2,128)S(1)}, s32[3,2]{0,1:T(2,128)}, u32[]{:S(2)}) copy-start(s32[3,2]{0,1:T(2,128)} %param.22) | copy-start | bytes 76
  5.8 8.5 %copy-start.12 = (s32[3]{0:T(128)S(1)}, s32[3]{0:T(128)}, u32[]{:S(2)}) copy-start(s32[3]{0:T(128)} %param.23) | copy-start | bytes 40
  5.8 8.7 %copy-start.1 = (f32[3,512,512]{2,1,0:T(8,128)S(1)}, f32[3,512,512]{2,1,0:T(8,128)}, u32[]{:S(2)}) copy-start(f32[3,512,512]{2,1,0:T(8,128)} %amps.1) | copy-start | bytes 9437188
  5.8 28.9 %collective-permute-start = (f32[2,512,256]{2,1,0:T(8,128)}, f32[2,512,256]{2,1,0:T(8,128)}, u32[]{:S(2)}, u32[]{:S(2)}) collective-permute-start(f32[2,512,256]{2,1,0:T(8,128)} %get-tuple-element.95), channel_id=1, source_target_pairs={{1,0},{2,1},{3,2},{5,4},{6,5},{7,6},{9,8},{10,9},{11,10},{13,12},{... | collective-permute-start | bytes 3145736 | tf_op jit(solution)/shard_map/ppermute | solution.py:573
  8.9 58.7 %collective-permute-start.4 = (f32[2,512,512]{2,1,0:T(8,128)}, f32[2,512,512]{2,1,0:T(8,128)}, u32[]{:S(2)}, u32[]{:S(2)}) collective-permute-start(f32[2,512,512]{2,1,0:T(8,128)} %slice.129), channel_id=1, source_target_pairs={{4,0},{5,1},{6,2},{7,3},{8,4},{9,5},{10,6},{11,7},{12,8},{13,9},{1... | collective-permute-start | bytes 6291464 | tf_op jit(solution)/shard_map/ppermute | solution.py:573
  10.8 45.6 %collective-permute-start.1 = (f32[2,512,256]{2,1,0:T(8,128)}, f32[2,512,256]{2,1,0:T(8,128)}, u32[]{:S(2)}, u32[]{:S(2)}) collective-permute-start(f32[2,512,256]{2,1,0:T(8,128)} %get-tuple-element.94), channel_id=1, source_target_pairs={{1,0},{2,1},{3,2},{5,4},{6,5},{7,6},{9,8},{10,9},{11,10},{13,12},{... | collective-permute-start | bytes 3145736 | tf_op jit(solution)/shard_map/ppermute | solution.py:573
  12.1 48.7 %collective-permute-start.2 = (f32[2,512,256]{2,1,0:T(8,128)}, f32[2,512,256]{2,1,0:T(8,128)}, u32[]{:S(2)}, u32[]{:S(2)}) collective-permute-start(f32[2,512,256]{2,1,0:T(8,128)} %get-tuple-element.95), channel_id=1, source_target_pairs={{4,0},{5,1},{6,2},{7,3},{8,4},{9,5},{10,6},{11,7},{12,8},{13,9},{1... | collective-permute-start | bytes 3145736 | tf_op jit(solution)/shard_map/ppermute | solution.py:573
  14.5 1.6 copy-start.2
  16.1 1.0 copy-start.3
  17.1 1.0 copy-start.4
  18.1 10.1 %copy-start = (s32[4,3]{1,0:T(4,128)}, s32[4,3]{1,0:T(4,128)S(1)}, u32[]{:S(2)}) copy-start(s32[4,3]{1,0:T(4,128)S(1)} %concatenate.17.meta) | copy-start | bytes 148
  28.2 2.7 %copy-start.5 = (f32[3,2,512,512]{3,2,1,0:T(8,128)}, f32[3,2,512,512]{3,2,1,0:T(8,128)S(1)}, u32[]{:S(2)}) copy-start(f32[3,2,512,512]{3,2,1,0:T(8,128)S(1)} %get-tuple-element.75.pupil_hbm) | copy-start | bytes 18874372
  30.9 1.7 copy-start.6
  32.7 34.9 %collective-permute-start.8 = (f32[2,512,256]{2,1,0:T(8,128)}, f32[2,512,256]{2,1,0:T(8,128)S(1)}, u32[]{:S(2)}, u32[]{:S(2)}) collective-permute-start(f32[2,512,256]{2,1,0:T(8,128)} %collective-permute-done.3.lower_b_hbm), channel_id=1, source_target_pairs={{5,4},{6,5},{7,6},{13,12},{14,13},{15,14},{21,20},{22,21},{23,22},... | collective-permute-start | bytes 3145736 | tf_op jit(solution)/shard_map/ppermute | solution.py:573
  34.6 33.0 %collective-permute-start.5 = (f32[2,512,256]{2,1,0:T(8,128)}, f32[2,512,256]{2,1,0:T(8,128)S(1)}, u32[]{:S(2)}, u32[]{:S(2)}) collective-permute-start(f32[2,512,256]{2,1,0:T(8,128)} %collective-permute-done.right_a_hbm), channel_id=1, source_target_pairs={{4,0},{5,1},{6,2},{7,3},{8,4},{9,5},{10,6},{11,7},{12,8},{13,9},{1... | collective-permute-start | bytes 3145736 | tf_op jit(solution)/shard_map/ppermute | solution.py:573
  57.8 5.2 %collective-permute-start.6 = (f32[2,512,128]{2,1,0:T(8,128)S(1)}, f32[2,512,128]{2,1,0:T(8,128)}, u32[]{:S(2)}, u32[]{:S(2)}) collective-permute-start(f32[2,512,128]{2,1,0:T(8,128)S(1)} %get-tuple-element.102), channel_id=1, source_target_pairs={{4,0},{5,1},{6,2},{7,3},{12,8},{13,9},{14,10},{15,11},{20,16},{21,... | collective-permute-start | bytes 1572872 | tf_op jit(solution)/shard_map/ppermute | solution.py:573
  60.8 2.9 %collective-permute-start.7 = (f32[2,512,128]{2,1,0:T(8,128)S(1)}, f32[2,512,128]{2,1,0:T(8,128)}, u32[]{:S(2)}, u32[]{:S(2)}) collective-permute-start(f32[2,512,128]{2,1,0:T(8,128)S(1)} %get-tuple-element.101), channel_id=1, source_target_pairs={{4,0},{5,1},{6,2},{7,3},{12,8},{13,9},{14,10},{15,11},{20,16},{21,... | collective-permute-start | bytes 1572872 | tf_op jit(solution)/shard_map/ppermute | solution.py:573
  67.6 1.0 copy-start.13
  67.6 1.4 copy-start.14
  88.3 20.6 %copy-start.9 = (f32[2,512,512]{2,1,0:T(8,128)S(1)}, f32[2,512,512]{2,1,0:T(8,128)}, u32[]{:S(2)}) copy-start(f32[2,512,512]{2,1,0:T(8,128)} %get-tuple-element.76) | copy-start | bytes 6291460
  89.8 19.2 %collective-permute-start.9 = (f32[512,512]{1,0:T(8,128)S(1)}, f32[512,512]{1,0:T(8,128)}, u32[]{:S(2)}, u32[]{:S(2)}) collective-permute-start(f32[512,512]{1,0:T(8,128)S(1)} %constant_dynamic-slice_fusion.3), channel_id=1, source_target_pairs={{0,4},{4,0},{8,12},{12,8},{16,20},{20,16},{24,28},{28,24},{1,5},{5... | collective-permute-start | bytes 3145736 | tf_op jit(solution)/shard_map/ppermute | solution.py:581
  89.9 20.6 %collective-permute-start.10 = (f32[2,512,256]{2,1,0:T(8,128)}, f32[2,512,256]{2,1,0:T(8,128)}, u32[]{:S(2)}, u32[]{:S(2)}) collective-permute-start(f32[2,512,256]{2,1,0:T(8,128)} %get-tuple-element.77), channel_id=1, source_target_pairs={{0,4},{1,5},{2,6},{3,7},{8,12},{9,13},{10,14},{11,15},{16,20},{17,... | collective-permute-start | bytes 3145736 | tf_op jit(solution)/shard_map/ppermute | solution.py:573
  91.2 39.8 %collective-permute-start.14 = (f32[2,512,256]{2,1,0:T(8,128)}, f32[2,512,256]{2,1,0:T(8,128)}, u32[]{:S(2)}, u32[]{:S(2)}) collective-permute-start(f32[2,512,256]{2,1,0:T(8,128)} %get-tuple-element.80), channel_id=1, source_target_pairs={{0,4},{1,5},{2,6},{3,7},{4,8},{5,9},{6,10},{7,11},{8,12},{9,13},{1... | collective-permute-start | bytes 3145736 | tf_op jit(solution)/shard_map/ppermute | solution.py:573
  104.8 26.2 %collective-permute-start.15 = (f32[2,512,256]{2,1,0:T(8,128)}, f32[2,512,256]{2,1,0:T(8,128)}, u32[]{:S(2)}, u32[]{:S(2)}) collective-permute-start(f32[2,512,256]{2,1,0:T(8,128)} %get-tuple-element.77), channel_id=1, source_target_pairs={{4,5},{5,6},{6,7},{12,13},{13,14},{14,15},{20,21},{21,22},{22,23},... | collective-permute-start | bytes 3145736 | tf_op jit(solution)/shard_map/ppermute | solution.py:573
  110.4 34.4 %copy-start.8 = (f32[2,512,512]{2,1,0:T(8,128)S(1)}, f32[2,512,512]{2,1,0:T(8,128)}, u32[]{:S(2)}) copy-start(f32[2,512,512]{2,1,0:T(8,128)} %get-tuple-element.86) | copy-start | bytes 6291460
  111.3 13.9 %collective-permute-start.11 = (f32[128,512]{1,0:T(8,128)}, f32[128,512]{1,0:T(8,128)}, u32[]{:S(2)}, u32[]{:S(2)}) collective-permute-start(f32[128,512]{1,0:T(8,128)} %get-tuple-element.98), channel_id=1, source_target_pairs={{0,8},{4,12},{8,16},{12,20},{16,24},{20,28},{24,0},{28,4},{1,9},{5... | collective-permute-start | bytes 786440 | tf_op jit(solution)/shard_map/ppermute | solution.py:595
  120.4 8.6 %collective-permute-start.12 = (f32[128,512]{1,0:T(8,128)}, f32[128,512]{1,0:T(8,128)}, u32[]{:S(2)}, u32[]{:S(2)}) collective-permute-start(f32[128,512]{1,0:T(8,128)} %get-tuple-element.100), channel_id=1, source_target_pairs={{0,16},{4,20},{8,24},{12,28},{16,0},{20,4},{24,8},{28,12},{1,17},{... | collective-permute-start | bytes 786440 | tf_op jit(solution)/shard_map/ppermute | solution.py:595
  120.4 9.4 %collective-permute-start.13 = (f32[128,512]{1,0:T(8,128)S(1)}, f32[128,512]{1,0:T(8,128)}, u32[]{:S(2)}, u32[]{:S(2)}) collective-permute-start(f32[128,512]{1,0:T(8,128)S(1)} %get-tuple-element.99), channel_id=1, source_target_pairs={{0,24},{4,28},{8,0},{12,4},{16,8},{20,12},{24,16},{28,20},{1,25},{... | collective-permute-start | bytes 786440 | tf_op jit(solution)/shard_map/ppermute | solution.py:595
  130.9 36.4 %collective-permute-start.19 = (f32[2,512,768]{2,1,0:T(8,128)}, f32[2,512,768]{2,1,0:T(8,128)}, u32[]{:S(2)}, u32[]{:S(2)}) collective-permute-start(f32[2,512,768]{2,1,0:T(8,128)} %get-tuple-element.82), channel_id=1, source_target_pairs={{0,4},{1,5},{2,6},{3,7},{4,8},{5,9},{6,10},{7,11},{8,12},{9,13},{1... | collective-permute-start | bytes 9437192 | tf_op jit(solution)/shard_map/ppermute | solution.py:573
  133.0 22.5 %collective-permute-start.16 = (f32[128,512]{1,0:T(8,128)S(1)}, f32[128,512]{1,0:T(8,128)S(1)}, u32[]{:S(2)}, u32[]{:S(2)}) collective-permute-start(f32[128,512]{1,0:T(8,128)S(1)} %add_add_fusion), channel_id=1, source_target_pairs={{0,2},{1,3},{2,0},{3,1},{4,6},{5,7},{6,4},{7,5},{8,10},{9,11},{10,... | collective-permute-start | bytes 786440 | tf_op jit(solution)/shard_map/ppermute | solution.py:595
  141.5 14.0 %collective-permute-start.17 = (f32[128,512]{1,0:T(8,128)S(1)}, f32[128,512]{1,0:T(8,128)S(1)}, u32[]{:S(2)}, u32[]{:S(2)}) collective-permute-start(f32[128,512]{1,0:T(8,128)S(1)} %add_add_fusion), channel_id=1, source_target_pairs={{0,1},{1,2},{2,3},{3,0},{4,5},{5,6},{6,7},{7,4},{8,9},{9,10},{10,1... | collective-permute-start | bytes 786440 | tf_op jit(solution)/shard_map/ppermute | solution.py:595
  142.3 14.2 %collective-permute-start.18 = (f32[128,512]{1,0:T(8,128)S(1)}, f32[128,512]{1,0:T(8,128)S(1)}, u32[]{:S(2)}, u32[]{:S(2)}) collective-permute-start(f32[128,512]{1,0:T(8,128)S(1)} %add_add_fusion), channel_id=1, source_target_pairs={{0,3},{1,0},{2,1},{3,2},{4,7},{5,4},{6,5},{7,6},{8,11},{9,8},{10,9... | collective-permute-start | bytes 786440 | tf_op jit(solution)/shard_map/ppermute | solution.py:595
  156.5 54.0 %collective-permute-start.23 = (f32[2,512,512]{2,1,0:T(8,128)}, f32[2,512,512]{2,1,0:T(8,128)S(1)}, u32[]{:S(2)}, u32[]{:S(2)}) collective-permute-start(f32[2,512,512]{2,1,0:T(8,128)} %maximum_add_fusion), channel_id=1, source_target_pairs={{0,1},{1,2},{2,3},{4,5},{5,6},{6,7},{8,9},{9,10},{10,11},{12,13},{... | collective-permute-start | bytes 6291464 | tf_op jit(solution)/shard_map/ppermute | solution.py:573
  167.4 10.3 %collective-permute-start.20 = (f32[128,512]{1,0:T(8,128)S(1)}, f32[128,512]{1,0:T(8,128)S(1)}, u32[]{:S(2)}, u32[]{:S(2)}) collective-permute-start(f32[128,512]{1,0:T(8,128)S(1)} %add_multiply_fusion), channel_id=1, source_target_pairs={{0,8},{4,12},{8,16},{12,20},{16,24},{20,28},{24,0},{28,4},{1,9},{5... | collective-permute-start | bytes 786440 | tf_op jit(solution)/shard_map/ppermute | solution.py:595
  168.0 13.5 %collective-permute-start.21 = (f32[128,512]{1,0:T(8,128)S(1)}, f32[128,512]{1,0:T(8,128)S(1)}, u32[]{:S(2)}, u32[]{:S(2)}) collective-permute-start(f32[128,512]{1,0:T(8,128)S(1)} %add_multiply_fusion), channel_id=1, source_target_pairs={{0,16},{4,20},{8,24},{12,28},{16,0},{20,4},{24,8},{28,12},{1,17},{... | collective-permute-start | bytes 786440 | tf_op jit(solution)/shard_map/ppermute | solution.py:595
  168.6 12.9 %collective-permute-start.22 = (f32[128,512]{1,0:T(8,128)S(1)}, f32[128,512]{1,0:T(8,128)S(1)}, u32[]{:S(2)}, u32[]{:S(2)}) collective-permute-start(f32[128,512]{1,0:T(8,128)S(1)} %add_multiply_fusion), channel_id=1, source_target_pairs={{0,24},{4,28},{8,0},{12,4},{16,8},{20,12},{24,16},{28,20},{1,25},{... | collective-permute-start | bytes 786440 | tf_op jit(solution)/shard_map/ppermute | solution.py:595
  177.6 5.2 %copy-start.10 = (f32[2,512,256]{2,1,0:T(8,128)S(1)}, f32[2,512,256]{2,1,0:T(8,128)}, u32[]{:S(2)}) copy-start(f32[2,512,256]{2,1,0:T(8,128)} %get-tuple-element.90) | copy-start | bytes 3145732
  181.5 6.9 %collective-permute-start.25 = (f32[512,512]{1,0:T(8,128)S(1)}, f32[512,512]{1,0:T(8,128)}, u32[]{:S(2)}, u32[]{:S(2)}) collective-permute-start(f32[512,512]{1,0:T(8,128)S(1)} %constant_dynamic-update-slice_fusion), channel_id=1, source_target_pairs={{0,4},{4,0},{8,12},{12,8},{16,20},{20,16},{24,28},{28,24},{1,5},{5... | collective-permute-start | bytes 3145736 | tf_op jit(solution)/shard_map/ppermute | solution.py:587
  185.1 25.5 %collective-permute-start.24 = (f32[2,512,256]{2,1,0:T(8,128)}, f32[2,512,256]{2,1,0:T(8,128)}, u32[]{:S(2)}, u32[]{:S(2)}) collective-permute-start(f32[2,512,256]{2,1,0:T(8,128)} %add.159), channel_id=1, source_target_pairs={{0,4},{1,5},{2,6},{3,7},{4,8},{5,9},{6,10},{7,11},{8,12},{9,13},{1... | collective-permute-start | bytes 3145736 | tf_op jit(solution)/shard_map/ppermute | solution.py:573

commit v12 on v11

--- a/solution.py
+++ b/solution.py
@@ -134,10 +134,10 @@
     mat_t_lo_hbm,
     own_out,
     right_out,
+    side_out,
     lower_ca_out,
     lower_b_out,
-    corner_a_out,
-    corner_b_out,
+    corner_out,
     dpup_out,
     region,
     grads,
@@ -222,14 +222,15 @@
         for load in slot_loads(slot):
             load.start()
 
+    cut = corner_out.shape[-1]
     lower_c_out = lower_ca_out.at[:, :, pl.ds(0, tile_cols - side)]
-    lower_a_out = lower_ca_out.at[:, :, pl.ds(tile_cols - side, half)]
+    lower_a_out = lower_ca_out.at[:, :, pl.ds(tile_cols - side, cut)]
     outs = (
-        (corner_a_out, bottom, tile_cols),
-        (corner_b_out, bottom, tile_cols + half),
+        (corner_out, bottom, tile_cols),
         (lower_c_out, bottom, side),
         (lower_a_out, bottom, 0),
-        (lower_b_out, bottom, half),
+        (lower_b_out, bottom, cut),
+        (side_out, pl.ds(0, tile_rows + side), tile_cols + cut),
         (right_out, top, tile_cols),
         (own_out, top, 0),
     )
@@ -240,8 +241,8 @@
         for n, (dst, rows, start) in enumerate(outs)
     ]
     dpup_store = pltpu.make_async_copy(dpup, dpup_out, out_sems.at[7])
-    lower_stores = stores[:5]
-    upper_stores = stores[5:]
+    lower_stores = stores[:4]
+    upper_stores = stores[4:]
 
     zero_rows = 16
 
@@ -448,6 +449,10 @@
         store.wait()
 
 
+def back_cut(side):
+    return 3 * side // 4
+
+
 def slots_call(meta, tile, parts, amps, pupils):
     side = pupils.shape[-1]
     short = side // RADIX
@@ -458,11 +463,16 @@
     anywhere = pl.BlockSpec(memory_space=pl.ANY)
     f32, bf16 = jnp.float32, jnp.bfloat16
     region = (2, tile_rows + side, tile_cols + side)
-    corner = parts[5]
-    right = jax.ShapeDtypeStruct((2, tile_rows, side), f32)
-    lower_ca = jax.ShapeDtypeStruct((2, side, tile_cols - side // 2), f32)
+    cut = back_cut(side)
     dpup = jax.ShapeDtypeStruct(pupils.shape[1:], f32)
-    outs = (tile, right, lower_ca, corner, corner, corner, dpup)
+    shapes = (
+        (tile_rows, cut),
+        (tile_rows + side, side - cut),
+        (side, tile_cols - side + cut),
+        (side, side - cut),
+        (side, cut),
+    )
+    outs = (tile, *(jax.ShapeDtypeStruct((2, *shape), f32) for shape in shapes), dpup)
     table = pltpu.VMEM(high.shape, bf16)
     return pl.pallas_call(
         slots_kernel,
@@ -670,7 +680,7 @@
         corner_up_b,
         corner_side,
     )
-    own_g, right_g, lower_ca_g, lower_b_g, corner_a_g, corner_b_g, dpup = slots_call(
+    own_g, right_g, side_g, lower_ca_g, lower_b_g, corner_g, dpup = slots_call(
         meta, spectrum, parts, amps, pupils
     )
 
@@ -680,26 +690,24 @@
     def right(i, j):
         return (i, j + 1)
 
+    cut = back_cut(side)
+    split_at = tile_cols - side
     part = halve(dpup.reshape(-1, side), 1)
-    back_a = send(corner_a_g, down)
-    back_side = send(corner_b_g, lambda i, j: (i, j + 1) if i % 2 else None)
-    back_down = send(corner_b_g, lambda i, j: None if i % 2 else (i + 1, j))
-    part, back_down = lax.optimization_barrier((part, back_down))
+    corner = send(corner_g, down)
+    beside = send(side_g, right)
     part = scatter(part, "ty", 2)
-    part, lower_ca_g, back_a, back_side = lax.optimization_barrier(
-        (part, lower_ca_g, back_a, back_side)
-    )
+    part, lower_ca_g, corner, beside = lax.optimization_barrier((part, lower_ca_g, corner, beside))
     lower_ca = send(lower_ca_g, down)
     part = sum_all(part, "tx") * (1.0 / math.sqrt(n_ty * n_tx))
-    right_g = right_g + jnp.concatenate([back_a, back_down], axis=2)
-    right_back = send(after(right_g, part), right)
+    right_back = send(after(right_g + corner, part), right)
     part = gather(after(part, lower_ca), "ty", 2)
-    lower_b = send(after(lower_b_g + back_side, part), down)
-    split_at = tile_cols - side
+    lower_b = send(after(lower_b_g + beside[:, tile_rows:], part), down)
     spec_grad = own_g.at[:, :, side:].add(lower_ca[:, :, :split_at])
-    spec_grad = spec_grad.at[:, :, :half].add(lower_ca[:, :, split_at:])
+    spec_grad = spec_grad.at[:, :, :cut].add(lower_ca[:, :, split_at:])
+    spec_grad = spec_grad.at[:, :, cut:side].add(beside[:, :tile_rows])
     part, spec_grad = lax.optimization_barrier((part, spec_grad))
-    spec_grad = spec_grad.at[:, :, :side].add(right_back.at[:, :, half:].add(lower_b))
+    spec_grad = spec_grad.at[:, :, cut:side].add(lower_b)
+    spec_grad = spec_grad.at[:, :, :cut].add(right_back)
     return spec_grad, double(part, 1).reshape(pupil.shape)
 
 

time: 218 us -> 219 us (level)
  waiting for transfers between devices: 65.4 us -> 76.9 us
  starting transfers between devices: 78.3 us -> 68.1 us
    ppermute x9, starting transfers between devices: 25.5 us -> 12.1 us  [stepped(): lax.ppermute(value, axis, [(i, (i + step * inner) % size) for i in range(...]
    ppermute x9, waiting for transfers between devices: 20.2 us -> 33.2 us  [stepped(): lax.ppermute(value, axis, [(i, (i + step * inner) % size) for i in range(...]
    ppermute x15 -> x14, starting transfers between devices: 51.5 us -> 55.2 us  [send(): return lax.ppermute(array, ('ty', 'tx'), along(rule, sizes))]
    ppermute x15 -> x14, waiting for transfers between devices: 45.2 us -> 43.8 us  [send(): return lax.ppermute(array, ('ty', 'tx'), along(rule, sizes))]
    unnamed x32 -> x30, local copies, waits for them, and re-layouts: 9.65 us -> 9.67 us
  transfers between devices with their start and end apart: 26 -> 25, of which waited for: 12 -> 11; matrix products, arithmetic and copies ran while one was open for 10% -> 11% of each run, Pallas kernels for 5% -> 5%
where the time goes in v12:
time: 219 us; the launch traced here: 216 us
  waiting for transfers between devices  76.9 us (35%)
  starting transfers between devices  68.1 us (31%)
  Pallas kernels  29.4 us (13%)
  other arithmetic  23 us (11%)
  local copies, waits for them, and re-layouts  18 us (8%)
    ppermute x14, starting transfers between devices, send(): return lax.ppermute(array, ('ty', 'tx'), along(rule, sizes))  55.2 us
    ppermute x14, waiting for transfers between devices, send(): return lax.ppermute(array, ('ty', 'tx'), along(rule, sizes))  43.8 us
    ppermute x9, waiting for transfers between devices, stepped(): lax.ppermute(value, axis, [(i, (i + step * inner) % size) for i in range(...  33.2 us
    pallas_call x1, Pallas kernels, slots_call(): pl.pallas_call(slots_kernel, out_shape=[jax.ShapeDtypeStruct(x.shape, f32...  19.4 us
    ppermute x9, starting transfers between devices, stepped(): lax.ppermute(value, axis, [(i, (i + step * inner) % size) for i in range(...  12.1 us
    pallas_call x1, Pallas kernels, prepare(): pl.pallas_call(prepare_kernel, grid=(slots,), out_shape=[jax.ShapeDtypeSt...  10 us
    unnamed x30, local copies, waits for them, and re-layouts  9.67 us
  transfers between devices with their start and end apart: 25, of which 11 were waited for; matrix products, arithmetic and copies ran while one was open for 11% of the time, Pallas kernels for 5%

profile of v12, /device:TPU:1, one launch (start us, length us, event | category | flops | bytes accessed | tf_op | source)
XLA Modules:
  0.0 216.4 jit_solution(9415818478922782017)
XLA Ops:
  0.6 3.1 %fusion.4 = (f32[2,512,256]{2,1,0:T(8,128)}, f32[2,512,256]{2,1,0:T(8,128)}) fusion(f32[2,512,1024]{2,1,0:T(8,128)} %tile_hbm.1), kind=kLoop, calls=%fused_computation.27 | loop fusion | bytes 4194304 | tf_op jit(solution)/shard_map/slice | solution.py:662
  3.8 2.2 %collective-permute-start.3 = (f32[2,512,256]{2,1,0:T(8,128)}, f32[2,512,256]{2,1,0:T(8,128)}, u32[]{:S(2)}, u32[]{:S(2)}) collective-permute-start(f32[2,512,256]{2,1,0:T(8,128)} %get-tuple-element.102), channel_id=1, source_target_pairs={{4,0},{5,1},{6,2},{7,3},{8,4},{9,5},{10,6},{11,7},{12,8},{13,9},{1... | collective-permute-start | bytes 3145736 | tf_op jit(solution)/shard_map/ppermute | solution.py:583
  6.0 1.3 collective-permute-start
  7.3 1.5 slice.159
  8.9 1.9 collective-permute-start.4
  10.8 1.3 collective-permute-start.1
  12.1 1.9 collective-permute-start.2
  14.1 0.1 copy.16
  14.2 0.1 copy.17
  14.2 0.1 copy.15
  14.3 0.1 pad_add_fusion
  14.4 0.0 copy-start.2
  14.4 1.6 copy-done.2
  16.0 1.0 copy-done.3
  17.1 1.0 copy-done.4
  18.1 10.0 %prepare.1 = (f32[3,512,512]{2,1,0:T(8,128)S(1)}, f32[3,2,512,512]{3,2,1,0:T(8,128)S(1)}) custom-call(s32[4,3]{1,0:T(4,128)S(1)} %concatenate.16.meta, f32[3,512,512]{2,1,0:T(8,128)S(1)} %copy-done.1, f32[2,512,512]{2,1,0:T(8,128)S(1)} %copy-done.2, bf16[512,512]{1,0:T(8,128)(2,1)S(1)} %copy-done.3, bf16[512,512]{1,0:T(8,128)(2,1)S(1)} %copy-done.4), custom_call_target="tpu_custom_call" | custom-call | flops 4831838208 | bytes 18874368 | tf_op jit(solution)/shard_map/prepare/pallas_call | solution.py:547
  28.2 2.7 %copy-done.5 = f32[3,2,512,512]{3,2,1,0:T(8,128)} copy-done((f32[3,2,512,512]{3,2,1,0:T(8,128)}, f32[3,2,512,512]{3,2,1,0:T(8,128)S(1)}, u32[]{:S(2)}) %copy-start.5) | copy-done | bytes 6291480
  30.8 1.8 copy-done.6
  32.6 1.3 collective-permute-start.8
  33.9 0.7 collective-permute-done.right_a_hbm
  34.6 1.9 collective-permute-start.5
  36.5 19.9 %collective-permute-done.1.right_b_hbm = f32[2,512,256]{2,1,0:T(8,128)} collective-permute-done((f32[2,512,256]{2,1,0:T(8,128)}, f32[2,512,256]{2,1,0:T(8,128)}, u32[]{:S(2)}, u32[]{:S(2)}) %collective-permute-start.1) | collective-permute-done | bytes 1048608 | tf_op jit(solution)/shard_map/ppermute | solution.py:583
  56.4 1.3 fusion.5
  57.7 3.1 %collective-permute-start.6 = (f32[2,512,128]{2,1,0:T(8,128)S(1)}, f32[2,512,128]{2,1,0:T(8,128)}, u32[]{:S(2)}, u32[]{:S(2)}) collective-permute-start(f32[2,512,128]{2,1,0:T(8,128)S(1)} %get-tuple-element.112), channel_id=1, source_target_pairs={{4,0},{5,1},{6,2},{7,3},{12,8},{13,9},{14,10},{15,11},{20,16},{21,... | collective-permute-start | bytes 1572872 | tf_op jit(solution)/shard_map/ppermute | solution.py:583
  60.8 2.1 collective-permute-start.7
  62.9 0.9 collective-permute-done.7.corner_up_b_hbm
  63.7 3.8 %collective-permute-done.8.corner_side_hbm = f32[2,512,256]{2,1,0:T(8,128)S(1)} collective-permute-done((f32[2,512,256]{2,1,0:T(8,128)}, f32[2,512,256]{2,1,0:T(8,128)S(1)}, u32[]{:S(2)}, u32[]{:S(2)}) %collective-permute-start.8) | collective-permute-done | bytes 1048608 | tf_op jit(solution)/shard_map/ppermute | solution.py:583
  67.6 1.0 copy-done.12
  68.6 0.3 copy-done.13
  68.9 19.4 %slots.1 = (f32[2,512,1024]{2,1,0:T(8,128)}, f32[2,512,384]{2,1,0:T(8,128)}, f32[2,1024,128]{2,1,0:T(8,128)}, f32[2,512,896]{2,1,0:T(8,128)}, f32[2,512,128]{2,1...) custom-call(s32[4,3]{1,0:T(4,128)} %copy-done, f32[2,512,1024]{2,1,0:T(8,128)} %tile_hbm.1, ...), custom_call_target="tpu_custom_call" | custom-call | flops 9663676416 | bytes 41943040 | tf_op jit(solution)/shard_map/slots/pallas_call | solution.py:477
  88.3 1.3 constant_dynamic-slice_fusion.3
  89.6 0.1 collective-permute-start.9
  89.7 16.6 %collective-permute-start.13 = (f32[2,512,384]{2,1,0:T(8,128)}, f32[2,512,384]{2,1,0:T(8,128)}, u32[]{:S(2)}, u32[]{:S(2)}) collective-permute-start(f32[2,512,384]{2,1,0:T(8,128)} %get-tuple-element.88), channel_id=1, source_target_pairs={{0,4},{1,5},{2,6},{3,7},{4,8},{5,9},{6,10},{7,11},{8,12},{9,13},{1... | collective-permute-start | bytes 4718600 | tf_op jit(solution)/shard_map/ppermute | solution.py:583
  106.3 7.5 %collective-permute-start.14 = (f32[2,1024,128]{2,1,0:T(8,128)}, f32[2,1024,128]{2,1,0:T(8,128)}, u32[]{:S(2)}, u32[]{:S(2)}) collective-permute-start(f32[2,1024,128]{2,1,0:T(8,128)} %get-tuple-element.89), channel_id=1, source_target_pairs={{0,1},{1,2},{2,3},{4,5},{5,6},{6,7},{8,9},{9,10},{10,11},{12,13},{... | collective-permute-start | bytes 3145736 | tf_op jit(solution)/shard_map/ppermute | solution.py:583
  113.9 1.7 dynamic-slice_add_fusion
  115.6 0.8 constant_dynamic-slice_fusion.2
  116.4 1.2 collective-permute-start.10
  117.6 1.2 collective-permute-start.12
  118.8 13.6 %collective-permute-done.10 = f32[128,512]{1,0:T(8,128)S(1)} collective-permute-done((f32[128,512]{1,0:T(8,128)}, f32[128,512]{1,0:T(8,128)S(1)}, u32[]{:S(2)}, u32[]{:S(2)}) %collective-permute-start.10) | collective-permute-done | bytes 262176 | tf_op jit(solution)/shard_map/ppermute | solution.py:605
  132.4 6.9 %collective-permute-done.11 = f32[128,512]{1,0:T(8,128)} collective-permute-done((f32[128,512]{1,0:T(8,128)S(1)}, f32[128,512]{1,0:T(8,128)}, u32[]{:S(2)}, u32[]{:S(2)}) %collective-permute-start.11) | collective-permute-done | bytes 262176 | tf_op jit(solution)/shard_map/ppermute | solution.py:605
  139.3 0.8 collective-permute-done.12
  140.1 1.1 add_add_fusion
  141.3 1.9 collective-permute-start.18
  143.2 2.4 %collective-permute-start.15 = (f32[128,512]{1,0:T(8,128)S(1)}, f32[128,512]{1,0:T(8,128)S(1)}, u32[]{:S(2)}, u32[]{:S(2)}) collective-permute-start(f32[128,512]{1,0:T(8,128)S(1)} %add_add_fusion), channel_id=1, source_target_pairs={{0,2},{1,3},{2,0},{3,1},{4,6},{5,7},{6,4},{7,5},{8,10},{9,11},{10,... | collective-permute-start | bytes 786440 | tf_op jit(solution)/shard_map/ppermute | solution.py:605
  145.6 3.3 %collective-permute-start.17 = (f32[128,512]{1,0:T(8,128)S(1)}, f32[128,512]{1,0:T(8,128)S(1)}, u32[]{:S(2)}, u32[]{:S(2)}) collective-permute-start(f32[128,512]{1,0:T(8,128)S(1)} %add_add_fusion), channel_id=1, source_target_pairs={{0,3},{1,0},{2,1},{3,2},{4,7},{5,4},{6,5},{7,6},{8,11},{9,8},{10,9... | collective-permute-start | bytes 786440 | tf_op jit(solution)/shard_map/ppermute | solution.py:605
  148.8 2.7 %add.168 = f32[2,512,384]{2,1,0:T(8,128)} add(f32[2,512,384]{2,1,0:T(8,128)S(1)} %copy-done.8, f32[2,512,384]{2,1,0:T(8,128)} %collective-permute-done.13) | non-fusion elementwise | flops 393216 | bytes 4718592 | tf_op jit(solution)/shard_map/add | solution.py:702
  151.5 11.0 %collective-permute-done.15 = f32[128,512]{1,0:T(8,128)S(1)} collective-permute-done((f32[128,512]{1,0:T(8,128)S(1)}, f32[128,512]{1,0:T(8,128)S(1)}, u32[]{:S(2)}, u32[]{:S(2)}) %collective-permute-start.15) | collective-permute-done | bytes 262176 | tf_op jit(solution)/shard_map/ppermute | solution.py:605
  162.6 0.1 add_multiply_fusion
  162.7 7.9 %collective-permute-start.23 = (f32[2,512,384]{2,1,0:T(8,128)}, f32[2,512,384]{2,1,0:T(8,128)S(1)}, u32[]{:S(2)}, u32[]{:S(2)}) collective-permute-start(f32[2,512,384]{2,1,0:T(8,128)} %add.168), channel_id=1, source_target_pairs={{0,1},{1,2},{2,3},{4,5},{5,6},{6,7},{8,9},{9,10},{10,11},{12,13},{... | collective-permute-start | bytes 4718600 | tf_op jit(solution)/shard_map/ppermute | solution.py:583
  170.6 12.7 %collective-permute-done.18 = f32[2,512,896]{2,1,0:T(8,128)} collective-permute-done((f32[2,512,896]{2,1,0:T(8,128)}, f32[2,512,896]{2,1,0:T(8,128)}, u32[]{:S(2)}, u32[]{:S(2)}) %collective-permute-start.18) | collective-permute-done | bytes 3670048 | tf_op jit(solution)/shard_map/ppermute | solution.py:583
  183.3 2.9 %collective-permute-start.19 = (f32[128,512]{1,0:T(8,128)S(1)}, f32[128,512]{1,0:T(8,128)S(1)}, u32[]{:S(2)}, u32[]{:S(2)}) collective-permute-start(f32[128,512]{1,0:T(8,128)S(1)} %add_multiply_fusion), channel_id=1, source_target_pairs={{0,8},{4,12},{8,16},{12,20},{16,24},{20,28},{24,0},{28,4},{1,9},{5... | collective-permute-start | bytes 786440 | tf_op jit(solution)/shard_map/ppermute | solution.py:605
  186.2 1.2 collective-permute-start.21
  187.4 4.0 %fusion = f32[2,512,1024]{2,1,0:T(8,128)} fusion(f32[2,512,1024]{2,1,0:T(8,128)} %get-tuple-element.93, f32[2,512,896]{2,1,0:T(8,128)} %collective-permute-done.18), kind=kLoop, calls=%fused_computation.1 | loop fusion | flops 524288 | bytes 6291456 | tf_op jit(solution)/shard_map/scatter-add | solution.py:705
  191.4 3.2 %fusion.2 = f32[2,512,1024]{2,1,0:T(8,128)} fusion(f32[2,512,1024]{2,1,0:T(8,128)} %fusion, f32[2,512,896]{2,1,0:T(8,128)} %collective-permute-done.18), kind=kLoop, calls=%fused_computation.6 | loop fusion | flops 393216 | bytes 4718592 | tf_op jit(solution)/shard_map/scatter-add | solution.py:706
  194.6 2.5 %slice_add_fusion.4 = (f32[2,512,128]{2,1,0:T(8,128)}, f32[2,512,1024]{2,1,0:T(8,128)}) fusion(f32[2,512,128]{2,1,0:T(8,128)S(1)} %copy-done.9, f32[2,1024,128]{2,1,0:T(8,128)} %collective-permute-done.14, f32[2,512,1024]{2,1,0:T(8,128)} %fusion.2), kind=kLoop, calls=%fused_computation.11 | loop fusion | flops 262144 | bytes 3145728 | tf_op jit(solution)/shard_map/add | solution.py:704
  197.1 0.1 broadcast_in_dim.4
  197.3 0.8 collective-permute-done.20
  198.1 4.3 %collective-permute-start.22 = (f32[2,512,128]{2,1,0:T(8,128)}, f32[2,512,128]{2,1,0:T(8,128)S(1)}, u32[]{:S(2)}, u32[]{:S(2)}) collective-permute-start(f32[2,512,128]{2,1,0:T(8,128)} %get-tuple-element.97), channel_id=1, source_target_pairs={{0,4},{1,5},{2,6},{3,7},{4,8},{5,9},{6,10},{7,11},{8,12},{9,13},{1... | collective-permute-start | bytes 1572872 | tf_op jit(solution)/shard_map/ppermute | solution.py:583
  202.4 0.7 collective-permute-start.24
  203.1 5.7 %collective-permute-done.22 = f32[2,512,128]{2,1,0:T(8,128)S(1)} collective-permute-done((f32[2,512,128]{2,1,0:T(8,128)}, f32[2,512,128]{2,1,0:T(8,128)S(1)}, u32[]{:S(2)}, u32[]{:S(2)}) %collective-permute-start.22) | collective-permute-done | bytes 524320 | tf_op jit(solution)/shard_map/ppermute | solution.py:583
  208.8 1.9 add_dynamic-update-slice_fusion
  210.7 2.7 %fusion.1 = f32[2,512,1024]{2,1,0:T(8,128)} fusion(f32[2,512,1024]{2,1,0:T(8,128)} %add_dynamic-update-slice_fusion, f32[2,512,384]{2,1,0:T(8,128)S(1)} %collective-permute-done.23), kind=kLoop, calls=%fused_computation.4 | loop fusion | flops 393216 | bytes 4718592 | tf_op jit(solution)/shard_map/scatter-add | solution.py:710
  213.4 1.4 broadcast_select_fusion.1
  214.9 1.5 pad_maximum_fusion
  (44 shorter events, 0.2 us)
Async XLA Ops:
  0.6 6.7 %copy-start.7 = (f32[2,512,1024]{2,1,0:T(8,128)S(1)}, f32[2,512,1024]{2,1,0:T(8,128)}, u32[]{:S(2)}) copy-start(f32[2,512,1024]{2,1,0:T(8,128)} %tile_hbm.1) | copy-start | bytes 12582916
  3.8 10.2 %copy-start.10 = (s32[3,2]{0,1:T(2,128)S(1)}, s32[3,2]{0,1:T(2,128)}, u32[]{:S(2)}) copy-start(s32[3,2]{0,1:T(2,128)} %param.24) | copy-start | bytes 76
  3.8 10.5 %copy-start.11 = (s32[3]{0:T(128)S(1)}, s32[3]{0:T(128)}, u32[]{:S(2)}) copy-start(s32[3]{0:T(128)} %param.25) | copy-start | bytes 40
  3.8 10.6 %copy-start.1 = (f32[3,512,512]{2,1,0:T(8,128)S(1)}, f32[3,512,512]{2,1,0:T(8,128)}, u32[]{:S(2)}) copy-start(f32[3,512,512]{2,1,0:T(8,128)} %amps.1) | copy-start | bytes 9437188
  3.8 28.8 %collective-permute-start.3 = (f32[2,512,256]{2,1,0:T(8,128)}, f32[2,512,256]{2,1,0:T(8,128)}, u32[]{:S(2)}, u32[]{:S(2)}) collective-permute-start(f32[2,512,256]{2,1,0:T(8,128)} %get-tuple-element.102), channel_id=1, source_target_pairs={{4,0},{5,1},{6,2},{7,3},{8,4},{9,5},{10,6},{11,7},{12,8},{13,9},{1... | collective-permute-start | bytes 3145736 | tf_op jit(solution)/shard_map/ppermute | solution.py:583
  6.0 28.6 %collective-permute-start = (f32[2,512,256]{2,1,0:T(8,128)}, f32[2,512,256]{2,1,0:T(8,128)}, u32[]{:S(2)}, u32[]{:S(2)}) collective-permute-start(f32[2,512,256]{2,1,0:T(8,128)} %get-tuple-element.103), channel_id=1, source_target_pairs={{1,0},{2,1},{3,2},{5,4},{6,5},{7,6},{9,8},{10,9},{11,10},{13,12},{... | collective-permute-start | bytes 3145736 | tf_op jit(solution)/shard_map/ppermute | solution.py:583
  8.9 58.7 %collective-permute-start.4 = (f32[2,512,512]{2,1,0:T(8,128)}, f32[2,512,512]{2,1,0:T(8,128)}, u32[]{:S(2)}, u32[]{:S(2)}) collective-permute-start(f32[2,512,512]{2,1,0:T(8,128)} %slice.159), channel_id=1, source_target_pairs={{4,0},{5,1},{6,2},{7,3},{8,4},{9,5},{10,6},{11,7},{12,8},{13,9},{1... | collective-permute-start | bytes 6291464 | tf_op jit(solution)/shard_map/ppermute | solution.py:583
  10.8 45.6 %collective-permute-start.1 = (f32[2,512,256]{2,1,0:T(8,128)}, f32[2,512,256]{2,1,0:T(8,128)}, u32[]{:S(2)}, u32[]{:S(2)}) collective-permute-start(f32[2,512,256]{2,1,0:T(8,128)} %get-tuple-element.102), channel_id=1, source_target_pairs={{1,0},{2,1},{3,2},{5,4},{6,5},{7,6},{9,8},{10,9},{11,10},{13,12},{... | collective-permute-start | bytes 3145736 | tf_op jit(solution)/shard_map/ppermute | solution.py:583
  12.1 48.7 %collective-permute-start.2 = (f32[2,512,256]{2,1,0:T(8,128)}, f32[2,512,256]{2,1,0:T(8,128)}, u32[]{:S(2)}, u32[]{:S(2)}) collective-permute-start(f32[2,512,256]{2,1,0:T(8,128)} %get-tuple-element.103), channel_id=1, source_target_pairs={{4,0},{5,1},{6,2},{7,3},{8,4},{9,5},{10,6},{11,7},{12,8},{13,9},{1... | collective-permute-start | bytes 3145736 | tf_op jit(solution)/shard_map/ppermute | solution.py:583
  14.4 1.6 copy-start.2
  16.0 1.0 copy-start.3
  17.1 1.0 copy-start.4
  18.1 10.0 %copy-start = (s32[4,3]{1,0:T(4,128)}, s32[4,3]{1,0:T(4,128)S(1)}, u32[]{:S(2)}) copy-start(s32[4,3]{1,0:T(4,128)S(1)} %concatenate.16.meta) | copy-start | bytes 148
  28.2 2.7 %copy-start.5 = (f32[3,2,512,512]{3,2,1,0:T(8,128)}, f32[3,2,512,512]{3,2,1,0:T(8,128)S(1)}, u32[]{:S(2)}) copy-start(f32[3,2,512,512]{3,2,1,0:T(8,128)S(1)} %get-tuple-element.85.pupil_hbm) | copy-start | bytes 18874372
  30.8 1.8 copy-start.6
  32.6 35.0 %collective-permute-start.8 = (f32[2,512,256]{2,1,0:T(8,128)}, f32[2,512,256]{2,1,0:T(8,128)S(1)}, u32[]{:S(2)}, u32[]{:S(2)}) collective-permute-start(f32[2,512,256]{2,1,0:T(8,128)} %collective-permute-done.3.lower_b_hbm), channel_id=1, source_target_pairs={{5,4},{6,5},{7,6},{13,12},{14,13},{15,14},{21,20},{22,21},{23,22},... | collective-permute-start | bytes 3145736 | tf_op jit(solution)/shard_map/ppermute | solution.py:583
  34.6 33.0 %collective-permute-start.5 = (f32[2,512,256]{2,1,0:T(8,128)}, f32[2,512,256]{2,1,0:T(8,128)S(1)}, u32[]{:S(2)}, u32[]{:S(2)}) collective-permute-start(f32[2,512,256]{2,1,0:T(8,128)} %collective-permute-done.right_a_hbm), channel_id=1, source_target_pairs={{4,0},{5,1},{6,2},{7,3},{8,4},{9,5},{10,6},{11,7},{12,8},{13,9},{1... | collective-permute-start | bytes 3145736 | tf_op jit(solution)/shard_map/ppermute | solution.py:583
  57.7 5.1 %collective-permute-start.6 = (f32[2,512,128]{2,1,0:T(8,128)S(1)}, f32[2,512,128]{2,1,0:T(8,128)}, u32[]{:S(2)}, u32[]{:S(2)}) collective-permute-start(f32[2,512,128]{2,1,0:T(8,128)S(1)} %get-tuple-element.112), channel_id=1, source_target_pairs={{4,0},{5,1},{6,2},{7,3},{12,8},{13,9},{14,10},{15,11},{20,16},{21,... | collective-permute-start | bytes 1572872 | tf_op jit(solution)/shard_map/ppermute | solution.py:583
  60.8 2.9 %collective-permute-start.7 = (f32[2,512,128]{2,1,0:T(8,128)S(1)}, f32[2,512,128]{2,1,0:T(8,128)}, u32[]{:S(2)}, u32[]{:S(2)}) collective-permute-start(f32[2,512,128]{2,1,0:T(8,128)S(1)} %get-tuple-element.111), channel_id=1, source_target_pairs={{4,0},{5,1},{6,2},{7,3},{12,8},{13,9},{14,10},{15,11},{20,16},{21,... | collective-permute-start | bytes 1572872 | tf_op jit(solution)/shard_map/ppermute | solution.py:583
  67.6 1.1 copy-start.12
  67.6 1.3 copy-start.13
  89.6 24.2 %collective-permute-start.9 = (f32[512,512]{1,0:T(8,128)S(1)}, f32[512,512]{1,0:T(8,128)}, u32[]{:S(2)}, u32[]{:S(2)}) collective-permute-start(f32[512,512]{1,0:T(8,128)S(1)} %constant_dynamic-slice_fusion.3), channel_id=1, source_target_pairs={{0,4},{4,0},{8,12},{12,8},{16,20},{20,16},{24,28},{28,24},{1,5},{5... | collective-permute-start | bytes 3145736 | tf_op jit(solution)/shard_map/ppermute | solution.py:591
  89.7 51.6 %collective-permute-start.13 = (f32[2,512,384]{2,1,0:T(8,128)}, f32[2,512,384]{2,1,0:T(8,128)}, u32[]{:S(2)}, u32[]{:S(2)}) collective-permute-start(f32[2,512,384]{2,1,0:T(8,128)} %get-tuple-element.88), channel_id=1, source_target_pairs={{0,4},{1,5},{2,6},{3,7},{4,8},{5,9},{6,10},{7,11},{8,12},{9,13},{1... | collective-permute-start | bytes 4718600 | tf_op jit(solution)/shard_map/ppermute | solution.py:583
  106.3 42.5 %copy-start.8 = (f32[2,512,384]{2,1,0:T(8,128)S(1)}, f32[2,512,384]{2,1,0:T(8,128)}, u32[]{:S(2)}) copy-start(f32[2,512,384]{2,1,0:T(8,128)} %get-tuple-element.98) | copy-start | bytes 4718596
  106.3 34.9 %collective-permute-start.14 = (f32[2,1024,128]{2,1,0:T(8,128)}, f32[2,1024,128]{2,1,0:T(8,128)}, u32[]{:S(2)}, u32[]{:S(2)}) collective-permute-start(f32[2,1024,128]{2,1,0:T(8,128)} %get-tuple-element.89), channel_id=1, source_target_pairs={{0,1},{1,2},{2,3},{4,5},{5,6},{6,7},{8,9},{9,10},{10,11},{12,13},{... | collective-permute-start | bytes 3145736 | tf_op jit(solution)/shard_map/ppermute | solution.py:583
  116.4 16.0 %collective-permute-start.10 = (f32[128,512]{1,0:T(8,128)}, f32[128,512]{1,0:T(8,128)S(1)}, u32[]{:S(2)}, u32[]{:S(2)}) collective-permute-start(f32[128,512]{1,0:T(8,128)} %get-tuple-element.108), channel_id=1, source_target_pairs={{0,8},{4,12},{8,16},{12,20},{16,24},{20,28},{24,0},{28,4},{1,9},{5... | collective-permute-start | bytes 786440 | tf_op jit(solution)/shard_map/ppermute | solution.py:605
  117.6 21.7 %collective-permute-start.11 = (f32[128,512]{1,0:T(8,128)S(1)}, f32[128,512]{1,0:T(8,128)}, u32[]{:S(2)}, u32[]{:S(2)}) collective-permute-start(f32[128,512]{1,0:T(8,128)S(1)} %get-tuple-element.110), channel_id=1, source_target_pairs={{0,16},{4,20},{8,24},{12,28},{16,0},{20,4},{24,8},{28,12},{1,17},{... | collective-permute-start | bytes 786440 | tf_op jit(solution)/shard_map/ppermute | solution.py:605
  117.6 22.5 %collective-permute-start.12 = (f32[128,512]{1,0:T(8,128)S(1)}, f32[128,512]{1,0:T(8,128)}, u32[]{:S(2)}, u32[]{:S(2)}) collective-permute-start(f32[128,512]{1,0:T(8,128)S(1)} %get-tuple-element.109), channel_id=1, source_target_pairs={{0,24},{4,28},{8,0},{12,4},{16,8},{20,12},{24,16},{28,20},{1,25},{... | collective-permute-start | bytes 786440 | tf_op jit(solution)/shard_map/ppermute | solution.py:605
  141.3 42.1 %collective-permute-start.18 = (f32[2,512,896]{2,1,0:T(8,128)}, f32[2,512,896]{2,1,0:T(8,128)}, u32[]{:S(2)}, u32[]{:S(2)}) collective-permute-start(f32[2,512,896]{2,1,0:T(8,128)} %get-tuple-element.91), channel_id=1, source_target_pairs={{0,4},{1,5},{2,6},{3,7},{4,8},{5,9},{6,10},{7,11},{8,12},{9,13},{1... | collective-permute-start | bytes 11010056 | tf_op jit(solution)/shard_map/ppermute | solution.py:583
  143.2 19.4 %collective-permute-start.15 = (f32[128,512]{1,0:T(8,128)S(1)}, f32[128,512]{1,0:T(8,128)S(1)}, u32[]{:S(2)}, u32[]{:S(2)}) collective-permute-start(f32[128,512]{1,0:T(8,128)S(1)} %add_add_fusion), channel_id=1, source_target_pairs={{0,2},{1,3},{2,0},{3,1},{4,6},{5,7},{6,4},{7,5},{8,10},{9,11},{10,... | collective-permute-start | bytes 786440 | tf_op jit(solution)/shard_map/ppermute | solution.py:605
  145.6 17.0 %collective-permute-start.16 = (f32[128,512]{1,0:T(8,128)S(1)}, f32[128,512]{1,0:T(8,128)S(1)}, u32[]{:S(2)}, u32[]{:S(2)}) collective-permute-start(f32[128,512]{1,0:T(8,128)S(1)} %add_add_fusion), channel_id=1, source_target_pairs={{0,1},{1,2},{2,3},{3,0},{4,5},{5,6},{6,7},{7,4},{8,9},{9,10},{10,1... | collective-permute-start | bytes 786440 | tf_op jit(solution)/shard_map/ppermute | solution.py:605
  145.6 17.0 %collective-permute-start.17 = (f32[128,512]{1,0:T(8,128)S(1)}, f32[128,512]{1,0:T(8,128)S(1)}, u32[]{:S(2)}, u32[]{:S(2)}) collective-permute-start(f32[128,512]{1,0:T(8,128)S(1)} %add_add_fusion), channel_id=1, source_target_pairs={{0,3},{1,0},{2,1},{3,2},{4,7},{5,4},{6,5},{7,6},{8,11},{9,8},{10,9... | collective-permute-start | bytes 786440 | tf_op jit(solution)/shard_map/ppermute | solution.py:605
  162.7 48.0 %collective-permute-start.23 = (f32[2,512,384]{2,1,0:T(8,128)}, f32[2,512,384]{2,1,0:T(8,128)S(1)}, u32[]{:S(2)}, u32[]{:S(2)}) collective-permute-start(f32[2,512,384]{2,1,0:T(8,128)} %add.168), channel_id=1, source_target_pairs={{0,1},{1,2},{2,3},{4,5},{5,6},{6,7},{8,9},{9,10},{10,11},{12,13},{... | collective-permute-start | bytes 4718600 | tf_op jit(solution)/shard_map/ppermute | solution.py:583
  183.3 13.9 %collective-permute-start.19 = (f32[128,512]{1,0:T(8,128)S(1)}, f32[128,512]{1,0:T(8,128)S(1)}, u32[]{:S(2)}, u32[]{:S(2)}) collective-permute-start(f32[128,512]{1,0:T(8,128)S(1)} %add_multiply_fusion), channel_id=1, source_target_pairs={{0,8},{4,12},{8,16},{12,20},{16,24},{20,28},{24,0},{28,4},{1,9},{5... | collective-permute-start | bytes 786440 | tf_op jit(solution)/shard_map/ppermute | solution.py:605
  186.2 11.9 %collective-permute-start.20 = (f32[128,512]{1,0:T(8,128)S(1)}, f32[128,512]{1,0:T(8,128)S(1)}, u32[]{:S(2)}, u32[]{:S(2)}) collective-permute-start(f32[128,512]{1,0:T(8,128)S(1)} %add_multiply_fusion), channel_id=1, source_target_pairs={{0,16},{4,20},{8,24},{12,28},{16,0},{20,4},{24,8},{28,12},{1,17},{... | collective-permute-start | bytes 786440 | tf_op jit(solution)/shard_map/ppermute | solution.py:605
  186.2 11.9 %collective-permute-start.21 = (f32[128,512]{1,0:T(8,128)S(1)}, f32[128,512]{1,0:T(8,128)S(1)}, u32[]{:S(2)}, u32[]{:S(2)}) collective-permute-start(f32[128,512]{1,0:T(8,128)S(1)} %add_multiply_fusion), channel_id=1, source_target_pairs={{0,24},{4,28},{8,0},{12,4},{16,8},{20,12},{24,16},{28,20},{1,25},{... | collective-permute-start | bytes 786440 | tf_op jit(solution)/shard_map/ppermute | solution.py:605
  191.4 3.3 %copy-start.9 = (f32[2,512,128]{2,1,0:T(8,128)S(1)}, f32[2,512,128]{2,1,0:T(8,128)}, u32[]{:S(2)}) copy-start(f32[2,512,128]{2,1,0:T(8,128)} %get-tuple-element.96) | copy-start | bytes 1572868
  198.1 10.7 %collective-permute-start.22 = (f32[2,512,128]{2,1,0:T(8,128)}, f32[2,512,128]{2,1,0:T(8,128)S(1)}, u32[]{:S(2)}, u32[]{:S(2)}) collective-permute-start(f32[2,512,128]{2,1,0:T(8,128)} %get-tuple-element.97), channel_id=1, source_target_pairs={{0,4},{1,5},{2,6},{3,7},{4,8},{5,9},{6,10},{7,11},{8,12},{9,13},{1... | collective-permute-start | bytes 1572872 | tf_op jit(solution)/shard_map/ppermute | solution.py:583
  202.4 11.0 %collective-permute-start.24 = (f32[512,512]{1,0:T(8,128)S(1)}, f32[512,512]{1,0:T(8,128)}, u32[]{:S(2)}, u32[]{:S(2)}) collective-permute-start(f32[512,512]{1,0:T(8,128)S(1)} %constant_dynamic-update-slice_fusion), channel_id=1, source_target_pairs={{0,4},{4,0},{8,12},{12,8},{16,20},{20,16},{24,28},{28,24},{1,5},{5... | collective-permute-start | bytes 3145736 | tf_op jit(solution)/shard_map/ppermute | solution.py:597

commit v13 on v12

--- a/solution.py
+++ b/solution.py
@@ -138,7 +138,8 @@
     lower_ca_out,
     lower_b_out,
     corner_out,
-    dpup_out,
+    keep_out,
+    give_out,
     region,
     grads,
     win,
@@ -240,7 +241,19 @@
         )
         for n, (dst, rows, start) in enumerate(outs)
     ]
-    dpup_store = pltpu.make_async_copy(dpup, dpup_out, out_sems.at[7])
+    dpup_stores = [
+        [
+            pltpu.make_async_copy(dpup.at[plane], keep_out, out_sems.at[7]),
+            pltpu.make_async_copy(dpup.at[1 - plane], give_out, out_sems.at[8]),
+        ]
+        for plane in range(2)
+    ]
+
+    def store_dpup():
+        for plane, copies in enumerate(dpup_stores):
+            for copy in copies:
+                pl.when(odd == plane)(copy.start)
+
     lower_stores = stores[:4]
     upper_stores = stores[4:]
 
@@ -407,7 +420,7 @@
                     dpup[plane, pl.ds(base + 8 * i, 8), :] += tile
 
         last = slot == count - 1
-        pl.when(last)(dpup_store.start)
+        pl.when(last)(store_dpup)
 
         zero = jnp.zeros((8, side), jnp.float32)
         for plane in range(2):
@@ -438,14 +451,15 @@
 
     @pl.when(count == 0)
     def _():
-        for store in [dpup_store] + lower_stores:
+        store_dpup()
+        for store in lower_stores:
             store.start()
         for load in loads + late_loads:
             load.wait()
 
     for store in upper_stores:
         store.start()
-    for store in [dpup_store] + stores:
+    for store in dpup_stores[0] + stores:
         store.wait()
 
 
@@ -464,7 +478,7 @@
     f32, bf16 = jnp.float32, jnp.bfloat16
     region = (2, tile_rows + side, tile_cols + side)
     cut = back_cut(side)
-    dpup = jax.ShapeDtypeStruct(pupils.shape[1:], f32)
+    plane = jax.ShapeDtypeStruct((side, side), f32)
     shapes = (
         (tile_rows, cut),
         (tile_rows + side, side - cut),
@@ -472,7 +486,7 @@
         (side, side - cut),
         (side, cut),
     )
-    outs = (tile, *(jax.ShapeDtypeStruct((2, *shape), f32) for shape in shapes), dpup)
+    outs = (tile, *(jax.ShapeDtypeStruct((2, *shape), f32) for shape in shapes), plane, plane)
     table = pltpu.VMEM(high.shape, bf16)
     return pl.pallas_call(
         slots_kernel,
@@ -499,7 +513,7 @@
             table,
             pltpu.SemaphoreType.DMA((12,)),
             pltpu.SemaphoreType.DMA((2, slots)),
-            pltpu.SemaphoreType.DMA((8,)),
+            pltpu.SemaphoreType.DMA((9,)),
         ],
         compiler_params=pltpu.CompilerParams(vmem_limit_bytes=56 * 1024 * 1024),
         cost_estimate=pl.CostEstimate(
@@ -583,15 +597,6 @@
     return lax.ppermute(array, ("ty", "tx"), along(rule, sizes))
 
 
-def halve(value, bit):
-    rows = value.shape[0] // 2
-    mine = lax.axis_index("ty") // bit % 2
-    kept = lax.dynamic_slice_in_dim(value, mine * rows, rows, 0)
-    sent = lax.dynamic_slice_in_dim(value, (1 - mine) * rows, rows, 0)
-    received = lax.ppermute(sent, "ty", [(i, i ^ bit) for i in range(lax.axis_size("ty"))])
-    return kept + received
-
-
 def double(value, bit):
     mine = lax.axis_index("ty") // bit % 2
     other = lax.ppermute(value, "ty", [(i, i ^ bit) for i in range(lax.axis_size("ty"))])
@@ -680,7 +685,7 @@
         corner_up_b,
         corner_side,
     )
-    own_g, right_g, side_g, lower_ca_g, lower_b_g, corner_g, dpup = slots_call(
+    own_g, right_g, side_g, lower_ca_g, lower_b_g, corner_g, keep, give = slots_call(
         meta, spectrum, parts, amps, pupils
     )
 
@@ -692,23 +697,26 @@
 
     cut = back_cut(side)
     split_at = tile_cols - side
-    part = halve(dpup.reshape(-1, side), 1)
+    part = keep + lax.ppermute(give, "ty", [(i, i ^ 1) for i in range(n_ty)])
     corner = send(corner_g, down)
     beside = send(side_g, right)
     part = scatter(part, "ty", 2)
     part, lower_ca_g, corner, beside = lax.optimization_barrier((part, lower_ca_g, corner, beside))
     lower_ca = send(lower_ca_g, down)
     part = sum_all(part, "tx") * (1.0 / math.sqrt(n_ty * n_tx))
+    spec_grad = own_g.at[:, :, cut:side].add(beside[:, :tile_rows])
+    part, spec_grad = lax.optimization_barrier((part, spec_grad))
     right_back = send(after(right_g + corner, part), right)
     part = gather(after(part, lower_ca), "ty", 2)
+    spec_grad = spec_grad.at[:, :, side:].add(lower_ca[:, :, :split_at])
+    spec_grad = spec_grad.at[:, :, :cut].add(lower_ca[:, :, split_at:])
+    part, spec_grad = lax.optimization_barrier((part, spec_grad))
     lower_b = send(after(lower_b_g + beside[:, tile_rows:], part), down)
-    spec_grad = own_g.at[:, :, side:].add(lower_ca[:, :, :split_at])
-    spec_grad = spec_grad.at[:, :, :cut].add(lower_ca[:, :, split_at:])
-    spec_grad = spec_grad.at[:, :, cut:side].add(beside[:, :tile_rows])
-    part, spec_grad = lax.optimization_barrier((part, spec_grad))
+    pupil_grad = double(part, 1)
+    spec_grad = spec_grad.at[:, :, :cut].add(right_back)
+    spec_grad, pupil_grad = lax.optimization_barrier((spec_grad, pupil_grad))
     spec_grad = spec_grad.at[:, :, cut:side].add(lower_b)
-    spec_grad = spec_grad.at[:, :, :cut].add(right_back)
-    return spec_grad, double(part, 1).reshape(pupil.shape)
+    return spec_grad, pupil_grad.reshape(pupil.shape)
 
 
 def solution(mesh):

time: 219 us -> 212 us (0.968)
  starting transfers between devices: 68.1 us -> 63.5 us
    ppermute x14, starting transfers between devices: 55.2 us -> 48.5 us  [send(): return lax.ppermute(array, ('ty', 'tx'), along(rule, sizes))]
    ppermute x14, waiting for transfers between devices: 43.8 us -> 39.9 us  [send(): return lax.ppermute(array, ('ty', 'tx'), along(rule, sizes))]
    unnamed x30 -> x36, local copies, waits for them, and re-layouts: 9.67 us -> 9.71 us
  transfers between devices with their start and end apart: 25 -> 25, of which waited for: 11 -> 12; matrix products, arithmetic and copies ran while one was open for 11% -> 12% of each run, Pallas kernels for 5% -> 5%
where the time goes in v13:
time: 212 us; the launch traced here: 209 us
  waiting for transfers between devices  75.3 us (36%)
  starting transfers between devices  63.5 us (30%)
  Pallas kernels  29.5 us (14%)
  other arithmetic  23.1 us (11%)
  local copies, waits for them, and re-layouts  16.9 us (8%)
    ppermute x14, starting transfers between devices, send(): return lax.ppermute(array, ('ty', 'tx'), along(rule, sizes))  48.5 us
    ppermute x14, waiting for transfers between devices, send(): return lax.ppermute(array, ('ty', 'tx'), along(rule, sizes))  39.9 us
    ppermute x9, waiting for transfers between devices, stepped(): lax.ppermute(value, axis, [(i, (i + step * inner) % size) for i in range(...  35.3 us
    pallas_call x1, Pallas kernels, slots_call(): pl.pallas_call(slots_kernel, out_shape=[jax.ShapeDtypeStruct(x.shape, f32...  19.4 us
    ppermute x9, starting transfers between devices, stepped(): lax.ppermute(value, axis, [(i, (i + step * inner) % size) for i in range(...  13.7 us
    pallas_call x1, Pallas kernels, prepare(): pl.pallas_call(prepare_kernel, grid=(slots,), out_shape=[jax.ShapeDtypeSt...  10.1 us
    unnamed x36, local copies, waits for them, and re-layouts  9.71 us
  transfers between devices with their start and end apart: 25, of which 12 were waited for; matrix products, arithmetic and copies ran while one was open for 12% of the time, Pallas kernels for 5%

profile of v13, /device:TPU:1, one launch (start us, length us, event | category | flops | bytes accessed | tf_op | source)
XLA Modules:
  0.0 209.3 jit_solution(178182052344070147)
XLA Ops:
  0.7 3.2 %fusion.2 = (f32[2,512,256]{2,1,0:T(8,128)}, f32[2,512,256]{2,1,0:T(8,128)}) fusion(f32[2,512,1024]{2,1,0:T(8,128)} %tile_hbm.1), kind=kLoop, calls=%fused_computation.23 | loop fusion | bytes 4194304 | tf_op jit(solution)/shard_map/slice | solution.py:667
  3.8 2.1 collective-permute-start.3
  5.9 1.3 collective-permute-start
  7.2 1.5 slice.159
  8.8 1.9 collective-permute-start.4
  10.7 1.3 collective-permute-start.1
  12.0 1.9 collective-permute-start.2
  14.0 0.1 copy.16
  14.1 0.1 copy.17
  14.2 0.1 copy.15
  14.3 0.1 pad_add_fusion
  14.4 1.6 copy-done.2
  15.9 1.0 copy-done.3
  17.0 1.0 copy-done.4
  18.0 10.1 %prepare.1 = (f32[3,512,512]{2,1,0:T(8,128)S(1)}, f32[3,2,512,512]{3,2,1,0:T(8,128)S(1)}) custom-call(s32[4,3]{1,0:T(4,128)S(1)} %concatenate.16.meta, f32[3,512,512]{2,1,0:T(8,128)S(1)} %copy-done.1, f32[2,512,512]{2,1,0:T(8,128)S(1)} %copy-done.2, bf16[512,512]{1,0:T(8,128)(2,1)S(1)} %copy-done.3, bf16[512,512]{1,0:T(8,128)(2,1)S(1)} %copy-done.4), custom_call_target="tpu_custom_call" | custom-call | flops 4831838208 | bytes 18874368 | tf_op jit(solution)/shard_map/prepare/pallas_call | solution.py:561
  28.1 2.7 %copy-done.5 = f32[3,2,512,512]{3,2,1,0:T(8,128)} copy-done((f32[3,2,512,512]{3,2,1,0:T(8,128)}, f32[3,2,512,512]{3,2,1,0:T(8,128)S(1)}, u32[]{:S(2)}) %copy-start.5) | copy-done | bytes 6291480
  30.8 1.8 copy-done.6
  32.6 1.3 collective-permute-start.8
  33.9 0.6 collective-permute-done.right_a_hbm
  34.5 1.9 collective-permute-start.5
  36.4 19.9 %collective-permute-done.1.right_b_hbm = f32[2,512,256]{2,1,0:T(8,128)} collective-permute-done((f32[2,512,256]{2,1,0:T(8,128)}, f32[2,512,256]{2,1,0:T(8,128)}, u32[]{:S(2)}, u32[]{:S(2)}) %collective-permute-start.1) | collective-permute-done | bytes 1048608 | tf_op jit(solution)/shard_map/ppermute | solution.py:597
  56.4 1.3 fusion.3
  57.6 2.3 %collective-permute-start.6 = (f32[2,512,128]{2,1,0:T(8,128)S(1)}, f32[2,512,128]{2,1,0:T(8,128)S(1)}, u32[]{:S(2)}, u32[]{:S(2)}) collective-permute-start(f32[2,512,128]{2,1,0:T(8,128)S(1)} %get-tuple-element.122), channel_id=1, source_target_pairs={{4,0},{5,1},{6,2},{7,3},{12,8},{13,9},{14,10},{15,11},{20,16},{21,... | collective-permute-start | bytes 1572872 | tf_op jit(solution)/shard_map/ppermute | solution.py:597
  59.9 1.3 collective-permute-start.7
  61.2 0.1 collective-permute-done.6.corner_up_a_hbm
  61.4 1.3 collective-permute-done.7.corner_up_b_hbm
  62.7 4.8 %collective-permute-done.8.corner_side_hbm = f32[2,512,256]{2,1,0:T(8,128)S(1)} collective-permute-done((f32[2,512,256]{2,1,0:T(8,128)}, f32[2,512,256]{2,1,0:T(8,128)S(1)}, u32[]{:S(2)}, u32[]{:S(2)}) %collective-permute-start.8) | collective-permute-done | bytes 1048608 | tf_op jit(solution)/shard_map/ppermute | solution.py:597
  67.5 0.9 copy-done.13
  68.5 0.4 copy-done.14
  68.9 19.4 %slots.1 = (f32[2,512,1024]{2,1,0:T(8,128)}, f32[2,512,384]{2,1,0:T(8,128)}, f32[2,1024,128]{2,1,0:T(8,128)}, f32[2,512,896]{2,1,0:T(8,128)}, f32[2,512,128]{2,1...) custom-call(s32[4,3]{1,0:T(4,128)} %copy-done, f32[2,512,1024]{2,1,0:T(8,128)} %tile_hbm.1, ...), custom_call_target="tpu_custom_call" | custom-call | flops 9663676416 | bytes 41943040 | tf_op jit(solution)/shard_map/slots/pallas_call | solution.py:491
  88.3 0.1 collective-permute-start.9
  88.4 12.0 %collective-permute-start.13 = (f32[2,512,384]{2,1,0:T(8,128)}, f32[2,512,384]{2,1,0:T(8,128)}, u32[]{:S(2)}, u32[]{:S(2)}) collective-permute-start(f32[2,512,384]{2,1,0:T(8,128)} %get-tuple-element.94), channel_id=1, source_target_pairs={{0,4},{1,5},{2,6},{3,7},{4,8},{5,9},{6,10},{7,11},{8,12},{9,13},{1... | collective-permute-start | bytes 4718600 | tf_op jit(solution)/shard_map/ppermute | solution.py:597
  100.4 8.3 %collective-permute-start.14 = (f32[2,1024,128]{2,1,0:T(8,128)}, f32[2,1024,128]{2,1,0:T(8,128)}, u32[]{:S(2)}, u32[]{:S(2)}) collective-permute-start(f32[2,1024,128]{2,1,0:T(8,128)} %get-tuple-element.95), channel_id=1, source_target_pairs={{0,1},{1,2},{2,3},{4,5},{5,6},{6,7},{8,9},{9,10},{10,11},{12,13},{... | collective-permute-start | bytes 3145736 | tf_op jit(solution)/shard_map/ppermute | solution.py:597
  108.6 1.7 add.129
  110.4 0.9 constant_dynamic-slice_fusion.2
  111.3 5.0 %collective-permute-start.10 = (f32[128,512]{1,0:T(8,128)}, f32[128,512]{1,0:T(8,128)}, u32[]{:S(2)}, u32[]{:S(2)}) collective-permute-start(f32[128,512]{1,0:T(8,128)} %get-tuple-element.118), channel_id=1, source_target_pairs={{0,8},{4,12},{8,16},{12,20},{16,24},{20,28},{24,0},{28,4},{1,9},{5... | collective-permute-start | bytes 786440 | tf_op jit(solution)/shard_map/ppermute | solution.py:610
  116.3 1.2 collective-permute-start.12
  117.5 9.0 %collective-permute-done.10 = f32[128,512]{1,0:T(8,128)} collective-permute-done((f32[128,512]{1,0:T(8,128)}, f32[128,512]{1,0:T(8,128)}, u32[]{:S(2)}, u32[]{:S(2)}) %collective-permute-start.10) | collective-permute-done | bytes 262176 | tf_op jit(solution)/shard_map/ppermute | solution.py:610
  126.4 11.6 %collective-permute-done.11 = f32[128,512]{1,0:T(8,128)} collective-permute-done((f32[128,512]{1,0:T(8,128)}, f32[128,512]{1,0:T(8,128)}, u32[]{:S(2)}, u32[]{:S(2)}) %collective-permute-start.11) | collective-permute-done | bytes 262176 | tf_op jit(solution)/shard_map/ppermute | solution.py:610
  138.0 0.8 collective-permute-done.12
  138.8 1.2 add_add_fusion
  140.0 1.9 collective-permute-start.18
  142.0 0.1 collective-permute-start.15
  142.1 2.0 collective-permute-start.16
  144.1 1.4 collective-permute-start.17
  145.5 2.7 %add.157 = f32[2,512,384]{2,1,0:T(8,128)} add(f32[2,512,384]{2,1,0:T(8,128)S(1)} %copy-done.8, f32[2,512,384]{2,1,0:T(8,128)} %collective-permute-done.13) | non-fusion elementwise | flops 393216 | bytes 4718592 | tf_op jit(solution)/shard_map/add | solution.py:709
  148.2 2.4 %slice_add_fusion.2 = (f32[2,512,128]{2,1,0:T(8,128)}, f32[2,512,1024]{2,1,0:T(8,128)}) fusion(f32[2,512,128]{2,1,0:T(8,128)S(1)} %copy-done.9, f32[2,1024,128]{2,1,0:T(8,128)} %collective-permute-done.14, f32[2,512,1024]{2,1,0:T(8,128)} %get-tuple-element.97), kind=kLoop, calls=%fused_computation.7 | loop fusion | flops 262144 | bytes 3145728 | tf_op jit(solution)/shard_map/add | solution.py:714
  150.6 10.8 %collective-permute-done.15 = f32[128,512]{1,0:T(8,128)S(1)} collective-permute-done((f32[128,512]{1,0:T(8,128)S(1)}, f32[128,512]{1,0:T(8,128)S(1)}, u32[]{:S(2)}, u32[]{:S(2)}) %collective-permute-start.15) | collective-permute-done | bytes 262176 | tf_op jit(solution)/shard_map/ppermute | solution.py:610
  161.4 0.1 add_multiply_fusion
  161.5 7.9 %collective-permute-start.22 = (f32[2,512,384]{2,1,0:T(8,128)}, f32[2,512,384]{2,1,0:T(8,128)S(1)}, u32[]{:S(2)}, u32[]{:S(2)}) collective-permute-start(f32[2,512,384]{2,1,0:T(8,128)} %add.157), channel_id=1, source_target_pairs={{0,1},{1,2},{2,3},{4,5},{5,6},{6,7},{8,9},{9,10},{10,11},{12,13},{... | collective-permute-start | bytes 4718600 | tf_op jit(solution)/shard_map/ppermute | solution.py:597
  169.4 12.6 %collective-permute-done.18 = f32[2,512,896]{2,1,0:T(8,128)} collective-permute-done((f32[2,512,896]{2,1,0:T(8,128)}, f32[2,512,896]{2,1,0:T(8,128)}, u32[]{:S(2)}, u32[]{:S(2)}) %collective-permute-start.18) | collective-permute-done | bytes 3670048 | tf_op jit(solution)/shard_map/ppermute | solution.py:597
  182.1 2.9 %collective-permute-start.19 = (f32[128,512]{1,0:T(8,128)S(1)}, f32[128,512]{1,0:T(8,128)S(1)}, u32[]{:S(2)}, u32[]{:S(2)}) collective-permute-start(f32[128,512]{1,0:T(8,128)S(1)} %add_multiply_fusion), channel_id=1, source_target_pairs={{0,8},{4,12},{8,16},{12,20},{16,24},{20,28},{24,0},{28,4},{1,9},{5... | collective-permute-start | bytes 786440 | tf_op jit(solution)/shard_map/ppermute | solution.py:610
  184.9 1.2 collective-permute-start.21
  186.1 4.0 %fusion = f32[2,512,1024]{2,1,0:T(8,128)} fusion(f32[2,512,1024]{2,1,0:T(8,128)} %get-tuple-element.102, f32[2,512,896]{2,1,0:T(8,128)} %collective-permute-done.18), kind=kLoop, calls=%fused_computation.1 | loop fusion | flops 524288 | bytes 6291456 | tf_op jit(solution)/shard_map/scatter-add | solution.py:711
  190.1 3.2 %fusion.1 = f32[2,512,1024]{2,1,0:T(8,128)} fusion(f32[2,512,1024]{2,1,0:T(8,128)} %fusion, f32[2,512,896]{2,1,0:T(8,128)} %collective-permute-done.18), kind=kLoop, calls=%fused_computation.4 | loop fusion | flops 393216 | bytes 4718592 | tf_op jit(solution)/shard_map/scatter-add | solution.py:712
  193.4 0.1 broadcast_in_dim.4
  193.6 3.2 %collective-permute-done.20 = f32[128,512]{1,0:T(8,128)S(1)} collective-permute-done((f32[128,512]{1,0:T(8,128)S(1)}, f32[128,512]{1,0:T(8,128)S(1)}, u32[]{:S(2)}, u32[]{:S(2)}) %collective-permute-start.20) | collective-permute-done | bytes 262176 | tf_op jit(solution)/shard_map/ppermute | solution.py:610
  196.9 1.2 collective-permute-start.23
  198.1 3.2 %collective-permute-start.24 = (f32[2,512,128]{2,1,0:T(8,128)S(1)}, f32[2,512,128]{2,1,0:T(8,128)S(1)}, u32[]{:S(2)}, u32[]{:S(2)}) collective-permute-start(f32[2,512,128]{2,1,0:T(8,128)S(1)} %copy-done.10), channel_id=1, source_target_pairs={{0,4},{1,5},{2,6},{3,7},{4,8},{5,9},{6,10},{7,11},{8,12},{9,13},{1... | collective-permute-start | bytes 1572872 | tf_op jit(solution)/shard_map/ppermute | solution.py:597
  201.2 0.5 collective-permute-done.22
  201.7 2.7 %add_dynamic-update-slice_fusion = f32[2,512,1024]{2,1,0:T(8,128)} fusion(f32[2,512,1024]{2,1,0:T(8,128)} %fusion.1, f32[2,512,384]{2,1,0:T(8,128)S(1)} %collective-permute-done.22), kind=kLoop, calls=%fused_computation.5 | loop fusion | flops 393216 | bytes 4718592 | tf_op jit(solution)/shard_map/scatter-add | solution.py:716
  204.4 1.4 broadcast_select_fusion.1
  205.9 1.5 pad_maximum_fusion
  207.4 1.9 add_dynamic-update-slice_fusion.1
  (49 shorter events, 0.2 us)
Async XLA Ops:
  0.6 6.6 %copy-start.7 = (f32[2,512,1024]{2,1,0:T(8,128)S(1)}, f32[2,512,1024]{2,1,0:T(8,128)}, u32[]{:S(2)}) copy-start(f32[2,512,1024]{2,1,0:T(8,128)} %tile_hbm.1) | copy-start | bytes 12582916
  0.6 13.3 %copy-start.11 = (s32[3,2]{0,1:T(2,128)S(1)}, s32[3,2]{0,1:T(2,128)}, u32[]{:S(2)}) copy-start(s32[3,2]{0,1:T(2,128)} %param.24) | copy-start | bytes 76
  0.7 13.5 %copy-start.12 = (s32[3]{0:T(128)S(1)}, s32[3]{0:T(128)}, u32[]{:S(2)}) copy-start(s32[3]{0:T(128)} %param.25) | copy-start | bytes 40
  0.7 13.7 %copy-start.1 = (f32[3,512,512]{2,1,0:T(8,128)S(1)}, f32[3,512,512]{2,1,0:T(8,128)}, u32[]{:S(2)}) copy-start(f32[3,512,512]{2,1,0:T(8,128)} %amps.1) | copy-start | bytes 9437188
  3.8 28.8 %collective-permute-start.3 = (f32[2,512,256]{2,1,0:T(8,128)}, f32[2,512,256]{2,1,0:T(8,128)}, u32[]{:S(2)}, u32[]{:S(2)}) collective-permute-start(f32[2,512,256]{2,1,0:T(8,128)} %get-tuple-element.112), channel_id=1, source_target_pairs={{4,0},{5,1},{6,2},{7,3},{8,4},{9,5},{10,6},{11,7},{12,8},{13,9},{1... | collective-permute-start | bytes 3145736 | tf_op jit(solution)/shard_map/ppermute | solution.py:597
  5.9 28.6 %collective-permute-start = (f32[2,512,256]{2,1,0:T(8,128)}, f32[2,512,256]{2,1,0:T(8,128)}, u32[]{:S(2)}, u32[]{:S(2)}) collective-permute-start(f32[2,512,256]{2,1,0:T(8,128)} %get-tuple-element.113), channel_id=1, source_target_pairs={{1,0},{2,1},{3,2},{5,4},{6,5},{7,6},{9,8},{10,9},{11,10},{13,12},{... | collective-permute-start | bytes 3145736 | tf_op jit(solution)/shard_map/ppermute | solution.py:597
  8.8 58.7 %collective-permute-start.4 = (f32[2,512,512]{2,1,0:T(8,128)}, f32[2,512,512]{2,1,0:T(8,128)}, u32[]{:S(2)}, u32[]{:S(2)}) collective-permute-start(f32[2,512,512]{2,1,0:T(8,128)} %slice.159), channel_id=1, source_target_pairs={{4,0},{5,1},{6,2},{7,3},{8,4},{9,5},{10,6},{11,7},{12,8},{13,9},{1... | collective-permute-start | bytes 6291464 | tf_op jit(solution)/shard_map/ppermute | solution.py:597
  10.7 45.6 %collective-permute-start.1 = (f32[2,512,256]{2,1,0:T(8,128)}, f32[2,512,256]{2,1,0:T(8,128)}, u32[]{:S(2)}, u32[]{:S(2)}) collective-permute-start(f32[2,512,256]{2,1,0:T(8,128)} %get-tuple-element.112), channel_id=1, source_target_pairs={{1,0},{2,1},{3,2},{5,4},{6,5},{7,6},{9,8},{10,9},{11,10},{13,12},{... | collective-permute-start | bytes 3145736 | tf_op jit(solution)/shard_map/ppermute | solution.py:597
  12.0 47.9 %collective-permute-start.2 = (f32[2,512,256]{2,1,0:T(8,128)}, f32[2,512,256]{2,1,0:T(8,128)}, u32[]{:S(2)}, u32[]{:S(2)}) collective-permute-start(f32[2,512,256]{2,1,0:T(8,128)} %get-tuple-element.113), channel_id=1, source_target_pairs={{4,0},{5,1},{6,2},{7,3},{8,4},{9,5},{10,6},{11,7},{12,8},{13,9},{1... | collective-permute-start | bytes 3145736 | tf_op jit(solution)/shard_map/ppermute | solution.py:597
  14.3 1.6 copy-start.2
  15.9 1.0 copy-start.3
  17.0 1.0 copy-start.4
  18.0 10.1 %copy-start = (s32[4,3]{1,0:T(4,128)}, s32[4,3]{1,0:T(4,128)S(1)}, u32[]{:S(2)}) copy-start(s32[4,3]{1,0:T(4,128)S(1)} %concatenate.16.meta) | copy-start | bytes 148
  28.1 2.7 %copy-start.5 = (f32[3,2,512,512]{3,2,1,0:T(8,128)}, f32[3,2,512,512]{3,2,1,0:T(8,128)S(1)}, u32[]{:S(2)}) copy-start(f32[3,2,512,512]{3,2,1,0:T(8,128)S(1)} %get-tuple-element.90.pupil_hbm) | copy-start | bytes 18874372
  30.8 1.8 copy-start.6
  32.6 34.9 %collective-permute-start.8 = (f32[2,512,256]{2,1,0:T(8,128)}, f32[2,512,256]{2,1,0:T(8,128)S(1)}, u32[]{:S(2)}, u32[]{:S(2)}) collective-permute-start(f32[2,512,256]{2,1,0:T(8,128)} %collective-permute-done.3.lower_b_hbm), channel_id=1, source_target_pairs={{5,4},{6,5},{7,6},{13,12},{14,13},{15,14},{21,20},{22,21},{23,22},... | collective-permute-start | bytes 3145736 | tf_op jit(solution)/shard_map/ppermute | solution.py:597
  34.5 33.0 %collective-permute-start.5 = (f32[2,512,256]{2,1,0:T(8,128)}, f32[2,512,256]{2,1,0:T(8,128)S(1)}, u32[]{:S(2)}, u32[]{:S(2)}) collective-permute-start(f32[2,512,256]{2,1,0:T(8,128)} %collective-permute-done.right_a_hbm), channel_id=1, source_target_pairs={{4,0},{5,1},{6,2},{7,3},{8,4},{9,5},{10,6},{11,7},{12,8},{13,9},{1... | collective-permute-start | bytes 3145736 | tf_op jit(solution)/shard_map/ppermute | solution.py:597
  57.6 3.8 %collective-permute-start.6 = (f32[2,512,128]{2,1,0:T(8,128)S(1)}, f32[2,512,128]{2,1,0:T(8,128)S(1)}, u32[]{:S(2)}, u32[]{:S(2)}) collective-permute-start(f32[2,512,128]{2,1,0:T(8,128)S(1)} %get-tuple-element.122), channel_id=1, source_target_pairs={{4,0},{5,1},{6,2},{7,3},{12,8},{13,9},{14,10},{15,11},{20,16},{21,... | collective-permute-start | bytes 1572872 | tf_op jit(solution)/shard_map/ppermute | solution.py:597
  59.9 2.8 %collective-permute-start.7 = (f32[2,512,128]{2,1,0:T(8,128)S(1)}, f32[2,512,128]{2,1,0:T(8,128)S(1)}, u32[]{:S(2)}, u32[]{:S(2)}) collective-permute-start(f32[2,512,128]{2,1,0:T(8,128)S(1)} %get-tuple-element.121), channel_id=1, source_target_pairs={{4,0},{5,1},{6,2},{7,3},{12,8},{13,9},{14,10},{15,11},{20,16},{21,... | collective-permute-start | bytes 1572872 | tf_op jit(solution)/shard_map/ppermute | solution.py:597
  61.4 6.1 %copy-start.15 = (f32[2,512,128]{2,1,0:T(8,128)}, f32[2,512,128]{2,1,0:T(8,128)S(1)}, u32[]{:S(2)}) copy-start(f32[2,512,128]{2,1,0:T(8,128)S(1)} %collective-permute-done.6.corner_up_a_hbm) | copy-start | bytes 1572868
  62.7 4.8 %copy-start.16 = (f32[2,512,128]{2,1,0:T(8,128)}, f32[2,512,128]{2,1,0:T(8,128)S(1)}, u32[]{:S(2)}) copy-start(f32[2,512,128]{2,1,0:T(8,128)S(1)} %collective-permute-done.7.corner_up_b_hbm) | copy-start | bytes 1572868
  67.5 1.0 copy-start.13
  67.5 1.4 copy-start.14
  88.3 57.2 %copy-start.8 = (f32[2,512,384]{2,1,0:T(8,128)S(1)}, f32[2,512,384]{2,1,0:T(8,128)}, u32[]{:S(2)}) copy-start(f32[2,512,384]{2,1,0:T(8,128)} %get-tuple-element.104) | copy-start | bytes 4718596
  88.3 20.3 %collective-permute-start.9 = (f32[512,512]{1,0:T(8,128)}, f32[512,512]{1,0:T(8,128)}, u32[]{:S(2)}, u32[]{:S(2)}) collective-permute-start(f32[512,512]{1,0:T(8,128)} %get-tuple-element.92), channel_id=1, source_target_pairs={{0,4},{4,0},{8,12},{12,8},{16,20},{20,16},{24,28},{28,24},{1,5},{5... | collective-permute-start | bytes 3145736 | tf_op jit(solution)/shard_map/ppermute | solution.py:700
  88.4 51.6 %collective-permute-start.13 = (f32[2,512,384]{2,1,0:T(8,128)}, f32[2,512,384]{2,1,0:T(8,128)}, u32[]{:S(2)}, u32[]{:S(2)}) collective-permute-start(f32[2,512,384]{2,1,0:T(8,128)} %get-tuple-element.94), channel_id=1, source_target_pairs={{0,4},{1,5},{2,6},{3,7},{4,8},{5,9},{6,10},{7,11},{8,12},{9,13},{1... | collective-permute-start | bytes 4718600 | tf_op jit(solution)/shard_map/ppermute | solution.py:597
  100.4 39.6 %collective-permute-start.14 = (f32[2,1024,128]{2,1,0:T(8,128)}, f32[2,1024,128]{2,1,0:T(8,128)}, u32[]{:S(2)}, u32[]{:S(2)}) collective-permute-start(f32[2,1024,128]{2,1,0:T(8,128)} %get-tuple-element.95), channel_id=1, source_target_pairs={{0,1},{1,2},{2,3},{4,5},{5,6},{6,7},{8,9},{9,10},{10,11},{12,13},{... | collective-permute-start | bytes 3145736 | tf_op jit(solution)/shard_map/ppermute | solution.py:597
  110.4 37.8 %copy-start.9 = (f32[2,512,128]{2,1,0:T(8,128)S(1)}, f32[2,512,128]{2,1,0:T(8,128)}, u32[]{:S(2)}) copy-start(f32[2,512,128]{2,1,0:T(8,128)} %get-tuple-element.109) | copy-start | bytes 1572868
  111.3 15.2 %collective-permute-start.10 = (f32[128,512]{1,0:T(8,128)}, f32[128,512]{1,0:T(8,128)}, u32[]{:S(2)}, u32[]{:S(2)}) collective-permute-start(f32[128,512]{1,0:T(8,128)} %get-tuple-element.118), channel_id=1, source_target_pairs={{0,8},{4,12},{8,16},{12,20},{16,24},{20,28},{24,0},{28,4},{1,9},{5... | collective-permute-start | bytes 786440 | tf_op jit(solution)/shard_map/ppermute | solution.py:610
  116.3 21.8 %collective-permute-start.11 = (f32[128,512]{1,0:T(8,128)}, f32[128,512]{1,0:T(8,128)}, u32[]{:S(2)}, u32[]{:S(2)}) collective-permute-start(f32[128,512]{1,0:T(8,128)} %get-tuple-element.120), channel_id=1, source_target_pairs={{0,16},{4,20},{8,24},{12,28},{16,0},{20,4},{24,8},{28,12},{1,17},{... | collective-permute-start | bytes 786440 | tf_op jit(solution)/shard_map/ppermute | solution.py:610
  116.3 22.5 %collective-permute-start.12 = (f32[128,512]{1,0:T(8,128)S(1)}, f32[128,512]{1,0:T(8,128)}, u32[]{:S(2)}, u32[]{:S(2)}) collective-permute-start(f32[128,512]{1,0:T(8,128)S(1)} %get-tuple-element.119), channel_id=1, source_target_pairs={{0,24},{4,28},{8,0},{12,4},{16,8},{20,12},{24,16},{28,20},{1,25},{... | collective-permute-start | bytes 786440 | tf_op jit(solution)/shard_map/ppermute | solution.py:610
  140.0 42.1 %collective-permute-start.18 = (f32[2,512,896]{2,1,0:T(8,128)}, f32[2,512,896]{2,1,0:T(8,128)}, u32[]{:S(2)}, u32[]{:S(2)}) collective-permute-start(f32[2,512,896]{2,1,0:T(8,128)} %get-tuple-element.100), channel_id=1, source_target_pairs={{0,4},{1,5},{2,6},{3,7},{4,8},{5,9},{6,10},{7,11},{8,12},{9,13},{1... | collective-permute-start | bytes 11010056 | tf_op jit(solution)/shard_map/ppermute | solution.py:597
  142.0 19.4 %collective-permute-start.15 = (f32[128,512]{1,0:T(8,128)S(1)}, f32[128,512]{1,0:T(8,128)S(1)}, u32[]{:S(2)}, u32[]{:S(2)}) collective-permute-start(f32[128,512]{1,0:T(8,128)S(1)} %add_add_fusion), channel_id=1, source_target_pairs={{0,2},{1,3},{2,0},{3,1},{4,6},{5,7},{6,4},{7,5},{8,10},{9,11},{10,... | collective-permute-start | bytes 786440 | tf_op jit(solution)/shard_map/ppermute | solution.py:610
  142.1 19.3 %collective-permute-start.16 = (f32[128,512]{1,0:T(8,128)S(1)}, f32[128,512]{1,0:T(8,128)S(1)}, u32[]{:S(2)}, u32[]{:S(2)}) collective-permute-start(f32[128,512]{1,0:T(8,128)S(1)} %add_add_fusion), channel_id=1, source_target_pairs={{0,1},{1,2},{2,3},{3,0},{4,5},{5,6},{6,7},{7,4},{8,9},{9,10},{10,1... | collective-permute-start | bytes 786440 | tf_op jit(solution)/shard_map/ppermute | solution.py:610
  144.1 17.3 %collective-permute-start.17 = (f32[128,512]{1,0:T(8,128)S(1)}, f32[128,512]{1,0:T(8,128)S(1)}, u32[]{:S(2)}, u32[]{:S(2)}) collective-permute-start(f32[128,512]{1,0:T(8,128)S(1)} %add_add_fusion), channel_id=1, source_target_pairs={{0,3},{1,0},{2,1},{3,2},{4,7},{5,4},{6,5},{7,6},{8,11},{9,8},{10,9... | collective-permute-start | bytes 786440 | tf_op jit(solution)/shard_map/ppermute | solution.py:610
  161.5 40.2 %collective-permute-start.22 = (f32[2,512,384]{2,1,0:T(8,128)}, f32[2,512,384]{2,1,0:T(8,128)S(1)}, u32[]{:S(2)}, u32[]{:S(2)}) collective-permute-start(f32[2,512,384]{2,1,0:T(8,128)} %add.157), channel_id=1, source_target_pairs={{0,1},{1,2},{2,3},{4,5},{5,6},{6,7},{8,9},{9,10},{10,11},{12,13},{... | collective-permute-start | bytes 4718600 | tf_op jit(solution)/shard_map/ppermute | solution.py:597
  182.1 11.5 %collective-permute-start.19 = (f32[128,512]{1,0:T(8,128)S(1)}, f32[128,512]{1,0:T(8,128)S(1)}, u32[]{:S(2)}, u32[]{:S(2)}) collective-permute-start(f32[128,512]{1,0:T(8,128)S(1)} %add_multiply_fusion), channel_id=1, source_target_pairs={{0,8},{4,12},{8,16},{12,20},{16,24},{20,28},{24,0},{28,4},{1,9},{5... | collective-permute-start | bytes 786440 | tf_op jit(solution)/shard_map/ppermute | solution.py:610
  184.9 11.9 %collective-permute-start.20 = (f32[128,512]{1,0:T(8,128)S(1)}, f32[128,512]{1,0:T(8,128)S(1)}, u32[]{:S(2)}, u32[]{:S(2)}) collective-permute-start(f32[128,512]{1,0:T(8,128)S(1)} %add_multiply_fusion), channel_id=1, source_target_pairs={{0,16},{4,20},{8,24},{12,28},{16,0},{20,4},{24,8},{28,12},{1,17},{... | collective-permute-start | bytes 786440 | tf_op jit(solution)/shard_map/ppermute | solution.py:610
  184.9 11.9 %collective-permute-start.21 = (f32[128,512]{1,0:T(8,128)S(1)}, f32[128,512]{1,0:T(8,128)S(1)}, u32[]{:S(2)}, u32[]{:S(2)}) collective-permute-start(f32[128,512]{1,0:T(8,128)S(1)} %add_multiply_fusion), channel_id=1, source_target_pairs={{0,24},{4,28},{8,0},{12,4},{16,8},{20,12},{24,16},{28,20},{1,25},{... | collective-permute-start | bytes 786440 | tf_op jit(solution)/shard_map/ppermute | solution.py:610
  190.1 7.9 %copy-start.10 = (f32[2,512,128]{2,1,0:T(8,128)S(1)}, f32[2,512,128]{2,1,0:T(8,128)}, u32[]{:S(2)}) copy-start(f32[2,512,128]{2,1,0:T(8,128)} %get-tuple-element.110) | copy-start | bytes 1572868
  196.9 7.6 %collective-permute-start.23 = (f32[512,512]{1,0:T(8,128)S(1)}, f32[512,512]{1,0:T(8,128)}, u32[]{:S(2)}, u32[]{:S(2)}) collective-permute-start(f32[512,512]{1,0:T(8,128)S(1)} %constant_dynamic-update-slice_fusion), channel_id=1, source_target_pairs={{0,4},{4,0},{8,12},{12,8},{16,20},{20,16},{24,28},{28,24},{1,5},{5... | collective-permute-start | bytes 3145736 | tf_op jit(solution)/shard_map/ppermute | solution.py:602
  198.1 9.3 %collective-permute-start.24 = (f32[2,512,128]{2,1,0:T(8,128)S(1)}, f32[2,512,128]{2,1,0:T(8,128)S(1)}, u32[]{:S(2)}, u32[]{:S(2)}) collective-permute-start(f32[2,512,128]{2,1,0:T(8,128)S(1)} %copy-done.10), channel_id=1, source_target_pairs={{0,4},{1,5},{2,6},{3,7},{4,8},{5,9},{6,10},{7,11},{8,12},{9,13},{1... | collective-permute-start | bytes 1572872 | tf_op jit(solution)/shard_map/ppermute | solution.py:597

commit v14 on v13

--- a/solution.py
+++ b/solution.py
@@ -225,12 +225,12 @@
 
     cut = corner_out.shape[-1]
     lower_c_out = lower_ca_out.at[:, :, pl.ds(0, tile_cols - side)]
-    lower_a_out = lower_ca_out.at[:, :, pl.ds(tile_cols - side, cut)]
+    lower_a_out = lower_ca_out.at[:, :, pl.ds(tile_cols - side, half)]
     outs = (
         (corner_out, bottom, tile_cols),
         (lower_c_out, bottom, side),
         (lower_a_out, bottom, 0),
-        (lower_b_out, bottom, cut),
+        (lower_b_out, bottom, half),
         (side_out, pl.ds(0, tile_rows + side), tile_cols + cut),
         (right_out, top, tile_cols),
         (own_out, top, 0),
@@ -482,8 +482,8 @@
     shapes = (
         (tile_rows, cut),
         (tile_rows + side, side - cut),
-        (side, tile_cols - side + cut),
-        (side, side - cut),
+        (side, tile_cols - side // 2),
+        (side, side // 2),
         (side, cut),
     )
     outs = (tile, *(jax.ShapeDtypeStruct((2, *shape), f32) for shape in shapes), plane, plane)
@@ -709,13 +709,14 @@
     right_back = send(after(right_g + corner, part), right)
     part = gather(after(part, lower_ca), "ty", 2)
     spec_grad = spec_grad.at[:, :, side:].add(lower_ca[:, :, :split_at])
-    spec_grad = spec_grad.at[:, :, :cut].add(lower_ca[:, :, split_at:])
+    spec_grad = spec_grad.at[:, :, :half].add(lower_ca[:, :, split_at:])
     part, spec_grad = lax.optimization_barrier((part, spec_grad))
-    lower_b = send(after(lower_b_g + beside[:, tile_rows:], part), down)
+    lower_b_g = lower_b_g.at[:, :, cut - half :].add(beside[:, tile_rows:])
+    lower_b = send(after(lower_b_g, part), down)
     pupil_grad = double(part, 1)
+    spec_grad, pupil_grad = lax.optimization_barrier((spec_grad, pupil_grad))
     spec_grad = spec_grad.at[:, :, :cut].add(right_back)
-    spec_grad, pupil_grad = lax.optimization_barrier((spec_grad, pupil_grad))
-    spec_grad = spec_grad.at[:, :, cut:side].add(lower_b)
+    spec_grad = spec_grad.at[:, :, half:side].add(lower_b)
     return spec_grad, pupil_grad.reshape(pupil.shape)
 
 

time: 212 us -> 212 us (level)
  starting transfers between devices: 63.5 us -> 66.8 us
    ppermute x9, starting transfers between devices: 13.7 us -> 17.9 us  [stepped(): lax.ppermute(value, axis, [(i, (i + step * inner) % size) for i in range(...]
    add x1 -> x0, other arithmetic: 2.43 us -> none  [body(): lower_b = send(after(lower_b_g + beside[:, tile_rows:], part), down)]
    scatter-add x2 -> x3, other arithmetic: 5.15 us -> 7.24 us  [the longest x1 2.59 us: body(): lower_b_g = lower_b_g.at[:, :, cut - half:].add(beside[:, tile_rows:])]
    unnamed x36 -> x34, local copies, waits for them, and re-layouts: 9.71 us -> 11.8 us
  transfers between devices with their start and end apart: 25 -> 25, of which waited for: 12 -> 13; matrix products, arithmetic and copies ran while one was open for 12% -> 11% of each run, Pallas kernels for 5% -> 5%
where the time goes in v14:
time: 212 us; the launch traced here: 211 us
  waiting for transfers between devices  73.3 us (35%)
  starting transfers between devices  66.8 us (32%)
  Pallas kernels  29.5 us (14%)
  other arithmetic  21.7 us (10%)
  local copies, waits for them, and re-layouts  18.8 us (9%)
    ppermute x14, starting transfers between devices, send(): return lax.ppermute(array, ('ty', 'tx'), along(rule, sizes))  47.7 us
    ppermute x14, waiting for transfers between devices, send(): return lax.ppermute(array, ('ty', 'tx'), along(rule, sizes))  39.8 us
    ppermute x9, waiting for transfers between devices, stepped(): lax.ppermute(value, axis, [(i, (i + step * inner) % size) for i in range(...  33.4 us
    pallas_call x1, Pallas kernels, slots_call(): pl.pallas_call(slots_kernel, out_shape=[jax.ShapeDtypeStruct(x.shape, f32...  19.4 us
    ppermute x9, starting transfers between devices, stepped(): lax.ppermute(value, axis, [(i, (i + step * inner) % size) for i in range(...  17.9 us
    unnamed x34, local copies, waits for them, and re-layouts  11.8 us
    pallas_call x1, Pallas kernels, prepare(): pl.pallas_call(prepare_kernel, grid=(slots,), out_shape=[jax.ShapeDtypeSt...  10.1 us
  transfers between devices with their start and end apart: 25, of which 13 were waited for; matrix products, arithmetic and copies ran while one was open for 11% of the time, Pallas kernels for 5%

profile of v14, /device:TPU:1, one launch (start us, length us, event | category | flops | bytes accessed | tf_op | source)
XLA Modules:
  0.0 211.1 jit_solution(12425969120030944583)
XLA Ops:
  0.6 3.2 %fusion.3 = (f32[2,512,256]{2,1,0:T(8,128)}, f32[2,512,256]{2,1,0:T(8,128)}) fusion(f32[2,512,1024]{2,1,0:T(8,128)} %tile_hbm.1), kind=kLoop, calls=%fused_computation.24 | loop fusion | bytes 4194304 | tf_op jit(solution)/shard_map/slice | solution.py:667
  3.8 2.2 %collective-permute-start.3 = (f32[2,512,256]{2,1,0:T(8,128)}, f32[2,512,256]{2,1,0:T(8,128)}, u32[]{:S(2)}, u32[]{:S(2)}) collective-permute-start(f32[2,512,256]{2,1,0:T(8,128)} %get-tuple-element.124), channel_id=1, source_target_pairs={{4,0},{5,1},{6,2},{7,3},{8,4},{9,5},{10,6},{11,7},{12,8},{13,9},{1... | collective-permute-start | bytes 3145736 | tf_op jit(solution)/shard_map/ppermute | solution.py:597
  6.0 1.3 collective-permute-start
  7.3 1.5 slice.183
  8.9 1.9 collective-permute-start.4
  10.8 1.3 collective-permute-start.1
  12.1 1.9 collective-permute-start.2
  14.1 0.1 copy.16
  14.2 0.1 copy.17
  14.3 0.1 copy.15
  14.5 1.6 copy-done.2
  16.0 1.0 copy-done.3
  17.1 1.0 copy-done.4
  18.1 10.1 %prepare.1 = (f32[3,512,512]{2,1,0:T(8,128)S(1)}, f32[3,2,512,512]{3,2,1,0:T(8,128)S(1)}) custom-call(s32[4,3]{1,0:T(4,128)S(1)} %concatenate.18.meta, f32[3,512,512]{2,1,0:T(8,128)S(1)} %copy-done.1, f32[2,512,512]{2,1,0:T(8,128)S(1)} %copy-done.2, bf16[512,512]{1,0:T(8,128)(2,1)S(1)} %copy-done.3, bf16[512,512]{1,0:T(8,128)(2,1)S(1)} %copy-done.4), custom_call_target="tpu_custom_call" | custom-call | flops 4831838208 | bytes 18874368 | tf_op jit(solution)/shard_map/prepare/pallas_call | solution.py:561
  28.2 2.7 %copy-done.5 = f32[3,2,512,512]{3,2,1,0:T(8,128)} copy-done((f32[3,2,512,512]{3,2,1,0:T(8,128)}, f32[3,2,512,512]{3,2,1,0:T(8,128)S(1)}, u32[]{:S(2)}) %copy-start.5) | copy-done | bytes 6291480
  30.9 1.7 copy-done.6
  32.7 1.3 collective-permute-start.8
  33.9 0.7 collective-permute-done.right_a_hbm
  34.6 1.9 collective-permute-start.5
  36.5 19.9 %collective-permute-done.1.right_b_hbm = f32[2,512,256]{2,1,0:T(8,128)} collective-permute-done((f32[2,512,256]{2,1,0:T(8,128)}, f32[2,512,256]{2,1,0:T(8,128)}, u32[]{:S(2)}, u32[]{:S(2)}) %collective-permute-start.1) | collective-permute-done | bytes 1048608 | tf_op jit(solution)/shard_map/ppermute | solution.py:597
  56.5 1.3 fusion.4
  57.7 2.3 %collective-permute-start.6 = (f32[2,512,128]{2,1,0:T(8,128)S(1)}, f32[2,512,128]{2,1,0:T(8,128)S(1)}, u32[]{:S(2)}, u32[]{:S(2)}) collective-permute-start(f32[2,512,128]{2,1,0:T(8,128)S(1)} %get-tuple-element.134), channel_id=1, source_target_pairs={{4,0},{5,1},{6,2},{7,3},{12,8},{13,9},{14,10},{15,11},{20,16},{21,... | collective-permute-start | bytes 1572872 | tf_op jit(solution)/shard_map/ppermute | solution.py:597
  60.0 1.3 collective-permute-start.7
  61.3 0.1 collective-permute-done.6.corner_up_a_hbm
  61.5 1.3 collective-permute-done.7.corner_up_b_hbm
  62.8 4.8 %collective-permute-done.8.corner_side_hbm = f32[2,512,256]{2,1,0:T(8,128)S(1)} collective-permute-done((f32[2,512,256]{2,1,0:T(8,128)}, f32[2,512,256]{2,1,0:T(8,128)S(1)}, u32[]{:S(2)}, u32[]{:S(2)}) %collective-permute-start.8) | collective-permute-done | bytes 1048608 | tf_op jit(solution)/shard_map/ppermute | solution.py:597
  67.6 0.9 copy-done.12
  68.6 0.4 copy-done.13
  69.0 19.4 %slots.1 = (f32[2,512,1024]{2,1,0:T(8,128)}, f32[2,512,384]{2,1,0:T(8,128)}, f32[2,1024,128]{2,1,0:T(8,128)}, f32[2,512,768]{2,1,0:T(8,128)}, f32[2,512,256]{2,1...) custom-call(s32[4,3]{1,0:T(4,128)} %copy-done, f32[2,512,1024]{2,1,0:T(8,128)} %tile_hbm.1, ...), custom_call_target="tpu_custom_call" | custom-call | flops 9663676416 | bytes 41943040 | tf_op jit(solution)/shard_map/slots/pallas_call | solution.py:491
  88.5 15.9 %collective-permute-start.13 = (f32[2,512,384]{2,1,0:T(8,128)}, f32[2,512,384]{2,1,0:T(8,128)S(1)}, u32[]{:S(2)}, u32[]{:S(2)}) collective-permute-start(f32[2,512,384]{2,1,0:T(8,128)} %get-tuple-element.106), channel_id=1, source_target_pairs={{0,4},{1,5},{2,6},{3,7},{4,8},{5,9},{6,10},{7,11},{8,12},{9,13},{1... | collective-permute-start | bytes 4718600 | tf_op jit(solution)/shard_map/ppermute | solution.py:597
  104.4 2.3 %collective-permute-start.14 = (f32[2,1024,128]{2,1,0:T(8,128)}, f32[2,1024,128]{2,1,0:T(8,128)}, u32[]{:S(2)}, u32[]{:S(2)}) collective-permute-start(f32[2,1024,128]{2,1,0:T(8,128)} %get-tuple-element.107), channel_id=1, source_target_pairs={{0,1},{1,2},{2,3},{4,5},{5,6},{6,7},{8,9},{9,10},{10,11},{12,13},{... | collective-permute-start | bytes 3145736 | tf_op jit(solution)/shard_map/ppermute | solution.py:597
  106.6 1.0 copy-done.9
  107.6 1.7 add.133
  109.4 0.8 constant_dynamic-slice_fusion.2
  110.2 7.0 %collective-permute-start.10 = (f32[128,512]{1,0:T(8,128)}, f32[128,512]{1,0:T(8,128)S(1)}, u32[]{:S(2)}, u32[]{:S(2)}) collective-permute-start(f32[128,512]{1,0:T(8,128)} %get-tuple-element.130), channel_id=1, source_target_pairs={{0,8},{4,12},{8,16},{12,20},{16,24},{20,28},{24,0},{28,4},{1,9},{5... | collective-permute-start | bytes 786440 | tf_op jit(solution)/shard_map/ppermute | solution.py:610
  117.2 1.2 collective-permute-start.12
  118.4 12.0 %collective-permute-done.10 = f32[128,512]{1,0:T(8,128)S(1)} collective-permute-done((f32[128,512]{1,0:T(8,128)}, f32[128,512]{1,0:T(8,128)S(1)}, u32[]{:S(2)}, u32[]{:S(2)}) %collective-permute-start.10) | collective-permute-done | bytes 262176 | tf_op jit(solution)/shard_map/ppermute | solution.py:610
  130.4 7.6 %collective-permute-done.11 = f32[128,512]{1,0:T(8,128)} collective-permute-done((f32[128,512]{1,0:T(8,128)S(1)}, f32[128,512]{1,0:T(8,128)}, u32[]{:S(2)}, u32[]{:S(2)}) %collective-permute-start.11) | collective-permute-done | bytes 262176 | tf_op jit(solution)/shard_map/ppermute | solution.py:610
  138.0 0.8 collective-permute-done.12
  138.9 1.1 add_add_fusion
  140.0 1.1 copy-done.8
  141.2 1.9 collective-permute-start.18
  143.2 2.4 %collective-permute-start.15 = (f32[128,512]{1,0:T(8,128)S(1)}, f32[128,512]{1,0:T(8,128)S(1)}, u32[]{:S(2)}, u32[]{:S(2)}) collective-permute-start(f32[128,512]{1,0:T(8,128)S(1)} %add_add_fusion), channel_id=1, source_target_pairs={{0,2},{1,3},{2,0},{3,1},{4,6},{5,7},{6,4},{7,5},{8,10},{9,11},{10,... | collective-permute-start | bytes 786440 | tf_op jit(solution)/shard_map/ppermute | solution.py:610
  145.6 3.3 %collective-permute-start.17 = (f32[128,512]{1,0:T(8,128)S(1)}, f32[128,512]{1,0:T(8,128)S(1)}, u32[]{:S(2)}, u32[]{:S(2)}) collective-permute-start(f32[128,512]{1,0:T(8,128)S(1)} %add_add_fusion), channel_id=1, source_target_pairs={{0,3},{1,0},{2,1},{3,2},{4,7},{5,4},{6,5},{7,6},{8,11},{9,8},{10,9... | collective-permute-start | bytes 786440 | tf_op jit(solution)/shard_map/ppermute | solution.py:610
  148.8 3.2 %add.161 = f32[2,512,384]{2,1,0:T(8,128)} add(f32[2,512,384]{2,1,0:T(8,128)} %get-tuple-element.118, f32[2,512,384]{2,1,0:T(8,128)} %copy-done.8) | non-fusion elementwise | flops 393216 | bytes 4718592 | tf_op jit(solution)/shard_map/add | solution.py:709
  152.1 2.6 %add_dynamic-update-slice_fusion.1 = (f32[2,512,256]{2,1,0:T(8,128)}, f32[2,512,1024]{2,1,0:T(8,128)}) fusion(f32[2,512,256]{2,1,0:T(8,128)} %get-tuple-element.121, f32[2,1024,128]{2,1,0:T(8,128)} %collective-permute-done.14, f32[2,512,1024]{2,1,0:T(8,128)} %get-tuple-element.109), kind=kLoop, calls=%fused_computation.8 | loop fusion | flops 262144 | bytes 3145728 | tf_op jit(solution)/shard_map/scatter-add | solution.py:714
  154.6 8.0 %collective-permute-done.15 = f32[128,512]{1,0:T(8,128)S(1)} collective-permute-done((f32[128,512]{1,0:T(8,128)S(1)}, f32[128,512]{1,0:T(8,128)S(1)}, u32[]{:S(2)}, u32[]{:S(2)}) %collective-permute-start.15) | collective-permute-done | bytes 262176 | tf_op jit(solution)/shard_map/ppermute | solution.py:610
  162.7 0.1 add_multiply_fusion
  162.8 9.0 %collective-permute-start.23 = (f32[2,512,384]{2,1,0:T(8,128)}, f32[2,512,384]{2,1,0:T(8,128)}, u32[]{:S(2)}, u32[]{:S(2)}) collective-permute-start(f32[2,512,384]{2,1,0:T(8,128)} %add.161), channel_id=1, source_target_pairs={{0,1},{1,2},{2,3},{4,5},{5,6},{6,7},{8,9},{9,10},{10,11},{12,13},{... | collective-permute-start | bytes 4718600 | tf_op jit(solution)/shard_map/ppermute | solution.py:597
  171.7 5.9 %collective-permute-done.18 = f32[2,512,768]{2,1,0:T(8,128)S(1)} collective-permute-done((f32[2,512,768]{2,1,0:T(8,128)}, f32[2,512,768]{2,1,0:T(8,128)S(1)}, u32[]{:S(2)}, u32[]{:S(2)}) %collective-permute-start.18) | collective-permute-done | bytes 3145760 | tf_op jit(solution)/shard_map/ppermute | solution.py:597
  177.6 2.9 %collective-permute-start.19 = (f32[128,512]{1,0:T(8,128)S(1)}, f32[128,512]{1,0:T(8,128)S(1)}, u32[]{:S(2)}, u32[]{:S(2)}) collective-permute-start(f32[128,512]{1,0:T(8,128)S(1)} %add_multiply_fusion), channel_id=1, source_target_pairs={{0,8},{4,12},{8,16},{12,20},{16,24},{20,28},{24,0},{28,4},{1,9},{5... | collective-permute-start | bytes 786440 | tf_op jit(solution)/shard_map/ppermute | solution.py:610
  180.5 1.2 collective-permute-start.21
  181.7 3.3 %fusion = f32[2,512,1024]{2,1,0:T(8,128)} fusion(f32[2,512,1024]{2,1,0:T(8,128)} %get-tuple-element.114, f32[2,512,768]{2,1,0:T(8,128)S(1)} %collective-permute-done.18), kind=kLoop, calls=%fused_computation.1 | loop fusion | flops 524288 | bytes 6291456 | tf_op jit(solution)/shard_map/scatter-add | solution.py:711
  184.9 2.3 %fusion.2 = f32[2,512,1024]{2,1,0:T(8,128)} fusion(f32[2,512,1024]{2,1,0:T(8,128)} %fusion, f32[2,512,768]{2,1,0:T(8,128)S(1)} %collective-permute-done.18), kind=kLoop, calls=%fused_computation.7 | loop fusion | flops 262144 | bytes 3145728 | tf_op jit(solution)/shard_map/scatter-add | solution.py:712
  187.3 0.1 broadcast_in_dim.4
  187.5 4.9 %collective-permute-done.20 = f32[128,512]{1,0:T(8,128)S(1)} collective-permute-done((f32[128,512]{1,0:T(8,128)S(1)}, f32[128,512]{1,0:T(8,128)S(1)}, u32[]{:S(2)}, u32[]{:S(2)}) %collective-permute-start.20) | collective-permute-done | bytes 262176 | tf_op jit(solution)/shard_map/ppermute | solution.py:610
  192.4 1.1 collective-permute-start.22
  193.5 3.2 %collective-permute-start.24 = (f32[2,512,256]{2,1,0:T(8,128)}, f32[2,512,256]{2,1,0:T(8,128)S(1)}, u32[]{:S(2)}, u32[]{:S(2)}) collective-permute-start(f32[2,512,256]{2,1,0:T(8,128)} %get-tuple-element.122), channel_id=1, source_target_pairs={{0,4},{1,5},{2,6},{3,7},{4,8},{5,9},{6,10},{7,11},{8,12},{9,13},{1... | collective-permute-start | bytes 3145736 | tf_op jit(solution)/shard_map/ppermute | solution.py:597
  196.8 0.2 broadcast_select_fusion.1
  197.0 1.5 pad_maximum_fusion
  198.5 4.5 %collective-permute-done.23 = f32[2,512,384]{2,1,0:T(8,128)} collective-permute-done((f32[2,512,384]{2,1,0:T(8,128)}, f32[2,512,384]{2,1,0:T(8,128)}, u32[]{:S(2)}, u32[]{:S(2)}) %collective-permute-start.23) | collective-permute-done | bytes 1572896 | tf_op jit(solution)/shard_map/ppermute | solution.py:597
  203.0 3.2 %add_dynamic-update-slice_fusion = f32[2,512,1024]{2,1,0:T(8,128)} fusion(f32[2,512,1024]{2,1,0:T(8,128)} %fusion.2, f32[2,512,384]{2,1,0:T(8,128)} %collective-permute-done.23), kind=kLoop, calls=%fused_computation.3 | loop fusion | flops 393216 | bytes 4718592 | tf_op jit(solution)/shard_map/scatter-add | solution.py:718
  206.2 2.6 %collective-permute-done.24 = f32[2,512,256]{2,1,0:T(8,128)S(1)} collective-permute-done((f32[2,512,256]{2,1,0:T(8,128)}, f32[2,512,256]{2,1,0:T(8,128)S(1)}, u32[]{:S(2)}, u32[]{:S(2)}) %collective-permute-start.24) | collective-permute-done | bytes 1048608 | tf_op jit(solution)/shard_map/ppermute | solution.py:597
  208.8 2.3 %fusion.1 = f32[2,512,1024]{2,1,0:T(8,128)} fusion(f32[2,512,1024]{2,1,0:T(8,128)} %add_dynamic-update-slice_fusion, f32[2,512,256]{2,1,0:T(8,128)S(1)} %collective-permute-done.24), kind=kLoop, calls=%fused_computation.5 | loop fusion | flops 262144 | bytes 3145728 | tf_op jit(solution)/shard_map/scatter-add | solution.py:719
  (47 shorter events, 0.3 us)
Async XLA Ops:
  0.6 6.7 %copy-start.7 = (f32[2,512,1024]{2,1,0:T(8,128)S(1)}, f32[2,512,1024]{2,1,0:T(8,128)}, u32[]{:S(2)}) copy-start(f32[2,512,1024]{2,1,0:T(8,128)} %tile_hbm.1) | copy-start | bytes 12582916
  3.8 10.2 %copy-start.10 = (s32[3,2]{0,1:T(2,128)S(1)}, s32[3,2]{0,1:T(2,128)}, u32[]{:S(2)}) copy-start(s32[3,2]{0,1:T(2,128)} %param.26) | copy-start | bytes 76
  3.8 10.5 %copy-start.11 = (s32[3]{0:T(128)S(1)}, s32[3]{0:T(128)}, u32[]{:S(2)}) copy-start(s32[3]{0:T(128)} %param.27) | copy-start | bytes 40
  3.8 10.6 %copy-start.1 = (f32[3,512,512]{2,1,0:T(8,128)S(1)}, f32[3,512,512]{2,1,0:T(8,128)}, u32[]{:S(2)}) copy-start(f32[3,512,512]{2,1,0:T(8,128)} %amps.1) | copy-start | bytes 9437188
  3.8 28.9 %collective-permute-start.3 = (f32[2,512,256]{2,1,0:T(8,128)}, f32[2,512,256]{2,1,0:T(8,128)}, u32[]{:S(2)}, u32[]{:S(2)}) collective-permute-start(f32[2,512,256]{2,1,0:T(8,128)} %get-tuple-element.124), channel_id=1, source_target_pairs={{4,0},{5,1},{6,2},{7,3},{8,4},{9,5},{10,6},{11,7},{12,8},{13,9},{1... | collective-permute-start | bytes 3145736 | tf_op jit(solution)/shard_map/ppermute | solution.py:597
  6.0 28.6 %collective-permute-start = (f32[2,512,256]{2,1,0:T(8,128)}, f32[2,512,256]{2,1,0:T(8,128)}, u32[]{:S(2)}, u32[]{:S(2)}) collective-permute-start(f32[2,512,256]{2,1,0:T(8,128)} %get-tuple-element.125), channel_id=1, source_target_pairs={{1,0},{2,1},{3,2},{5,4},{6,5},{7,6},{9,8},{10,9},{11,10},{13,12},{... | collective-permute-start | bytes 3145736 | tf_op jit(solution)/shard_map/ppermute | solution.py:597
  8.9 58.7 %collective-permute-start.4 = (f32[2,512,512]{2,1,0:T(8,128)}, f32[2,512,512]{2,1,0:T(8,128)}, u32[]{:S(2)}, u32[]{:S(2)}) collective-permute-start(f32[2,512,512]{2,1,0:T(8,128)} %slice.183), channel_id=1, source_target_pairs={{4,0},{5,1},{6,2},{7,3},{8,4},{9,5},{10,6},{11,7},{12,8},{13,9},{1... | collective-permute-start | bytes 6291464 | tf_op jit(solution)/shard_map/ppermute | solution.py:597
  10.8 45.6 %collective-permute-start.1 = (f32[2,512,256]{2,1,0:T(8,128)}, f32[2,512,256]{2,1,0:T(8,128)}, u32[]{:S(2)}, u32[]{:S(2)}) collective-permute-start(f32[2,512,256]{2,1,0:T(8,128)} %get-tuple-element.124), channel_id=1, source_target_pairs={{1,0},{2,1},{3,2},{5,4},{6,5},{7,6},{9,8},{10,9},{11,10},{13,12},{... | collective-permute-start | bytes 3145736 | tf_op jit(solution)/shard_map/ppermute | solution.py:597
  12.1 47.9 %collective-permute-start.2 = (f32[2,512,256]{2,1,0:T(8,128)}, f32[2,512,256]{2,1,0:T(8,128)}, u32[]{:S(2)}, u32[]{:S(2)}) collective-permute-start(f32[2,512,256]{2,1,0:T(8,128)} %get-tuple-element.125), channel_id=1, source_target_pairs={{4,0},{5,1},{6,2},{7,3},{8,4},{9,5},{10,6},{11,7},{12,8},{13,9},{1... | collective-permute-start | bytes 3145736 | tf_op jit(solution)/shard_map/ppermute | solution.py:597
  14.4 1.6 copy-start.2
  16.0 1.0 copy-start.3
  17.1 1.0 copy-start.4
  18.1 10.1 %copy-start = (s32[4,3]{1,0:T(4,128)}, s32[4,3]{1,0:T(4,128)S(1)}, u32[]{:S(2)}) copy-start(s32[4,3]{1,0:T(4,128)S(1)} %concatenate.18.meta) | copy-start | bytes 148
  28.2 2.7 %copy-start.5 = (f32[3,2,512,512]{3,2,1,0:T(8,128)}, f32[3,2,512,512]{3,2,1,0:T(8,128)S(1)}, u32[]{:S(2)}) copy-start(f32[3,2,512,512]{3,2,1,0:T(8,128)S(1)} %get-tuple-element.102.pupil_hbm) | copy-start | bytes 18874372
  30.9 1.7 copy-start.6
  32.7 34.9 %collective-permute-start.8 = (f32[2,512,256]{2,1,0:T(8,128)}, f32[2,512,256]{2,1,0:T(8,128)S(1)}, u32[]{:S(2)}, u32[]{:S(2)}) collective-permute-start(f32[2,512,256]{2,1,0:T(8,128)} %collective-permute-done.3.lower_b_hbm), channel_id=1, source_target_pairs={{5,4},{6,5},{7,6},{13,12},{14,13},{15,14},{21,20},{22,21},{23,22},... | collective-permute-start | bytes 3145736 | tf_op jit(solution)/shard_map/ppermute | solution.py:597
  34.6 33.0 %collective-permute-start.5 = (f32[2,512,256]{2,1,0:T(8,128)}, f32[2,512,256]{2,1,0:T(8,128)S(1)}, u32[]{:S(2)}, u32[]{:S(2)}) collective-permute-start(f32[2,512,256]{2,1,0:T(8,128)} %collective-permute-done.right_a_hbm), channel_id=1, source_target_pairs={{4,0},{5,1},{6,2},{7,3},{8,4},{9,5},{10,6},{11,7},{12,8},{13,9},{1... | collective-permute-start | bytes 3145736 | tf_op jit(solution)/shard_map/ppermute | solution.py:597
  57.7 3.8 %collective-permute-start.6 = (f32[2,512,128]{2,1,0:T(8,128)S(1)}, f32[2,512,128]{2,1,0:T(8,128)S(1)}, u32[]{:S(2)}, u32[]{:S(2)}) collective-permute-start(f32[2,512,128]{2,1,0:T(8,128)S(1)} %get-tuple-element.134), channel_id=1, source_target_pairs={{4,0},{5,1},{6,2},{7,3},{12,8},{13,9},{14,10},{15,11},{20,16},{21,... | collective-permute-start | bytes 1572872 | tf_op jit(solution)/shard_map/ppermute | solution.py:597
  60.0 2.8 %collective-permute-start.7 = (f32[2,512,128]{2,1,0:T(8,128)S(1)}, f32[2,512,128]{2,1,0:T(8,128)S(1)}, u32[]{:S(2)}, u32[]{:S(2)}) collective-permute-start(f32[2,512,128]{2,1,0:T(8,128)S(1)} %get-tuple-element.133), channel_id=1, source_target_pairs={{4,0},{5,1},{6,2},{7,3},{12,8},{13,9},{14,10},{15,11},{20,16},{21,... | collective-permute-start | bytes 1572872 | tf_op jit(solution)/shard_map/ppermute | solution.py:597
  61.5 6.1 %copy-start.14 = (f32[2,512,128]{2,1,0:T(8,128)}, f32[2,512,128]{2,1,0:T(8,128)S(1)}, u32[]{:S(2)}) copy-start(f32[2,512,128]{2,1,0:T(8,128)S(1)} %collective-permute-done.6.corner_up_a_hbm) | copy-start | bytes 1572868
  62.8 4.8 %copy-start.15 = (f32[2,512,128]{2,1,0:T(8,128)}, f32[2,512,128]{2,1,0:T(8,128)S(1)}, u32[]{:S(2)}) copy-start(f32[2,512,128]{2,1,0:T(8,128)S(1)} %collective-permute-done.7.corner_up_b_hbm) | copy-start | bytes 1572868
  67.6 1.0 copy-start.12
  67.6 1.4 copy-start.13
  88.4 18.3 %collective-permute-start.9 = (f32[512,512]{1,0:T(8,128)}, f32[512,512]{1,0:T(8,128)S(1)}, u32[]{:S(2)}, u32[]{:S(2)}) collective-permute-start(f32[512,512]{1,0:T(8,128)} %get-tuple-element.104), channel_id=1, source_target_pairs={{0,4},{4,0},{8,12},{12,8},{16,20},{20,16},{24,28},{28,24},{1,5},{5... | collective-permute-start | bytes 3145736 | tf_op jit(solution)/shard_map/ppermute | solution.py:700
  88.5 51.6 %collective-permute-start.13 = (f32[2,512,384]{2,1,0:T(8,128)}, f32[2,512,384]{2,1,0:T(8,128)S(1)}, u32[]{:S(2)}, u32[]{:S(2)}) collective-permute-start(f32[2,512,384]{2,1,0:T(8,128)} %get-tuple-element.106), channel_id=1, source_target_pairs={{0,4},{1,5},{2,6},{3,7},{4,8},{5,9},{6,10},{7,11},{8,12},{9,13},{1... | collective-permute-start | bytes 4718600 | tf_op jit(solution)/shard_map/ppermute | solution.py:597
  104.4 35.7 %collective-permute-start.14 = (f32[2,1024,128]{2,1,0:T(8,128)}, f32[2,1024,128]{2,1,0:T(8,128)}, u32[]{:S(2)}, u32[]{:S(2)}) collective-permute-start(f32[2,1024,128]{2,1,0:T(8,128)} %get-tuple-element.107), channel_id=1, source_target_pairs={{0,1},{1,2},{2,3},{4,5},{5,6},{6,7},{8,9},{9,10},{10,11},{12,13},{... | collective-permute-start | bytes 3145736 | tf_op jit(solution)/shard_map/ppermute | solution.py:597
  106.6 1.0 copy-start.9
  110.2 20.3 %collective-permute-start.10 = (f32[128,512]{1,0:T(8,128)}, f32[128,512]{1,0:T(8,128)S(1)}, u32[]{:S(2)}, u32[]{:S(2)}) collective-permute-start(f32[128,512]{1,0:T(8,128)} %get-tuple-element.130), channel_id=1, source_target_pairs={{0,8},{4,12},{8,16},{12,20},{16,24},{20,28},{24,0},{28,4},{1,9},{5... | collective-permute-start | bytes 786440 | tf_op jit(solution)/shard_map/ppermute | solution.py:610
  117.2 20.8 %collective-permute-start.11 = (f32[128,512]{1,0:T(8,128)S(1)}, f32[128,512]{1,0:T(8,128)}, u32[]{:S(2)}, u32[]{:S(2)}) collective-permute-start(f32[128,512]{1,0:T(8,128)S(1)} %get-tuple-element.132), channel_id=1, source_target_pairs={{0,16},{4,20},{8,24},{12,28},{16,0},{20,4},{24,8},{28,12},{1,17},{... | collective-permute-start | bytes 786440 | tf_op jit(solution)/shard_map/ppermute | solution.py:610
  117.2 21.7 %collective-permute-start.12 = (f32[128,512]{1,0:T(8,128)S(1)}, f32[128,512]{1,0:T(8,128)}, u32[]{:S(2)}, u32[]{:S(2)}) collective-permute-start(f32[128,512]{1,0:T(8,128)S(1)} %get-tuple-element.131), channel_id=1, source_target_pairs={{0,24},{4,28},{8,0},{12,4},{16,8},{20,12},{24,16},{28,20},{1,25},{... | collective-permute-start | bytes 786440 | tf_op jit(solution)/shard_map/ppermute | solution.py:610
  140.0 1.2 copy-start.8
  141.2 36.4 %collective-permute-start.18 = (f32[2,512,768]{2,1,0:T(8,128)}, f32[2,512,768]{2,1,0:T(8,128)S(1)}, u32[]{:S(2)}, u32[]{:S(2)}) collective-permute-start(f32[2,512,768]{2,1,0:T(8,128)} %get-tuple-element.112), channel_id=1, source_target_pairs={{0,4},{1,5},{2,6},{3,7},{4,8},{5,9},{6,10},{7,11},{8,12},{9,13},{1... | collective-permute-start | bytes 9437192 | tf_op jit(solution)/shard_map/ppermute | solution.py:597
  143.2 19.5 %collective-permute-start.15 = (f32[128,512]{1,0:T(8,128)S(1)}, f32[128,512]{1,0:T(8,128)S(1)}, u32[]{:S(2)}, u32[]{:S(2)}) collective-permute-start(f32[128,512]{1,0:T(8,128)S(1)} %add_add_fusion), channel_id=1, source_target_pairs={{0,2},{1,3},{2,0},{3,1},{4,6},{5,7},{6,4},{7,5},{8,10},{9,11},{10,... | collective-permute-start | bytes 786440 | tf_op jit(solution)/shard_map/ppermute | solution.py:610
  145.6 17.1 %collective-permute-start.16 = (f32[128,512]{1,0:T(8,128)S(1)}, f32[128,512]{1,0:T(8,128)S(1)}, u32[]{:S(2)}, u32[]{:S(2)}) collective-permute-start(f32[128,512]{1,0:T(8,128)S(1)} %add_add_fusion), channel_id=1, source_target_pairs={{0,1},{1,2},{2,3},{3,0},{4,5},{5,6},{6,7},{7,4},{8,9},{9,10},{10,1... | collective-permute-start | bytes 786440 | tf_op jit(solution)/shard_map/ppermute | solution.py:610
  145.6 17.1 %collective-permute-start.17 = (f32[128,512]{1,0:T(8,128)S(1)}, f32[128,512]{1,0:T(8,128)S(1)}, u32[]{:S(2)}, u32[]{:S(2)}) collective-permute-start(f32[128,512]{1,0:T(8,128)S(1)} %add_add_fusion), channel_id=1, source_target_pairs={{0,3},{1,0},{2,1},{3,2},{4,7},{5,4},{6,5},{7,6},{8,11},{9,8},{10,9... | collective-permute-start | bytes 786440 | tf_op jit(solution)/shard_map/ppermute | solution.py:610
  162.8 40.3 %collective-permute-start.23 = (f32[2,512,384]{2,1,0:T(8,128)}, f32[2,512,384]{2,1,0:T(8,128)}, u32[]{:S(2)}, u32[]{:S(2)}) collective-permute-start(f32[2,512,384]{2,1,0:T(8,128)} %add.161), channel_id=1, source_target_pairs={{0,1},{1,2},{2,3},{4,5},{5,6},{6,7},{8,9},{9,10},{10,11},{12,13},{... | collective-permute-start | bytes 4718600 | tf_op jit(solution)/shard_map/ppermute | solution.py:597
  177.6 9.8 %collective-permute-start.19 = (f32[128,512]{1,0:T(8,128)S(1)}, f32[128,512]{1,0:T(8,128)S(1)}, u32[]{:S(2)}, u32[]{:S(2)}) collective-permute-start(f32[128,512]{1,0:T(8,128)S(1)} %add_multiply_fusion), channel_id=1, source_target_pairs={{0,8},{4,12},{8,16},{12,20},{16,24},{20,28},{24,0},{28,4},{1,9},{5... | collective-permute-start | bytes 786440 | tf_op jit(solution)/shard_map/ppermute | solution.py:610
  180.5 11.9 %collective-permute-start.20 = (f32[128,512]{1,0:T(8,128)S(1)}, f32[128,512]{1,0:T(8,128)S(1)}, u32[]{:S(2)}, u32[]{:S(2)}) collective-permute-start(f32[128,512]{1,0:T(8,128)S(1)} %add_multiply_fusion), channel_id=1, source_target_pairs={{0,16},{4,20},{8,24},{12,28},{16,0},{20,4},{24,8},{28,12},{1,17},{... | collective-permute-start | bytes 786440 | tf_op jit(solution)/shard_map/ppermute | solution.py:610
  180.5 11.9 %collective-permute-start.21 = (f32[128,512]{1,0:T(8,128)S(1)}, f32[128,512]{1,0:T(8,128)S(1)}, u32[]{:S(2)}, u32[]{:S(2)}) collective-permute-start(f32[128,512]{1,0:T(8,128)S(1)} %add_multiply_fusion), channel_id=1, source_target_pairs={{0,24},{4,28},{8,0},{12,4},{16,8},{20,12},{24,16},{28,20},{1,25},{... | collective-permute-start | bytes 786440 | tf_op jit(solution)/shard_map/ppermute | solution.py:610
  192.4 4.3 %collective-permute-start.22 = (f32[512,512]{1,0:T(8,128)S(1)}, f32[512,512]{1,0:T(8,128)S(1)}, u32[]{:S(2)}, u32[]{:S(2)}) collective-permute-start(f32[512,512]{1,0:T(8,128)S(1)} %constant_dynamic-update-slice_fusion), channel_id=1, source_target_pairs={{0,4},{4,0},{8,12},{12,8},{16,20},{20,16},{24,28},{28,24},{1,5},{5... | collective-permute-start | bytes 3145736 | tf_op jit(solution)/shard_map/ppermute | solution.py:602
  193.5 15.3 %collective-permute-start.24 = (f32[2,512,256]{2,1,0:T(8,128)}, f32[2,512,256]{2,1,0:T(8,128)S(1)}, u32[]{:S(2)}, u32[]{:S(2)}) collective-permute-start(f32[2,512,256]{2,1,0:T(8,128)} %get-tuple-element.122), channel_id=1, source_target_pairs={{0,4},{1,5},{2,6},{3,7},{4,8},{5,9},{6,10},{7,11},{8,12},{9,13},{1... | collective-permute-start | bytes 3145736 | tf_op jit(solution)/shard_map/ppermute | solution.py:597
